TPU v7x, 256 devices: a whole 4x4x8 slice. The times are simulated.
256 devices in a mesh: row: 32 (over z, x), col: 8 (over y, core).
Axes of the slice: x: 4, y: 4, z: 8, core: 2. Of those that a mesh axis runs over, the one named last changes fastest.
Arguments:
- solution_field: float32 [32, 262144], P(None, ('row', 'col')), may hold values from -6 to 6
- residual: float32 [32, 262144], P(None, ('row', 'col')), may hold values from -420 to 420
- direction: float32 [32, 262144], P(None, ('row', 'col')), may hold values from -420 to 420
- positions: bfloat16 [2, 262144], P(None, ('row', 'col')), may hold values from -6 to 6
- tile_pairs: int32 [2, 393216], P(None, ('row', 'col')), may hold values from 0 to 255, as said below
- pair_count: int32 [256], P(('row', 'col')), may hold values from 0 to 1536, as said below
Outputs:
- solution_next: float32 [32, 262144], P(None, ('row', 'col'))
- residual_next: float32 [32, 262144], P(None, ('row', 'col'))
- direction_next: float32 [32, 262144], P(None, ('row', 'col'))
Inputs may be any that keep to these rules, and one draw needn't show every extreme that they name: `tile_pairs`: row 0 holds local row tiles below 64, row 1 local column tiles below 256. The live pairs of one slot block are distinct and strictly upper (I < J); entries in slots that are not live are in range but carry nothing. `pair_count`: some slot block is full in every draw.
All inputs are finite; a program needn't handle non-finite values.
Results may differ from a plain program's by a relative error of at most 0.007.
Values may be sent and summed in bfloat16 or wider, within the bound.
No kernel may reach another device: no remote copies, remote signals or barrier semaphores. Data moves between devices by JAX's collectives and lax.ppermute only.
A program may use at most 64 MiB of HBM per device.

v0:
```python
import math

import jax
import jax.numpy as jnp
from jax import lax
from jax.sharding import PartitionSpec as P

TILE = 128


AMPLITUDE = 0.025
NUGGET = 2.0
RADIUS = 1.0
HIGHEST = lax.Precision.HIGHEST


def kernel_tile(near_side, far_side):
    differ = near_side[..., :, None] - far_side[..., None, :]
    distance = jnp.sqrt(jnp.sum(differ * differ, axis=0)) / RADIUS
    remain = jnp.maximum(1.0 - distance, 0.0)
    return AMPLITUDE * remain**4 * (4.0 * distance + 1.0)


def cross_gram_matrix(former, latter):
    return lax.dot_general(
        former,
        latter,
        (((1,), (1,)), ((), ())),
        precision=HIGHEST,
        preferred_element_type=jnp.float32,
    )


def apply_left(matrix, vectors):
    return jnp.dot(matrix.T, vectors, precision=HIGHEST)


def symmetric_solve(matrix, target):
    balanced = 0.5 * (matrix + matrix.T)
    factor = jnp.linalg.cholesky(balanced)
    middle = lax.linalg.triangular_solve(factor, target, left_side=True, lower=True)
    return lax.linalg.triangular_solve(factor, middle, left_side=True, lower=True, transpose_a=True)


def on_device(solution_field, residual, direction, positions, tile_pairs, pair_count):
    probes, own_points = direction.shape
    own_tiles = own_points // TILE
    dir_half = direction.astype(jnp.bfloat16)
    row_dir, row_pos = (
        lax.all_gather(dir_half, "col", axis=1, tiled=True),
        lax.all_gather(positions, "col", axis=1, tiled=True),
    )
    col_dir, col_pos = (
        lax.all_gather(dir_half, "row", axis=1, tiled=True),
        lax.all_gather(positions, "row", axis=1, tiled=True),
    )
    own_pos = positions.astype(jnp.float32).reshape(2, own_tiles, TILE)
    diagonal = kernel_tile(own_pos, own_pos).astype(jnp.bfloat16)
    own_product = jnp.einsum(
        "npq,knq->knp",
        diagonal,
        dir_half.reshape(probes, own_tiles, TILE),
        preferred_element_type=jnp.float32,
    ).reshape(probes, own_points)
    row_tiles = row_dir.shape[1] // TILE
    col_tiles = col_dir.shape[1] // TILE
    row_vector = row_dir.reshape(probes, row_tiles, TILE)
    column_vector = col_dir.reshape(probes, col_tiles, TILE)
    row_coord = row_pos.reshape(2, row_tiles, TILE)
    col_coord = col_pos.reshape(2, col_tiles, TILE)
    row_range = jnp.arange(row_tiles, dtype=jnp.int32)
    col_range = jnp.arange(col_tiles, dtype=jnp.int32)
    slot_total = tile_pairs.shape[1]
    block_size = math.gcd(slot_total, 64)
    live_count = pair_count[0]

    def stepped(block_no, running_totals):
        row_acc, col_acc = running_totals
        first_slot = block_no * block_size
        row_index = lax.dynamic_slice_in_dim(tile_pairs[0], first_slot, block_size)
        col_index = lax.dynamic_slice_in_dim(tile_pairs[1], first_slot, block_size)
        live_mask = first_slot + jnp.arange(block_size, dtype=jnp.int32) < live_count
        row_chosen_index = (row_index[:, None] == row_range[None, :]).astype(jnp.bfloat16)
        column_chosen_index = (col_index[:, None] == col_range[None, :]).astype(jnp.bfloat16)
        near_side = jnp.einsum(
            "bt,ctq->cbq", row_chosen_index, row_coord, preferred_element_type=jnp.float32
        )
        far_side = jnp.einsum(
            "bt,ctq->cbq", column_chosen_index, col_coord, preferred_element_type=jnp.float32
        )
        row_sel = jnp.einsum(
            "di,siz->sdz", row_chosen_index, row_vector, preferred_element_type=jnp.float32
        ).astype(jnp.bfloat16)
        col_sel = jnp.einsum(
            "di,siz->sdz", column_chosen_index, column_vector, preferred_element_type=jnp.float32
        ).astype(jnp.bfloat16)
        kernel_block = kernel_tile(near_side, far_side)
        kernel_block = jnp.where(live_mask[:, None, None], kernel_block, 0.0).astype(jnp.bfloat16)
        forward_step = jnp.einsum(
            "bpq,kbq->kbp", kernel_block, col_sel, preferred_element_type=jnp.float32
        )
        backward = jnp.einsum(
            "bpq,kbp->kbq", kernel_block, row_sel, preferred_element_type=jnp.float32
        )
        row_add = jnp.einsum(
            "bt,kbp->ktp",
            row_chosen_index.astype(jnp.float32),
            forward_step,
            precision=HIGHEST,
            preferred_element_type=jnp.float32,
        )
        col_add = jnp.einsum(
            "au,lax->lux",
            column_chosen_index.astype(jnp.float32),
            backward,
            precision=HIGHEST,
            preferred_element_type=jnp.float32,
        )
        return (row_acc + row_add, col_acc + col_add)

    start_totals = (
        jnp.zeros((probes, row_tiles, TILE), jnp.float32),
        jnp.zeros((probes, col_tiles, TILE), jnp.float32),
    )
    row_acc, col_acc = lax.fori_loop(0, slot_total // block_size, stepped, start_totals)
    row_flat = row_acc.reshape(probes, row_tiles * TILE)
    col_flat = col_acc.reshape(probes, col_tiles * TILE)
    row_whole = lax.psum(row_flat.astype(jnp.bfloat16), "col").astype(jnp.float32)
    row_part = lax.dynamic_slice_in_dim(
        row_whole, lax.axis_index("col") * own_points, own_points, 1
    )
    col_whole = lax.psum(col_flat.astype(jnp.bfloat16), "row").astype(jnp.float32)
    col_part = lax.dynamic_slice_in_dim(
        col_whole, lax.axis_index("row") * own_points, own_points, 1
    )
    applied = NUGGET * direction + own_product + row_part + col_part
    curvature, crossing, norm_old = lax.psum(
        (
            cross_gram_matrix(direction, applied),
            cross_gram_matrix(direction, residual),
            cross_gram_matrix(residual, residual),
        ),
        ("row", "col"),
    )
    step_size = symmetric_solve(curvature, crossing)
    residual_next = residual - apply_left(step_size, applied)
    norm_new = lax.psum(cross_gram_matrix(residual_next, residual_next), ("row", "col"))
    solution_next = solution_field + apply_left(step_size, direction)
    mix_weight = symmetric_solve(norm_old, norm_new)
    direction_next = residual_next + apply_left(mix_weight, direction)
    return (solution_next, residual_next, direction_next)


def solution(mesh):
    in_specs = (
        P(None, ("row", "col")),
        P(None, ("row", "col")),
        P(None, ("row", "col")),
        P(None, ("row", "col")),
        P(None, ("row", "col")),
        P(("row", "col")),
    )
    out_specs = (P(None, ("row", "col")), P(None, ("row", "col")), P(None, ("row", "col")))
    return jax.shard_map(
        on_device, mesh=mesh, in_specs=in_specs, out_specs=out_specs, check_vma=False
    )
```

profile of v0, /device:TPU:16, one launch (start us, length us, event | category | flops | bytes accessed | tf_op | source)
XLA Modules:
  0.0 935.4 jit_solution(9719922890757837557)
XLA Ops:
  8.9 13.0 %all_gather.13 = bf16[2,8192]{1,0:T(2,128)(2,1)S(1)} all-gather(bf16[2,1024]{1,0:T(2,128)(2,1)} %param.16), channel_id=1, replica_groups=mesh['row'=32,'col'=8] {'col'}, dimensions={1}, use_global_device_ids=true | all-gather | bytes 36864 | tf_op jit(solution)/shard_map/all_gather | solution.py:51
  21.8 45.1 %all_gather.14 = bf16[2,32768]{1,0:T(2,128)(2,1)S(1)} all-gather(bf16[2,1024]{1,0:T(2,128)(2,1)} %param.16), channel_id=1, replica_groups=mesh['row'=32,'col'=8] {'row'}, dimensions={1}, use_global_device_ids=true | all-gather | bytes 135168 | tf_op jit(solution)/shard_map/all_gather | solution.py:55
  67.0 13.4 %all_gather.15 = bf16[32,8192]{1,0:T(8,128)(2,1)S(1)} all-gather(bf16[32,1024]{1,0:T(8,128)(2,1)} %convert_element_type.65), channel_id=1, replica_groups=mesh['row'=32,'col'=8] {'col'}, dimensions={1}, use_global_device_ids=true | all-gather | bytes 589824 | tf_op jit(solution)/shard_map/all_gather | solution.py:50
  81.3 10.7 %all-gather.2.cloned.1.call-done = bf16[32,32768]{1,0:T(8,128)(2,1)} async-done(((bf16[32,1024]{1,0:T(8,128)(2,1)}), bf16[32,32768]{1,0:T(8,128)(2,1)}) %all-gather.2.cloned.1.call-update) | async-done | bytes 2097168 | tf_op jit(solution)/shard_map/all_gather | solution.py:54
  95.4 445.1 %while.16 = (s32[]{:T(128)}, f32[32,64,128]{2,1,0:T(8,128)}, f32[32,256,128]{1,2,0:T(8,128)}, s32[2,1536]{1,0:T(2,128)S(1)}, bf16[32,256,128]{2,1,0:T(8,128)(2,1...) while((s32[]{:T(128)}, f32[32,64,128]{2,1,0:T(8,128)}, ...), condition=%wide.region_3.4_spmd.clone, body=%wide.region_1.3_spmd.clone.sunk | while | flops 1338044544 | bytes 76475288 | solution.py:125
  120.9 3.8 fusion.117
  139.5 3.8 fusion.117
  158.1 3.8 fusion.117
  176.7 3.8 fusion.117
  195.3 3.8 fusion.117
  213.9 3.8 fusion.117
  232.5 3.8 fusion.117
  269.7 3.8 fusion.117
  288.3 3.8 fusion.117
  306.9 3.8 fusion.117
  344.1 3.8 fusion.117
  362.7 3.8 fusion.117
  381.3 3.8 fusion.117
  399.9 3.8 fusion.117
  548.6 4.3 copy.70
  554.2 48.0 %all-reduce.5.cloned.1.call-done = bf16[32,8192]{1,0:T(8,128)(2,1)} async-done(((bf16[32,8192]{1,0:T(8,128)(2,1)}), bf16[32,8192]{1,0:T(8,128)(2,1)}) %all-reduce.5.cloned.1.call-update) | async-done | bytes 524304 | tf_op jit(solution)/shard_map/psum | solution.py:128
  602.2 161.6 %all-reduce.7.cloned.1.call-done = bf16[32,32768]{1,0:T(8,128)(2,1)} async-done(((bf16[32,32768]{1,0:T(8,128)(2,1)}), bf16[32,32768]{1,0:T(8,128)(2,1)}) %all-reduce.7.cloned.1.call-update) | async-done | bytes 2097168 | tf_op jit(solution)/shard_map/psum | solution.py:132
  764.9 72.3 %all-reduce.1 = (f32[32,32]{1,0:T(8,128)S(1)}, f32[32,32]{1,0:T(8,128)S(1)}) all-reduce(f32[32,32]{1,0:T(8,128)S(1)} %fusion.54, f32[32,32]{1,0:T(8,128)S(1)} %convolution_bitcast_fusion.6), channel_id=1, replica_groups=mesh['row'=32,'col'=8] {'row','col'}, use_global_device_ids=true, to_apply=%region_9.11 | all-reduce | flops 2048 | bytes 16384 | tf_op jit(solution)/shard_map/psum | solution.py:137
  846.9 73.8 %all-reduce = (f32[32,32]{1,0:T(8,128)S(1)}, f32[32,32]{1,0:T(8,128)S(1)}) all-reduce(f32[32,32]{1,0:T(8,128)S(1)} %fusion.56, f32[32,32]{1,0:T(8,128)S(1)} %fusion.55), channel_id=1, replica_groups=mesh['row'=32,'col'=8] {'row','col'}, use_global_device_ids=true, to_apply=%region_11.15 | all-reduce | flops 2048 | bytes 16384 | tf_op jit(solution)/shard_map/psum | solution.py:147
  (504 shorter events, 423.8 us)
Async XLA Ops:
  7.2 88.2 %copy-start.6 = (s32[2,1536]{1,0:T(2,128)S(1)}, s32[2,1536]{1,0:T(2,128)}, u32[]{:S(2)}) copy-start(s32[2,1536]{1,0:T(2,128)} %param.17) | copy-start | bytes 36868
  7.2 84.8 %all-gather.2.cloned.1.call-start = ((), (), s32[]{:S(2)}) async-start(), calls=%async_computation | async-start | bytes 2162688 | tf_op jit(solution)/shard_map/all_gather | solution.py:54
  8.8 593.4 %all-reduce.5.cloned.1.call-start = ((), (), s32[]{:S(2)}) async-start(), calls=%async_computation.1 | async-start | bytes 1048576 | tf_op jit(solution)/shard_map/psum | solution.py:128
  120.9 5.9 copy-start
  139.5 5.9 copy-start
  158.1 5.9 copy-start
  176.7 5.9 copy-start
  195.3 5.9 copy-start
  213.9 5.9 copy-start
  232.5 5.9 copy-start
  251.1 5.9 copy-start
  269.7 5.9 copy-start
  288.3 5.9 copy-start
  306.9 5.9 copy-start
  325.5 5.9 copy-start
  344.1 5.9 copy-start
  381.3 5.9 copy-start
  399.9 5.9 copy-start
  455.7 5.9 copy-start
  474.3 5.9 copy-start
  530.1 5.9 copy-start
  542.9 220.8 %all-reduce.7.cloned.1.call-start = ((), (), s32[]{:S(2)}) async-start(), calls=%async_computation.2 | async-start | bytes 4194304 | tf_op jit(solution)/shard_map/psum | solution.py:132
  548.5 295.9 %copy-start.7 = (f32[32,1024]{1,0:T(8,128)S(1)}, f32[32,1024]{1,0:T(8,128)}, u32[]{:S(2)}) copy-start(f32[32,1024]{1,0:T(8,128)} %param.13) | copy-start | bytes 393220
  846.6 82.3 %copy-start.5 = (f32[32,1024]{1,0:T(8,128)}, f32[32,1024]{1,0:T(8,128)S(1)}, u32[]{:S(2)}) copy-start(f32[32,1024]{1,0:T(8,128)S(1)} %convolution_subtract_fusion) | copy-start | bytes 393220
  (57 other events, 173.2 us)
Sparse Core Ops, SparseCore 0:
  11.2 80.7 all-gather.1
  543.0 59.0 all-reduce.4
  606.1 157.5 all-reduce.6
where the time goes:
time: 940 us; the launch traced here: 935 us
  matrix products  256 us (27%)
  waiting for transfers between devices  220 us (23%)
  blocking collectives  218 us (23%)
  other arithmetic  164 us (17%)
  local copies, waits for them, and re-layouts  61.3 us (7%)
  between operations  14 us (1%)
    psum x1, waiting for transfers between devices, on_device(): lax.psum(col_flat.astype(jnp.bfloat16), 'row').astype(jnp.float32)  162 us
    dot_general x24, matrix products, stepped(): jnp.einsum('bt,kbp->ktp', row_chosen_index.astype(jnp.float32), forward_s...  90.4 us
    psum x1, blocking collectives, on_device(): lax.psum(cross_gram_matrix(residual_next, residual_next), ('row', 'col'))  73.8 us
    psum x1, blocking collectives, on_device(): lax.psum((cross_gram_matrix(direction, applied), cross_gram_matrix(direct...  72.3 us
    reduce_sum x25, other arithmetic, kernel_tile(): distance = jnp.sqrt(jnp.sum(differ * differ, axis=0)) / RADIUS  66.6 us
    dot_general x24, matrix products, stepped(): jnp.einsum('au,lax->lux', column_chosen_index.astype(jnp.float32), backwa...  59.7 us
    convert_element_type x24, other arithmetic, stepped(): jnp.where(live_mask[:, None, None], kernel_block, 0.0).astype(jnp.bfloat16)  59 us
    psum x1, waiting for transfers between devices, on_device(): lax.psum(row_flat.astype(jnp.bfloat16), 'col').astype(jnp.float32)  48 us
  transfers between devices with their start and end apart: 3, of which 3 were waited for; matrix products, arithmetic and copies ran while one was open for 1% of the time, Pallas kernels for 0%

commit v1 on v0

v1 whole, which is shorter than its diff:
```python
import functools

import jax
import jax.numpy as jnp
import numpy as np
from jax import lax
from jax.experimental import pallas as pl
from jax.experimental.pallas import tpu as pltpu
from jax.sharding import Mesh
from jax.sharding import PartitionSpec as P

TILE = 128
PROBES = 32
UNROLL = 16
NUGGET = 2.0
KERNEL_SCALE = 0.1
HIGHEST = lax.Precision.HIGHEST
f32, bf16 = jnp.float32, jnp.bfloat16
VMEM = pl.BlockSpec(memory_space=pltpu.VMEM)
SMEM = pl.BlockSpec(memory_space=pltpu.SMEM)
NT = (((1,), (1,)), ((), ()))
NN = (((1,), (0,)), ((), ()))
TN = (((0,), (0,)), ((), ()))
PARAMS = pltpu.CompilerParams(vmem_limit_bytes=48 * 2**20)


def pack_kernel(direction_ref, positions_ref, packed_ref):
    for t in range(8):
        packed_ref[t * 32 : (t + 1) * 32, :] = direction_ref[:, t * TILE : (t + 1) * TILE].astype(bf16)
    where = positions_ref[...].astype(f32)
    rows = [where[d : d + 1, t * TILE : (t + 1) * TILE] for d in range(2) for t in range(8)]
    packed_ref[256:272, :] = jnp.concatenate(rows, 0).astype(bf16)


def radial(square):
    distance = pl.reciprocal(lax.rsqrt(square), approx=True)
    remain = jnp.maximum(1.0 - distance, 0.0)
    remain2 = remain * remain
    return ((remain2 * remain2) * (1.25 - remain)).astype(bf16)


def pair_kernel(place_ref, pairs_ref, own_ref, row_ref, col_ref, row_out, col_out, own_out, px, py, qx, qy, row_acc, col_acc):
    live, y_own, core_own = place_ref[0], place_ref[1], place_ref[2]
    row_acc[...] = jnp.zeros_like(row_acc)
    col_acc[...] = jnp.zeros_like(col_acc)

    def col_prepare(r, carry):
        where = col_ref[r, 256:272, :].astype(f32)
        for t in range(8):
            qx[r * 8 + t] = jnp.broadcast_to(where[t : t + 1], (8, TILE))
            qy[r * 8 + t] = jnp.broadcast_to(where[8 + t : 9 + t], (8, TILE))
        return carry

    lax.fori_loop(0, 32, col_prepare, 0)

    def spread(line):
        return jnp.broadcast_to(line, (TILE, TILE)).T

    def row_prepare(r, carry):
        where = row_ref[r, 256:272, :].astype(f32)
        for t in range(8):
            px[r * 8 + t] = spread(where[t : t + 1])
            py[r * 8 + t] = spread(where[8 + t : 9 + t])
        return carry

    lax.fori_loop(0, 8, row_prepare, 0)

    where = own_ref[256:272, :].astype(f32)
    for t in range(8):
        dx = spread(where[t : t + 1]) - where[t : t + 1]
        dy = spread(where[8 + t : 9 + t]) - where[8 + t : 9 + t]
        block = radial(dx * dx + dy * dy)
        own_out[:, t * TILE : (t + 1) * TILE] = KERNEL_SCALE * lax.dot_general(
            own_ref[t * 32 : (t + 1) * 32, :], block, NT, preferred_element_type=f32
        )

    def body(i, carry):
        results = []
        for u in range(UNROLL):
            e = i * UNROLL + u
            a, b = pairs_ref[0, e], pairs_ref[1, e]
            keep = jnp.where(e < live, 1.0, 0.0).astype(bf16)
            shift = (y_own - (a >> 4)) & 3
            slot = shift + 4 * (((a >> 3) & 1) ^ core_own)
            tile = slot * 8 + (a & 7)
            near = row_ref[slot, pl.ds(pl.multiple_of((a & 7) * 32, 32), 32), :] * keep
            far = col_ref[b >> 3, pl.ds(pl.multiple_of((b & 7) * 32, 32), 32), :] * keep
            dx = px[tile].reshape(16, 8, TILE) - qx[b][None]
            dy = py[tile].reshape(16, 8, TILE) - qy[b][None]
            block = radial((dx * dx + dy * dy).reshape(TILE, TILE))
            forward = lax.dot_general(far, block, NT, preferred_element_type=f32)
            backward = lax.dot_general(near, block, NN, preferred_element_type=f32)
            results.append((tile, b, forward, backward))
        for tile, b, forward, backward in results:
            row_acc[tile] += forward
            col_acc[b] += backward
        return carry

    lax.fori_loop(0, (live + UNROLL - 1) // UNROLL, body, 0)

    def finish(out, acc):
        def step(r, carry):
            for t in range(8):
                out[r, t * 32 : (t + 1) * 32, :] = (KERNEL_SCALE * acc[r * 8 + t]).astype(bf16)
            return carry

        lax.fori_loop(0, out.shape[0], step, 0)

    finish(row_out, row_acc)
    finish(col_out, col_acc)


def dot32(former, latter, dims):
    return lax.dot_general(former, latter, dims, precision=HIGHEST, preferred_element_type=f32)


def gram_kernel(direction_ref, residual_ref, own_ref, row_ref, col_ref, image_ref, gram_ref):
    for t in range(8):
        here = slice(t * 32, (t + 1) * 32)
        lanes = slice(t * TILE, (t + 1) * TILE)
        total = NUGGET * direction_ref[:, lanes] + own_ref[:, lanes]
        for part in range(row_ref.shape[0]):
            total = total + row_ref[part, here, :].astype(f32)
        for part in range(col_ref.shape[0]):
            total = total + col_ref[part, here, :].astype(f32)
        image_ref[:, lanes] = total
    direction, residual, image = direction_ref[...], residual_ref[...], image_ref[...]
    gram_ref[0:32, 0:32] = dot32(direction, image, NT)
    gram_ref[0:32, 32:64] = dot32(direction, residual, NT)
    gram_ref[0:32, 64:96] = dot32(residual, residual, NT)
    gram_ref[0:32, 96:128] = dot32(residual, image, NT)
    square = dot32(image, image, NT)
    for t in range(4):
        gram_ref[32:40, t * 32 : (t + 1) * 32] = square[t * 8 : (t + 1) * 8]


def solve_kernel(gram_ref, solution_ref, residual_ref, direction_ref, image_ref, solution_out, residual_out, direction_out):
    gram = gram_ref[...]
    curvature, crossing = gram[0:32, 0:32], gram[0:32, 32:64]
    norm_old, mixed = gram[0:32, 64:96], gram[0:32, 96:128]
    square = jnp.concatenate([gram[32:40, t * 32 : (t + 1) * 32] for t in range(4)], 0)
    row = lax.broadcasted_iota(jnp.int32, (32, 64), 0)
    lane = lax.broadcasted_iota(jnp.int32, (32, 64), 1)
    unit = jnp.where(row[:, :32] == lane[:, :32], 1.0, 0.0).astype(f32)
    first = jnp.concatenate([0.5 * (curvature + curvature.T), crossing], 1)
    second = jnp.concatenate([0.5 * (norm_old + norm_old.T), unit], 1)

    def eliminate(table, k):
        pivot_row = table[k : k + 1, :] / table[k : k + 1, k : k + 1]
        return jnp.where(row == k, pivot_row, table - table[:, k : k + 1] * pivot_row)

    for k in range(32):
        first, second = eliminate(first, k), eliminate(second, k)
    alpha, inverse = first[:, 32:64], second[:, 32:64]
    cross = dot32(mixed, alpha, NN)
    norm_new = 0.5 * (norm_old + norm_old.T) - cross - cross.T + dot32(alpha, dot32(square, alpha, NN), TN)
    beta = dot32(inverse, norm_new, NN)
    direction = direction_ref[...]
    residual_next = residual_ref[...] - dot32(alpha, image_ref[...], TN)
    residual_out[...] = residual_next
    solution_out[...] = solution_ref[...] + dot32(alpha, direction, TN)
    direction_out[...] = residual_next + dot32(beta, direction, TN)


def shifts(value, axis, size):
    return [lax.ppermute(value, axis, [(i, (i + k) % size) for i in range(size)]) for k in range(1, size)]


def swap(value):
    return lax.ppermute(value, "core", [(0, 1), (1, 0)])


def on_device(solution_field, residual, direction, positions, tile_pairs, pair_count):
    shape = jax.ShapeDtypeStruct
    own_points = direction.shape[1]
    y_own, core_own = lax.axis_index("y"), lax.axis_index("core")
    packed = pl.pallas_call(
        pack_kernel, out_shape=shape((272, TILE), bf16), in_specs=[VMEM] * 2, out_specs=VMEM, name="pack"
    )(direction, positions)
    row_half = jnp.stack([packed] + shifts(packed, "y", 4))
    row_all = jnp.concatenate([row_half, swap(row_half)], 0)
    col_all = lax.all_gather(lax.all_gather(packed, "x"), "z").reshape(32, 272, TILE)
    place = jnp.stack([pair_count[0], y_own, core_own]).astype(jnp.int32)
    row_sum, col_sum, own_product = pl.pallas_call(
        pair_kernel,
        out_shape=(shape((8, 256, TILE), bf16), shape((32, 256, TILE), bf16), shape((PROBES, own_points), f32)),
        in_specs=[SMEM, SMEM, VMEM, VMEM, VMEM],
        out_specs=(VMEM, VMEM, VMEM),
        scratch_shapes=[
            pltpu.VMEM((64, TILE, TILE), f32),
            pltpu.VMEM((64, TILE, TILE), f32),
            pltpu.VMEM((256, 8, TILE), f32),
            pltpu.VMEM((256, 8, TILE), f32),
            pltpu.VMEM((64, PROBES, TILE), f32),
            pltpu.VMEM((256, PROBES, TILE), f32),
        ],
        compiler_params=PARAMS,
        name="pairs",
    )(place, tile_pairs, packed, row_all, col_all)
    half = row_sum[:4].astype(f32) + swap(row_sum[4:]).astype(f32)
    half = half.astype(bf16)
    row_parts = [half[0]] + [
        lax.ppermute(half[k], "y", [(i, (i - k) % 4) for i in range(4)]) for k in range(1, 4)
    ]
    row_parts = jnp.stack(row_parts)
    col_parts = lax.all_to_all(col_sum, ("z", "x"), 0, 0)
    image, gram = pl.pallas_call(
        gram_kernel,
        out_shape=(shape((PROBES, own_points), f32), shape((40, TILE), f32)),
        in_specs=[VMEM] * 5,
        out_specs=(VMEM, VMEM),
        compiler_params=PARAMS,
        name="gram",
    )(direction, residual, own_product, row_parts, col_parts)
    gram = gram + swap(gram)
    for axis, size in (("y", 4), ("x", 4), ("z", 8)):
        gram = sum(shifts(gram, axis, size), gram)
    return pl.pallas_call(
        solve_kernel,
        out_shape=(shape((PROBES, own_points), f32),) * 3,
        in_specs=[VMEM] * 5,
        out_specs=(VMEM,) * 3,
        compiler_params=PARAMS,
        name="solve",
    )(gram, solution_field, residual, direction, image)


def solution(mesh):
    fine = Mesh(np.asarray(mesh.devices).reshape(8, 4, 4, 2), ("z", "x", "y", "core"))
    points = P(None, ("z", "x", "y", "core"))
    return jax.shard_map(
        on_device,
        mesh=fine,
        in_specs=(points,) * 5 + (P(("z", "x", "y", "core")),),
        out_specs=(points,) * 3,
        check_vma=False,
    )
```

time: 940 us -> 237 us (0.25)
  matrix products: 256 us -> 0 us
  blocking collectives: 218 us -> 14.4 us
  other arithmetic: 164 us -> 1.14 us
  waiting for transfers between devices: 220 us -> 93.2 us
  Pallas kernels: 0 us -> 74.2 us
  local copies, waits for them, and re-layouts: 61.3 us -> 4 us
  starting transfers between devices: 0.3 us -> 34.3 us
    dot_general x200 -> x0, matrix products: 256 us -> none  [the longest x24 90.4 us: stepped(): jnp.einsum('bt,kbp->ktp', row_chosen_index.astype(jnp.float32), forward_s...]
    psum x2 -> x0, waiting for transfers between devices: 210 us -> none  [the longest x1 162 us: on_device(): lax.psum(col_flat.astype(jnp.bfloat16), 'row').astype(jnp.float32)]
    psum x2 -> x0, blocking collectives: 146 us -> none  [the longest x1 73.8 us: on_device(): lax.psum(cross_gram_matrix(residual_next, residual_next), ('row', 'col'))]
    pallas_call x0 -> x4, Pallas kernels: none -> 74.2 us  [the longest x1 66.9 us: on_device(): pl.pallas_call(pair_kernel, out_shape=(shape((8, 256, TILE), bf16), shape...]
    reduce_sum x25 -> x0, other arithmetic: 66.6 us -> none  [kernel_tile(): distance = jnp.sqrt(jnp.sum(differ * differ, axis=0)) / RADIUS]
    convert_element_type x27 -> x1, other arithmetic: 64.3 us -> 0.07 us  [on_device(): half = half.astype(bf16)]
    all_gather x3 -> x1, blocking collectives: 71.5 us -> 14.4 us  [on_device(): lax.all_gather(packed, 'x')]
    while x144 -> x0, local copies, waits for them, and re-layouts: 46.2 us -> none
  transfers between devices with their start and end apart: 3 -> 24, of which waited for: 3 -> 18; matrix products, arithmetic and copies ran while one was open for 1% -> 1% of each run, Pallas kernels for 0% -> 0%
where the time goes in v1:
time: 237 us; the launch traced here: 236 us
  waiting for transfers between devices  93.2 us (39%)
  Pallas kernels  74.2 us (31%)
  starting transfers between devices  34.3 us (14%)
  between operations  14.9 us (6%)
  blocking collectives  14.4 us (6%)
  local copies, waits for them, and re-layouts  4 us (2%)
    pallas_call x1, Pallas kernels, on_device(): pl.pallas_call(pair_kernel, out_shape=(shape((8, 256, TILE), bf16), shape...  66.9 us
    all_to_all x1, waiting for transfers between devices, on_device(): col_parts = lax.all_to_all(col_sum, ('z', 'x'), 0, 0)  37 us
    all_gather x1, waiting for transfers between devices, on_device(): lax.all_gather(lax.all_gather(packed, 'x'), 'z').reshape(32, 272, TILE)  32.6 us
    ppermute x16, starting transfers between devices, shifts(): lax.ppermute(value, axis, [(i, (i + k) % size) for i in range(size)])  24.3 us
    ppermute x16, waiting for transfers between devices, shifts(): lax.ppermute(value, axis, [(i, (i + k) % size) for i in range(size)])  15.3 us
    all_gather x1, blocking collectives, on_device(): lax.all_gather(packed, 'x')  14.4 us
    all_to_all x1, starting transfers between devices, on_device(): col_parts = lax.all_to_all(col_sum, ('z', 'x'), 0, 0)  6.42 us
  transfers between devices with their start and end apart: 24, of which 18 were waited for; matrix products, arithmetic and copies ran while one was open for 1% of the time, Pallas kernels for 0%

profile of v1, /device:TPU:16, one launch (start us, length us, event | category | flops | bytes accessed | tf_op | source)
XLA Modules:
  0.0 236.0 jit_solution(14303496746637024811)
XLA Ops:
  7.2 1.6 pack.1.own_ref
  8.8 14.4 %all-gather = bf16[1088,128]{1,0:T(8,128)(2,1)} all-gather(bf16[272,128]{1,0:T(8,128)(2,1)} %pack.1.own_ref), channel_id=2, replica_groups=mesh['z'=8,'x'=4,'y'=4,'core'=2] {'x'}, dimensions={0}, use_global_device_ids=true | all-gather | bytes 348160 | tf_op jit(solution)/shard_map/all_gather | solution.py:182
  23.7 2.9 %collective-permute-start.1 = (bf16[272,128]{1,0:T(8,128)(2,1)}, bf16[272,128]{1,0:T(8,128)(2,1)S(1)}, u32[]{:S(2)}, u32[]{:S(2)}) collective-permute-start(bf16[272,128]{1,0:T(8,128)(2,1)} %pack.1.own_ref), channel_id=1, source_target_pairs={{0,4},{2,6},{4,0},{6,2},{1,5},{3,7},{5,1},{7,3},{8,12},{10,14},{12... | collective-permute-start | bytes 208904 | tf_op jit(solution)/shard_map/ppermute | solution.py:166
  32.2 1.5 collective-permute-done.3
  33.8 32.6 %all-gather.4.cloned.1.call-done.col_ref = bf16[32,272,128]{2,1,0:T(8,128)(2,1)} async-done(((bf16[4,272,128]{2,1,0:T(8,128)(2,1)}), bf16[32,272,128]{2,1,0:T(8,128)(2,1)}) %all-gather.4.cloned.1.call-update) | async-done | bytes 2228240 | tf_op jit(solution)/shard_map/all_gather | solution.py:182
  66.3 1.6 copy-done
  67.9 66.9 %pairs.1 = (bf16[8,256,128]{2,1,0:T(8,128)(2,1)S(1)}, bf16[32,256,128]{2,1,0:T(8,128)(2,1)S(1)}, f32[32,1024]{1,0:T(8,128)S(1)}) custom-call(s32[3]{0:T(128)S(1)} %pad_add_fusion.place_ref, s32[2,1536]{1,0:T(2,128)S(1)} %copy-done.6, bf16[272,128]{1,0:T(8,128)(2,1)S(1)} %copy-done.2, bf16[8,272,128]{2,1,0:T(8,128)(2,1)S(1)} %constant_dynamic-update-slice_fusion.row_ref, ...), custom_call_target="tpu_custom_call" | custom-call | tf_op jit(solution)/shard_map/pairs/pallas_call | solution.py:184
  136.2 6.4 %all-to-all-start = ((bf16[32,256,128]{2,1,0:T(8,128)(2,1)}), bf16[32,256,128]{2,1,0:T(8,128)(2,1)S(1)}, u32[]{:S(2)}, u32[]{:S(2)}) async-start(bf16[32,256,128]{2,1,0:T(8,128)(2,1)} %copy-done.1), calls=%async_computation | async-start | bytes 4194304 | tf_op jit(solution)/shard_map/all_to_all | solution.py:206
  142.7 1.5 collective-permute-done.4
  144.4 1.5 collective-permute-start.7
  148.7 3.0 %collective-permute-done.6 = bf16[256,128]{1,0:T(8,128)(2,1)S(1)} collective-permute-done((bf16[256,128]{1,0:T(8,128)(2,1)S(1)}, bf16[256,128]{1,0:T(8,128)(2,1)S(1)}, u32[]{:S(2)}, u32[]{:S(2)}) %collective-permute-start.6) | collective-permute-done | bytes 65568 | tf_op jit(solution)/shard_map/ppermute | solution.py:203
  151.8 37.0 %all-to-all-done.col_ref = bf16[32,256,128]{2,1,0:T(8,128)(2,1)S(1)} async-done(((bf16[32,256,128]{2,1,0:T(8,128)(2,1)}), bf16[32,256,128]{2,1,0:T(8,128)(2,1)S(1)}, u32[]{:S(2)}, u32[]{:S(2)}) %all-to-all-start) | async-done | bytes 2097184 | tf_op jit(solution)/shard_map/all_to_all | solution.py:206
  192.5 2.7 %collective-permute-start.10 = (f32[40,128]{1,0:T(8,128)S(1)}, f32[40,128]{1,0:T(8,128)S(1)}, u32[]{:S(2)}, u32[]{:S(2)}) collective-permute-start(f32[40,128]{1,0:T(8,128)S(1)} %add.46), channel_id=1, source_target_pairs={{0,4},{2,6},{4,0},{6,2},{1,5},{3,7},{5,1},{7,3},{8,12},{10,14},{12... | collective-permute-start | bytes 61448 | tf_op jit(solution)/shard_map/ppermute | solution.py:166
  195.2 2.6 %collective-permute-done.10 = f32[40,128]{1,0:T(8,128)S(1)} collective-permute-done((f32[40,128]{1,0:T(8,128)S(1)}, f32[40,128]{1,0:T(8,128)S(1)}, u32[]{:S(2)}, u32[]{:S(2)}) %collective-permute-start.10) | collective-permute-done | bytes 20512 | tf_op jit(solution)/shard_map/ppermute | solution.py:166
  199.0 2.9 %collective-permute-start.14 = (f32[40,128]{1,0:T(8,128)S(1)}, f32[40,128]{1,0:T(8,128)S(1)}, u32[]{:S(2)}, u32[]{:S(2)}) collective-permute-start(f32[40,128]{1,0:T(8,128)S(1)} %add_add_fusion.2), channel_id=1, source_target_pairs={{0,24},{8,0},{16,8},{24,16},{1,25},{9,1},{17,9},{25,17},{2,26},{10... | collective-permute-start | bytes 61448 | tf_op jit(solution)/shard_map/ppermute | solution.py:166
  201.9 1.5 collective-permute-start.13
  203.7 3.5 %collective-permute-done.13 = f32[40,128]{1,0:T(8,128)S(1)} collective-permute-done((f32[40,128]{1,0:T(8,128)S(1)}, f32[40,128]{1,0:T(8,128)S(1)}, u32[]{:S(2)}, u32[]{:S(2)}) %collective-permute-start.13) | collective-permute-done | bytes 20512 | tf_op jit(solution)/shard_map/ppermute | solution.py:166
  209.7 2.9 %collective-permute-start.19 = (f32[40,128]{1,0:T(8,128)S(1)}, f32[40,128]{1,0:T(8,128)S(1)}, u32[]{:S(2)}, u32[]{:S(2)}) collective-permute-start(f32[40,128]{1,0:T(8,128)S(1)} %add_add_fusion.1), channel_id=1, source_target_pairs={{0,160},{32,192},{64,224},{96,0},{128,32},{160,64},{192,96},{224,1... | collective-permute-start | bytes 61448 | tf_op jit(solution)/shard_map/ppermute | solution.py:166
  212.6 3.0 %collective-permute-start.18 = (f32[40,128]{1,0:T(8,128)S(1)}, f32[40,128]{1,0:T(8,128)S(1)}, u32[]{:S(2)}, u32[]{:S(2)}) collective-permute-start(f32[40,128]{1,0:T(8,128)S(1)} %add_add_fusion.1), channel_id=1, source_target_pairs={{0,128},{32,160},{64,192},{96,224},{128,0},{160,32},{192,64},{224,... | collective-permute-start | bytes 61448 | tf_op jit(solution)/shard_map/ppermute | solution.py:166
  215.6 2.4 %collective-permute-start.17 = (f32[40,128]{1,0:T(8,128)S(1)}, f32[40,128]{1,0:T(8,128)S(1)}, u32[]{:S(2)}, u32[]{:S(2)}) collective-permute-start(f32[40,128]{1,0:T(8,128)S(1)} %add_add_fusion.1), channel_id=1, source_target_pairs={{0,96},{32,128},{64,160},{96,192},{128,224},{160,0},{192,32},{224,... | collective-permute-start | bytes 61448 | tf_op jit(solution)/shard_map/ppermute | solution.py:166
  218.0 1.4 collective-permute-start.16
  220.3 2.1 collective-permute-done.17
  222.4 1.5 collective-permute-done.16
  224.5 4.7 %solve.1 = (f32[32,1024]{1,0:T(8,128)}, f32[32,1024]{1,0:T(8,128)}, f32[32,1024]{1,0:T(8,128)}) custom-call(f32[40,128]{1,0:T(8,128)S(1)} %add_add_fusion.gram_ref, f32[32,1024]{1,0:T(8,128)S(1)} %copy-done.5, f32[32,1024]{1,0:T(8,128)S(1)} %copy-done.4, f32[32,1024]{1,0:T(8,128)S(1)} %copy-done.3, f32[32,1024]{1,0:T(8,128)S(1)} %get-tuple-element.12.image_ref), custom_call_target="tpu_custom_call" | custom-call | tf_op jit(solution)/shard_map/solve/pallas_call | solution.py:218
  (59 shorter events, 18.9 us)
Async XLA Ops:
  7.2 59.1 %all-gather.4.cloned.1.call-start = ((), (), s32[]{:S(2)}) async-start(), calls=%async_computation.1 | async-start | bytes 2506752 | tf_op jit(solution)/shard_map/all_gather | solution.py:182
  23.2 5.6 %collective-permute-start.2 = (bf16[272,128]{1,0:T(8,128)(2,1)}, bf16[272,128]{1,0:T(8,128)(2,1)S(1)}, u32[]{:S(2)}, u32[]{:S(2)}) collective-permute-start(bf16[272,128]{1,0:T(8,128)(2,1)} %pack.1.own_ref), channel_id=1, source_target_pairs={{0,6},{2,0},{4,2},{6,4},{1,7},{3,1},{5,3},{7,5},{8,14},{10,8},{12,... | collective-permute-start | bytes 208904 | tf_op jit(solution)/shard_map/ppermute | solution.py:166
  23.7 6.0 %collective-permute-start.1 = (bf16[272,128]{1,0:T(8,128)(2,1)}, bf16[272,128]{1,0:T(8,128)(2,1)S(1)}, u32[]{:S(2)}, u32[]{:S(2)}) collective-permute-start(bf16[272,128]{1,0:T(8,128)(2,1)} %pack.1.own_ref), channel_id=1, source_target_pairs={{0,4},{2,6},{4,0},{6,2},{1,5},{3,7},{5,1},{7,3},{8,12},{10,14},{12... | collective-permute-start | bytes 208904 | tf_op jit(solution)/shard_map/ppermute | solution.py:166
  26.6 4.5 %collective-permute-start = (bf16[272,128]{1,0:T(8,128)(2,1)}, bf16[272,128]{1,0:T(8,128)(2,1)S(1)}, u32[]{:S(2)}, u32[]{:S(2)}) collective-permute-start(bf16[272,128]{1,0:T(8,128)(2,1)} %pack.1.own_ref), channel_id=1, source_target_pairs={{0,2},{2,4},{4,6},{6,0},{1,3},{3,5},{5,7},{7,1},{8,10},{10,12},{12... | collective-permute-start | bytes 208904 | tf_op jit(solution)/shard_map/ppermute | solution.py:166
  32.1 1.6 collective-permute-start.3
  136.2 52.7 %all-to-all-start = ((bf16[32,256,128]{2,1,0:T(8,128)(2,1)}), bf16[32,256,128]{2,1,0:T(8,128)(2,1)S(1)}, u32[]{:S(2)}, u32[]{:S(2)}) async-start(bf16[32,256,128]{2,1,0:T(8,128)(2,1)} %copy-done.1), calls=%async_computation | async-start | bytes 4194304 | tf_op jit(solution)/shard_map/all_to_all | solution.py:206
  142.6 1.6 collective-permute-start.4
  144.4 4.3 %collective-permute-start.7 = (bf16[256,128]{1,0:T(8,128)(2,1)S(1)}, bf16[256,128]{1,0:T(8,128)(2,1)S(1)}, u32[]{:S(2)}, u32[]{:S(2)}) collective-permute-start(bf16[256,128]{1,0:T(8,128)(2,1)S(1)} %get-tuple-element.14), channel_id=1, source_target_pairs={{0,2},{2,4},{4,6},{6,0},{1,3},{3,5},{5,7},{7,1},{8,10},{10,12},{12... | collective-permute-start | bytes 196616 | tf_op jit(solution)/shard_map/ppermute | solution.py:203
  145.9 5.8 %collective-permute-start.6 = (bf16[256,128]{1,0:T(8,128)(2,1)S(1)}, bf16[256,128]{1,0:T(8,128)(2,1)S(1)}, u32[]{:S(2)}, u32[]{:S(2)}) collective-permute-start(bf16[256,128]{1,0:T(8,128)(2,1)S(1)} %get-tuple-element.15), channel_id=1, source_target_pairs={{0,4},{2,6},{4,0},{6,2},{1,5},{3,7},{5,1},{7,3},{8,12},{10,14},{12... | collective-permute-start | bytes 196616 | tf_op jit(solution)/shard_map/ppermute | solution.py:203
  147.0 4.8 %collective-permute-start.5 = (bf16[256,128]{1,0:T(8,128)(2,1)S(1)}, bf16[256,128]{1,0:T(8,128)(2,1)S(1)}, u32[]{:S(2)}, u32[]{:S(2)}) collective-permute-start(bf16[256,128]{1,0:T(8,128)(2,1)S(1)} %get-tuple-element.16), channel_id=1, source_target_pairs={{0,6},{2,0},{4,2},{6,4},{1,7},{3,1},{5,3},{7,5},{8,14},{10,8},{12,... | collective-permute-start | bytes 196616 | tf_op jit(solution)/shard_map/ppermute | solution.py:203
  189.9 1.2 collective-permute-start.8
  191.1 4.1 %collective-permute-start.11 = (f32[40,128]{1,0:T(8,128)S(1)}, f32[40,128]{1,0:T(8,128)S(1)}, u32[]{:S(2)}, u32[]{:S(2)}) collective-permute-start(f32[40,128]{1,0:T(8,128)S(1)} %add.46), channel_id=1, source_target_pairs={{0,6},{2,0},{4,2},{6,4},{1,7},{3,1},{5,3},{7,5},{8,14},{10,8},{12,... | collective-permute-start | bytes 61448 | tf_op jit(solution)/shard_map/ppermute | solution.py:166
  192.5 5.4 %collective-permute-start.10 = (f32[40,128]{1,0:T(8,128)S(1)}, f32[40,128]{1,0:T(8,128)S(1)}, u32[]{:S(2)}, u32[]{:S(2)}) collective-permute-start(f32[40,128]{1,0:T(8,128)S(1)} %add.46), channel_id=1, source_target_pairs={{0,4},{2,6},{4,0},{6,2},{1,5},{3,7},{5,1},{7,3},{8,12},{10,14},{12... | collective-permute-start | bytes 61448 | tf_op jit(solution)/shard_map/ppermute | solution.py:166
  195.2 3.8 %collective-permute-start.9 = (f32[40,128]{1,0:T(8,128)S(1)}, f32[40,128]{1,0:T(8,128)S(1)}, u32[]{:S(2)}, u32[]{:S(2)}) collective-permute-start(f32[40,128]{1,0:T(8,128)S(1)} %add.46), channel_id=1, source_target_pairs={{0,2},{2,4},{4,6},{6,0},{1,3},{3,5},{5,7},{7,1},{8,10},{10,12},{12... | collective-permute-start | bytes 61448 | tf_op jit(solution)/shard_map/ppermute | solution.py:166
  199.0 4.7 %collective-permute-start.14 = (f32[40,128]{1,0:T(8,128)S(1)}, f32[40,128]{1,0:T(8,128)S(1)}, u32[]{:S(2)}, u32[]{:S(2)}) collective-permute-start(f32[40,128]{1,0:T(8,128)S(1)} %add_add_fusion.2), channel_id=1, source_target_pairs={{0,24},{8,0},{16,8},{24,16},{1,25},{9,1},{17,9},{25,17},{2,26},{10... | collective-permute-start | bytes 61448 | tf_op jit(solution)/shard_map/ppermute | solution.py:166
  201.9 5.3 %collective-permute-start.13 = (f32[40,128]{1,0:T(8,128)S(1)}, f32[40,128]{1,0:T(8,128)S(1)}, u32[]{:S(2)}, u32[]{:S(2)}) collective-permute-start(f32[40,128]{1,0:T(8,128)S(1)} %add_add_fusion.2), channel_id=1, source_target_pairs={{0,16},{8,24},{16,0},{24,8},{1,17},{9,25},{17,1},{25,9},{2,18},{10... | collective-permute-start | bytes 61448 | tf_op jit(solution)/shard_map/ppermute | solution.py:166
  203.5 5.0 %collective-permute-start.12 = (f32[40,128]{1,0:T(8,128)S(1)}, f32[40,128]{1,0:T(8,128)S(1)}, u32[]{:S(2)}, u32[]{:S(2)}) collective-permute-start(f32[40,128]{1,0:T(8,128)S(1)} %add_add_fusion.2), channel_id=1, source_target_pairs={{0,8},{8,16},{16,24},{24,0},{1,9},{9,17},{17,25},{25,1},{2,10},{10... | collective-permute-start | bytes 61448 | tf_op jit(solution)/shard_map/ppermute | solution.py:166
  208.5 9.5 %collective-permute-start.21 = (f32[40,128]{1,0:T(8,128)S(1)}, f32[40,128]{1,0:T(8,128)S(1)}, u32[]{:S(2)}, u32[]{:S(2)}) collective-permute-start(f32[40,128]{1,0:T(8,128)S(1)} %add_add_fusion.1), channel_id=1, source_target_pairs={{0,224},{32,0},{64,32},{96,64},{128,96},{160,128},{192,160},{224,1... | collective-permute-start | bytes 61448 | tf_op jit(solution)/shard_map/ppermute | solution.py:166
  208.6 10.9 %collective-permute-start.20 = (f32[40,128]{1,0:T(8,128)S(1)}, f32[40,128]{1,0:T(8,128)S(1)}, u32[]{:S(2)}, u32[]{:S(2)}) collective-permute-start(f32[40,128]{1,0:T(8,128)S(1)} %add_add_fusion.1), channel_id=1, source_target_pairs={{0,192},{32,224},{64,0},{96,32},{128,64},{160,96},{192,128},{224,1... | collective-permute-start | bytes 61448 | tf_op jit(solution)/shard_map/ppermute | solution.py:166
  209.7 10.3 %collective-permute-start.19 = (f32[40,128]{1,0:T(8,128)S(1)}, f32[40,128]{1,0:T(8,128)S(1)}, u32[]{:S(2)}, u32[]{:S(2)}) collective-permute-start(f32[40,128]{1,0:T(8,128)S(1)} %add_add_fusion.1), channel_id=1, source_target_pairs={{0,160},{32,192},{64,224},{96,0},{128,32},{160,64},{192,96},{224,1... | collective-permute-start | bytes 61448 | tf_op jit(solution)/shard_map/ppermute | solution.py:166
  212.6 7.7 %collective-permute-start.18 = (f32[40,128]{1,0:T(8,128)S(1)}, f32[40,128]{1,0:T(8,128)S(1)}, u32[]{:S(2)}, u32[]{:S(2)}) collective-permute-start(f32[40,128]{1,0:T(8,128)S(1)} %add_add_fusion.1), channel_id=1, source_target_pairs={{0,128},{32,160},{64,192},{96,224},{128,0},{160,32},{192,64},{224,... | collective-permute-start | bytes 61448 | tf_op jit(solution)/shard_map/ppermute | solution.py:166
  215.6 6.8 %collective-permute-start.17 = (f32[40,128]{1,0:T(8,128)S(1)}, f32[40,128]{1,0:T(8,128)S(1)}, u32[]{:S(2)}, u32[]{:S(2)}) collective-permute-start(f32[40,128]{1,0:T(8,128)S(1)} %add_add_fusion.1), channel_id=1, source_target_pairs={{0,96},{32,128},{64,160},{96,192},{128,224},{160,0},{192,32},{224,... | collective-permute-start | bytes 61448 | tf_op jit(solution)/shard_map/ppermute | solution.py:166
  218.0 5.9 %collective-permute-start.16 = (f32[40,128]{1,0:T(8,128)S(1)}, f32[40,128]{1,0:T(8,128)S(1)}, u32[]{:S(2)}, u32[]{:S(2)}) collective-permute-start(f32[40,128]{1,0:T(8,128)S(1)} %add_add_fusion.1), channel_id=1, source_target_pairs={{0,64},{32,96},{64,128},{96,160},{128,192},{160,224},{192,0},{224,... | collective-permute-start | bytes 61448 | tf_op jit(solution)/shard_map/ppermute | solution.py:166
  219.4 5.0 %collective-permute-start.15 = (f32[40,128]{1,0:T(8,128)S(1)}, f32[40,128]{1,0:T(8,128)S(1)}, u32[]{:S(2)}, u32[]{:S(2)}) collective-permute-start(f32[40,128]{1,0:T(8,128)S(1)} %add_add_fusion.1), channel_id=1, source_target_pairs={{0,32},{32,64},{64,96},{96,128},{128,160},{160,192},{192,224},{224... | collective-permute-start | bytes 61448 | tf_op jit(solution)/shard_map/ppermute | solution.py:166
  (7 other events, 292.2 us)
Sparse Core Ops, SparseCore 0:
  23.3 42.9 all-gather.3

commit v2 on v1

--- a/solution.py
+++ b/solution.py
@@ -11,7 +11,10 @@
 
 TILE = 128
 PROBES = 32
-UNROLL = 16
+UNROLL = 32
+TAIL = 8
+PARTS = 4
+BIN = 1536 + UNROLL
 NUGGET = 2.0
 KERNEL_SCALE = 0.1
 HIGHEST = lax.Precision.HIGHEST
@@ -21,15 +24,22 @@
 NT = (((1,), (1,)), ((), ()))
 NN = (((1,), (0,)), ((), ()))
 TN = (((0,), (0,)), ((), ()))
-PARAMS = pltpu.CompilerParams(vmem_limit_bytes=48 * 2**20)
+PARAMS = pltpu.CompilerParams(vmem_limit_bytes=16 * 2**20)
+
+
+def cost(microseconds):
+    return pl.CostEstimate(flops=0, bytes_accessed=int(microseconds * 3_500_000), transcendentals=0)
 
 
 def pack_kernel(direction_ref, positions_ref, packed_ref):
-    for t in range(8):
-        packed_ref[t * 32 : (t + 1) * 32, :] = direction_ref[:, t * TILE : (t + 1) * TILE].astype(bf16)
     where = positions_ref[...].astype(f32)
-    rows = [where[d : d + 1, t * TILE : (t + 1) * TILE] for d in range(2) for t in range(8)]
-    packed_ref[256:272, :] = jnp.concatenate(rows, 0).astype(bf16)
+    for h in range(2):
+        for t in range(4):
+            lanes = slice((h * 4 + t) * TILE, (h * 4 + t + 1) * TILE)
+            packed_ref[h * 144 + t * 32 : h * 144 + (t + 1) * 32, :] = direction_ref[:, lanes].astype(bf16)
+        rows = [where[d : d + 1, (h * 4 + t) * TILE : (h * 4 + t + 1) * TILE] for d in range(2) for t in range(4)]
+        rows.append(jnp.zeros((8, TILE), f32))
+        packed_ref[h * 144 + 128 : h * 144 + 144, :] = jnp.concatenate(rows, 0).astype(bf16)
 
 
 def radial(square):
@@ -39,75 +49,120 @@
     return ((remain2 * remain2) * (1.25 - remain)).astype(bf16)
 
 
-def pair_kernel(place_ref, pairs_ref, own_ref, row_ref, col_ref, row_out, col_out, own_out, px, py, qx, qy, row_acc, col_acc):
+def bin_kernel(place_ref, pairs_ref, bins_ref, count_ref):
     live, y_own, core_own = place_ref[0], place_ref[1], place_ref[2]
-    row_acc[...] = jnp.zeros_like(row_acc)
+
+    def step(e, ends):
+        a, b = pairs_ref[0, e], pairs_ref[1, e]
+        shift = (y_own - (a >> 4)) & 3
+        slot = shift + 4 * (((a >> 3) & 1) ^ core_own)
+        tile = slot * 8 + (a & 7)
+        part = (b >> 1) & 3
+        far = ((b >> 3) << 1) + (b & 1)
+        end = jnp.where(part < 2, jnp.where(part == 0, ends[0], ends[1]), jnp.where(part == 2, ends[2], ends[3]))
+        bins_ref[part * BIN + end] = tile + (far << 8)
+        return tuple(ends[p] + (part == p).astype(jnp.int32) for p in range(PARTS))
+
+    ends = lax.fori_loop(0, live, step, (jnp.int32(0),) * PARTS)
+    for p in range(PARTS):
+        count_ref[p] = ends[p]
+        for j in range(UNROLL):
+            bins_ref[p * BIN + ends[p] + j] = 0
+
+
+def spread(line):
+    return jnp.broadcast_to(line, (TILE, TILE)).T
+
+
+def row_kernel(own_ref, row_ref, px, py, near_out, own_out):
+    def step(r, carry):
+        for h in range(2):
+            where = row_ref[r, h * 144 + 128 : h * 144 + 144, :].astype(f32)
+            for t in range(4):
+                px[r * 8 + h * 4 + t] = spread(where[t : t + 1])
+                py[r * 8 + h * 4 + t] = spread(where[4 + t : 5 + t])
+                near_out[r * 8 + h * 4 + t] = row_ref[r, h * 144 + t * 32 : h * 144 + (t + 1) * 32, :]
+        return carry
+
+    lax.fori_loop(0, 8, step, 0)
+    for h in range(2):
+        where = own_ref[h * 144 + 128 : h * 144 + 144, :].astype(f32)
+        for t in range(4):
+            dx = spread(where[t : t + 1]) - where[t : t + 1]
+            dy = spread(where[4 + t : 5 + t]) - where[4 + t : 5 + t]
+            block = radial(dx * dx + dy * dy)
+            own = own_ref[h * 144 + t * 32 : h * 144 + (t + 1) * 32, :]
+            own_out[:, (h * 4 + t) * TILE : (h * 4 + t + 1) * TILE] = KERNEL_SCALE * lax.dot_general(
+                own, block, NT, preferred_element_type=f32
+            )
+
+
+def part_kernel(part, *refs):
+    if part == 0:
+        count_ref, bins_ref, px, py, near_ref, col_ref, row_acc, col_out, qx, qy, col_acc = refs
+        row_acc[...] = jnp.zeros_like(row_acc)
+    elif part < PARTS - 1:
+        count_ref, bins_ref, px, py, near_ref, col_ref, unused, row_acc, col_out, qx, qy, col_acc = refs
+    else:
+        count_ref, bins_ref, px, py, near_ref, col_ref, row_acc, row_out, col_out, qx, qy, col_acc = refs
+    first = part % 2 * 2
+    live = count_ref[part]
     col_acc[...] = jnp.zeros_like(col_acc)
 
     def col_prepare(r, carry):
-        where = col_ref[r, 256:272, :].astype(f32)
-        for t in range(8):
-            qx[r * 8 + t] = jnp.broadcast_to(where[t : t + 1], (8, TILE))
-            qy[r * 8 + t] = jnp.broadcast_to(where[8 + t : 9 + t], (8, TILE))
+        where = col_ref[r, 128:144, :].astype(f32)
+        for t in range(2):
+            qx[r * 2 + t] = jnp.broadcast_to(where[first + t : first + t + 1], (8, TILE))
+            qy[r * 2 + t] = jnp.broadcast_to(where[4 + first + t : 5 + first + t], (8, TILE))
         return carry
 
     lax.fori_loop(0, 32, col_prepare, 0)
 
-    def spread(line):
-        return jnp.broadcast_to(line, (TILE, TILE)).T
-
-    def row_prepare(r, carry):
-        where = row_ref[r, 256:272, :].astype(f32)
-        for t in range(8):
-            px[r * 8 + t] = spread(where[t : t + 1])
-            py[r * 8 + t] = spread(where[8 + t : 9 + t])
-        return carry
-
-    lax.fori_loop(0, 8, row_prepare, 0)
-
-    where = own_ref[256:272, :].astype(f32)
-    for t in range(8):
-        dx = spread(where[t : t + 1]) - where[t : t + 1]
-        dy = spread(where[8 + t : 9 + t]) - where[8 + t : 9 + t]
-        block = radial(dx * dx + dy * dy)
-        own_out[:, t * TILE : (t + 1) * TILE] = KERNEL_SCALE * lax.dot_general(
-            own_ref[t * 32 : (t + 1) * 32, :], block, NT, preferred_element_type=f32
-        )
-
-    def body(i, carry):
+    def several(start, number):
         results = []
-        for u in range(UNROLL):
-            e = i * UNROLL + u
-            a, b = pairs_ref[0, e], pairs_ref[1, e]
+        for u in range(number):
+            e = start + u
+            both = bins_ref[part * BIN + e]
+            a, b = both & 255, both >> 8
             keep = jnp.where(e < live, 1.0, 0.0).astype(bf16)
-            shift = (y_own - (a >> 4)) & 3
-            slot = shift + 4 * (((a >> 3) & 1) ^ core_own)
-            tile = slot * 8 + (a & 7)
-            near = row_ref[slot, pl.ds(pl.multiple_of((a & 7) * 32, 32), 32), :] * keep
-            far = col_ref[b >> 3, pl.ds(pl.multiple_of((b & 7) * 32, 32), 32), :] * keep
-            dx = px[tile].reshape(16, 8, TILE) - qx[b][None]
-            dy = py[tile].reshape(16, 8, TILE) - qy[b][None]
+            near = near_ref[a] * keep
+            far = col_ref[b >> 1, pl.ds(pl.multiple_of((first + (b & 1)) * 32, 32), 32), :] * keep
+            dx = px[a].reshape(16, 8, TILE) - qx[b][None]
+            dy = py[a].reshape(16, 8, TILE) - qy[b][None]
             block = radial((dx * dx + dy * dy).reshape(TILE, TILE))
             forward = lax.dot_general(far, block, NT, preferred_element_type=f32)
             backward = lax.dot_general(near, block, NN, preferred_element_type=f32)
-            results.append((tile, b, forward, backward))
-        for tile, b, forward, backward in results:
-            row_acc[tile] += forward
+            results.append((a, b, forward, backward))
+        for a, b, forward, backward in results:
+            row_acc[a] += forward
             col_acc[b] += backward
-        return carry
-
-    lax.fori_loop(0, (live + UNROLL - 1) // UNROLL, body, 0)
-
-    def finish(out, acc):
-        def step(r, carry):
+
+    def body(i, carry):
+        several(i * UNROLL, UNROLL)
+        return carry
+
+    def tail(i, carry):
+        several(whole * UNROLL + i * TAIL, TAIL)
+        return carry
+
+    whole = live // UNROLL
+    lax.fori_loop(0, whole, body, 0)
+    lax.fori_loop(0, (live - whole * UNROLL + TAIL - 1) // TAIL, tail, 0)
+
+    def finish(r, carry):
+        for t in range(2):
+            col_out[r, t * 32 : (t + 1) * 32, :] = (KERNEL_SCALE * col_acc[r * 2 + t]).astype(bf16)
+        return carry
+
+    lax.fori_loop(0, 32, finish, 0)
+    if part == PARTS - 1:
+
+        def finish_row(r, carry):
             for t in range(8):
-                out[r, t * 32 : (t + 1) * 32, :] = (KERNEL_SCALE * acc[r * 8 + t]).astype(bf16)
+                row_out[r, t * 32 : (t + 1) * 32, :] = (KERNEL_SCALE * row_acc[r * 8 + t]).astype(bf16)
             return carry
 
-        lax.fori_loop(0, out.shape[0], step, 0)
-
-    finish(row_out, row_acc)
-    finish(col_out, col_acc)
+        lax.fori_loop(0, 8, finish_row, 0)
 
 
 def dot32(former, latter, dims):
@@ -175,35 +230,74 @@
     own_points = direction.shape[1]
     y_own, core_own = lax.axis_index("y"), lax.axis_index("core")
     packed = pl.pallas_call(
-        pack_kernel, out_shape=shape((272, TILE), bf16), in_specs=[VMEM] * 2, out_specs=VMEM, name="pack"
+        pack_kernel, out_shape=shape((288, TILE), bf16), in_specs=[VMEM] * 2, out_specs=VMEM, name="pack"
     )(direction, positions)
-    row_half = jnp.stack([packed] + shifts(packed, "y", 4))
-    row_all = jnp.concatenate([row_half, swap(row_half)], 0)
-    col_all = lax.all_gather(lax.all_gather(packed, "x"), "z").reshape(32, 272, TILE)
+    chip = jnp.stack([packed, swap(packed)])
+    around = shifts(chip, "y", 4)
+    x_all = lax.all_gather(packed, "x")
+    cols = [lax.all_gather(x_all[:, h * 144 : (h + 1) * 144], "z").reshape(32, 144, TILE) for h in range(2)]
     place = jnp.stack([pair_count[0], y_own, core_own]).astype(jnp.int32)
-    row_sum, col_sum, own_product = pl.pallas_call(
-        pair_kernel,
-        out_shape=(shape((8, 256, TILE), bf16), shape((32, 256, TILE), bf16), shape((PROBES, own_points), f32)),
-        in_specs=[SMEM, SMEM, VMEM, VMEM, VMEM],
-        out_specs=(VMEM, VMEM, VMEM),
-        scratch_shapes=[
-            pltpu.VMEM((64, TILE, TILE), f32),
-            pltpu.VMEM((64, TILE, TILE), f32),
-            pltpu.VMEM((256, 8, TILE), f32),
-            pltpu.VMEM((256, 8, TILE), f32),
-            pltpu.VMEM((64, PROBES, TILE), f32),
-            pltpu.VMEM((256, PROBES, TILE), f32),
-        ],
+    bins, counts = pl.pallas_call(
+        bin_kernel,
+        out_shape=(shape((PARTS * BIN,), jnp.int32), shape((PARTS,), jnp.int32)),
+        in_specs=[SMEM, SMEM],
+        out_specs=(SMEM, SMEM),
+        name="bins",
+        cost_estimate=cost(8),
+    )(place, tile_pairs)
+    row_all = jnp.concatenate([v[:1] for v in [chip] + around] + [v[1:] for v in [chip] + around], 0)
+    px, py, near, own_product = pl.pallas_call(
+        row_kernel,
+        out_shape=(
+            shape((64, TILE, TILE), f32),
+            shape((64, TILE, TILE), f32),
+            shape((64, PROBES, TILE), bf16),
+            shape((PROBES, own_points), f32),
+        ),
+        in_specs=[VMEM] * 2,
+        out_specs=(VMEM,) * 4,
         compiler_params=PARAMS,
-        name="pairs",
-    )(place, tile_pairs, packed, row_all, col_all)
-    half = row_sum[:4].astype(f32) + swap(row_sum[4:]).astype(f32)
-    half = half.astype(bf16)
+        name="rows",
+        cost_estimate=cost(6),
+    )(packed, row_all)
+    totals = None
+    col_sums = []
+    for part in range(PARTS):
+        last = part == PARTS - 1
+        total_shape = shape((64, PROBES, TILE), f32)
+        row_shape = shape((8, 256, TILE), bf16) if last else total_shape
+        operands = (counts, bins, px, py, near, cols[part // 2])
+        alias = {}
+        scratch = [pltpu.VMEM((64, 8, TILE), f32), pltpu.VMEM((64, 8, TILE), f32), pltpu.VMEM((64, PROBES, TILE), f32)]
+        if part == 1:
+            totals, cols[1] = lax.optimization_barrier((totals, cols[1]))
+        if part > 1:
+            totals, col_sums[part - 2] = lax.optimization_barrier((totals, col_sums[part - 2]))
+        if part > 0:
+            operands = operands + (totals,)
+            alias = {} if last else {6: 0}
+        totals, col_sum = pl.pallas_call(
+            functools.partial(part_kernel, part),
+            out_shape=(row_shape, shape((32, 64, TILE), bf16)),
+            in_specs=[SMEM] * 2 + [VMEM] * (len(operands) - 2),
+            out_specs=(VMEM, VMEM),
+            scratch_shapes=scratch,
+            input_output_aliases=alias,
+            compiler_params=PARAMS,
+            name="pairs",
+            cost_estimate=cost(16),
+        )(*operands)
+        col_sum = col_sum.reshape(8, 4 * 64, TILE)
+        if part > 0:
+            col_sum, col_sums[part - 1] = lax.optimization_barrier((col_sum, col_sums[part - 1]))
+        col_sums.append(lax.psum_scatter(col_sum, "z", scatter_dimension=0, tiled=False).reshape(4, 64, TILE))
+    row_sum = totals
+    half = (row_sum[:4].astype(f32) + swap(row_sum[4:]).astype(f32)).astype(bf16)
     row_parts = [half[0]] + [
         lax.ppermute(half[k], "y", [(i, (i - k) % 4) for i in range(4)]) for k in range(1, 4)
     ]
     row_parts = jnp.stack(row_parts)
-    col_parts = lax.all_to_all(col_sum, ("z", "x"), 0, 0)
+    col_parts = lax.all_to_all(jnp.concatenate(col_sums, 1), "x", 0, 0)
     image, gram = pl.pallas_call(
         gram_kernel,
         out_shape=(shape((PROBES, own_points), f32), shape((40, TILE), f32)),

time: 237 us -> 322 us (1.36)
  waiting for transfers between devices: 93.2 us -> 162 us
  Pallas kernels: 74.2 us -> 36.2 us
  local copies, waits for them, and re-layouts: 4 us -> 31.2 us
  starting transfers between devices: 34.3 us -> 60 us
    reduce_scatter x0 -> x4, waiting for transfers between devices: none -> 121 us  [on_device(): lax.psum_scatter(col_sum, 'z', scatter_dimension=0, tiled=False)]
    pallas_call x2 -> x7, Pallas kernels: 68.4 us -> 30.8 us  [the longest x4 19.3 us: on_device(): pl.pallas_call(functools.partial(part_kernel, part), out_shape=(row_shape...]
    all_to_all x1, waiting for transfers between devices: 37 us -> 0.01 us  [on_device(): col_parts = lax.all_to_all(jnp.concatenate(col_sums, 1), 'x', 0, 0)]
    ppermute x16, starting transfers between devices: 24.3 us -> 51.9 us  [shifts(): lax.ppermute(value, axis, [(i, (i + k) % size) for i in range(size)])]
    unnamed x18 -> x57, local copies, waits for them, and re-layouts: 3.92 us -> 30.4 us
    all_gather x1 -> x2, waiting for transfers between devices: 32.6 us -> 14.6 us  [on_device(): lax.all_gather(x_all[:, h * 144:(h + 1) * 144], 'z').reshape(32, 144, TILE)]
    ppermute x16, waiting for transfers between devices: 15.3 us -> 18.5 us  [shifts(): lax.ppermute(value, axis, [(i, (i + k) % size) for i in range(size)])]
  transfers between devices with their start and end apart: 24 -> 29, of which waited for: 18 -> 17; matrix products, arithmetic and copies ran while one was open for 1% -> 1% of each run, Pallas kernels for 0% -> 9%
where the time goes in v2:
time: 322 us; the launch traced here: 320 us
  waiting for transfers between devices  162 us (50%)
  starting transfers between devices  60 us (19%)
  Pallas kernels  36.2 us (11%)
  local copies, waits for them, and re-layouts  31.2 us (10%)
  between operations  15 us (5%)
  blocking collectives  12.9 us (4%)
  other arithmetic  3.32 us (1%)
    reduce_scatter x4, waiting for transfers between devices, on_device(): lax.psum_scatter(col_sum, 'z', scatter_dimension=0, tiled=False)  121 us
    ppermute x16, starting transfers between devices, shifts(): lax.ppermute(value, axis, [(i, (i + k) % size) for i in range(size)])  51.9 us
    unnamed x57, local copies, waits for them, and re-layouts  30.4 us
    pallas_call x4, Pallas kernels, on_device(): pl.pallas_call(functools.partial(part_kernel, part), out_shape=(row_shape...  19.3 us
    ppermute x16, waiting for transfers between devices, shifts(): lax.ppermute(value, axis, [(i, (i + k) % size) for i in range(size)])  18.5 us
    all_gather x2, waiting for transfers between devices, on_device(): lax.all_gather(x_all[:, h * 144:(h + 1) * 144], 'z').reshape(32, 144, TILE)  14.6 us
    all_gather x1, blocking collectives, on_device(): x_all = lax.all_gather(packed, 'x')  12.9 us
    pallas_call x1, Pallas kernels, on_device(): pl.pallas_call(bin_kernel, out_shape=(shape((PARTS * BIN,), jnp.int32), s...  6.78 us
  transfers between devices with their start and end apart: 29, of which 17 were waited for; matrix products, arithmetic and copies ran while one was open for 1% of the time, Pallas kernels for 9%

profile of v2, /device:TPU:16, one launch (start us, length us, event | category | flops | bytes accessed | tf_op | source)
XLA Modules:
  0.0 320.3 jit_solution(3204224413818486044)
XLA Ops:
  8.8 12.9 %all-gather = bf16[1152,128]{1,0:T(8,128)(2,1)S(1)} all-gather(bf16[288,128]{1,0:T(8,128)(2,1)} %pack.1.own_ref), channel_id=2, replica_groups=mesh['z'=8,'x'=4,'y'=4,'core'=2] {'x'}, dimensions={0}, use_global_device_ids=true | all-gather | bytes 368640 | tf_op jit(solution)/shard_map/all_gather | solution.py:237
  24.6 6.8 %bins.1 = (s32[6272]{0:T(1024)}, s32[4]{0:T(128)}) custom-call(s32[3]{0:T(128)} %pad_add_fusion.place_ref, s32[2,1536]{1,0:T(2,128)} %pairs_ref.1), custom_call_target="tpu_custom_call" | custom-call | bytes 28000000 | tf_op jit(solution)/shard_map/bins/pallas_call | solution.py:240
  32.3 26.4 %collective-permute-start.1 = (bf16[2,288,128]{2,1,0:T(8,128)(2,1)S(1)}, bf16[2,288,128]{2,1,0:T(8,128)(2,1)S(1)}, u32[]{:S(2)}, u32[]{:S(2)}) collective-permute-start(bf16[2,288,128]{2,1,0:T(8,128)(2,1)S(1)} %pad_maximum_fusion.2), channel_id=1, source_target_pairs={{0,2},{2,4},{4,6},{6,0},{1,3},{3,5},{5,7},{7,1},{8,10},{10,12},{12... | collective-permute-start | bytes 442376 | tf_op jit(solution)/shard_map/ppermute | solution.py:221
  61.6 5.7 %collective-permute-done.2 = bf16[2,288,128]{2,1,0:T(8,128)(2,1)S(1)} collective-permute-done((bf16[2,288,128]{2,1,0:T(8,128)(2,1)S(1)}, bf16[2,288,128]{2,1,0:T(8,128)(2,1)S(1)}, u32[]{:S(2)}, u32[]{:S(2)}) %collective-permute-start.2) | collective-permute-done | bytes 147488 | tf_op jit(solution)/shard_map/ppermute | solution.py:221
  68.3 3.1 rows.1
  83.2 5.1 %pairs.4 = (f32[64,32,128]{2,1,0:T(8,128)S(1)}, bf16[32,64,128]{2,1,0:T(8,128)(2,1)}) custom-call(s32[4]{0:T(128)S(1)} %copy-done.23, s32[6272]{0:T(1024)S(1)} %copy-done.17, f32[64,128,128]{2,1,0:T(8,128)S(1)} %copy-done.1, f32[64,128,128]{2,1,0:T(8,128)S(1)} %copy-done.6, bf16[64,32,128]{2,1,0:T(8,128)(2,1)S(1)} %get-tuple-element.36.refs_4_, ...), custom_call_target="tpu_custom_call" | custom-call | bytes 56000000 | tf_op jit(solution)/shard_map/pairs/pallas_call | solution.py:279
  88.3 14.6 %all-gather.8.cloned.1.call-done.refs_5_ = bf16[32,144,128]{2,1,0:T(8,128)(2,1)} async-done(((bf16[4,144,128]{2,1,0:T(8,128)(2,1)}), bf16[32,144,128]{2,1,0:T(8,128)(2,1)}) %all-gather.8.cloned.1.call-update) | async-done | bytes 1179664 | tf_op jit(solution)/shard_map/all_gather | solution.py:238
  108.6 5.0 %pairs.5 = (f32[64,32,128]{2,1,0:T(8,128)S(1)}, bf16[32,64,128]{2,1,0:T(8,128)(2,1)}) custom-call(s32[4]{0:T(128)S(1)} %copy-done.24, s32[6272]{0:T(1024)S(1)} %copy-done.18, f32[64,128,128]{2,1,0:T(8,128)S(1)} %copy-done.2, f32[64,128,128]{2,1,0:T(8,128)S(1)} %copy-done.7, ...), custom_call_target="tpu_custom_call", output_to_operand_aliasing={{0}: (6, {})} | custom-call | bytes 56000000 | tf_op jit(solution)/shard_map/pairs/pallas_call | solution.py:279
  113.6 27.6 %reduce-scatter.5.cloned.1.call-done = bf16[1,256,128]{2,1,0:T(8,128)(2,1)} async-done(((bf16[8,256,128]{2,1,0:T(8,128)(2,1)}), bf16[1,256,128]{2,1,0:T(8,128)(2,1)}) %reduce-scatter.5.cloned.1.call-update) | async-done | bytes 65552 | tf_op jit(solution)/shard_map/reduce_scatter | solution.py:293
  145.7 4.6 %pairs.6 = (f32[64,32,128]{2,1,0:T(8,128)S(1)}, bf16[32,64,128]{2,1,0:T(8,128)(2,1)}) custom-call(s32[4]{0:T(128)S(1)} %copy-done.24, s32[6272]{0:T(1024)S(1)} %copy-done.18, f32[64,128,128]{2,1,0:T(8,128)S(1)} %copy-done.3, f32[64,128,128]{2,1,0:T(8,128)S(1)} %copy-done.8, ...), custom_call_target="tpu_custom_call", output_to_operand_aliasing={{0}: (6, {})} | custom-call | bytes 56000000 | tf_op jit(solution)/shard_map/pairs/pallas_call | solution.py:279
  150.3 29.4 %reduce-scatter.7.cloned.1.call-done = bf16[1,256,128]{2,1,0:T(8,128)(2,1)} async-done(((bf16[8,256,128]{2,1,0:T(8,128)(2,1)}), bf16[1,256,128]{2,1,0:T(8,128)(2,1)}) %reduce-scatter.7.cloned.1.call-update) | async-done | bytes 65552 | tf_op jit(solution)/shard_map/reduce_scatter | solution.py:293
  184.9 4.7 %pairs.7 = (bf16[8,256,128]{2,1,0:T(8,128)(2,1)S(1)}, bf16[32,64,128]{2,1,0:T(8,128)(2,1)S(1)}) custom-call(s32[4]{0:T(128)S(1)} %copy-done.24, s32[6272]{0:T(1024)S(1)} %copy-done.19, f32[64,128,128]{2,1,0:T(8,128)S(1)} %copy-done.4, f32[64,128,128]{2,1,0:T(8,128)S(1)} %copy-done.9, bf16[64,32,128]{2,1,0:T(8,128)(2,1)S(1)} %get-tuple-element.36.refs_4_, ...), custom_call_target="tpu_custom_call" | custom-call | bytes 56000000 | tf_op jit(solution)/shard_map/pairs/pallas_call | solution.py:279
  190.4 27.5 %reduce-scatter.9.cloned.1.call-done = bf16[1,256,128]{2,1,0:T(8,128)(2,1)} async-done(((bf16[8,256,128]{2,1,0:T(8,128)(2,1)}), bf16[1,256,128]{2,1,0:T(8,128)(2,1)}) %reduce-scatter.9.cloned.1.call-update) | async-done | bytes 65552 | tf_op jit(solution)/shard_map/reduce_scatter | solution.py:293
  219.6 36.7 %reduce-scatter.11.cloned.1.call-done = bf16[1,256,128]{2,1,0:T(8,128)(2,1)} async-done(((bf16[8,256,128]{2,1,0:T(8,128)(2,1)}), bf16[1,256,128]{2,1,0:T(8,128)(2,1)}) %reduce-scatter.11.cloned.1.call-update) | async-done | bytes 65552 | tf_op jit(solution)/shard_map/reduce_scatter | solution.py:293
  258.0 4.2 %all-to-all-start = ((bf16[4,256,128]{2,1,0:T(8,128)(2,1)}), bf16[4,256,128]{2,1,0:T(8,128)(2,1)S(1)}, u32[]{:S(2)}, u32[]{:S(2)}) async-start(bf16[4,256,128]{2,1,0:T(8,128)(2,1)} %pad_maximum_fusion.1), calls=%async_computation.4 | async-start | bytes 524288 | tf_op jit(solution)/shard_map/all_to_all | solution.py:300
  266.7 2.8 collective-permute-done.6
  273.6 3.4 %collective-permute-start.10 = (f32[40,128]{1,0:T(8,128)S(1)}, f32[40,128]{1,0:T(8,128)S(1)}, u32[]{:S(2)}, u32[]{:S(2)}) collective-permute-start(f32[40,128]{1,0:T(8,128)S(1)} %add.54), channel_id=1, source_target_pairs={{0,4},{2,6},{4,0},{6,2},{1,5},{3,7},{5,1},{7,3},{8,12},{10,14},{12... | collective-permute-start | bytes 61448 | tf_op jit(solution)/shard_map/ppermute | solution.py:221
  280.8 3.3 %collective-permute-start.14 = (f32[40,128]{1,0:T(8,128)S(1)}, f32[40,128]{1,0:T(8,128)S(1)}, u32[]{:S(2)}, u32[]{:S(2)}) collective-permute-start(f32[40,128]{1,0:T(8,128)S(1)} %add_add_fusion.2), channel_id=1, source_target_pairs={{0,24},{8,0},{16,8},{24,16},{1,25},{9,1},{17,9},{25,17},{2,26},{10... | collective-permute-start | bytes 61448 | tf_op jit(solution)/shard_map/ppermute | solution.py:221
  285.9 3.6 %collective-permute-done.13 = f32[40,128]{1,0:T(8,128)S(1)} collective-permute-done((f32[40,128]{1,0:T(8,128)S(1)}, f32[40,128]{1,0:T(8,128)S(1)}, u32[]{:S(2)}, u32[]{:S(2)}) %collective-permute-start.13) | collective-permute-done | bytes 20512 | tf_op jit(solution)/shard_map/ppermute | solution.py:221
  293.7 2.2 collective-permute-start.19
  295.9 2.2 collective-permute-start.18
  299.9 3.9 %collective-permute-start.16 = (f32[40,128]{1,0:T(8,128)S(1)}, f32[40,128]{1,0:T(8,128)S(1)}, u32[]{:S(2)}, u32[]{:S(2)}) collective-permute-start(f32[40,128]{1,0:T(8,128)S(1)} %add_add_fusion.1), channel_id=1, source_target_pairs={{0,64},{32,96},{64,128},{96,160},{128,192},{160,224},{192,0},{224,... | collective-permute-start | bytes 61448 | tf_op jit(solution)/shard_map/ppermute | solution.py:221
  305.8 3.0 collective-permute-done.15
  308.8 4.7 %solve.1 = (f32[32,1024]{1,0:T(8,128)}, f32[32,1024]{1,0:T(8,128)}, f32[32,1024]{1,0:T(8,128)}) custom-call(f32[40,128]{1,0:T(8,128)S(1)} %add_add_fusion.gram_ref, f32[32,1024]{1,0:T(8,128)S(1)} %copy-done.22, f32[32,1024]{1,0:T(8,128)S(1)} %copy-done.16, f32[32,1024]{1,0:T(8,128)S(1)} %copy-done.14, f32[32,1024]{1,0:T(8,128)S(1)} %get-tuple-element.58.image_ref), custom_call_target="tpu_custom_call" | custom-call | tf_op jit(solution)/shard_map/solve/pallas_call | solution.py:312
  (120 shorter events, 62.1 us)
Async XLA Ops:
  7.2 69.0 %all-gather.6.cloned.1.call-start = ((), (), s32[]{:S(2)}) async-start(), calls=%async_computation.9 | async-start | bytes 1327104 | tf_op jit(solution)/shard_map/all_gather | solution.py:238
  22.4 80.6 %all-gather.8.cloned.1.call-start = ((), (), s32[]{:S(2)}) async-start(), calls=%async_computation.10 | async-start | bytes 1327104 | tf_op jit(solution)/shard_map/all_gather | solution.py:238
  23.1 118.1 %reduce-scatter.5.cloned.1.call-start = ((), (), s32[]{:S(2)}) async-start(), calls=%async_computation.5 | async-start | bytes 589824 | tf_op jit(solution)/shard_map/reduce_scatter | solution.py:293
  23.2 8.2 %collective-permute-start = (bf16[288,128]{1,0:T(8,128)(2,1)}, bf16[288,128]{1,0:T(8,128)(2,1)S(1)}, u32[]{:S(2)}, u32[]{:S(2)}) collective-permute-start(bf16[288,128]{1,0:T(8,128)(2,1)} %pack.1.own_ref), channel_id=1, source_target_pairs={{0,1},{1,0},{2,3},{3,2},{4,5},{5,4},{6,7},{7,6},{8,9},{9,8},{10,11... | collective-permute-start | bytes 221192 | tf_op jit(solution)/shard_map/ppermute | solution.py:225
  32.3 29.3 %collective-permute-start.1 = (bf16[2,288,128]{2,1,0:T(8,128)(2,1)S(1)}, bf16[2,288,128]{2,1,0:T(8,128)(2,1)S(1)}, u32[]{:S(2)}, u32[]{:S(2)}) collective-permute-start(bf16[2,288,128]{2,1,0:T(8,128)(2,1)S(1)} %pad_maximum_fusion.2), channel_id=1, source_target_pairs={{0,2},{2,4},{4,6},{6,0},{1,3},{3,5},{5,7},{7,1},{8,10},{10,12},{12... | collective-permute-start | bytes 442376 | tf_op jit(solution)/shard_map/ppermute | solution.py:221
  59.5 7.8 %collective-permute-start.3 = (bf16[2,288,128]{2,1,0:T(8,128)(2,1)S(1)}, bf16[2,288,128]{2,1,0:T(8,128)(2,1)S(1)}, u32[]{:S(2)}, u32[]{:S(2)}) collective-permute-start(bf16[2,288,128]{2,1,0:T(8,128)(2,1)S(1)} %pad_maximum_fusion.2), channel_id=1, source_target_pairs={{0,6},{2,0},{4,2},{6,4},{1,7},{3,1},{5,3},{7,5},{8,14},{10,8},{12,... | collective-permute-start | bytes 442376 | tf_op jit(solution)/shard_map/ppermute | solution.py:221
  59.5 7.8 %collective-permute-start.2 = (bf16[2,288,128]{2,1,0:T(8,128)(2,1)S(1)}, bf16[2,288,128]{2,1,0:T(8,128)(2,1)S(1)}, u32[]{:S(2)}, u32[]{:S(2)}) collective-permute-start(bf16[2,288,128]{2,1,0:T(8,128)(2,1)S(1)} %pad_maximum_fusion.2), channel_id=1, source_target_pairs={{0,4},{2,6},{4,0},{6,2},{1,5},{3,7},{5,1},{7,3},{8,12},{10,14},{12... | collective-permute-start | bytes 442376 | tf_op jit(solution)/shard_map/ppermute | solution.py:221
  88.3 91.4 %reduce-scatter.7.cloned.1.call-start = ((), (), s32[]{:S(2)}) async-start(), calls=%async_computation.6 | async-start | bytes 589824 | tf_op jit(solution)/shard_map/reduce_scatter | solution.py:293
  141.2 76.6 %reduce-scatter.9.cloned.1.call-start = ((), (), s32[]{:S(2)}) async-start(), calls=%async_computation.7 | async-start | bytes 589824 | tf_op jit(solution)/shard_map/reduce_scatter | solution.py:293
  179.7 76.6 %reduce-scatter.11.cloned.1.call-start = ((), (), s32[]{:S(2)}) async-start(), calls=%async_computation.8 | async-start | bytes 589824 | tf_op jit(solution)/shard_map/reduce_scatter | solution.py:293
  258.0 11.5 %all-to-all-start = ((bf16[4,256,128]{2,1,0:T(8,128)(2,1)}), bf16[4,256,128]{2,1,0:T(8,128)(2,1)S(1)}, u32[]{:S(2)}, u32[]{:S(2)}) async-start(bf16[4,256,128]{2,1,0:T(8,128)(2,1)} %pad_maximum_fusion.1), calls=%async_computation.4 | async-start | bytes 524288 | tf_op jit(solution)/shard_map/all_to_all | solution.py:300
  263.7 5.8 %collective-permute-start.6 = (bf16[256,128]{1,0:T(8,128)(2,1)S(1)}, bf16[256,128]{1,0:T(8,128)(2,1)S(1)}, u32[]{:S(2)}, u32[]{:S(2)}) collective-permute-start(bf16[256,128]{1,0:T(8,128)(2,1)S(1)} %get-tuple-element.63), channel_id=1, source_target_pairs={{0,4},{2,6},{4,0},{6,2},{1,5},{3,7},{5,1},{7,3},{8,12},{10,14},{12... | collective-permute-start | bytes 196616 | tf_op jit(solution)/shard_map/ppermute | solution.py:297
  264.4 5.0 %collective-permute-start.5 = (bf16[256,128]{1,0:T(8,128)(2,1)S(1)}, bf16[256,128]{1,0:T(8,128)(2,1)S(1)}, u32[]{:S(2)}, u32[]{:S(2)}) collective-permute-start(bf16[256,128]{1,0:T(8,128)(2,1)S(1)} %get-tuple-element.64), channel_id=1, source_target_pairs={{0,6},{2,0},{4,2},{6,4},{1,7},{3,1},{5,3},{7,5},{8,14},{10,8},{12,... | collective-permute-start | bytes 196616 | tf_op jit(solution)/shard_map/ppermute | solution.py:297
  273.6 5.3 %collective-permute-start.10 = (f32[40,128]{1,0:T(8,128)S(1)}, f32[40,128]{1,0:T(8,128)S(1)}, u32[]{:S(2)}, u32[]{:S(2)}) collective-permute-start(f32[40,128]{1,0:T(8,128)S(1)} %add.54), channel_id=1, source_target_pairs={{0,4},{2,6},{4,0},{6,2},{1,5},{3,7},{5,1},{7,3},{8,12},{10,14},{12... | collective-permute-start | bytes 61448 | tf_op jit(solution)/shard_map/ppermute | solution.py:221
  280.8 5.0 %collective-permute-start.14 = (f32[40,128]{1,0:T(8,128)S(1)}, f32[40,128]{1,0:T(8,128)S(1)}, u32[]{:S(2)}, u32[]{:S(2)}) collective-permute-start(f32[40,128]{1,0:T(8,128)S(1)} %add_add_fusion.2), channel_id=1, source_target_pairs={{0,24},{8,0},{16,8},{24,16},{1,25},{9,1},{17,9},{25,17},{2,26},{10... | collective-permute-start | bytes 61448 | tf_op jit(solution)/shard_map/ppermute | solution.py:221
  284.2 5.3 %collective-permute-start.13 = (f32[40,128]{1,0:T(8,128)S(1)}, f32[40,128]{1,0:T(8,128)S(1)}, u32[]{:S(2)}, u32[]{:S(2)}) collective-permute-start(f32[40,128]{1,0:T(8,128)S(1)} %add_add_fusion.2), channel_id=1, source_target_pairs={{0,16},{8,24},{16,0},{24,8},{1,17},{9,25},{17,1},{25,9},{2,18},{10... | collective-permute-start | bytes 61448 | tf_op jit(solution)/shard_map/ppermute | solution.py:221
  285.0 5.0 %collective-permute-start.12 = (f32[40,128]{1,0:T(8,128)S(1)}, f32[40,128]{1,0:T(8,128)S(1)}, u32[]{:S(2)}, u32[]{:S(2)}) collective-permute-start(f32[40,128]{1,0:T(8,128)S(1)} %add_add_fusion.2), channel_id=1, source_target_pairs={{0,8},{8,16},{16,24},{24,0},{1,9},{9,17},{17,25},{25,1},{2,10},{10... | collective-permute-start | bytes 61448 | tf_op jit(solution)/shard_map/ppermute | solution.py:221
  290.0 9.8 %collective-permute-start.21 = (f32[40,128]{1,0:T(8,128)S(1)}, f32[40,128]{1,0:T(8,128)S(1)}, u32[]{:S(2)}, u32[]{:S(2)}) collective-permute-start(f32[40,128]{1,0:T(8,128)S(1)} %add_add_fusion.1), channel_id=1, source_target_pairs={{0,224},{32,0},{64,32},{96,64},{128,96},{160,128},{192,160},{224,1... | collective-permute-start | bytes 61448 | tf_op jit(solution)/shard_map/ppermute | solution.py:221
  291.5 12.2 %collective-permute-start.20 = (f32[40,128]{1,0:T(8,128)S(1)}, f32[40,128]{1,0:T(8,128)S(1)}, u32[]{:S(2)}, u32[]{:S(2)}) collective-permute-start(f32[40,128]{1,0:T(8,128)S(1)} %add_add_fusion.1), channel_id=1, source_target_pairs={{0,192},{32,224},{64,0},{96,32},{128,64},{160,96},{192,128},{224,1... | collective-permute-start | bytes 61448 | tf_op jit(solution)/shard_map/ppermute | solution.py:221
  293.7 10.1 %collective-permute-start.19 = (f32[40,128]{1,0:T(8,128)S(1)}, f32[40,128]{1,0:T(8,128)S(1)}, u32[]{:S(2)}, u32[]{:S(2)}) collective-permute-start(f32[40,128]{1,0:T(8,128)S(1)} %add_add_fusion.1), channel_id=1, source_target_pairs={{0,160},{32,192},{64,224},{96,0},{128,32},{160,64},{192,96},{224,1... | collective-permute-start | bytes 61448 | tf_op jit(solution)/shard_map/ppermute | solution.py:221
  295.9 7.9 %collective-permute-start.18 = (f32[40,128]{1,0:T(8,128)S(1)}, f32[40,128]{1,0:T(8,128)S(1)}, u32[]{:S(2)}, u32[]{:S(2)}) collective-permute-start(f32[40,128]{1,0:T(8,128)S(1)} %add_add_fusion.1), channel_id=1, source_target_pairs={{0,128},{32,160},{64,192},{96,224},{128,0},{160,32},{192,64},{224,... | collective-permute-start | bytes 61448 | tf_op jit(solution)/shard_map/ppermute | solution.py:221
  298.1 6.9 %collective-permute-start.17 = (f32[40,128]{1,0:T(8,128)S(1)}, f32[40,128]{1,0:T(8,128)S(1)}, u32[]{:S(2)}, u32[]{:S(2)}) collective-permute-start(f32[40,128]{1,0:T(8,128)S(1)} %add_add_fusion.1), channel_id=1, source_target_pairs={{0,96},{32,128},{64,160},{96,192},{128,224},{160,0},{192,32},{224,... | collective-permute-start | bytes 61448 | tf_op jit(solution)/shard_map/ppermute | solution.py:221
  299.9 5.9 %collective-permute-start.16 = (f32[40,128]{1,0:T(8,128)S(1)}, f32[40,128]{1,0:T(8,128)S(1)}, u32[]{:S(2)}, u32[]{:S(2)}) collective-permute-start(f32[40,128]{1,0:T(8,128)S(1)} %add_add_fusion.1), channel_id=1, source_target_pairs={{0,64},{32,96},{64,128},{96,160},{128,192},{160,224},{192,0},{224,... | collective-permute-start | bytes 61448 | tf_op jit(solution)/shard_map/ppermute | solution.py:221
  303.7 5.0 %collective-permute-start.15 = (f32[40,128]{1,0:T(8,128)S(1)}, f32[40,128]{1,0:T(8,128)S(1)}, u32[]{:S(2)}, u32[]{:S(2)}) collective-permute-start(f32[40,128]{1,0:T(8,128)S(1)} %add_add_fusion.1), channel_id=1, source_target_pairs={{0,32},{32,64},{64,96},{96,128},{128,160},{160,192},{192,224},{224... | collective-permute-start | bytes 61448 | tf_op jit(solution)/shard_map/ppermute | solution.py:221
  (30 other events, 405.2 us)
Sparse Core Ops, SparseCore 0:
  22.5 41.1 all-gather.5
  65.5 37.3 all-gather.7
  105.5 35.7 reduce-scatter.4
  143.7 35.8 reduce-scatter.6
  182.0 35.7 reduce-scatter.8
  220.4 35.8 reduce-scatter.10

commit v3 on v1

v3 whole, which is shorter than its diff:
```python
import functools

import jax
import jax.numpy as jnp
import numpy as np
from jax import lax
from jax.experimental import pallas as pl
from jax.experimental.pallas import tpu as pltpu
from jax.sharding import Mesh
from jax.sharding import PartitionSpec as P

TILE = 128
PROBES = 32
UNROLL = 32
TAIL = 8
SPLIT = 5
BIN = 1536 + 2 * UNROLL
NUGGET = 2.0
KERNEL_SCALE = 0.1
HIGHEST = lax.Precision.HIGHEST
f32, bf16 = jnp.float32, jnp.bfloat16
VMEM = pl.BlockSpec(memory_space=pltpu.VMEM)
SMEM = pl.BlockSpec(memory_space=pltpu.SMEM)
NT = (((1,), (1,)), ((), ()))
NN = (((1,), (0,)), ((), ()))
TN = (((0,), (0,)), ((), ()))
PARAMS = pltpu.CompilerParams(vmem_limit_bytes=24 * 2**20)


def pack_kernel(direction_ref, positions_ref, packed_ref):
    for t in range(8):
        packed_ref[t * 32 : (t + 1) * 32, :] = direction_ref[:, t * TILE : (t + 1) * TILE].astype(bf16)
    where = positions_ref[...].astype(f32)
    rows = [where[d : d + 1, t * TILE : (t + 1) * TILE] for d in range(2) for t in range(8)]
    packed_ref[256:272, :] = jnp.concatenate(rows, 0).astype(bf16)


def radial(square):
    distance = pl.reciprocal(lax.rsqrt(square), approx=True)
    remain = jnp.maximum(1.0 - distance, 0.0)
    remain2 = remain * remain
    return ((remain2 * remain2) * (1.25 - remain)).astype(bf16)


def bin_kernel(place_ref, pairs_ref, bins_ref, count_ref):
    live, y_own, core_own = place_ref[0], place_ref[1], place_ref[2]

    def step(i, front):
        for u in range(8):
            e = i * 8 + u
            a, b = pairs_ref[0, e], pairs_ref[1, e]
            shift = (y_own - (a >> 4)) & 3
            slot = shift + ((((a >> 3) & 1) ^ core_own) << 2)
            entry = (slot << 3) + (a & 7) + (b << 8) + ((e < live).astype(jnp.int32) << 16)
            first = (b & 7) < SPLIT
            bins_ref[jnp.where(first, front, BIN - 1 - (e - front))] = entry
            front = front + first.astype(jnp.int32)
        return front

    groups = (live + 7) >> 3
    front = lax.fori_loop(0, groups, step, jnp.int32(0))
    back = groups * 8 - front
    count_ref[0] = front
    count_ref[1] = back
    for j in range(TAIL):
        bins_ref[front + j] = 0
        bins_ref[BIN - 1 - back - j] = SPLIT << 8


def spread(line):
    return jnp.broadcast_to(line, (TILE, TILE)).T


def part_kernel(part, *refs):
    if part == 0:
        count_ref, bins_ref, own_ref, near_ref, col_ref, row_acc, col_out, own_out, px, py, qx, qy, col_acc = refs
        row_acc[...] = jnp.zeros_like(row_acc)
        where = own_ref[256:272, :].astype(f32)
        for t in range(8):
            dx = spread(where[t : t + 1]) - where[t : t + 1]
            dy = spread(where[8 + t : 9 + t]) - where[8 + t : 9 + t]
            block = radial(dx * dx + dy * dy)
            own_out[:, t * TILE : (t + 1) * TILE] = KERNEL_SCALE * lax.dot_general(
                own_ref[t * 32 : (t + 1) * 32, :], block, NT, preferred_element_type=f32
            )
    else:
        count_ref, bins_ref, near_ref, col_ref, row_acc, row_out, col_out, px, py, qx, qy, col_acc = refs
    def row_prepare(r, carry):
        where = near_ref[r, 256:272, :].astype(f32)
        for t in range(8):
            px[r * 8 + t] = spread(where[t : t + 1])
            py[r * 8 + t] = spread(where[8 + t : 9 + t])
        return carry

    lax.fori_loop(0, 8, row_prepare, 0)
    tiles = range(SPLIT) if part == 0 else range(SPLIT, 8)
    first, number = tiles[0], len(tiles)
    live = count_ref[part]
    col_acc[...] = jnp.zeros_like(col_acc)

    def col_prepare(r, carry):
        where = col_ref[r, 256:272, :].astype(f32)
        for t in tiles:
            qx[r * 8 + t] = jnp.broadcast_to(where[t : t + 1], (8, TILE))
            qy[r * 8 + t] = jnp.broadcast_to(where[8 + t : 9 + t], (8, TILE))
        return carry

    lax.fori_loop(0, 32, col_prepare, 0)

    def several(start, size):
        results = []
        for u in range(size):
            e = start + u
            both = bins_ref[e if part == 0 else BIN - 1 - e]
            a, b = both & 63, (both >> 8) & 255
            keep = jnp.where(e < live, both >> 16, 0).astype(f32).astype(bf16)
            near = near_ref[a >> 3, pl.ds(pl.multiple_of((a & 7) * 32, 32), 32), :] * keep
            far = col_ref[b >> 3, pl.ds(pl.multiple_of((b & 7) * 32, 32), 32), :] * keep
            dx = px[a].reshape(16, 8, TILE) - qx[b][None]
            dy = py[a].reshape(16, 8, TILE) - qy[b][None]
            block = radial((dx * dx + dy * dy).reshape(TILE, TILE))
            forward = lax.dot_general(far, block, NT, preferred_element_type=f32)
            backward = lax.dot_general(near, block, NN, preferred_element_type=f32)
            results.append((a, b, forward, backward))
        for a, b, forward, backward in results:
            row_acc[a] += forward
            col_acc[b] += backward

    whole = live // UNROLL

    def body(i, carry):
        several(i * UNROLL, UNROLL)
        return carry

    def tail(i, carry):
        several(whole * UNROLL + i * TAIL, TAIL)
        return carry

    lax.fori_loop(0, whole, body, 0)
    lax.fori_loop(0, (live - whole * UNROLL + TAIL - 1) // TAIL, tail, 0)

    def finish(r, carry):
        for t in range(number):
            col_out[(r & 3) * 8 + (r >> 2), t * 32 : (t + 1) * 32, :] = (KERNEL_SCALE * col_acc[r * 8 + first + t]).astype(bf16)
        return carry

    lax.fori_loop(0, 32, finish, 0)
    if part == 1:

        def finish_row(r, carry):
            for t in range(8):
                row_out[r, t * 32 : (t + 1) * 32, :] = (KERNEL_SCALE * row_acc[r * 8 + t]).astype(bf16)
            return carry

        lax.fori_loop(0, 8, finish_row, 0)


def dot32(former, latter, dims):
    return lax.dot_general(former, latter, dims, precision=HIGHEST, preferred_element_type=f32)


def gram_kernel(direction_ref, residual_ref, own_ref, row_ref, col0_ref, col1_ref, image_ref, gram_ref):
    for t in range(8):
        here = slice(t * 32, (t + 1) * 32)
        lanes = slice(t * TILE, (t + 1) * TILE)
        total = NUGGET * direction_ref[:, lanes] + own_ref[:, lanes]
        for part in range(row_ref.shape[0]):
            total = total + row_ref[part, here, :].astype(f32)
        col_ref, place = (col0_ref, t) if t < SPLIT else (col1_ref, t - SPLIT)
        for part in range(col_ref.shape[0]):
            total = total + col_ref[part, place * 32 : (place + 1) * 32, :].astype(f32)
        image_ref[:, lanes] = total
    direction, residual, image = direction_ref[...], residual_ref[...], image_ref[...]
    gram_ref[0:32, 0:32] = dot32(direction, image, NT)
    gram_ref[0:32, 32:64] = dot32(direction, residual, NT)
    gram_ref[0:32, 64:96] = dot32(residual, residual, NT)
    gram_ref[0:32, 96:128] = dot32(residual, image, NT)
    square = dot32(image, image, NT)
    for t in range(4):
        gram_ref[32:40, t * 32 : (t + 1) * 32] = square[t * 8 : (t + 1) * 8]


def solve_kernel(gram_ref, solution_ref, residual_ref, direction_ref, image_ref, solution_out, residual_out, direction_out):
    gram = gram_ref[...]
    curvature, crossing = gram[0:32, 0:32], gram[0:32, 32:64]
    norm_old, mixed = gram[0:32, 64:96], gram[0:32, 96:128]
    square = jnp.concatenate([gram[32:40, t * 32 : (t + 1) * 32] for t in range(4)], 0)
    row = lax.broadcasted_iota(jnp.int32, (32, 64), 0)
    lane = lax.broadcasted_iota(jnp.int32, (32, 64), 1)
    unit = jnp.where(row[:, :32] == lane[:, :32], 1.0, 0.0).astype(f32)
    first = jnp.concatenate([0.5 * (curvature + curvature.T), crossing], 1)
    second = jnp.concatenate([0.5 * (norm_old + norm_old.T), unit], 1)

    def eliminate(table, k):
        pivot_row = table[k : k + 1, :] / table[k : k + 1, k : k + 1]
        return jnp.where(row == k, pivot_row, table - table[:, k : k + 1] * pivot_row)

    for k in range(32):
        first, second = eliminate(first, k), eliminate(second, k)
    alpha, inverse = first[:, 32:64], second[:, 32:64]
    cross = dot32(mixed, alpha, NN)
    norm_new = 0.5 * (norm_old + norm_old.T) - cross - cross.T + dot32(alpha, dot32(square, alpha, NN), TN)
    beta = dot32(inverse, norm_new, NN)
    direction = direction_ref[...]
    residual_next = residual_ref[...] - dot32(alpha, image_ref[...], TN)
    residual_out[...] = residual_next
    solution_out[...] = solution_ref[...] + dot32(alpha, direction, TN)
    direction_out[...] = residual_next + dot32(beta, direction, TN)


def shifts(value, axis, size):
    return [lax.ppermute(value, axis, [(i, (i + k) % size) for i in range(size)]) for k in range(1, size)]


def swap(value):
    return lax.ppermute(value, "core", [(0, 1), (1, 0)])


def on_device(solution_field, residual, direction, positions, tile_pairs, pair_count):
    shape = jax.ShapeDtypeStruct
    own_points = direction.shape[1]
    y_own, core_own = lax.axis_index("y"), lax.axis_index("core")
    packed = pl.pallas_call(
        pack_kernel, out_shape=shape((272, TILE), bf16), in_specs=[VMEM] * 2, out_specs=VMEM, name="pack"
    )(direction, positions)
    packed, other = lax.optimization_barrier((packed, swap(packed)))
    chip = jnp.stack([packed, other])
    around = shifts(chip, "y", 4)
    x_all = lax.all_gather(packed, "x")
    x_all, around = lax.optimization_barrier((x_all, around))
    col_all = lax.all_gather(x_all, "z").reshape(32, 272, TILE)
    row_all = jnp.concatenate([v[:1] for v in [chip] + around] + [v[1:] for v in [chip] + around], 0)
    place = jnp.stack([pair_count[0], y_own, core_own]).astype(jnp.int32)
    bins, counts = pl.pallas_call(
        bin_kernel,
        out_shape=(shape((BIN,), jnp.int32), shape((2,), jnp.int32)),
        in_specs=[SMEM, SMEM],
        out_specs=(SMEM, SMEM),
        name="bins",
    )(place, tile_pairs)
    acc = shape((64, PROBES, TILE), f32)
    scratch = [pltpu.VMEM((64, TILE, TILE), f32)] * 2
    scratch += [pltpu.VMEM((256, 8, TILE), f32), pltpu.VMEM((256, 8, TILE), f32), pltpu.VMEM((256, PROBES, TILE), f32)]

    def reduced(col_out):
        number = col_out.shape[1] // 32
        blocks = lax.all_to_all(col_out.reshape(4, 8 * number * 32, TILE), "x", 0, 0)
        blocks = jnp.sum(blocks.astype(f32), 0).astype(bf16)
        return blocks.reshape(8, number * 32, TILE)

    row_acc, col_first, own_product = pl.pallas_call(
        functools.partial(part_kernel, 0),
        out_shape=(acc, shape((32, SPLIT * 32, TILE), bf16), shape((PROBES, own_points), f32)),
        in_specs=[SMEM] * 2 + [VMEM] * 3,
        out_specs=(VMEM,) * 3,
        scratch_shapes=scratch,
        compiler_params=PARAMS,
        name="pairs_first",
    )(counts, bins, packed, row_all, col_all)
    row_sum, col_second = pl.pallas_call(
        functools.partial(part_kernel, 1),
        out_shape=(shape((8, 256, TILE), bf16), shape((32, (8 - SPLIT) * 32, TILE), bf16)),
        in_specs=[SMEM] * 2 + [VMEM] * 3,
        out_specs=(VMEM,) * 2,
        scratch_shapes=scratch,
        compiler_params=PARAMS,
        name="pairs_second",
    )(counts, bins, row_all, col_all, row_acc)
    first = reduced(col_first)
    second, first = lax.optimization_barrier((col_second, first))
    second = reduced(second)
    col_first = lax.all_to_all(first, "z", 0, 0)
    half = (row_sum[:4].astype(f32) + swap(row_sum[4:]).astype(f32)).astype(bf16)
    row_parts = [half[0]] + [
        lax.ppermute(half[k], "y", [(i, (i - k) % 4) for i in range(4)]) for k in range(1, 4)
    ]
    row_parts = jnp.stack(row_parts)
    col_second = lax.all_to_all(second, "z", 0, 0)
    image, gram = pl.pallas_call(
        gram_kernel,
        out_shape=(shape((PROBES, own_points), f32), shape((40, TILE), f32)),
        in_specs=[VMEM] * 6,
        out_specs=(VMEM, VMEM),
        compiler_params=PARAMS,
        name="gram",
    )(direction, residual, own_product, row_parts, col_first, col_second)
    gram = gram + swap(gram)
    for axis, size in (("y", 4), ("x", 4), ("z", 8)):
        gram = sum(shifts(gram, axis, size), gram)
    return pl.pallas_call(
        solve_kernel,
        out_shape=(shape((PROBES, own_points), f32),) * 3,
        in_specs=[VMEM] * 5,
        out_specs=(VMEM,) * 3,
        compiler_params=PARAMS,
        name="solve",
    )(gram, solution_field, residual, direction, image)


def solution(mesh):
    fine = Mesh(np.asarray(mesh.devices).reshape(8, 4, 4, 2), ("z", "x", "y", "core"))
    points = P(None, ("z", "x", "y", "core"))
    return jax.shard_map(
        on_device,
        mesh=fine,
        in_specs=(points,) * 5 + (P(("z", "x", "y", "core")),),
        out_specs=(points,) * 3,
        check_vma=False,
    )
```

time: 237 us -> 242 us (1.021)
  Pallas kernels: 74.2 us -> 30 us
  starting transfers between devices: 34.3 us -> 70.8 us
  blocking collectives: 14.4 us -> 39.1 us
  waiting for transfers between devices: 93.2 us -> 73 us
  local copies, waits for them, and re-layouts: 4 us -> 8.19 us
  other arithmetic: 1.14 us -> 4.83 us
    pallas_call x1 -> x3, Pallas kernels: 66.9 us -> 22.9 us  [the longest x1 10.7 us: on_device(): pl.pallas_call(functools.partial(part_kernel, 0), out_shape=(acc, shape((...]
    all_to_all x1 -> x3, starting transfers between devices: 6.42 us -> 40.3 us  [the longest x1 31.6 us: reduced(): lax.all_to_all(col_out.reshape(4, 8 * number * 32, TILE), 'x', 0, 0)]
    all_to_all x0 -> x1, blocking collectives: none -> 25.9 us  [reduced(): lax.all_to_all(col_out.reshape(4, 8 * number * 32, TILE), 'x', 0, 0)]
    all_to_all x1 -> x3, waiting for transfers between devices: 37 us -> 17.4 us  [the longest x1 8.62 us: on_device(): col_first = lax.all_to_all(first, 'z', 0, 0)]
    all_gather x1, waiting for transfers between devices: 32.6 us -> 36.8 us  [on_device(): col_all = lax.all_gather(x_all, 'z').reshape(32, 272, TILE)]
    unnamed x18 -> x37, local copies, waits for them, and re-layouts: 3.92 us -> 8.13 us
    ppermute x16, waiting for transfers between devices: 15.3 us -> 11.4 us  [shifts(): lax.ppermute(value, axis, [(i, (i + k) % size) for i in range(size)])]
    reduce_sum x0 -> x2, other arithmetic: none -> 3.2 us  [reduced(): blocks = jnp.sum(blocks.astype(f32), 0).astype(bf16)]
  transfers between devices with their start and end apart: 24 -> 26, of which waited for: 18 -> 17; matrix products, arithmetic and copies ran while one was open for 1% -> 1% of each run, Pallas kernels for 0% -> 5%
where the time goes in v3:
time: 242 us; the launch traced here: 241 us
  waiting for transfers between devices  73 us (30%)
  starting transfers between devices  70.8 us (29%)
  blocking collectives  39.1 us (16%)
  Pallas kernels  30 us (12%)
  between operations  14.9 us (6%)
  local copies, waits for them, and re-layouts  8.19 us (3%)
  other arithmetic  4.83 us (2%)
    all_gather x1, waiting for transfers between devices, on_device(): col_all = lax.all_gather(x_all, 'z').reshape(32, 272, TILE)  36.8 us
    all_to_all x1, starting transfers between devices, reduced(): lax.all_to_all(col_out.reshape(4, 8 * number * 32, TILE), 'x', 0, 0)  31.6 us
    ppermute x16, starting transfers between devices, shifts(): lax.ppermute(value, axis, [(i, (i + k) % size) for i in range(size)])  26.4 us
    all_to_all x1, blocking collectives, reduced(): lax.all_to_all(col_out.reshape(4, 8 * number * 32, TILE), 'x', 0, 0)  25.9 us
    all_gather x1, blocking collectives, on_device(): x_all = lax.all_gather(packed, 'x')  13.2 us
    ppermute x16, waiting for transfers between devices, shifts(): lax.ppermute(value, axis, [(i, (i + k) % size) for i in range(size)])  11.4 us
    pallas_call x1, Pallas kernels, on_device(): pl.pallas_call(functools.partial(part_kernel, 0), out_shape=(acc, shape((...  10.7 us
    all_to_all x1, waiting for transfers between devices, on_device(): col_first = lax.all_to_all(first, 'z', 0, 0)  8.62 us
  transfers between devices with their start and end apart: 26, of which 17 were waited for; matrix products, arithmetic and copies ran while one was open for 1% of the time, Pallas kernels for 5%

profile of v3, /device:TPU:16, one launch (start us, length us, event | category | flops | bytes accessed | tf_op | source)
XLA Modules:
  0.0 240.8 jit_solution(1534518937659932464)
XLA Ops:
  11.7 2.9 %collective-permute-start.2 = (bf16[2,272,128]{2,1,0:T(8,128)(2,1)S(1)}, bf16[2,272,128]{2,1,0:T(8,128)(2,1)S(1)}, u32[]{:S(2)}, u32[]{:S(2)}) collective-permute-start(bf16[2,272,128]{2,1,0:T(8,128)(2,1)S(1)} %pad_maximum_fusion.1), channel_id=1, source_target_pairs={{0,4},{2,6},{4,0},{6,2},{1,5},{3,7},{5,1},{7,3},{8,12},{10,14},{12... | collective-permute-start | bytes 417800 | tf_op jit(solution)/shard_map/ppermute | solution.py:212
  15.9 13.2 %all-gather = bf16[1088,128]{1,0:T(8,128)(2,1)} all-gather(bf16[272,128]{1,0:T(8,128)(2,1)} %pack.1.refs_2_), channel_id=2, replica_groups=mesh['z'=8,'x'=4,'y'=4,'core'=2] {'x'}, dimensions={0}, use_global_device_ids=true | all-gather | bytes 348160 | tf_op jit(solution)/shard_map/all_gather | solution.py:229
  30.4 4.1 %bins.1 = (s32[1600]{0:T(1024)}, s32[2]{0:T(128)}) custom-call(s32[3]{0:T(128)} %pad_add_fusion.place_ref, s32[2,1536]{1,0:T(2,128)} %pairs_ref.1), custom_call_target="tpu_custom_call" | custom-call | tf_op jit(solution)/shard_map/bins/pallas_call | solution.py:234
  35.6 36.8 %all-gather.4.cloned.1.call-done.refs_4_.refs_3_ = bf16[32,272,128]{2,1,0:T(8,128)(2,1)} async-done(((bf16[4,272,128]{2,1,0:T(8,128)(2,1)}), bf16[32,272,128]{2,1,0:T(8,128)(2,1)}) %all-gather.4.cloned.1.call-update) | async-done | bytes 2228240 | tf_op jit(solution)/shard_map/all_gather | solution.py:231
  75.4 10.7 %pairs_first.1 = (f32[64,32,128]{2,1,0:T(8,128)S(1)}, bf16[32,160,128]{2,1,0:T(8,128)(2,1)S(1)}, f32[32,1024]{1,0:T(8,128)S(1)}) custom-call(s32[2]{0:T(128)S(1)} %copy-done.13, s32[1600]{0:T(1024)S(1)} %copy-done.11, bf16[272,128]{1,0:T(8,128)(2,1)S(1)} %copy-done.2, bf16[8,272,128]{2,1,0:T(8,128)(2,1)S(1)} %slice_dynamic-update-slice_fusion.refs_3_.refs_2_, ...), custom_call_target="tpu_custom_call" | custom-call | tf_op jit(solution)/shard_map/pairs_first/pallas_call | solution.py:251
  88.2 31.6 %all-to-all-start = ((bf16[4,1280,128]{2,1,0:T(8,128)(2,1)}), bf16[4,1280,128]{2,1,0:T(8,128)(2,1)}, u32[]{:S(2)}, u32[]{:S(2)}) async-start(bf16[4,1280,128]{2,1,0:T(8,128)(2,1)} %bitcast.21), calls=%async_computation | async-start | bytes 2621440 | tf_op jit(solution)/shard_map/all_to_all | solution.py:247
  121.0 8.1 %pairs_second.1 = (bf16[8,256,128]{2,1,0:T(8,128)(2,1)S(1)}, bf16[32,96,128]{2,1,0:T(8,128)(2,1)S(1)}) custom-call(s32[2]{0:T(128)S(1)} %copy-done.14, s32[1600]{0:T(1024)S(1)} %copy-done.12, bf16[8,272,128]{2,1,0:T(8,128)(2,1)S(1)} %slice_dynamic-update-slice_fusion.refs_3_.refs_2_, bf16[32,272,128]{2,1,0:T(8,128)(2,1)S(1)} %copy-done.1, ...), custom_call_target="tpu_custom_call" | custom-call | tf_op jit(solution)/shard_map/pairs_second/pallas_call | solution.py:260
  130.0 6.3 %all-to-all-done = bf16[4,1280,128]{2,1,0:T(8,128)(2,1)} async-done(((bf16[4,1280,128]{2,1,0:T(8,128)(2,1)}), bf16[4,1280,128]{2,1,0:T(8,128)(2,1)}, u32[]{:S(2)}, u32[]{:S(2)}) %all-to-all-start) | async-done | bytes 1310752 | tf_op jit(solution)/shard_map/all_to_all | solution.py:247
  136.3 2.4 reduce_sum.24
  138.7 25.9 %all_to_all.20 = bf16[4,768,128]{2,1,0:T(8,128)(2,1)S(1)} all-to-all(bf16[4,768,128]{2,1,0:T(8,128)(2,1)S(1)} %bitcast.22), channel_id=1, replica_groups=mesh['z'=8,'x'=4,'y'=4,'core'=2] {'x'}, dimensions={0} | all-to-all | bytes 1572864 | tf_op jit(solution)/shard_map/all_to_all | solution.py:247
  164.6 5.3 %all-to-all-start.1 = ((bf16[8,160,128]{2,1,0:T(8,128)(2,1)}), bf16[8,160,128]{2,1,0:T(8,128)(2,1)S(1)}, u32[]{:S(2)}, u32[]{:S(2)}) async-start(bf16[8,160,128]{2,1,0:T(8,128)(2,1)} %bitcast.12), calls=%async_computation.1 | async-start | bytes 655360 | tf_op jit(solution)/shard_map/all_to_all | solution.py:272
  172.4 8.6 %all-to-all-done.1.col0_ref = bf16[8,160,128]{2,1,0:T(8,128)(2,1)S(1)} async-done(((bf16[8,160,128]{2,1,0:T(8,128)(2,1)}), bf16[8,160,128]{2,1,0:T(8,128)(2,1)S(1)}, u32[]{:S(2)}, u32[]{:S(2)}) %all-to-all-start.1) | async-done | bytes 327712 | tf_op jit(solution)/shard_map/all_to_all | solution.py:272
  181.1 3.4 %all-to-all-start.3 = ((bf16[8,96,128]{2,1,0:T(8,128)(2,1)}), bf16[8,96,128]{2,1,0:T(8,128)(2,1)S(1)}, u32[]{:S(2)}, u32[]{:S(2)}) async-start(bf16[8,96,128]{2,1,0:T(8,128)(2,1)} %bitcast.14), calls=%async_computation.3 | async-start | bytes 393216 | tf_op jit(solution)/shard_map/all_to_all | solution.py:278
  186.4 2.1 collective-permute-start.5
  188.8 2.5 %collective-permute-done.6 = bf16[256,128]{1,0:T(8,128)(2,1)S(1)} collective-permute-done((bf16[256,128]{1,0:T(8,128)(2,1)S(1)}, bf16[256,128]{1,0:T(8,128)(2,1)S(1)}, u32[]{:S(2)}, u32[]{:S(2)}) %collective-permute-start.6) | collective-permute-done | bytes 65568 | tf_op jit(solution)/shard_map/ppermute | solution.py:275
  191.7 2.5 %all-to-all-done.3.col1_ref = bf16[8,96,128]{2,1,0:T(8,128)(2,1)S(1)} async-done(((bf16[8,96,128]{2,1,0:T(8,128)(2,1)}), bf16[8,96,128]{2,1,0:T(8,128)(2,1)S(1)}, u32[]{:S(2)}, u32[]{:S(2)}) %all-to-all-start.3) | async-done | bytes 196640 | tf_op jit(solution)/shard_map/all_to_all | solution.py:278
  196.6 2.7 %collective-permute-start.10 = (f32[40,128]{1,0:T(8,128)S(1)}, f32[40,128]{1,0:T(8,128)S(1)}, u32[]{:S(2)}, u32[]{:S(2)}) collective-permute-start(f32[40,128]{1,0:T(8,128)S(1)} %add.46), channel_id=1, source_target_pairs={{0,4},{2,6},{4,0},{6,2},{1,5},{3,7},{5,1},{7,3},{8,12},{10,14},{12... | collective-permute-start | bytes 61448 | tf_op jit(solution)/shard_map/ppermute | solution.py:212
  206.9 2.7 %collective-permute-done.13 = f32[40,128]{1,0:T(8,128)S(1)} collective-permute-done((f32[40,128]{1,0:T(8,128)S(1)}, f32[40,128]{1,0:T(8,128)S(1)}, u32[]{:S(2)}, u32[]{:S(2)}) %collective-permute-start.13) | collective-permute-done | bytes 20512 | tf_op jit(solution)/shard_map/ppermute | solution.py:212
  210.8 2.3 collective-permute-start.21
  213.1 2.3 collective-permute-start.20
  216.9 3.6 %collective-permute-start.18 = (f32[40,128]{1,0:T(8,128)S(1)}, f32[40,128]{1,0:T(8,128)S(1)}, u32[]{:S(2)}, u32[]{:S(2)}) collective-permute-start(f32[40,128]{1,0:T(8,128)S(1)} %add_add_fusion.1), channel_id=1, source_target_pairs={{0,128},{32,160},{64,192},{96,224},{128,0},{160,32},{192,64},{224,... | collective-permute-start | bytes 61448 | tf_op jit(solution)/shard_map/ppermute | solution.py:212
  220.7 3.6 %collective-permute-start.16 = (f32[40,128]{1,0:T(8,128)S(1)}, f32[40,128]{1,0:T(8,128)S(1)}, u32[]{:S(2)}, u32[]{:S(2)}) collective-permute-start(f32[40,128]{1,0:T(8,128)S(1)} %add_add_fusion.1), channel_id=1, source_target_pairs={{0,64},{32,96},{64,128},{96,160},{128,192},{160,224},{192,0},{224,... | collective-permute-start | bytes 61448 | tf_op jit(solution)/shard_map/ppermute | solution.py:212
  227.3 2.0 collective-permute-done.15
  229.3 4.7 %solve.1 = (f32[32,1024]{1,0:T(8,128)}, f32[32,1024]{1,0:T(8,128)}, f32[32,1024]{1,0:T(8,128)}) custom-call(f32[40,128]{1,0:T(8,128)S(1)} %add_add_fusion.gram_ref, f32[32,1024]{1,0:T(8,128)S(1)} %copy-done.10, f32[32,1024]{1,0:T(8,128)S(1)} %copy-done.9, f32[32,1024]{1,0:T(8,128)S(1)} %copy-done.4, f32[32,1024]{1,0:T(8,128)S(1)} %get-tuple-element.36.image_ref), custom_call_target="tpu_custom_call" | custom-call | tf_op jit(solution)/shard_map/solve/pallas_call | solution.py:290
  (87 shorter events, 35.7 us)
Async XLA Ops:
  7.2 65.3 %all-gather.4.cloned.1.call-start = ((), (), s32[]{:S(2)}) async-start(), calls=%async_computation.4 | async-start | bytes 2506752 | tf_op jit(solution)/shard_map/all_gather | solution.py:231
  11.1 18.0 %collective-permute-start.3 = (bf16[2,272,128]{2,1,0:T(8,128)(2,1)S(1)}, bf16[2,272,128]{2,1,0:T(8,128)(2,1)S(1)}, u32[]{:S(2)}, u32[]{:S(2)}) collective-permute-start(bf16[2,272,128]{2,1,0:T(8,128)(2,1)S(1)} %pad_maximum_fusion.1), channel_id=1, source_target_pairs={{0,6},{2,0},{4,2},{6,4},{1,7},{3,1},{5,3},{7,5},{8,14},{10,8},{12,... | collective-permute-start | bytes 417800 | tf_op jit(solution)/shard_map/ppermute | solution.py:212
  11.7 17.5 %collective-permute-start.2 = (bf16[2,272,128]{2,1,0:T(8,128)(2,1)S(1)}, bf16[2,272,128]{2,1,0:T(8,128)(2,1)S(1)}, u32[]{:S(2)}, u32[]{:S(2)}) collective-permute-start(bf16[2,272,128]{2,1,0:T(8,128)(2,1)S(1)} %pad_maximum_fusion.1), channel_id=1, source_target_pairs={{0,4},{2,6},{4,0},{6,2},{1,5},{3,7},{5,1},{7,3},{8,12},{10,14},{12... | collective-permute-start | bytes 417800 | tf_op jit(solution)/shard_map/ppermute | solution.py:212
  14.6 14.6 %collective-permute-start.1 = (bf16[2,272,128]{2,1,0:T(8,128)(2,1)S(1)}, bf16[2,272,128]{2,1,0:T(8,128)(2,1)S(1)}, u32[]{:S(2)}, u32[]{:S(2)}) collective-permute-start(bf16[2,272,128]{2,1,0:T(8,128)(2,1)S(1)} %pad_maximum_fusion.1), channel_id=1, source_target_pairs={{0,2},{2,4},{4,6},{6,0},{1,3},{3,5},{5,7},{7,1},{8,10},{10,12},{12... | collective-permute-start | bytes 417800 | tf_op jit(solution)/shard_map/ppermute | solution.py:212
  88.2 48.1 %all-to-all-start = ((bf16[4,1280,128]{2,1,0:T(8,128)(2,1)}), bf16[4,1280,128]{2,1,0:T(8,128)(2,1)}, u32[]{:S(2)}, u32[]{:S(2)}) async-start(bf16[4,1280,128]{2,1,0:T(8,128)(2,1)} %bitcast.21), calls=%async_computation | async-start | bytes 2621440 | tf_op jit(solution)/shard_map/all_to_all | solution.py:247
  164.6 16.5 %all-to-all-start.1 = ((bf16[8,160,128]{2,1,0:T(8,128)(2,1)}), bf16[8,160,128]{2,1,0:T(8,128)(2,1)S(1)}, u32[]{:S(2)}, u32[]{:S(2)}) async-start(bf16[8,160,128]{2,1,0:T(8,128)(2,1)} %bitcast.12), calls=%async_computation.1 | async-start | bytes 655360 | tf_op jit(solution)/shard_map/all_to_all | solution.py:272
  169.9 1.6 collective-permute-start.4
  181.1 13.1 %all-to-all-start.3 = ((bf16[8,96,128]{2,1,0:T(8,128)(2,1)}), bf16[8,96,128]{2,1,0:T(8,128)(2,1)S(1)}, u32[]{:S(2)}, u32[]{:S(2)}) async-start(bf16[8,96,128]{2,1,0:T(8,128)(2,1)} %bitcast.14), calls=%async_computation.3 | async-start | bytes 393216 | tf_op jit(solution)/shard_map/all_to_all | solution.py:278
  184.5 4.3 %collective-permute-start.7 = (bf16[256,128]{1,0:T(8,128)(2,1)S(1)}, bf16[256,128]{1,0:T(8,128)(2,1)S(1)}, u32[]{:S(2)}, u32[]{:S(2)}) collective-permute-start(bf16[256,128]{1,0:T(8,128)(2,1)S(1)} %get-tuple-element.38), channel_id=1, source_target_pairs={{0,2},{2,4},{4,6},{6,0},{1,3},{3,5},{5,7},{7,1},{8,10},{10,12},{12... | collective-permute-start | bytes 196616 | tf_op jit(solution)/shard_map/ppermute | solution.py:275
  185.5 5.8 %collective-permute-start.6 = (bf16[256,128]{1,0:T(8,128)(2,1)S(1)}, bf16[256,128]{1,0:T(8,128)(2,1)S(1)}, u32[]{:S(2)}, u32[]{:S(2)}) collective-permute-start(bf16[256,128]{1,0:T(8,128)(2,1)S(1)} %get-tuple-element.39), channel_id=1, source_target_pairs={{0,4},{2,6},{4,0},{6,2},{1,5},{3,7},{5,1},{7,3},{8,12},{10,14},{12... | collective-permute-start | bytes 196616 | tf_op jit(solution)/shard_map/ppermute | solution.py:275
  186.4 5.2 %collective-permute-start.5 = (bf16[256,128]{1,0:T(8,128)(2,1)S(1)}, bf16[256,128]{1,0:T(8,128)(2,1)S(1)}, u32[]{:S(2)}, u32[]{:S(2)}) collective-permute-start(bf16[256,128]{1,0:T(8,128)(2,1)S(1)} %get-tuple-element.40), channel_id=1, source_target_pairs={{0,6},{2,0},{4,2},{6,4},{1,7},{3,1},{5,3},{7,5},{8,14},{10,8},{12,... | collective-permute-start | bytes 196616 | tf_op jit(solution)/shard_map/ppermute | solution.py:275
  196.2 3.9 %collective-permute-start.11 = (f32[40,128]{1,0:T(8,128)S(1)}, f32[40,128]{1,0:T(8,128)S(1)}, u32[]{:S(2)}, u32[]{:S(2)}) collective-permute-start(f32[40,128]{1,0:T(8,128)S(1)} %add.46), channel_id=1, source_target_pairs={{0,6},{2,0},{4,2},{6,4},{1,7},{3,1},{5,3},{7,5},{8,14},{10,8},{12,... | collective-permute-start | bytes 61448 | tf_op jit(solution)/shard_map/ppermute | solution.py:212
  196.6 5.3 %collective-permute-start.10 = (f32[40,128]{1,0:T(8,128)S(1)}, f32[40,128]{1,0:T(8,128)S(1)}, u32[]{:S(2)}, u32[]{:S(2)}) collective-permute-start(f32[40,128]{1,0:T(8,128)S(1)} %add.46), channel_id=1, source_target_pairs={{0,4},{2,6},{4,0},{6,2},{1,5},{3,7},{5,1},{7,3},{8,12},{10,14},{12... | collective-permute-start | bytes 61448 | tf_op jit(solution)/shard_map/ppermute | solution.py:212
  199.3 3.8 %collective-permute-start.9 = (f32[40,128]{1,0:T(8,128)S(1)}, f32[40,128]{1,0:T(8,128)S(1)}, u32[]{:S(2)}, u32[]{:S(2)}) collective-permute-start(f32[40,128]{1,0:T(8,128)S(1)} %add.46), channel_id=1, source_target_pairs={{0,2},{2,4},{4,6},{6,0},{1,3},{3,5},{5,7},{7,1},{8,10},{10,12},{12... | collective-permute-start | bytes 61448 | tf_op jit(solution)/shard_map/ppermute | solution.py:212
  203.0 3.9 %collective-permute-start.14 = (f32[40,128]{1,0:T(8,128)S(1)}, f32[40,128]{1,0:T(8,128)S(1)}, u32[]{:S(2)}, u32[]{:S(2)}) collective-permute-start(f32[40,128]{1,0:T(8,128)S(1)} %add_add_fusion.2), channel_id=1, source_target_pairs={{0,24},{8,0},{16,8},{24,16},{1,25},{9,1},{17,9},{25,17},{2,26},{10... | collective-permute-start | bytes 61448 | tf_op jit(solution)/shard_map/ppermute | solution.py:212
  204.3 5.3 %collective-permute-start.13 = (f32[40,128]{1,0:T(8,128)S(1)}, f32[40,128]{1,0:T(8,128)S(1)}, u32[]{:S(2)}, u32[]{:S(2)}) collective-permute-start(f32[40,128]{1,0:T(8,128)S(1)} %add_add_fusion.2), channel_id=1, source_target_pairs={{0,16},{8,24},{16,0},{24,8},{1,17},{9,25},{17,1},{25,9},{2,18},{10... | collective-permute-start | bytes 61448 | tf_op jit(solution)/shard_map/ppermute | solution.py:212
  205.8 5.0 %collective-permute-start.12 = (f32[40,128]{1,0:T(8,128)S(1)}, f32[40,128]{1,0:T(8,128)S(1)}, u32[]{:S(2)}, u32[]{:S(2)}) collective-permute-start(f32[40,128]{1,0:T(8,128)S(1)} %add_add_fusion.2), channel_id=1, source_target_pairs={{0,8},{8,16},{16,24},{24,0},{1,9},{9,17},{17,25},{25,1},{2,10},{10... | collective-permute-start | bytes 61448 | tf_op jit(solution)/shard_map/ppermute | solution.py:212
  210.8 9.9 %collective-permute-start.21 = (f32[40,128]{1,0:T(8,128)S(1)}, f32[40,128]{1,0:T(8,128)S(1)}, u32[]{:S(2)}, u32[]{:S(2)}) collective-permute-start(f32[40,128]{1,0:T(8,128)S(1)} %add_add_fusion.1), channel_id=1, source_target_pairs={{0,224},{32,0},{64,32},{96,64},{128,96},{160,128},{192,160},{224,1... | collective-permute-start | bytes 61448 | tf_op jit(solution)/shard_map/ppermute | solution.py:212
  213.1 11.2 %collective-permute-start.20 = (f32[40,128]{1,0:T(8,128)S(1)}, f32[40,128]{1,0:T(8,128)S(1)}, u32[]{:S(2)}, u32[]{:S(2)}) collective-permute-start(f32[40,128]{1,0:T(8,128)S(1)} %add_add_fusion.1), channel_id=1, source_target_pairs={{0,192},{32,224},{64,0},{96,32},{128,64},{160,96},{192,128},{224,1... | collective-permute-start | bytes 61448 | tf_op jit(solution)/shard_map/ppermute | solution.py:212
  215.4 10.3 %collective-permute-start.19 = (f32[40,128]{1,0:T(8,128)S(1)}, f32[40,128]{1,0:T(8,128)S(1)}, u32[]{:S(2)}, u32[]{:S(2)}) collective-permute-start(f32[40,128]{1,0:T(8,128)S(1)} %add_add_fusion.1), channel_id=1, source_target_pairs={{0,160},{32,192},{64,224},{96,0},{128,32},{160,64},{192,96},{224,1... | collective-permute-start | bytes 61448 | tf_op jit(solution)/shard_map/ppermute | solution.py:212
  216.9 8.9 %collective-permute-start.18 = (f32[40,128]{1,0:T(8,128)S(1)}, f32[40,128]{1,0:T(8,128)S(1)}, u32[]{:S(2)}, u32[]{:S(2)}) collective-permute-start(f32[40,128]{1,0:T(8,128)S(1)} %add_add_fusion.1), channel_id=1, source_target_pairs={{0,128},{32,160},{64,192},{96,224},{128,0},{160,32},{192,64},{224,... | collective-permute-start | bytes 61448 | tf_op jit(solution)/shard_map/ppermute | solution.py:212
  220.5 6.8 %collective-permute-start.17 = (f32[40,128]{1,0:T(8,128)S(1)}, f32[40,128]{1,0:T(8,128)S(1)}, u32[]{:S(2)}, u32[]{:S(2)}) collective-permute-start(f32[40,128]{1,0:T(8,128)S(1)} %add_add_fusion.1), channel_id=1, source_target_pairs={{0,96},{32,128},{64,160},{96,192},{128,224},{160,0},{192,32},{224,... | collective-permute-start | bytes 61448 | tf_op jit(solution)/shard_map/ppermute | solution.py:212
  220.7 6.6 %collective-permute-start.16 = (f32[40,128]{1,0:T(8,128)S(1)}, f32[40,128]{1,0:T(8,128)S(1)}, u32[]{:S(2)}, u32[]{:S(2)}) collective-permute-start(f32[40,128]{1,0:T(8,128)S(1)} %add_add_fusion.1), channel_id=1, source_target_pairs={{0,64},{32,96},{64,128},{96,160},{128,192},{160,224},{192,0},{224,... | collective-permute-start | bytes 61448 | tf_op jit(solution)/shard_map/ppermute | solution.py:212
  224.3 5.0 %collective-permute-start.15 = (f32[40,128]{1,0:T(8,128)S(1)}, f32[40,128]{1,0:T(8,128)S(1)}, u32[]{:S(2)}, u32[]{:S(2)}) collective-permute-start(f32[40,128]{1,0:T(8,128)S(1)} %add_add_fusion.1), channel_id=1, source_target_pairs={{0,32},{32,64},{64,96},{96,128},{128,160},{160,192},{192,224},{224... | collective-permute-start | bytes 61448 | tf_op jit(solution)/shard_map/ppermute | solution.py:212
  (17 other events, 260.6 us)
Sparse Core Ops, SparseCore 0:
  29.3 43.0 all-gather.3

commit v4 on v3

--- a/solution.py
+++ b/solution.py
@@ -13,7 +13,7 @@
 PROBES = 32
 UNROLL = 32
 TAIL = 8
-SPLIT = 5
+SPLIT = 6
 BIN = 1536 + 2 * UNROLL
 NUGGET = 2.0
 KERNEL_SCALE = 0.1
@@ -42,8 +42,8 @@
     return ((remain2 * remain2) * (1.25 - remain)).astype(bf16)
 
 
-def bin_kernel(place_ref, pairs_ref, bins_ref, count_ref):
-    live, y_own, core_own = place_ref[0], place_ref[1], place_ref[2]
+def bin_kernel(place_ref, pairs_ref, after_ref, bins_ref, count_ref):
+    live, x_own, y_own, core_own = place_ref[0], place_ref[1], place_ref[2], place_ref[3]
 
     def step(i, front):
         for u in range(8):
@@ -51,7 +51,8 @@
             a, b = pairs_ref[0, e], pairs_ref[1, e]
             shift = (y_own - (a >> 4)) & 3
             slot = shift + ((((a >> 3) & 1) ^ core_own) << 2)
-            entry = (slot << 3) + (a & 7) + (b << 8) + ((e < live).astype(jnp.int32) << 16)
+            far = ((((x_own - (b >> 3)) & 3) << 3) + (b >> 5) << 3) + (b & 7)
+            entry = (slot << 3) + (a & 7) + (far << 8) + ((e < live).astype(jnp.int32) << 16)
             first = (b & 7) < SPLIT
             bins_ref[jnp.where(first, front, BIN - 1 - (e - front))] = entry
             front = front + first.astype(jnp.int32)
@@ -67,29 +68,30 @@
         bins_ref[BIN - 1 - back - j] = SPLIT << 8
 
 
-def spread(line):
-    return jnp.broadcast_to(line, (TILE, TILE)).T
+def spread(strip, t):
+    return jnp.broadcast_to(strip[:, t : t + 1], (TILE, TILE))
 
 
 def part_kernel(part, *refs):
     if part == 0:
-        count_ref, bins_ref, own_ref, near_ref, col_ref, row_acc, col_out, own_out, px, py, qx, qy, col_acc = refs
+        count_ref, bins_ref, own_ref, near_ref, col_ref, row_acc, own_out, *col_out, px, py, qx, qy, col_acc = refs
         row_acc[...] = jnp.zeros_like(row_acc)
         where = own_ref[256:272, :].astype(f32)
+        strip = where.T
         for t in range(8):
-            dx = spread(where[t : t + 1]) - where[t : t + 1]
-            dy = spread(where[8 + t : 9 + t]) - where[8 + t : 9 + t]
+            dx = spread(strip, t) - where[t : t + 1]
+            dy = spread(strip, 8 + t) - where[8 + t : 9 + t]
             block = radial(dx * dx + dy * dy)
             own_out[:, t * TILE : (t + 1) * TILE] = KERNEL_SCALE * lax.dot_general(
                 own_ref[t * 32 : (t + 1) * 32, :], block, NT, preferred_element_type=f32
             )
     else:
-        count_ref, bins_ref, near_ref, col_ref, row_acc, row_out, col_out, px, py, qx, qy, col_acc = refs
+        count_ref, bins_ref, near_ref, col_ref, row_acc, row_out, *col_out, px, py, qx, qy, col_acc = refs
     def row_prepare(r, carry):
-        where = near_ref[r, 256:272, :].astype(f32)
+        strip = near_ref[r, 256:272, :].astype(f32).T
         for t in range(8):
-            px[r * 8 + t] = spread(where[t : t + 1])
-            py[r * 8 + t] = spread(where[8 + t : 9 + t])
+            px[r * 8 + t] = spread(strip, t)
+            py[r * 8 + t] = spread(strip, 8 + t)
         return carry
 
     lax.fori_loop(0, 8, row_prepare, 0)
@@ -99,7 +101,7 @@
     col_acc[...] = jnp.zeros_like(col_acc)
 
     def col_prepare(r, carry):
-        where = col_ref[r, 256:272, :].astype(f32)
+        where = col_ref[(r & 7) * 4 + (r >> 3), 256:272, :].astype(f32)
         for t in tiles:
             qx[r * 8 + t] = jnp.broadcast_to(where[t : t + 1], (8, TILE))
             qy[r * 8 + t] = jnp.broadcast_to(where[8 + t : 9 + t], (8, TILE))
@@ -115,7 +117,7 @@
             a, b = both & 63, (both >> 8) & 255
             keep = jnp.where(e < live, both >> 16, 0).astype(f32).astype(bf16)
             near = near_ref[a >> 3, pl.ds(pl.multiple_of((a & 7) * 32, 32), 32), :] * keep
-            far = col_ref[b >> 3, pl.ds(pl.multiple_of((b & 7) * 32, 32), 32), :] * keep
+            far = col_ref[((b >> 3) & 7) * 4 + (b >> 6), pl.ds(pl.multiple_of((b & 7) * 32, 32), 32), :] * keep
             dx = px[a].reshape(16, 8, TILE) - qx[b][None]
             dy = py[a].reshape(16, 8, TILE) - qy[b][None]
             block = radial((dx * dx + dy * dy).reshape(TILE, TILE))
@@ -139,12 +141,14 @@
     lax.fori_loop(0, whole, body, 0)
     lax.fori_loop(0, (live - whole * UNROLL + TAIL - 1) // TAIL, tail, 0)
 
-    def finish(r, carry):
-        for t in range(number):
-            col_out[(r & 3) * 8 + (r >> 2), t * 32 : (t + 1) * 32, :] = (KERNEL_SCALE * col_acc[r * 8 + first + t]).astype(bf16)
-        return carry
-
-    lax.fori_loop(0, 32, finish, 0)
+    def finish(z, carry):
+        for k in range(4):
+            for t in range(number):
+                total = KERNEL_SCALE * col_acc[k * 64 + z * 8 + first + t]
+                col_out[k][z, t * 32 : (t + 1) * 32, :] = total.astype(bf16)
+        return carry
+
+    lax.fori_loop(0, 8, finish, 0)
     if part == 1:
 
         def finish_row(r, carry):
@@ -155,20 +159,28 @@
         lax.fori_loop(0, 8, finish_row, 0)
 
 
+def add_kernel(own0, a0, b0, c0, own1, a1, b1, c1, out):
+    for z in range(8):
+        for rows, parts in ((slice(0, SPLIT * 32), (own0, a0, b0, c0)), (slice(SPLIT * 32, 256), (own1, a1, b1, c1))):
+            total = parts[0][z].astype(f32)
+            for part in parts[1:]:
+                total = total + part[z].astype(f32)
+            out[z, rows, :] = total.astype(bf16)
+
+
 def dot32(former, latter, dims):
     return lax.dot_general(former, latter, dims, precision=HIGHEST, preferred_element_type=f32)
 
 
-def gram_kernel(direction_ref, residual_ref, own_ref, row_ref, col0_ref, col1_ref, image_ref, gram_ref):
+def gram_kernel(direction_ref, residual_ref, own_ref, row_ref, col_ref, image_ref, gram_ref):
     for t in range(8):
         here = slice(t * 32, (t + 1) * 32)
         lanes = slice(t * TILE, (t + 1) * TILE)
         total = NUGGET * direction_ref[:, lanes] + own_ref[:, lanes]
         for part in range(row_ref.shape[0]):
             total = total + row_ref[part, here, :].astype(f32)
-        col_ref, place = (col0_ref, t) if t < SPLIT else (col1_ref, t - SPLIT)
         for part in range(col_ref.shape[0]):
-            total = total + col_ref[part, place * 32 : (place + 1) * 32, :].astype(f32)
+            total = total + col_ref[part, here, :].astype(f32)
         image_ref[:, lanes] = total
     direction, residual, image = direction_ref[...], residual_ref[...], image_ref[...]
     gram_ref[0:32, 0:32] = dot32(direction, image, NT)
@@ -219,74 +231,78 @@
 def on_device(solution_field, residual, direction, positions, tile_pairs, pair_count):
     shape = jax.ShapeDtypeStruct
     own_points = direction.shape[1]
-    y_own, core_own = lax.axis_index("y"), lax.axis_index("core")
+    x_own, y_own, core_own = lax.axis_index("x"), lax.axis_index("y"), lax.axis_index("core")
     packed = pl.pallas_call(
         pack_kernel, out_shape=shape((272, TILE), bf16), in_specs=[VMEM] * 2, out_specs=VMEM, name="pack"
     )(direction, positions)
-    packed, other = lax.optimization_barrier((packed, swap(packed)))
-    chip = jnp.stack([packed, other])
+    x_all = jnp.stack([packed] + shifts(packed, "x", 4))
+    col_all = lax.all_gather(x_all, "z").reshape(32, 272, TILE)
+    chip = jnp.stack([packed, swap(packed)])
     around = shifts(chip, "y", 4)
-    x_all = lax.all_gather(packed, "x")
-    x_all, around = lax.optimization_barrier((x_all, around))
-    col_all = lax.all_gather(x_all, "z").reshape(32, 272, TILE)
     row_all = jnp.concatenate([v[:1] for v in [chip] + around] + [v[1:] for v in [chip] + around], 0)
-    place = jnp.stack([pair_count[0], y_own, core_own]).astype(jnp.int32)
+    place = jnp.stack([pair_count[0], x_own, y_own, core_own]).astype(jnp.int32)
     bins, counts = pl.pallas_call(
         bin_kernel,
         out_shape=(shape((BIN,), jnp.int32), shape((2,), jnp.int32)),
-        in_specs=[SMEM, SMEM],
+        in_specs=[SMEM, SMEM, pl.BlockSpec(memory_space=pl.ANY)],
         out_specs=(SMEM, SMEM),
         name="bins",
-    )(place, tile_pairs)
+    )(place, tile_pairs, row_all)
     acc = shape((64, PROBES, TILE), f32)
     scratch = [pltpu.VMEM((64, TILE, TILE), f32)] * 2
     scratch += [pltpu.VMEM((256, 8, TILE), f32), pltpu.VMEM((256, 8, TILE), f32), pltpu.VMEM((256, PROBES, TILE), f32)]
 
-    def reduced(col_out):
-        number = col_out.shape[1] // 32
-        blocks = lax.all_to_all(col_out.reshape(4, 8 * number * 32, TILE), "x", 0, 0)
-        blocks = jnp.sum(blocks.astype(f32), 0).astype(bf16)
-        return blocks.reshape(8, number * 32, TILE)
-
-    row_acc, col_first, own_product = pl.pallas_call(
+    def blocks(number):
+        return (shape((8, number * 32, TILE), bf16),) * 4
+
+    def sent(col_out):
+        return [lax.ppermute(col_out[k], "x", [(i, (i - k) % 4) for i in range(4)]) for k in range(1, 4)]
+
+    row_acc, own_product, *col_first = pl.pallas_call(
         functools.partial(part_kernel, 0),
-        out_shape=(acc, shape((32, SPLIT * 32, TILE), bf16), shape((PROBES, own_points), f32)),
+        out_shape=(acc, shape((PROBES, own_points), f32)) + blocks(SPLIT),
         in_specs=[SMEM] * 2 + [VMEM] * 3,
-        out_specs=(VMEM,) * 3,
+        out_specs=(VMEM,) * 6,
         scratch_shapes=scratch,
         compiler_params=PARAMS,
         name="pairs_first",
     )(counts, bins, packed, row_all, col_all)
-    row_sum, col_second = pl.pallas_call(
+    row_sum, *col_second = pl.pallas_call(
         functools.partial(part_kernel, 1),
-        out_shape=(shape((8, 256, TILE), bf16), shape((32, (8 - SPLIT) * 32, TILE), bf16)),
+        out_shape=(shape((8, 256, TILE), bf16),) + blocks(8 - SPLIT),
         in_specs=[SMEM] * 2 + [VMEM] * 3,
-        out_specs=(VMEM,) * 2,
+        out_specs=(VMEM,) * 5,
         scratch_shapes=scratch,
         compiler_params=PARAMS,
         name="pairs_second",
     )(counts, bins, row_all, col_all, row_acc)
-    first = reduced(col_first)
-    second, first = lax.optimization_barrier((col_second, first))
-    second = reduced(second)
-    col_first = lax.all_to_all(first, "z", 0, 0)
+    sums = pl.pallas_call(
+        add_kernel,
+        out_shape=shape((8, 256, TILE), bf16),
+        in_specs=[VMEM] * 8,
+        out_specs=VMEM,
+        compiler_params=PARAMS,
+        name="add",
+    )(col_first[0], *sent(col_first), col_second[0], *sent(col_second))
+    col_parts = lax.all_to_all(sums, "z", 0, 0)
     half = (row_sum[:4].astype(f32) + swap(row_sum[4:]).astype(f32)).astype(bf16)
     row_parts = [half[0]] + [
         lax.ppermute(half[k], "y", [(i, (i - k) % 4) for i in range(4)]) for k in range(1, 4)
     ]
     row_parts = jnp.stack(row_parts)
-    col_second = lax.all_to_all(second, "z", 0, 0)
     image, gram = pl.pallas_call(
         gram_kernel,
         out_shape=(shape((PROBES, own_points), f32), shape((40, TILE), f32)),
-        in_specs=[VMEM] * 6,
+        in_specs=[VMEM] * 5,
         out_specs=(VMEM, VMEM),
         compiler_params=PARAMS,
         name="gram",
-    )(direction, residual, own_product, row_parts, col_first, col_second)
+    )(direction, residual, own_product, row_parts, col_parts)
     gram = gram + swap(gram)
-    for axis, size in (("y", 4), ("x", 4), ("z", 8)):
-        gram = sum(shifts(gram, axis, size), gram)
+    gram = sum(shifts(gram, "y", 4), gram)
+    gram = sum(shifts(gram, "x", 4), gram)
+    gram = gram + lax.ppermute(gram, "z", [(i, (i + 4) % 8) for i in range(8)])
+    gram = sum(shifts(gram, "z", 8)[:3], gram)
     return pl.pallas_call(
         solve_kernel,
         out_shape=(shape((PROBES, own_points), f32),) * 3,

time: 242 us -> 213 us (0.88)
  Pallas kernels: 30 us -> 94.3 us
  blocking collectives: 39.1 us -> 0 us
  starting transfers between devices: 70.8 us -> 37.9 us
  waiting for transfers between devices: 73 us -> 55.5 us
    pallas_call x1, Pallas kernels: 10.7 us -> 47.9 us  [on_device(): pl.pallas_call(functools.partial(part_kernel, 0), out_shape=(acc, shape((...]
    all_to_all x3 -> x1, starting transfers between devices: 40.3 us -> 5 us  [on_device(): col_parts = lax.all_to_all(sums, 'z', 0, 0)]
    all_gather x1, waiting for transfers between devices: 36.8 us -> 7.05 us  [on_device(): col_all = lax.all_gather(x_all, 'z').reshape(32, 272, TILE)]
    all_to_all x1 -> x0, blocking collectives: 25.9 us -> none  [reduced(): lax.all_to_all(col_out.reshape(4, 8 * number * 32, TILE), 'x', 0, 0)]
    pallas_call x1, Pallas kernels: 4.14 us -> 21.2 us  [on_device(): pl.pallas_call(bin_kernel, out_shape=(shape((BIN,), jnp.int32), shape((2,...]
    all_gather x1 -> x0, blocking collectives: 13.2 us -> none  [on_device(): x_all = lax.all_gather(packed, 'x')]
    ppermute x0 -> x7, waiting for transfers between devices: none -> 12.5 us  [the longest x1 7.21 us: on_device(): gram = gram + lax.ppermute(gram, 'z', [(i, (i + 4) % 8) for i in range(8)])]
    ppermute x0 -> x7, starting transfers between devices: none -> 11.2 us  [the longest x6 10.6 us: sent(): lax.ppermute(col_out[k], 'x', [(i, (i - k) % 4) for i in range(4)])]
  transfers between devices with their start and end apart: 26 -> 30, of which waited for: 17 -> 21; matrix products, arithmetic and copies ran while one was open for 1% -> 1% of each run, Pallas kernels for 5% -> 19%
where the time goes in v4:
time: 213 us; the launch traced here: 212 us
  Pallas kernels  94.3 us (44%)
  waiting for transfers between devices  55.5 us (26%)
  starting transfers between devices  37.9 us (18%)
  between operations  14.9 us (7%)
  local copies, waits for them, and re-layouts  5.88 us (3%)
  other arithmetic  3.29 us (2%)
    pallas_call x1, Pallas kernels, on_device(): pl.pallas_call(functools.partial(part_kernel, 0), out_shape=(acc, shape((...  47.9 us
    ppermute x15, waiting for transfers between devices, shifts(): lax.ppermute(value, axis, [(i, (i + k) % size) for i in range(size)])  21.4 us
    pallas_call x1, Pallas kernels, on_device(): pl.pallas_call(bin_kernel, out_shape=(shape((BIN,), jnp.int32), shape((2,...  21.2 us
    ppermute x15, starting transfers between devices, shifts(): lax.ppermute(value, axis, [(i, (i + k) % size) for i in range(size)])  18.2 us
    pallas_call x1, Pallas kernels, on_device(): pl.pallas_call(functools.partial(part_kernel, 1), out_shape=(shape((8, 25...  17.2 us
    ppermute x6, starting transfers between devices, sent(): lax.ppermute(col_out[k], 'x', [(i, (i - k) % 4) for i in range(4)])  10.6 us
    all_to_all x1, waiting for transfers between devices, on_device(): col_parts = lax.all_to_all(sums, 'z', 0, 0)  7.93 us
    ppermute x1, waiting for transfers between devices, on_device(): gram = gram + lax.ppermute(gram, 'z', [(i, (i + 4) % 8) for i in range(8)])  7.21 us
  transfers between devices with their start and end apart: 30, of which 21 were waited for; matrix products, arithmetic and copies ran while one was open for 1% of the time, Pallas kernels for 19%

profile of v4, /device:TPU:16, one launch (start us, length us, event | category | flops | bytes accessed | tf_op | source)
XLA Modules:
  0.0 211.7 jit_solution(9293324426227193264)
XLA Ops:
  8.8 2.8 %collective-permute-start.6 = (bf16[272,128]{1,0:T(8,128)(2,1)}, bf16[272,128]{1,0:T(8,128)(2,1)S(1)}, u32[]{:S(2)}, u32[]{:S(2)}) collective-permute-start(bf16[272,128]{1,0:T(8,128)(2,1)} %pack.1.refs_2_), channel_id=1, source_target_pairs={{0,24},{8,0},{16,8},{24,16},{1,25},{9,1},{17,9},{25,17},{2,26},{10... | collective-permute-start | bytes 208904 | tf_op jit(solution)/shard_map/ppermute | solution.py:224
  14.2 3.5 %collective-permute-done.5 = bf16[272,128]{1,0:T(8,128)(2,1)S(1)} collective-permute-done((bf16[272,128]{1,0:T(8,128)(2,1)}, bf16[272,128]{1,0:T(8,128)(2,1)S(1)}, u32[]{:S(2)}, u32[]{:S(2)}) %collective-permute-start.5) | collective-permute-done | bytes 69664 | tf_op jit(solution)/shard_map/ppermute | solution.py:224
  18.4 1.6 pad_maximum_fusion
  28.3 5.1 %collective-permute-done.2 = bf16[2,272,128]{2,1,0:T(8,128)(2,1)S(1)} collective-permute-done((bf16[2,272,128]{2,1,0:T(8,128)(2,1)S(1)}, bf16[2,272,128]{2,1,0:T(8,128)(2,1)S(1)}, u32[]{:S(2)}, u32[]{:S(2)}) %collective-permute-start.2) | collective-permute-done | bytes 139296 | tf_op jit(solution)/shard_map/ppermute | solution.py:224
  34.4 21.2 %bins.1 = (s32[1600]{0:T(1024)}, s32[2]{0:T(128)}) custom-call(s32[4]{0:T(128)} %pad_add_fusion.place_ref, s32[2,1536]{1,0:T(2,128)} %pairs_ref.1, bf16[8,272,128]{2,1,0:T(8,128)(2,1)} %copy-done.2), custom_call_target="tpu_custom_call" | custom-call | tf_op jit(solution)/shard_map/bins/pallas_call | solution.py:244
  55.6 7.1 %all-gather.3.cloned.1.call-done.refs_4_.refs_3_ = bf16[32,272,128]{2,1,0:T(8,128)(2,1)} async-done(((bf16[4,272,128]{2,1,0:T(8,128)(2,1)}), bf16[32,272,128]{2,1,0:T(8,128)(2,1)}) %all-gather.3.cloned.1.call-update) | async-done | bytes 2228240 | tf_op jit(solution)/shard_map/all_gather | solution.py:239
  66.7 47.9 %pairs_first.1 = (f32[64,32,128]{2,1,0:T(8,128)S(1)}, f32[32,1024]{1,0:T(8,128)S(1)}, bf16[8,192,128]{2,1,0:T(8,128)(2,1)S(1)}, bf16[8,192,128]{2,1,0:T(8,128)(2...) custom-call(s32[2]{0:T(128)S(1)} %copy-done.10, s32[1600]{0:T(1024)S(1)} %copy-done.9, ...), custom_call_target="tpu_custom_call" | custom-call | tf_op jit(solution)/shard_map/pairs_first/pallas_call | solution.py:261
  114.5 2.0 collective-permute-start.11
  117.9 17.2 %pairs_second.1 = (bf16[8,256,128]{2,1,0:T(8,128)(2,1)S(1)}, bf16[8,64,128]{2,1,0:T(8,128)(2,1)S(1)}, bf16[8,64,128]{2,1,0:T(8,128)(2,1)S(1)}, bf16[8,64,128]{2,1,0:T(8,128)(2,1)S(1)}, bf16[8,64,128]{2,1,0:T(8,128)(2,1)S(1)}) custom-call(s32[2]{0:T(128)S(1)} %copy-done.10, s32[1600]{0:T(1024)S(1)} %copy-done.9, bf16[8,272,128]{2,1,0:T(8,128)(2,1)S(1)} %copy-done.4, ...), custom_call_target="tpu_custom_call" | custom-call | tf_op jit(solution)/shard_map/pairs_second/pallas_call | solution.py:270
  135.0 3.4 %collective-permute-start.14 = (bf16[8,64,128]{2,1,0:T(8,128)(2,1)S(1)}, bf16[8,64,128]{2,1,0:T(8,128)(2,1)S(1)}, u32[]{:S(2)}, u32[]{:S(2)}) collective-permute-start(bf16[8,64,128]{2,1,0:T(8,128)(2,1)S(1)} %get-tuple-element.28), channel_id=1, source_target_pairs={{0,24},{8,0},{16,8},{24,16},{1,25},{9,1},{17,9},{25,17},{2,26},{10... | collective-permute-start | bytes 393224 | tf_op jit(solution)/shard_map/ppermute | solution.py:259
  138.4 1.8 collective-permute-start.15
  141.2 2.0 collective-permute-start.16
  143.2 2.7 %collective-permute-done.15.b1 = bf16[8,64,128]{2,1,0:T(8,128)(2,1)S(1)} collective-permute-done((bf16[8,64,128]{2,1,0:T(8,128)(2,1)S(1)}, bf16[8,64,128]{2,1,0:T(8,128)(2,1)S(1)}, u32[]{:S(2)}, u32[]{:S(2)}) %collective-permute-start.15) | collective-permute-done | bytes 131104 | tf_op jit(solution)/shard_map/ppermute | solution.py:259
  145.9 1.7 collective-permute-done.16.c1
  148.7 5.0 %all-to-all-start = ((bf16[8,256,128]{2,1,0:T(8,128)(2,1)}), bf16[8,256,128]{2,1,0:T(8,128)(2,1)S(1)}, u32[]{:S(2)}, u32[]{:S(2)}) async-start(bf16[8,256,128]{2,1,0:T(8,128)(2,1)} %add.65), calls=%async_computation | async-start | bytes 1048576 | tf_op jit(solution)/shard_map/all_to_all | solution.py:287
  158.1 2.9 %collective-permute-done.9 = bf16[256,128]{1,0:T(8,128)(2,1)S(1)} collective-permute-done((bf16[256,128]{1,0:T(8,128)(2,1)S(1)}, bf16[256,128]{1,0:T(8,128)(2,1)S(1)}, u32[]{:S(2)}, u32[]{:S(2)}) %collective-permute-start.9) | collective-permute-done | bytes 65568 | tf_op jit(solution)/shard_map/ppermute | solution.py:290
  161.1 7.9 %all-to-all-done.col_ref = bf16[8,256,128]{2,1,0:T(8,128)(2,1)S(1)} async-done(((bf16[8,256,128]{2,1,0:T(8,128)(2,1)}), bf16[8,256,128]{2,1,0:T(8,128)(2,1)S(1)}, u32[]{:S(2)}, u32[]{:S(2)}) %all-to-all-start) | async-done | bytes 524320 | tf_op jit(solution)/shard_map/all_to_all | solution.py:287
  171.4 2.4 %collective-permute-start.19 = (f32[40,128]{1,0:T(8,128)S(1)}, f32[40,128]{1,0:T(8,128)S(1)}, u32[]{:S(2)}, u32[]{:S(2)}) collective-permute-start(f32[40,128]{1,0:T(8,128)S(1)} %add.38), channel_id=1, source_target_pairs={{0,4},{2,6},{4,0},{6,2},{1,5},{3,7},{5,1},{7,3},{8,12},{10,14},{12... | collective-permute-start | bytes 61448 | tf_op jit(solution)/shard_map/ppermute | solution.py:224
  174.8 1.8 collective-permute-done.19
  181.6 2.4 %collective-permute-done.22 = f32[40,128]{1,0:T(8,128)S(1)} collective-permute-done((f32[40,128]{1,0:T(8,128)S(1)}, f32[40,128]{1,0:T(8,128)S(1)}, u32[]{:S(2)}, u32[]{:S(2)}) %collective-permute-start.22) | collective-permute-done | bytes 20512 | tf_op jit(solution)/shard_map/ppermute | solution.py:224
  186.0 7.2 %collective-permute-done.24 = f32[40,128]{1,0:T(8,128)S(1)} collective-permute-done((f32[40,128]{1,0:T(8,128)S(1)}, f32[40,128]{1,0:T(8,128)S(1)}, u32[]{:S(2)}, u32[]{:S(2)}) %collective-permute-start.24) | collective-permute-done | bytes 20512 | tf_op jit(solution)/shard_map/ppermute | solution.py:304
  193.2 1.9 collective-permute-start.26
  196.6 3.4 %collective-permute-done.27 = f32[40,128]{1,0:T(8,128)S(1)} collective-permute-done((f32[40,128]{1,0:T(8,128)S(1)}, f32[40,128]{1,0:T(8,128)S(1)}, u32[]{:S(2)}, u32[]{:S(2)}) %collective-permute-start.27) | collective-permute-done | bytes 20512 | tf_op jit(solution)/shard_map/ppermute | solution.py:224
  200.2 4.7 %solve.1 = (f32[32,1024]{1,0:T(8,128)}, f32[32,1024]{1,0:T(8,128)}, f32[32,1024]{1,0:T(8,128)}) custom-call(f32[40,128]{1,0:T(8,128)S(1)} %add_add_fusion.gram_ref, f32[32,1024]{1,0:T(8,128)S(1)} %copy-done.8, f32[32,1024]{1,0:T(8,128)S(1)} %copy-done.7, f32[32,1024]{1,0:T(8,128)S(1)} %copy-done.6, f32[32,1024]{1,0:T(8,128)S(1)} %get-tuple-element.32.image_ref), custom_call_target="tpu_custom_call" | custom-call | tf_op jit(solution)/shard_map/solve/pallas_call | solution.py:306
  (86 shorter events, 37.3 us)
Async XLA Ops:
  7.2 55.5 %all-gather.3.cloned.1.call-start = ((), (), s32[]{:S(2)}) async-start(), calls=%async_computation.1 | async-start | bytes 2506752 | tf_op jit(solution)/shard_map/all_gather | solution.py:239
  8.8 5.4 %collective-permute-start.6 = (bf16[272,128]{1,0:T(8,128)(2,1)}, bf16[272,128]{1,0:T(8,128)(2,1)S(1)}, u32[]{:S(2)}, u32[]{:S(2)}) collective-permute-start(bf16[272,128]{1,0:T(8,128)(2,1)} %pack.1.refs_2_), channel_id=1, source_target_pairs={{0,24},{8,0},{16,8},{24,16},{1,25},{9,1},{17,9},{25,17},{2,26},{10... | collective-permute-start | bytes 208904 | tf_op jit(solution)/shard_map/ppermute | solution.py:224
  11.5 6.1 %collective-permute-start.5 = (bf16[272,128]{1,0:T(8,128)(2,1)}, bf16[272,128]{1,0:T(8,128)(2,1)S(1)}, u32[]{:S(2)}, u32[]{:S(2)}) collective-permute-start(bf16[272,128]{1,0:T(8,128)(2,1)} %pack.1.refs_2_), channel_id=1, source_target_pairs={{0,16},{8,24},{16,0},{24,8},{1,17},{9,25},{17,1},{25,9},{2,18},{10... | collective-permute-start | bytes 208904 | tf_op jit(solution)/shard_map/ppermute | solution.py:224
  12.3 6.0 %collective-permute-start.4 = (bf16[272,128]{1,0:T(8,128)(2,1)}, bf16[272,128]{1,0:T(8,128)(2,1)S(1)}, u32[]{:S(2)}, u32[]{:S(2)}) collective-permute-start(bf16[272,128]{1,0:T(8,128)(2,1)} %pack.1.refs_2_), channel_id=1, source_target_pairs={{0,8},{8,16},{16,24},{24,0},{1,9},{9,17},{17,25},{25,1},{2,10},{10... | collective-permute-start | bytes 208904 | tf_op jit(solution)/shard_map/ppermute | solution.py:224
  22.5 5.8 %collective-permute-start.1 = (bf16[2,272,128]{2,1,0:T(8,128)(2,1)S(1)}, bf16[2,272,128]{2,1,0:T(8,128)(2,1)S(1)}, u32[]{:S(2)}, u32[]{:S(2)}) collective-permute-start(bf16[2,272,128]{2,1,0:T(8,128)(2,1)S(1)} %pad_maximum_fusion.2), channel_id=1, source_target_pairs={{0,2},{2,4},{4,6},{6,0},{1,3},{3,5},{5,7},{7,1},{8,10},{10,12},{12... | collective-permute-start | bytes 417800 | tf_op jit(solution)/shard_map/ppermute | solution.py:224
  26.0 7.4 %collective-permute-start.3 = (bf16[2,272,128]{2,1,0:T(8,128)(2,1)S(1)}, bf16[2,272,128]{2,1,0:T(8,128)(2,1)S(1)}, u32[]{:S(2)}, u32[]{:S(2)}) collective-permute-start(bf16[2,272,128]{2,1,0:T(8,128)(2,1)S(1)} %pad_maximum_fusion.2), channel_id=1, source_target_pairs={{0,6},{2,0},{4,2},{6,4},{1,7},{3,1},{5,3},{7,5},{8,14},{10,8},{12,... | collective-permute-start | bytes 417800 | tf_op jit(solution)/shard_map/ppermute | solution.py:224
  26.8 6.7 %collective-permute-start.2 = (bf16[2,272,128]{2,1,0:T(8,128)(2,1)S(1)}, bf16[2,272,128]{2,1,0:T(8,128)(2,1)S(1)}, u32[]{:S(2)}, u32[]{:S(2)}) collective-permute-start(bf16[2,272,128]{2,1,0:T(8,128)(2,1)S(1)} %pad_maximum_fusion.2), channel_id=1, source_target_pairs={{0,4},{2,6},{4,0},{6,2},{1,5},{3,7},{5,1},{7,3},{8,12},{10,14},{12... | collective-permute-start | bytes 417800 | tf_op jit(solution)/shard_map/ppermute | solution.py:224
  114.5 33.0 %collective-permute-start.11 = (bf16[8,192,128]{2,1,0:T(8,128)(2,1)S(1)}, bf16[8,192,128]{2,1,0:T(8,128)(2,1)S(1)}, u32[]{:S(2)}, u32[]{:S(2)}) collective-permute-start(bf16[8,192,128]{2,1,0:T(8,128)(2,1)S(1)} %get-tuple-element.24), channel_id=1, source_target_pairs={{0,24},{8,0},{16,8},{24,16},{1,25},{9,1},{17,9},{25,17},{2,26},{10... | collective-permute-start | bytes 1179656 | tf_op jit(solution)/shard_map/ppermute | solution.py:259
  116.5 31.0 %collective-permute-start.12 = (bf16[8,192,128]{2,1,0:T(8,128)(2,1)S(1)}, bf16[8,192,128]{2,1,0:T(8,128)(2,1)S(1)}, u32[]{:S(2)}, u32[]{:S(2)}) collective-permute-start(bf16[8,192,128]{2,1,0:T(8,128)(2,1)S(1)} %get-tuple-element.25), channel_id=1, source_target_pairs={{0,16},{8,24},{16,0},{24,8},{1,17},{9,25},{17,1},{25,9},{2,18},{10... | collective-permute-start | bytes 1179656 | tf_op jit(solution)/shard_map/ppermute | solution.py:259
  117.4 30.2 %collective-permute-start.13 = (bf16[8,192,128]{2,1,0:T(8,128)(2,1)S(1)}, bf16[8,192,128]{2,1,0:T(8,128)(2,1)S(1)}, u32[]{:S(2)}, u32[]{:S(2)}) collective-permute-start(bf16[8,192,128]{2,1,0:T(8,128)(2,1)S(1)} %get-tuple-element.26), channel_id=1, source_target_pairs={{0,8},{8,16},{16,24},{24,0},{1,9},{9,17},{17,25},{25,1},{2,10},{10... | collective-permute-start | bytes 1179656 | tf_op jit(solution)/shard_map/ppermute | solution.py:259
  135.0 6.1 %collective-permute-start.14 = (bf16[8,64,128]{2,1,0:T(8,128)(2,1)S(1)}, bf16[8,64,128]{2,1,0:T(8,128)(2,1)S(1)}, u32[]{:S(2)}, u32[]{:S(2)}) collective-permute-start(bf16[8,64,128]{2,1,0:T(8,128)(2,1)S(1)} %get-tuple-element.28), channel_id=1, source_target_pairs={{0,24},{8,0},{16,8},{24,16},{1,25},{9,1},{17,9},{25,17},{2,26},{10... | collective-permute-start | bytes 393224 | tf_op jit(solution)/shard_map/ppermute | solution.py:259
  138.4 7.5 %collective-permute-start.15 = (bf16[8,64,128]{2,1,0:T(8,128)(2,1)S(1)}, bf16[8,64,128]{2,1,0:T(8,128)(2,1)S(1)}, u32[]{:S(2)}, u32[]{:S(2)}) collective-permute-start(bf16[8,64,128]{2,1,0:T(8,128)(2,1)S(1)} %get-tuple-element.29), channel_id=1, source_target_pairs={{0,16},{8,24},{16,0},{24,8},{1,17},{9,25},{17,1},{25,9},{2,18},{10... | collective-permute-start | bytes 393224 | tf_op jit(solution)/shard_map/ppermute | solution.py:259
  141.2 6.4 %collective-permute-start.16 = (bf16[8,64,128]{2,1,0:T(8,128)(2,1)S(1)}, bf16[8,64,128]{2,1,0:T(8,128)(2,1)S(1)}, u32[]{:S(2)}, u32[]{:S(2)}) collective-permute-start(bf16[8,64,128]{2,1,0:T(8,128)(2,1)S(1)} %get-tuple-element.30), channel_id=1, source_target_pairs={{0,8},{8,16},{16,24},{24,0},{1,9},{9,17},{17,25},{25,1},{2,10},{10... | collective-permute-start | bytes 393224 | tf_op jit(solution)/shard_map/ppermute | solution.py:259
  145.9 7.8 %collective-permute-start.7 = (bf16[4,256,128]{2,1,0:T(8,128)(2,1)S(1)}, bf16[4,256,128]{2,1,0:T(8,128)(2,1)S(1)}, u32[]{:S(2)}, u32[]{:S(2)}) collective-permute-start(bf16[4,256,128]{2,1,0:T(8,128)(2,1)S(1)} %slice.43), channel_id=1, source_target_pairs={{0,1},{1,0},{2,3},{3,2},{4,5},{5,4},{6,7},{7,6},{8,9},{9,8},{10,11... | collective-permute-start | bytes 786440 | tf_op jit(solution)/shard_map/ppermute | solution.py:228
  148.7 20.3 %all-to-all-start = ((bf16[8,256,128]{2,1,0:T(8,128)(2,1)}), bf16[8,256,128]{2,1,0:T(8,128)(2,1)S(1)}, u32[]{:S(2)}, u32[]{:S(2)}) async-start(bf16[8,256,128]{2,1,0:T(8,128)(2,1)} %add.65), calls=%async_computation | async-start | bytes 1048576 | tf_op jit(solution)/shard_map/all_to_all | solution.py:287
  155.3 5.8 %collective-permute-start.9 = (bf16[256,128]{1,0:T(8,128)(2,1)S(1)}, bf16[256,128]{1,0:T(8,128)(2,1)S(1)}, u32[]{:S(2)}, u32[]{:S(2)}) collective-permute-start(bf16[256,128]{1,0:T(8,128)(2,1)S(1)} %get-tuple-element.35), channel_id=1, source_target_pairs={{0,4},{2,6},{4,0},{6,2},{1,5},{3,7},{5,1},{7,3},{8,12},{10,14},{12... | collective-permute-start | bytes 196616 | tf_op jit(solution)/shard_map/ppermute | solution.py:290
  156.7 4.4 %collective-permute-start.8 = (bf16[256,128]{1,0:T(8,128)(2,1)S(1)}, bf16[256,128]{1,0:T(8,128)(2,1)S(1)}, u32[]{:S(2)}, u32[]{:S(2)}) collective-permute-start(bf16[256,128]{1,0:T(8,128)(2,1)S(1)} %get-tuple-element.36), channel_id=1, source_target_pairs={{0,6},{2,0},{4,2},{6,4},{1,7},{3,1},{5,3},{7,5},{8,14},{10,8},{12,... | collective-permute-start | bytes 196616 | tf_op jit(solution)/shard_map/ppermute | solution.py:290
  171.4 5.3 %collective-permute-start.19 = (f32[40,128]{1,0:T(8,128)S(1)}, f32[40,128]{1,0:T(8,128)S(1)}, u32[]{:S(2)}, u32[]{:S(2)}) collective-permute-start(f32[40,128]{1,0:T(8,128)S(1)} %add.38), channel_id=1, source_target_pairs={{0,4},{2,6},{4,0},{6,2},{1,5},{3,7},{5,1},{7,3},{8,12},{10,14},{12... | collective-permute-start | bytes 61448 | tf_op jit(solution)/shard_map/ppermute | solution.py:224
  178.7 5.3 %collective-permute-start.22 = (f32[40,128]{1,0:T(8,128)S(1)}, f32[40,128]{1,0:T(8,128)S(1)}, u32[]{:S(2)}, u32[]{:S(2)}) collective-permute-start(f32[40,128]{1,0:T(8,128)S(1)} %add_add_fusion.2), channel_id=1, source_target_pairs={{0,16},{8,24},{16,0},{24,8},{1,17},{9,25},{17,1},{25,9},{2,18},{10... | collective-permute-start | bytes 61448 | tf_op jit(solution)/shard_map/ppermute | solution.py:224
  180.3 5.0 %collective-permute-start.21 = (f32[40,128]{1,0:T(8,128)S(1)}, f32[40,128]{1,0:T(8,128)S(1)}, u32[]{:S(2)}, u32[]{:S(2)}) collective-permute-start(f32[40,128]{1,0:T(8,128)S(1)} %add_add_fusion.2), channel_id=1, source_target_pairs={{0,8},{8,16},{16,24},{24,0},{1,9},{9,17},{17,25},{25,1},{2,10},{10... | collective-permute-start | bytes 61448 | tf_op jit(solution)/shard_map/ppermute | solution.py:224
  185.3 7.9 %collective-permute-start.24 = (f32[40,128]{1,0:T(8,128)S(1)}, f32[40,128]{1,0:T(8,128)S(1)}, u32[]{:S(2)}, u32[]{:S(2)}) collective-permute-start(f32[40,128]{1,0:T(8,128)S(1)} %add_add_fusion.1), channel_id=1, source_target_pairs={{0,128},{32,160},{64,192},{96,224},{128,0},{160,32},{192,64},{224,... | collective-permute-start | bytes 61448 | tf_op jit(solution)/shard_map/ppermute | solution.py:304
  193.2 6.8 %collective-permute-start.27 = (f32[40,128]{1,0:T(8,128)S(1)}, f32[40,128]{1,0:T(8,128)S(1)}, u32[]{:S(2)}, u32[]{:S(2)}) collective-permute-start(f32[40,128]{1,0:T(8,128)S(1)} %add.45), channel_id=1, source_target_pairs={{0,96},{32,128},{64,160},{96,192},{128,224},{160,0},{192,32},{224,... | collective-permute-start | bytes 61448 | tf_op jit(solution)/shard_map/ppermute | solution.py:224
  193.2 6.8 %collective-permute-start.26 = (f32[40,128]{1,0:T(8,128)S(1)}, f32[40,128]{1,0:T(8,128)S(1)}, u32[]{:S(2)}, u32[]{:S(2)}) collective-permute-start(f32[40,128]{1,0:T(8,128)S(1)} %add.45), channel_id=1, source_target_pairs={{0,64},{32,96},{64,128},{96,160},{128,192},{160,224},{192,0},{224,... | collective-permute-start | bytes 61448 | tf_op jit(solution)/shard_map/ppermute | solution.py:224
  195.1 5.1 %collective-permute-start.25 = (f32[40,128]{1,0:T(8,128)S(1)}, f32[40,128]{1,0:T(8,128)S(1)}, u32[]{:S(2)}, u32[]{:S(2)}) collective-permute-start(f32[40,128]{1,0:T(8,128)S(1)} %add.45), channel_id=1, source_target_pairs={{0,32},{32,64},{64,96},{96,128},{128,160},{160,192},{192,224},{224... | collective-permute-start | bytes 61448 | tf_op jit(solution)/shard_map/ppermute | solution.py:224
  (17 other events, 274.3 us)
Sparse Core Ops, SparseCore 0:
  20.2 42.4 all-gather.2

commit v5 on v4

--- a/solution.py
+++ b/solution.py
@@ -24,7 +24,8 @@
 NT = (((1,), (1,)), ((), ()))
 NN = (((1,), (0,)), ((), ()))
 TN = (((0,), (0,)), ((), ()))
-PARAMS = pltpu.CompilerParams(vmem_limit_bytes=24 * 2**20)
+PARAMS = pltpu.CompilerParams(vmem_limit_bytes=16 * 2**20)
+SMALL = pltpu.CompilerParams(vmem_limit_bytes=4 * 2**20)
 
 
 def pack_kernel(direction_ref, positions_ref, packed_ref):
@@ -42,25 +43,24 @@
     return ((remain2 * remain2) * (1.25 - remain)).astype(bf16)
 
 
-def bin_kernel(place_ref, pairs_ref, after_ref, bins_ref, count_ref):
-    live, x_own, y_own, core_own = place_ref[0], place_ref[1], place_ref[2], place_ref[3]
+def bin_kernel(live_ref, pairs_ref, after_ref, bins_ref, count_ref):
+    live = live_ref[0]
+
+    def put(e, front):
+        a, b = pairs_ref[0, e], pairs_ref[1, e]
+        first = (b & 7) < SPLIT
+        bins_ref[jnp.where(first, front, BIN - 1 - e + front)] = a + (b << 8)
+        return front + first.astype(jnp.int32)
 
     def step(i, front):
         for u in range(8):
-            e = i * 8 + u
-            a, b = pairs_ref[0, e], pairs_ref[1, e]
-            shift = (y_own - (a >> 4)) & 3
-            slot = shift + ((((a >> 3) & 1) ^ core_own) << 2)
-            far = ((((x_own - (b >> 3)) & 3) << 3) + (b >> 5) << 3) + (b & 7)
-            entry = (slot << 3) + (a & 7) + (far << 8) + ((e < live).astype(jnp.int32) << 16)
-            first = (b & 7) < SPLIT
-            bins_ref[jnp.where(first, front, BIN - 1 - (e - front))] = entry
-            front = front + first.astype(jnp.int32)
+            front = put(i * 8 + u, front)
         return front
 
-    groups = (live + 7) >> 3
+    groups = live >> 3
     front = lax.fori_loop(0, groups, step, jnp.int32(0))
-    back = groups * 8 - front
+    front = lax.fori_loop(groups * 8, live, put, front)
+    back = live - front
     count_ref[0] = front
     count_ref[1] = back
     for j in range(TAIL):
@@ -72,21 +72,7 @@
     return jnp.broadcast_to(strip[:, t : t + 1], (TILE, TILE))
 
 
-def part_kernel(part, *refs):
-    if part == 0:
-        count_ref, bins_ref, own_ref, near_ref, col_ref, row_acc, own_out, *col_out, px, py, qx, qy, col_acc = refs
-        row_acc[...] = jnp.zeros_like(row_acc)
-        where = own_ref[256:272, :].astype(f32)
-        strip = where.T
-        for t in range(8):
-            dx = spread(strip, t) - where[t : t + 1]
-            dy = spread(strip, 8 + t) - where[8 + t : 9 + t]
-            block = radial(dx * dx + dy * dy)
-            own_out[:, t * TILE : (t + 1) * TILE] = KERNEL_SCALE * lax.dot_general(
-                own_ref[t * 32 : (t + 1) * 32, :], block, NT, preferred_element_type=f32
-            )
-    else:
-        count_ref, bins_ref, near_ref, col_ref, row_acc, row_out, *col_out, px, py, qx, qy, col_acc = refs
+def row_kernel(own_ref, near_ref, px, py, own_out):
     def row_prepare(r, carry):
         strip = near_ref[r, 256:272, :].astype(f32).T
         for t in range(8):
@@ -95,13 +81,31 @@
         return carry
 
     lax.fori_loop(0, 8, row_prepare, 0)
+    where = own_ref[256:272, :].astype(f32)
+    strip = where.T
+    for t in range(8):
+        dx = spread(strip, t) - where[t : t + 1]
+        dy = spread(strip, 8 + t) - where[8 + t : 9 + t]
+        block = radial(dx * dx + dy * dy)
+        own_out[:, t * TILE : (t + 1) * TILE] = KERNEL_SCALE * lax.dot_general(
+            own_ref[t * 32 : (t + 1) * 32, :], block, NT, preferred_element_type=f32
+        )
+
+
+def part_kernel(part, place_ref, count_ref, bins_ref, near_ref, px, py, col_ref, *refs):
+    if part == 0:
+        row_acc, *col_out, qx, qy, col_acc = refs
+        row_acc[...] = jnp.zeros_like(row_acc)
+    else:
+        row_acc, row_out, *col_out, qx, qy, col_acc = refs
+    x_own, y_own, z_own, core_own = place_ref[0], place_ref[1], place_ref[2], place_ref[3]
     tiles = range(SPLIT) if part == 0 else range(SPLIT, 8)
     first, number = tiles[0], len(tiles)
     live = count_ref[part]
     col_acc[...] = jnp.zeros_like(col_acc)
 
     def col_prepare(r, carry):
-        where = col_ref[(r & 7) * 4 + (r >> 3), 256:272, :].astype(f32)
+        where = col_ref[r, 256:272, :].astype(f32)
         for t in tiles:
             qx[r * 8 + t] = jnp.broadcast_to(where[t : t + 1], (8, TILE))
             qy[r * 8 + t] = jnp.broadcast_to(where[8 + t : 9 + t], (8, TILE))
@@ -114,10 +118,14 @@
         for u in range(size):
             e = start + u
             both = bins_ref[e if part == 0 else BIN - 1 - e]
-            a, b = both & 63, (both >> 8) & 255
-            keep = jnp.where(e < live, both >> 16, 0).astype(f32).astype(bf16)
-            near = near_ref[a >> 3, pl.ds(pl.multiple_of((a & 7) * 32, 32), 32), :] * keep
-            far = col_ref[((b >> 3) & 7) * 4 + (b >> 6), pl.ds(pl.multiple_of((b & 7) * 32, 32), 32), :] * keep
+            a, b = both & 255, both >> 8
+            keep = jnp.where(e < live, 1.0, 0.0).astype(bf16)
+            near_slot = ((y_own - (a >> 4)) & 3) + ((((a >> 3) & 1) ^ core_own) << 2)
+            far_slot = (((x_own - (b >> 3)) & 3) << 3) + ((z_own - (b >> 5)) & 7)
+            near = near_ref[near_slot, pl.ds(pl.multiple_of((a & 7) * 32, 32), 32), :] * keep
+            far = col_ref[far_slot, pl.ds(pl.multiple_of((b & 7) * 32, 32), 32), :] * keep
+            a = (near_slot << 3) + (a & 7)
+            b = (far_slot << 3) + (b & 7)
             dx = px[a].reshape(16, 8, TILE) - qx[b][None]
             dy = py[a].reshape(16, 8, TILE) - qy[b][None]
             block = radial((dx * dx + dy * dy).reshape(TILE, TILE))
@@ -145,7 +153,7 @@
         for k in range(4):
             for t in range(number):
                 total = KERNEL_SCALE * col_acc[k * 64 + z * 8 + first + t]
-                col_out[k][z, t * 32 : (t + 1) * 32, :] = total.astype(bf16)
+                col_out[k][(z_own - z) & 7, t * 32 : (t + 1) * 32, :] = total.astype(bf16)
         return carry
 
     lax.fori_loop(0, 8, finish, 0)
@@ -231,26 +239,37 @@
 def on_device(solution_field, residual, direction, positions, tile_pairs, pair_count):
     shape = jax.ShapeDtypeStruct
     own_points = direction.shape[1]
-    x_own, y_own, core_own = lax.axis_index("x"), lax.axis_index("y"), lax.axis_index("core")
     packed = pl.pallas_call(
-        pack_kernel, out_shape=shape((272, TILE), bf16), in_specs=[VMEM] * 2, out_specs=VMEM, name="pack"
+        pack_kernel, out_shape=shape((272, TILE), bf16), in_specs=[VMEM] * 2, out_specs=VMEM, compiler_params=SMALL, name="pack"
     )(direction, positions)
-    x_all = jnp.stack([packed] + shifts(packed, "x", 4))
-    col_all = lax.all_gather(x_all, "z").reshape(32, 272, TILE)
+    z_all = jnp.stack([packed] + shifts(packed, "z", 8))
+    up, down = [(i, (i + 1) % 4) for i in range(4)], [(i, (i - 1) % 4) for i in range(4)]
+    x_below, x_above = lax.ppermute(z_all, "x", up), lax.ppermute(z_all, "x", down)
+    x_far = [lax.ppermute(x_below[:4], "x", up), lax.ppermute(x_above[4:], "x", down)]
+    col_all = jnp.concatenate([z_all, x_below, *x_far, x_above], 0)
     chip = jnp.stack([packed, swap(packed)])
     around = shifts(chip, "y", 4)
     row_all = jnp.concatenate([v[:1] for v in [chip] + around] + [v[1:] for v in [chip] + around], 0)
-    place = jnp.stack([pair_count[0], x_own, y_own, core_own]).astype(jnp.int32)
+    place = jnp.stack([lax.axis_index(name) for name in ("x", "y", "z", "core")]).astype(jnp.int32)
     bins, counts = pl.pallas_call(
         bin_kernel,
         out_shape=(shape((BIN,), jnp.int32), shape((2,), jnp.int32)),
-        in_specs=[SMEM, SMEM, pl.BlockSpec(memory_space=pl.ANY)],
+        in_specs=[SMEM, SMEM, VMEM],
         out_specs=(SMEM, SMEM),
+        compiler_params=SMALL,
         name="bins",
-    )(place, tile_pairs, row_all)
+    )(pair_count, tile_pairs, x_above[0, :16])
+    spread_shape = shape((64, TILE, TILE), f32)
+    px, py, own_product = pl.pallas_call(
+        row_kernel,
+        out_shape=(spread_shape, spread_shape, shape((PROBES, own_points), f32)),
+        in_specs=[VMEM] * 2,
+        out_specs=(VMEM,) * 3,
+        compiler_params=PARAMS,
+        name="rows",
+    )(packed, row_all)
     acc = shape((64, PROBES, TILE), f32)
-    scratch = [pltpu.VMEM((64, TILE, TILE), f32)] * 2
-    scratch += [pltpu.VMEM((256, 8, TILE), f32), pltpu.VMEM((256, 8, TILE), f32), pltpu.VMEM((256, PROBES, TILE), f32)]
+    scratch = [pltpu.VMEM((256, 8, TILE), f32), pltpu.VMEM((256, 8, TILE), f32), pltpu.VMEM((256, PROBES, TILE), f32)]
 
     def blocks(number):
         return (shape((8, number * 32, TILE), bf16),) * 4
@@ -258,24 +277,24 @@
     def sent(col_out):
         return [lax.ppermute(col_out[k], "x", [(i, (i - k) % 4) for i in range(4)]) for k in range(1, 4)]
 
-    row_acc, own_product, *col_first = pl.pallas_call(
+    row_acc, *col_first = pl.pallas_call(
         functools.partial(part_kernel, 0),
-        out_shape=(acc, shape((PROBES, own_points), f32)) + blocks(SPLIT),
-        in_specs=[SMEM] * 2 + [VMEM] * 3,
-        out_specs=(VMEM,) * 6,
+        out_shape=(acc,) + blocks(SPLIT),
+        in_specs=[SMEM] * 3 + [VMEM] * 4,
+        out_specs=(VMEM,) * 5,
         scratch_shapes=scratch,
         compiler_params=PARAMS,
         name="pairs_first",
-    )(counts, bins, packed, row_all, col_all)
+    )(place, counts, bins, row_all, px, py, col_all)
     row_sum, *col_second = pl.pallas_call(
         functools.partial(part_kernel, 1),
         out_shape=(shape((8, 256, TILE), bf16),) + blocks(8 - SPLIT),
-        in_specs=[SMEM] * 2 + [VMEM] * 3,
+        in_specs=[SMEM] * 3 + [VMEM] * 5,
         out_specs=(VMEM,) * 5,
         scratch_shapes=scratch,
         compiler_params=PARAMS,
         name="pairs_second",
-    )(counts, bins, row_all, col_all, row_acc)
+    )(place, counts, bins, row_all, px, py, col_all, row_acc)
     sums = pl.pallas_call(
         add_kernel,
         out_shape=shape((8, 256, TILE), bf16),

time: 213 us -> 203 us (0.953)
  starting transfers between devices: 37.9 us -> 111 us
  Pallas kernels: 94.3 us -> 26 us
  between operations: 14.9 us -> 1.6 us
  waiting for transfers between devices: 55.5 us -> 60.5 us
  local copies, waits for them, and re-layouts: 5.88 us -> 2.23 us
  other arithmetic: 3.29 us -> 0.23 us
    ppermute x6, starting transfers between devices: 10.6 us -> 59.9 us  [sent(): lax.ppermute(col_out[k], 'x', [(i, (i - k) % 4) for i in range(4)])]
    pallas_call x1 -> x2, Pallas kernels: 47.9 us -> 12.5 us  [the longest x1 9.28 us: on_device(): pl.pallas_call(functools.partial(part_kernel, 0), out_shape=(acc,) + bloc...]
    pallas_call x1, Pallas kernels: 21.2 us -> 3.19 us  [on_device(): pl.pallas_call(bin_kernel, out_shape=(shape((BIN,), jnp.int32), shape((2,...]
    pallas_call x1, Pallas kernels: 17.2 us -> 3.72 us  [on_device(): pl.pallas_call(functools.partial(part_kernel, 1), out_shape=(shape((8, 25...]
    ppermute x15 -> x19, starting transfers between devices: 18.2 us -> 31.3 us  [shifts(): lax.ppermute(value, axis, [(i, (i + k) % size) for i in range(size)])]
    ppermute x15 -> x19, waiting for transfers between devices: 21.4 us -> 31.1 us  [shifts(): lax.ppermute(value, axis, [(i, (i + k) % size) for i in range(size)])]
    all_gather x1 -> x0, waiting for transfers between devices: 7.05 us -> none  [on_device(): col_all = lax.all_gather(x_all, 'z').reshape(32, 272, TILE)]
    ppermute x0 -> x4, starting transfers between devices: none -> 6.7 us  [the longest x1 2.2 us: on_device(): lax.ppermute(x_above[4:], 'x', down)]
  transfers between devices with their start and end apart: 30 -> 37, of which waited for: 21 -> 21; matrix products, arithmetic and copies ran while one was open for 1% -> 0% of each run, Pallas kernels for 19% -> 6%
where the time goes in v5:
time: 203 us; the launch traced here: 201 us
  starting transfers between devices  111 us (55%)
  waiting for transfers between devices  60.5 us (30%)
  Pallas kernels  26 us (13%)
  local copies, waits for them, and re-layouts  2.23 us (1%)
    ppermute x6, starting transfers between devices, sent(): lax.ppermute(col_out[k], 'x', [(i, (i - k) % 4) for i in range(4)])  59.9 us
    ppermute x19, starting transfers between devices, shifts(): lax.ppermute(value, axis, [(i, (i + k) % size) for i in range(size)])  31.3 us
    ppermute x19, waiting for transfers between devices, shifts(): lax.ppermute(value, axis, [(i, (i + k) % size) for i in range(size)])  31.1 us
    pallas_call x1, Pallas kernels, on_device(): pl.pallas_call(functools.partial(part_kernel, 0), out_shape=(acc,) + bloc...  9.28 us
    all_to_all x1, starting transfers between devices, on_device(): col_parts = lax.all_to_all(sums, 'z', 0, 0)  7.25 us
    ppermute x1, waiting for transfers between devices, on_device(): gram = gram + lax.ppermute(gram, 'z', [(i, (i + 4) % 8) for i in range(8)])  7.17 us
    ppermute x6, waiting for transfers between devices, sent(): lax.ppermute(col_out[k], 'x', [(i, (i - k) % 4) for i in range(4)])  4.94 us
    ppermute x1, waiting for transfers between devices, on_device(): lax.ppermute(z_all, 'x', up)  4.84 us
  transfers between devices with their start and end apart: 37, of which 21 were waited for; matrix products, arithmetic and copies ran while one was open for 0% of the time, Pallas kernels for 6%

profile of v5, /device:TPU:16, one launch (start us, length us, event | category | flops | bytes accessed | tf_op | source)
XLA Modules:
  0.0 201.2 jit_solution(4065520218646310065)
XLA Ops:
  2.2 5.9 %collective-permute-start.10 = (bf16[272,128]{1,0:T(8,128)(2,1)S(1)}, bf16[272,128]{1,0:T(8,128)(2,1)S(1)}, u32[]{:S(2)}, u32[]{:S(2)}) collective-permute-start(bf16[272,128]{1,0:T(8,128)(2,1)S(1)} %pack.1.own_ref), channel_id=1, source_target_pairs={{0,224},{32,0},{64,32},{96,64},{128,96},{160,128},{192,160},{224,1... | collective-permute-start | bytes 208904 | tf_op jit(solution)/shard_map/ppermute | solution.py:232
  10.1 5.0 %collective-permute-start.7 = (bf16[272,128]{1,0:T(8,128)(2,1)S(1)}, bf16[272,128]{1,0:T(8,128)(2,1)S(1)}, u32[]{:S(2)}, u32[]{:S(2)}) collective-permute-start(bf16[272,128]{1,0:T(8,128)(2,1)S(1)} %pack.1.own_ref), channel_id=1, source_target_pairs={{0,128},{32,160},{64,192},{96,224},{128,0},{160,32},{192,64},{224,... | collective-permute-start | bytes 208904 | tf_op jit(solution)/shard_map/ppermute | solution.py:232
  16.9 3.7 %collective-permute-done.4 = bf16[272,128]{1,0:T(8,128)(2,1)S(1)} collective-permute-done((bf16[272,128]{1,0:T(8,128)(2,1)S(1)}, bf16[272,128]{1,0:T(8,128)(2,1)S(1)}, u32[]{:S(2)}, u32[]{:S(2)}) %collective-permute-start.4) | collective-permute-done | bytes 69664 | tf_op jit(solution)/shard_map/ppermute | solution.py:232
  21.2 5.9 %collective-permute-done.5 = bf16[272,128]{1,0:T(8,128)(2,1)S(1)} collective-permute-done((bf16[272,128]{1,0:T(8,128)(2,1)S(1)}, bf16[272,128]{1,0:T(8,128)(2,1)S(1)}, u32[]{:S(2)}, u32[]{:S(2)}) %collective-permute-start.5) | collective-permute-done | bytes 69664 | tf_op jit(solution)/shard_map/ppermute | solution.py:232
  28.4 8.5 %collective-permute-done.6 = bf16[272,128]{1,0:T(8,128)(2,1)S(1)} collective-permute-done((bf16[272,128]{1,0:T(8,128)(2,1)S(1)}, bf16[272,128]{1,0:T(8,128)(2,1)S(1)}, u32[]{:S(2)}, u32[]{:S(2)}) %collective-permute-start.6) | collective-permute-done | bytes 69664 | tf_op jit(solution)/shard_map/ppermute | solution.py:232
  37.4 3.0 %collective-permute-start.2 = (bf16[2,272,128]{2,1,0:T(8,128)(2,1)S(1)}, bf16[2,272,128]{2,1,0:T(8,128)(2,1)S(1)}, u32[]{:S(2)}, u32[]{:S(2)}) collective-permute-start(bf16[2,272,128]{2,1,0:T(8,128)(2,1)S(1)} %pad_maximum_fusion.1), channel_id=1, source_target_pairs={{0,4},{2,6},{4,0},{6,2},{1,5},{3,7},{5,1},{7,3},{8,12},{10,14},{12... | collective-permute-start | bytes 417800 | tf_op jit(solution)/shard_map/ppermute | solution.py:232
  45.7 3.2 %rows.1 = (f32[64,128,128]{2,1,0:T(8,128)S(1)}, f32[64,128,128]{2,1,0:T(8,128)S(1)}, f32[32,1024]{1,0:T(8,128)S(1)}) custom-call(bf16[272,128]{1,0:T(8,128)(2,1)S(1)} %pack.1.own_ref, bf16[8,272,128]{2,1,0:T(8,128)(2,1)S(1)} %slice_dynamic-update-slice_fusion.near_ref), custom_call_target="tpu_custom_call" | custom-call | tf_op jit(solution)/shard_map/rows/pallas_call | solution.py:263
  48.9 4.8 %collective-permute-done.12 = bf16[8,272,128]{2,1,0:T(8,128)(2,1)S(1)} collective-permute-done((bf16[8,272,128]{2,1,0:T(8,128)(2,1)S(1)}, bf16[8,272,128]{2,1,0:T(8,128)(2,1)S(1)}, u32[]{:S(2)}, u32[]{:S(2)}) %collective-permute-start.12) | collective-permute-done | bytes 557088 | tf_op jit(solution)/shard_map/ppermute | solution.py:247
  57.2 3.2 %bins.1 = (s32[1600]{0:T(1024)S(1)}, s32[2]{0:T(128)S(1)}) custom-call(s32[1]{0:T(128)S(6)} %copy.34.live_ref, s32[2,1536]{1,0:T(2,128)S(1)} %copy-done.4, bf16[16,128]{1,0:T(8,128)(2,1)S(1)} %slice_bitcast_fusion.3.after_ref), custom_call_target="tpu_custom_call" | custom-call | tf_op jit(solution)/shard_map/bins/pallas_call | solution.py:254
  61.8 9.3 %pairs_first.1 = (f32[64,32,128]{2,1,0:T(8,128)S(1)}, bf16[8,192,128]{2,1,0:T(8,128)(2,1)S(1)}, bf16[8,192,128]{2,1,0:T(8,128)(2,1)S(1)}, bf16[8,192,128]{2,1,0:T(8,128)(2,1)S(1)}, bf16[8,192,128]{2,1,0:T(8,128)(2,1)S(1)}) custom-call(s32[4]{0:T(128)S(1)} %pad_add_fusion.place_ref, s32[2]{0:T(128)S(1)} %get-tuple-element.21.count_ref, ...), custom_call_target="tpu_custom_call" | custom-call | tf_op jit(solution)/shard_map/pairs_first/pallas_call | solution.py:280
  72.9 41.5 %collective-permute-start.20 = (bf16[8,192,128]{2,1,0:T(8,128)(2,1)S(1)}, bf16[8,192,128]{2,1,0:T(8,128)(2,1)S(1)}, u32[]{:S(2)}, u32[]{:S(2)}) collective-permute-start(bf16[8,192,128]{2,1,0:T(8,128)(2,1)S(1)} %get-tuple-element.29), channel_id=1, source_target_pairs={{0,16},{8,24},{16,0},{24,8},{1,17},{9,25},{17,1},{25,9},{2,18},{10... | collective-permute-start | bytes 1179656 | tf_op jit(solution)/shard_map/ppermute | solution.py:278
  115.7 3.7 %pairs_second.1 = (bf16[8,256,128]{2,1,0:T(8,128)(2,1)S(1)}, bf16[8,64,128]{2,1,0:T(8,128)(2,1)S(1)}, bf16[8,64,128]{2,1,0:T(8,128)(2,1)S(1)}, bf16[8,64,128]{2,1,0:T(8,128)(2,1)S(1)}, bf16[8,64,128]{2,1,0:T(8,128)(2,1)S(1)}) custom-call(s32[4]{0:T(128)S(1)} %pad_add_fusion.place_ref, s32[2]{0:T(128)S(1)} %get-tuple-element.21.count_ref, ...), custom_call_target="tpu_custom_call" | custom-call | tf_op jit(solution)/shard_map/pairs_second/pallas_call | solution.py:289
  119.4 2.4 %collective-permute-start.22 = (bf16[8,64,128]{2,1,0:T(8,128)(2,1)S(1)}, bf16[8,64,128]{2,1,0:T(8,128)(2,1)S(1)}, u32[]{:S(2)}, u32[]{:S(2)}) collective-permute-start(bf16[8,64,128]{2,1,0:T(8,128)(2,1)S(1)} %get-tuple-element.32), channel_id=1, source_target_pairs={{0,24},{8,0},{16,8},{24,16},{1,25},{9,1},{17,9},{25,17},{2,26},{10... | collective-permute-start | bytes 393224 | tf_op jit(solution)/shard_map/ppermute | solution.py:278
  121.8 10.9 %collective-permute-start.23 = (bf16[8,64,128]{2,1,0:T(8,128)(2,1)S(1)}, bf16[8,64,128]{2,1,0:T(8,128)(2,1)S(1)}, u32[]{:S(2)}, u32[]{:S(2)}) collective-permute-start(bf16[8,64,128]{2,1,0:T(8,128)(2,1)S(1)} %get-tuple-element.33), channel_id=1, source_target_pairs={{0,16},{8,24},{16,0},{24,8},{1,17},{9,25},{17,1},{25,9},{2,18},{10... | collective-permute-start | bytes 393224 | tf_op jit(solution)/shard_map/ppermute | solution.py:278
  135.7 4.0 %collective-permute-done.24.c1 = bf16[8,64,128]{2,1,0:T(8,128)(2,1)S(1)} collective-permute-done((bf16[8,64,128]{2,1,0:T(8,128)(2,1)S(1)}, bf16[8,64,128]{2,1,0:T(8,128)(2,1)S(1)}, u32[]{:S(2)}, u32[]{:S(2)}) %collective-permute-start.24) | collective-permute-done | bytes 131104 | tf_op jit(solution)/shard_map/ppermute | solution.py:278
  140.9 7.3 %all-to-all-start = ((bf16[8,256,128]{2,1,0:T(8,128)(2,1)}), bf16[8,256,128]{2,1,0:T(8,128)(2,1)S(1)}, u32[]{:S(2)}, u32[]{:S(2)}) async-start(bf16[8,256,128]{2,1,0:T(8,128)(2,1)} %add.65), calls=%async_computation | async-start | bytes 1048576 | tf_op jit(solution)/shard_map/all_to_all | solution.py:306
  150.2 2.5 %collective-permute-start.17 = (bf16[256,128]{1,0:T(8,128)(2,1)S(1)}, bf16[256,128]{1,0:T(8,128)(2,1)S(1)}, u32[]{:S(2)}, u32[]{:S(2)}) collective-permute-start(bf16[256,128]{1,0:T(8,128)(2,1)S(1)} %get-tuple-element.39), channel_id=1, source_target_pairs={{0,4},{2,6},{4,0},{6,2},{1,5},{3,7},{5,1},{7,3},{8,12},{10,14},{12... | collective-permute-start | bytes 196616 | tf_op jit(solution)/shard_map/ppermute | solution.py:309
  153.6 2.4 %collective-permute-done.17 = bf16[256,128]{1,0:T(8,128)(2,1)S(1)} collective-permute-done((bf16[256,128]{1,0:T(8,128)(2,1)S(1)}, bf16[256,128]{1,0:T(8,128)(2,1)S(1)}, u32[]{:S(2)}, u32[]{:S(2)}) %collective-permute-start.17) | collective-permute-done | bytes 65568 | tf_op jit(solution)/shard_map/ppermute | solution.py:309
  157.0 4.6 %all-to-all-done.col_ref = bf16[8,256,128]{2,1,0:T(8,128)(2,1)S(1)} async-done(((bf16[8,256,128]{2,1,0:T(8,128)(2,1)}), bf16[8,256,128]{2,1,0:T(8,128)(2,1)S(1)}, u32[]{:S(2)}, u32[]{:S(2)}) %all-to-all-start) | async-done | bytes 524320 | tf_op jit(solution)/shard_map/all_to_all | solution.py:306
  163.9 5.6 %collective-permute-start.28 = (f32[40,128]{1,0:T(8,128)S(1)}, f32[40,128]{1,0:T(8,128)S(1)}, u32[]{:S(2)}, u32[]{:S(2)}) collective-permute-start(f32[40,128]{1,0:T(8,128)S(1)} %add.38), channel_id=1, source_target_pairs={{0,6},{2,0},{4,2},{6,4},{1,7},{3,1},{5,3},{7,5},{8,14},{10,8},{12,... | collective-permute-start | bytes 61448 | tf_op jit(solution)/shard_map/ppermute | solution.py:232
  171.6 3.1 %collective-permute-done.27 = f32[40,128]{1,0:T(8,128)S(1)} collective-permute-done((f32[40,128]{1,0:T(8,128)S(1)}, f32[40,128]{1,0:T(8,128)S(1)}, u32[]{:S(2)}, u32[]{:S(2)}) %collective-permute-start.27) | collective-permute-done | bytes 20512 | tf_op jit(solution)/shard_map/ppermute | solution.py:232
  182.2 7.2 %collective-permute-done.32 = f32[40,128]{1,0:T(8,128)S(1)} collective-permute-done((f32[40,128]{1,0:T(8,128)S(1)}, f32[40,128]{1,0:T(8,128)S(1)}, u32[]{:S(2)}, u32[]{:S(2)}) %collective-permute-start.32) | collective-permute-done | bytes 20512 | tf_op jit(solution)/shard_map/ppermute | solution.py:323
  192.8 3.5 %collective-permute-done.35 = f32[40,128]{1,0:T(8,128)S(1)} collective-permute-done((f32[40,128]{1,0:T(8,128)S(1)}, f32[40,128]{1,0:T(8,128)S(1)}, u32[]{:S(2)}, u32[]{:S(2)}) %collective-permute-start.35) | collective-permute-done | bytes 20512 | tf_op jit(solution)/shard_map/ppermute | solution.py:232
  196.5 4.7 %solve.1 = (f32[32,1024]{1,0:T(8,128)}, f32[32,1024]{1,0:T(8,128)}, f32[32,1024]{1,0:T(8,128)}) custom-call(f32[40,128]{1,0:T(8,128)S(1)} %add_add_fusion.gram_ref, f32[32,1024]{1,0:T(8,128)S(1)} %copy-done.3, f32[32,1024]{1,0:T(8,128)S(1)} %copy-done.2, f32[32,1024]{1,0:T(8,128)S(1)} %copy-done.1, f32[32,1024]{1,0:T(8,128)S(1)} %get-tuple-element.36.image_ref), custom_call_target="tpu_custom_call" | custom-call | tf_op jit(solution)/shard_map/solve/pallas_call | solution.py:325
  (104 shorter events, 43.6 us)
Async XLA Ops:
  2.2 38.3 %collective-permute-start.10 = (bf16[272,128]{1,0:T(8,128)(2,1)S(1)}, bf16[272,128]{1,0:T(8,128)(2,1)S(1)}, u32[]{:S(2)}, u32[]{:S(2)}) collective-permute-start(bf16[272,128]{1,0:T(8,128)(2,1)S(1)} %pack.1.own_ref), channel_id=1, source_target_pairs={{0,224},{32,0},{64,32},{96,64},{128,96},{160,128},{192,160},{224,1... | collective-permute-start | bytes 208904 | tf_op jit(solution)/shard_map/ppermute | solution.py:232
  8.2 32.3 %collective-permute-start.9 = (bf16[272,128]{1,0:T(8,128)(2,1)S(1)}, bf16[272,128]{1,0:T(8,128)(2,1)S(1)}, u32[]{:S(2)}, u32[]{:S(2)}) collective-permute-start(bf16[272,128]{1,0:T(8,128)(2,1)S(1)} %pack.1.own_ref), channel_id=1, source_target_pairs={{0,192},{32,224},{64,0},{96,32},{128,64},{160,96},{192,128},{224,1... | collective-permute-start | bytes 208904 | tf_op jit(solution)/shard_map/ppermute | solution.py:232
  9.6 30.8 %collective-permute-start.8 = (bf16[272,128]{1,0:T(8,128)(2,1)S(1)}, bf16[272,128]{1,0:T(8,128)(2,1)S(1)}, u32[]{:S(2)}, u32[]{:S(2)}) collective-permute-start(bf16[272,128]{1,0:T(8,128)(2,1)S(1)} %pack.1.own_ref), channel_id=1, source_target_pairs={{0,160},{32,192},{64,224},{96,0},{128,32},{160,64},{192,96},{224,1... | collective-permute-start | bytes 208904 | tf_op jit(solution)/shard_map/ppermute | solution.py:232
  10.1 27.3 %collective-permute-start.7 = (bf16[272,128]{1,0:T(8,128)(2,1)S(1)}, bf16[272,128]{1,0:T(8,128)(2,1)S(1)}, u32[]{:S(2)}, u32[]{:S(2)}) collective-permute-start(bf16[272,128]{1,0:T(8,128)(2,1)S(1)} %pack.1.own_ref), channel_id=1, source_target_pairs={{0,128},{32,160},{64,192},{96,224},{128,0},{160,32},{192,64},{224,... | collective-permute-start | bytes 208904 | tf_op jit(solution)/shard_map/ppermute | solution.py:232
  20.6 6.4 %collective-permute-start.5 = (bf16[272,128]{1,0:T(8,128)(2,1)S(1)}, bf16[272,128]{1,0:T(8,128)(2,1)S(1)}, u32[]{:S(2)}, u32[]{:S(2)}) collective-permute-start(bf16[272,128]{1,0:T(8,128)(2,1)S(1)} %pack.1.own_ref), channel_id=1, source_target_pairs={{0,64},{32,96},{64,128},{96,160},{128,192},{160,224},{192,0},{224,... | collective-permute-start | bytes 208904 | tf_op jit(solution)/shard_map/ppermute | solution.py:232
  28.3 8.5 %collective-permute-start.6 = (bf16[272,128]{1,0:T(8,128)(2,1)S(1)}, bf16[272,128]{1,0:T(8,128)(2,1)S(1)}, u32[]{:S(2)}, u32[]{:S(2)}) collective-permute-start(bf16[272,128]{1,0:T(8,128)(2,1)S(1)} %pack.1.own_ref), channel_id=1, source_target_pairs={{0,96},{32,128},{64,160},{96,192},{128,224},{160,0},{192,32},{224,... | collective-permute-start | bytes 208904 | tf_op jit(solution)/shard_map/ppermute | solution.py:232
  36.9 8.7 %collective-permute-start.3 = (bf16[2,272,128]{2,1,0:T(8,128)(2,1)S(1)}, bf16[2,272,128]{2,1,0:T(8,128)(2,1)S(1)}, u32[]{:S(2)}, u32[]{:S(2)}) collective-permute-start(bf16[2,272,128]{2,1,0:T(8,128)(2,1)S(1)} %pad_maximum_fusion.1), channel_id=1, source_target_pairs={{0,6},{2,0},{4,2},{6,4},{1,7},{3,1},{5,3},{7,5},{8,14},{10,8},{12,... | collective-permute-start | bytes 417800 | tf_op jit(solution)/shard_map/ppermute | solution.py:232
  37.4 8.2 %collective-permute-start.2 = (bf16[2,272,128]{2,1,0:T(8,128)(2,1)S(1)}, bf16[2,272,128]{2,1,0:T(8,128)(2,1)S(1)}, u32[]{:S(2)}, u32[]{:S(2)}) collective-permute-start(bf16[2,272,128]{2,1,0:T(8,128)(2,1)S(1)} %pad_maximum_fusion.1), channel_id=1, source_target_pairs={{0,4},{2,6},{4,0},{6,2},{1,5},{3,7},{5,1},{7,3},{8,12},{10,14},{12... | collective-permute-start | bytes 417800 | tf_op jit(solution)/shard_map/ppermute | solution.py:232
  40.6 13.1 %collective-permute-start.12 = (bf16[8,272,128]{2,1,0:T(8,128)(2,1)S(1)}, bf16[8,272,128]{2,1,0:T(8,128)(2,1)S(1)}, u32[]{:S(2)}, u32[]{:S(2)}) collective-permute-start(bf16[8,272,128]{2,1,0:T(8,128)(2,1)S(1)} %get-tuple-element.42), channel_id=1, source_target_pairs={{0,8},{8,16},{16,24},{24,0},{1,9},{9,17},{17,25},{25,1},{2,10},{10... | collective-permute-start | bytes 1671176 | tf_op jit(solution)/shard_map/ppermute | solution.py:247
  42.2 12.8 %collective-permute-start.11 = (bf16[8,272,128]{2,1,0:T(8,128)(2,1)S(1)}, bf16[8,272,128]{2,1,0:T(8,128)(2,1)S(1)}, u32[]{:S(2)}, u32[]{:S(2)}) collective-permute-start(bf16[8,272,128]{2,1,0:T(8,128)(2,1)S(1)} %get-tuple-element.42), channel_id=1, source_target_pairs={{0,24},{8,0},{16,8},{24,16},{1,25},{9,1},{17,9},{25,17},{2,26},{10... | collective-permute-start | bytes 1671176 | tf_op jit(solution)/shard_map/ppermute | solution.py:247
  53.8 7.8 %collective-permute-start.13 = (bf16[4,272,128]{2,1,0:T(8,128)(2,1)S(1)}, bf16[4,272,128]{2,1,0:T(8,128)(2,1)S(1)}, u32[]{:S(2)}, u32[]{:S(2)}) collective-permute-start(bf16[4,272,128]{2,1,0:T(8,128)(2,1)S(1)} %slice.67), channel_id=1, source_target_pairs={{0,8},{8,16},{16,24},{24,0},{1,9},{9,17},{17,25},{25,1},{2,10},{10... | collective-permute-start | bytes 835592 | tf_op jit(solution)/shard_map/ppermute | solution.py:248
  55.0 6.7 %collective-permute-start.14 = (bf16[4,272,128]{2,1,0:T(8,128)(2,1)S(1)}, bf16[4,272,128]{2,1,0:T(8,128)(2,1)S(1)}, u32[]{:S(2)}, u32[]{:S(2)}) collective-permute-start(bf16[4,272,128]{2,1,0:T(8,128)(2,1)S(1)} %slice.68), channel_id=1, source_target_pairs={{0,24},{8,0},{16,8},{24,16},{1,25},{9,1},{17,9},{25,17},{2,26},{10... | collective-permute-start | bytes 835592 | tf_op jit(solution)/shard_map/ppermute | solution.py:248
  71.1 68.7 %collective-permute-start.19 = (bf16[8,192,128]{2,1,0:T(8,128)(2,1)S(1)}, bf16[8,192,128]{2,1,0:T(8,128)(2,1)S(1)}, u32[]{:S(2)}, u32[]{:S(2)}) collective-permute-start(bf16[8,192,128]{2,1,0:T(8,128)(2,1)S(1)} %get-tuple-element.28), channel_id=1, source_target_pairs={{0,24},{8,0},{16,8},{24,16},{1,25},{9,1},{17,9},{25,17},{2,26},{10... | collective-permute-start | bytes 1179656 | tf_op jit(solution)/shard_map/ppermute | solution.py:278
  72.9 66.9 %collective-permute-start.20 = (bf16[8,192,128]{2,1,0:T(8,128)(2,1)S(1)}, bf16[8,192,128]{2,1,0:T(8,128)(2,1)S(1)}, u32[]{:S(2)}, u32[]{:S(2)}) collective-permute-start(bf16[8,192,128]{2,1,0:T(8,128)(2,1)S(1)} %get-tuple-element.29), channel_id=1, source_target_pairs={{0,16},{8,24},{16,0},{24,8},{1,17},{9,25},{17,1},{25,9},{2,18},{10... | collective-permute-start | bytes 1179656 | tf_op jit(solution)/shard_map/ppermute | solution.py:278
  114.4 25.4 %collective-permute-start.21 = (bf16[8,192,128]{2,1,0:T(8,128)(2,1)S(1)}, bf16[8,192,128]{2,1,0:T(8,128)(2,1)S(1)}, u32[]{:S(2)}, u32[]{:S(2)}) collective-permute-start(bf16[8,192,128]{2,1,0:T(8,128)(2,1)S(1)} %get-tuple-element.30), channel_id=1, source_target_pairs={{0,8},{8,16},{16,24},{24,0},{1,9},{9,17},{17,25},{25,1},{2,10},{10... | collective-permute-start | bytes 1179656 | tf_op jit(solution)/shard_map/ppermute | solution.py:278
  119.4 14.2 %collective-permute-start.22 = (bf16[8,64,128]{2,1,0:T(8,128)(2,1)S(1)}, bf16[8,64,128]{2,1,0:T(8,128)(2,1)S(1)}, u32[]{:S(2)}, u32[]{:S(2)}) collective-permute-start(bf16[8,64,128]{2,1,0:T(8,128)(2,1)S(1)} %get-tuple-element.32), channel_id=1, source_target_pairs={{0,24},{8,0},{16,8},{24,16},{1,25},{9,1},{17,9},{25,17},{2,26},{10... | collective-permute-start | bytes 393224 | tf_op jit(solution)/shard_map/ppermute | solution.py:278
  121.8 13.8 %collective-permute-start.23 = (bf16[8,64,128]{2,1,0:T(8,128)(2,1)S(1)}, bf16[8,64,128]{2,1,0:T(8,128)(2,1)S(1)}, u32[]{:S(2)}, u32[]{:S(2)}) collective-permute-start(bf16[8,64,128]{2,1,0:T(8,128)(2,1)S(1)} %get-tuple-element.33), channel_id=1, source_target_pairs={{0,16},{8,24},{16,0},{24,8},{1,17},{9,25},{17,1},{25,9},{2,18},{10... | collective-permute-start | bytes 393224 | tf_op jit(solution)/shard_map/ppermute | solution.py:278
  133.6 6.2 %collective-permute-start.24 = (bf16[8,64,128]{2,1,0:T(8,128)(2,1)S(1)}, bf16[8,64,128]{2,1,0:T(8,128)(2,1)S(1)}, u32[]{:S(2)}, u32[]{:S(2)}) collective-permute-start(bf16[8,64,128]{2,1,0:T(8,128)(2,1)S(1)} %get-tuple-element.34), channel_id=1, source_target_pairs={{0,8},{8,16},{16,24},{24,0},{1,9},{9,17},{17,25},{25,1},{2,10},{10... | collective-permute-start | bytes 393224 | tf_op jit(solution)/shard_map/ppermute | solution.py:278
  135.6 12.5 %collective-permute-start.15 = (bf16[4,256,128]{2,1,0:T(8,128)(2,1)S(1)}, bf16[4,256,128]{2,1,0:T(8,128)(2,1)S(1)}, u32[]{:S(2)}, u32[]{:S(2)}) collective-permute-start(bf16[4,256,128]{2,1,0:T(8,128)(2,1)S(1)} %slice.55), channel_id=1, source_target_pairs={{0,1},{1,0},{2,3},{3,2},{4,5},{5,4},{6,7},{7,6},{8,9},{9,8},{10,11... | collective-permute-start | bytes 786440 | tf_op jit(solution)/shard_map/ppermute | solution.py:236
  140.9 20.8 %all-to-all-start = ((bf16[8,256,128]{2,1,0:T(8,128)(2,1)}), bf16[8,256,128]{2,1,0:T(8,128)(2,1)S(1)}, u32[]{:S(2)}, u32[]{:S(2)}) async-start(bf16[8,256,128]{2,1,0:T(8,128)(2,1)} %add.65), calls=%async_computation | async-start | bytes 1048576 | tf_op jit(solution)/shard_map/all_to_all | solution.py:306
  163.9 7.7 %collective-permute-start.28 = (f32[40,128]{1,0:T(8,128)S(1)}, f32[40,128]{1,0:T(8,128)S(1)}, u32[]{:S(2)}, u32[]{:S(2)}) collective-permute-start(f32[40,128]{1,0:T(8,128)S(1)} %add.38), channel_id=1, source_target_pairs={{0,6},{2,0},{4,2},{6,4},{1,7},{3,1},{5,3},{7,5},{8,14},{10,8},{12,... | collective-permute-start | bytes 61448 | tf_op jit(solution)/shard_map/ppermute | solution.py:232
  181.5 7.8 %collective-permute-start.32 = (f32[40,128]{1,0:T(8,128)S(1)}, f32[40,128]{1,0:T(8,128)S(1)}, u32[]{:S(2)}, u32[]{:S(2)}) collective-permute-start(f32[40,128]{1,0:T(8,128)S(1)} %add_add_fusion.1), channel_id=1, source_target_pairs={{0,128},{32,160},{64,192},{96,224},{128,0},{160,32},{192,64},{224,... | collective-permute-start | bytes 61448 | tf_op jit(solution)/shard_map/ppermute | solution.py:323
  189.4 6.9 %collective-permute-start.35 = (f32[40,128]{1,0:T(8,128)S(1)}, f32[40,128]{1,0:T(8,128)S(1)}, u32[]{:S(2)}, u32[]{:S(2)}) collective-permute-start(f32[40,128]{1,0:T(8,128)S(1)} %add.45), channel_id=1, source_target_pairs={{0,96},{32,128},{64,160},{96,192},{128,224},{160,0},{192,32},{224,... | collective-permute-start | bytes 61448 | tf_op jit(solution)/shard_map/ppermute | solution.py:232
  189.4 6.9 %collective-permute-start.34 = (f32[40,128]{1,0:T(8,128)S(1)}, f32[40,128]{1,0:T(8,128)S(1)}, u32[]{:S(2)}, u32[]{:S(2)}) collective-permute-start(f32[40,128]{1,0:T(8,128)S(1)} %add.45), channel_id=1, source_target_pairs={{0,64},{32,96},{64,128},{96,160},{128,192},{160,224},{192,0},{224,... | collective-permute-start | bytes 61448 | tf_op jit(solution)/shard_map/ppermute | solution.py:232
  (19 other events, 195.5 us)

commit v6 on v5

--- a/solution.py
+++ b/solution.py
@@ -92,6 +92,11 @@
         )
 
 
+def z_slot(distance):
+    low, high = distance & 3, distance >> 2
+    return (low << 1) + (high ^ (low & (low >> 1)))
+
+
 def part_kernel(part, place_ref, count_ref, bins_ref, near_ref, px, py, col_ref, *refs):
     if part == 0:
         row_acc, *col_out, qx, qy, col_acc = refs
@@ -121,7 +126,8 @@
             a, b = both & 255, both >> 8
             keep = jnp.where(e < live, 1.0, 0.0).astype(bf16)
             near_slot = ((y_own - (a >> 4)) & 3) + ((((a >> 3) & 1) ^ core_own) << 2)
-            far_slot = (((x_own - (b >> 3)) & 3) << 3) + ((z_own - (b >> 5)) & 7)
+            z_far = (z_own - (b >> 5)) & 7
+            far_slot = (((x_own - (b >> 3)) & 3) << 3) + z_slot(z_far)
             near = near_ref[near_slot, pl.ds(pl.multiple_of((a & 7) * 32, 32), 32), :] * keep
             far = col_ref[far_slot, pl.ds(pl.multiple_of((b & 7) * 32, 32), 32), :] * keep
             a = (near_slot << 3) + (a & 7)
@@ -152,7 +158,7 @@
     def finish(z, carry):
         for k in range(4):
             for t in range(number):
-                total = KERNEL_SCALE * col_acc[k * 64 + z * 8 + first + t]
+                total = KERNEL_SCALE * col_acc[k * 64 + z_slot(z) * 8 + first + t]
                 col_out[k][(z_own - z) & 7, t * 32 : (t + 1) * 32, :] = total.astype(bf16)
         return carry
 
@@ -242,12 +248,21 @@
     packed = pl.pallas_call(
         pack_kernel, out_shape=shape((272, TILE), bf16), in_specs=[VMEM] * 2, out_specs=VMEM, compiler_params=SMALL, name="pack"
     )(direction, positions)
-    z_all = jnp.stack([packed] + shifts(packed, "z", 8))
-    up, down = [(i, (i + 1) % 4) for i in range(4)], [(i, (i - 1) % 4) for i in range(4)]
-    x_below, x_above = lax.ppermute(z_all, "x", up), lax.ppermute(z_all, "x", down)
-    x_far = [lax.ppermute(x_below[:4], "x", up), lax.ppermute(x_above[4:], "x", down)]
-    col_all = jnp.concatenate([z_all, x_below, *x_far, x_above], 0)
-    chip = jnp.stack([packed, swap(packed)])
+    def moved(value, axis, size, shift):
+        return lax.ppermute(value, axis, [(i, (i + shift) % size) for i in range(size)])
+
+    other = swap(packed)
+    pair = jnp.stack([packed, moved(packed, "z", 8, 4)])
+    one, two, back = [moved(pair, "z", 8, shift) for shift in (1, 2, -1)]
+    pair_below, pair_above = moved(pair, "x", 4, 1), moved(pair, "x", 4, -1)
+    rest = jnp.concatenate([one, two, back], 0)
+    rest_below, rest_above = moved(rest, "x", 4, 1), moved(rest, "x", 4, -1)
+    far_below = moved(jnp.concatenate([pair_below[:1], rest_below[:3]], 0), "x", 4, 1)
+    far_above = moved(jnp.concatenate([pair_above[1:], rest_above[3:]], 0), "x", 4, -1)
+    col_all = jnp.concatenate(
+        [pair, rest, pair_below, rest_below, far_below[:1], far_above[:1], far_below[1:], far_above[1:], pair_above, rest_above], 0
+    )
+    chip, pair_below = lax.optimization_barrier((jnp.stack([packed, other]), pair_below))
     around = shifts(chip, "y", 4)
     row_all = jnp.concatenate([v[:1] for v in [chip] + around] + [v[1:] for v in [chip] + around], 0)
     place = jnp.stack([lax.axis_index(name) for name in ("x", "y", "z", "core")]).astype(jnp.int32)
@@ -258,7 +273,7 @@
         out_specs=(SMEM, SMEM),
         compiler_params=SMALL,
         name="bins",
-    )(pair_count, tile_pairs, x_above[0, :16])
+    )(pair_count, tile_pairs, rest_above[0, :16])
     spread_shape = shape((64, TILE, TILE), f32)
     px, py, own_product = pl.pallas_call(
         row_kernel,

time: 203 us -> 190 us (0.936)
  waiting for transfers between devices: 60.5 us -> 49.5 us
    ppermute x19 -> x12, waiting for transfers between devices: 31.1 us -> 12 us  [shifts(): lax.ppermute(value, axis, [(i, (i + k) % size) for i in range(size)])]
    ppermute x19 -> x12, starting transfers between devices: 31.3 us -> 14.7 us  [shifts(): lax.ppermute(value, axis, [(i, (i + k) % size) for i in range(size)])]
    ppermute x4 -> x10, starting transfers between devices: 6.7 us -> 21.8 us  [moved(): lax.ppermute(value, axis, [(i, (i + shift) % size) for i in range(size)])]
    ppermute x4 -> x10, waiting for transfers between devices: 5.98 us -> 13.7 us  [moved(): lax.ppermute(value, axis, [(i, (i + shift) % size) for i in range(size)])]
  transfers between devices with their start and end apart: 37 -> 36, of which waited for: 21 -> 20; matrix products, arithmetic and copies ran while one was open for 0% -> 0% of each run, Pallas kernels for 6% -> 6%
where the time goes in v6:
time: 190 us
  starting transfers between devices  110 us (58%)
  waiting for transfers between devices  49.5 us (26%)
  Pallas kernels  25.7 us (14%)
  local copies, waits for them, and re-layouts  2.21 us (1%)
    ppermute x6, starting transfers between devices, sent(): lax.ppermute(col_out[k], 'x', [(i, (i - k) % 4) for i in range(4)])  59.7 us
    ppermute x10, starting transfers between devices, moved(): lax.ppermute(value, axis, [(i, (i + shift) % size) for i in range(size)])  21.8 us
    ppermute x12, starting transfers between devices, shifts(): lax.ppermute(value, axis, [(i, (i + k) % size) for i in range(size)])  14.7 us
    ppermute x10, waiting for transfers between devices, moved(): lax.ppermute(value, axis, [(i, (i + shift) % size) for i in range(size)])  13.7 us
    ppermute x12, waiting for transfers between devices, shifts(): lax.ppermute(value, axis, [(i, (i + k) % size) for i in range(size)])  12 us
    pallas_call x1, Pallas kernels, on_device(): pl.pallas_call(functools.partial(part_kernel, 0), out_shape=(acc,) + bloc...  8.75 us
    all_to_all x1, starting transfers between devices, on_device(): col_parts = lax.all_to_all(sums, 'z', 0, 0)  8.47 us
    ppermute x1, waiting for transfers between devices, on_device(): gram = gram + lax.ppermute(gram, 'z', [(i, (i + 4) % 8) for i in range(8)])  7.28 us
  transfers between devices with their start and end apart: 36, of which 20 were waited for; matrix products, arithmetic and copies ran while one was open for 0% of the time, Pallas kernels for 6%

profile of v6, /device:TPU:16, one launch (start us, length us, event | category | flops | bytes accessed | tf_op | source)
XLA Modules:
  0.0 189.5 jit_solution(6431475509943951868)
XLA Ops:
  2.2 7.3 %collective-permute-start.1 = (bf16[272,128]{1,0:T(8,128)(2,1)S(1)}, bf16[272,128]{1,0:T(8,128)(2,1)S(1)}, u32[]{:S(2)}, u32[]{:S(2)}) collective-permute-start(bf16[272,128]{1,0:T(8,128)(2,1)S(1)} %pack.1.own_ref), channel_id=1, source_target_pairs={{0,128},{32,160},{64,192},{96,224},{128,0},{160,32},{192,64},{224,... | collective-permute-start | bytes 208904 | tf_op jit(solution)/shard_map/ppermute | solution.py:252
  12.2 2.8 %collective-permute-start.12 = (bf16[2,272,128]{2,1,0:T(8,128)(2,1)S(1)}, bf16[2,272,128]{2,1,0:T(8,128)(2,1)S(1)}, u32[]{:S(2)}, u32[]{:S(2)}) collective-permute-start(bf16[2,272,128]{2,1,0:T(8,128)(2,1)S(1)} %get-tuple-element.49), channel_id=1, source_target_pairs={{0,24},{8,0},{16,8},{24,16},{1,25},{9,1},{17,9},{25,17},{2,26},{10... | collective-permute-start | bytes 417800 | tf_op jit(solution)/shard_map/ppermute | solution.py:252
  15.0 4.4 %collective-permute-start.8 = (bf16[2,272,128]{2,1,0:T(8,128)(2,1)S(1)}, bf16[2,272,128]{2,1,0:T(8,128)(2,1)S(1)}, u32[]{:S(2)}, u32[]{:S(2)}) collective-permute-start(bf16[2,272,128]{2,1,0:T(8,128)(2,1)S(1)} %get-tuple-element.49), channel_id=1, source_target_pairs={{0,224},{32,0},{64,32},{96,64},{128,96},{160,128},{192,160},{224,1... | collective-permute-start | bytes 417800 | tf_op jit(solution)/shard_map/ppermute | solution.py:252
  19.9 6.2 %collective-permute-done.2 = bf16[2,272,128]{2,1,0:T(8,128)(2,1)S(1)} collective-permute-done((bf16[2,272,128]{2,1,0:T(8,128)(2,1)S(1)}, bf16[2,272,128]{2,1,0:T(8,128)(2,1)S(1)}, u32[]{:S(2)}, u32[]{:S(2)}) %collective-permute-start.2) | collective-permute-done | bytes 139296 | tf_op jit(solution)/shard_map/ppermute | solution.py:252
  26.6 2.5 %collective-permute-done.6 = bf16[2,272,128]{2,1,0:T(8,128)(2,1)S(1)} collective-permute-done((bf16[2,272,128]{2,1,0:T(8,128)(2,1)S(1)}, bf16[2,272,128]{2,1,0:T(8,128)(2,1)S(1)}, u32[]{:S(2)}, u32[]{:S(2)}) %collective-permute-start.6) | collective-permute-done | bytes 139296 | tf_op jit(solution)/shard_map/ppermute | solution.py:252
  32.1 3.3 %collective-permute-start.9 = (bf16[6,272,128]{2,1,0:T(8,128)(2,1)S(1)}, bf16[6,272,128]{2,1,0:T(8,128)(2,1)S(1)}, u32[]{:S(2)}, u32[]{:S(2)}) collective-permute-start(bf16[6,272,128]{2,1,0:T(8,128)(2,1)S(1)} %get-tuple-element.44), channel_id=1, source_target_pairs={{0,24},{8,0},{16,8},{24,16},{1,25},{9,1},{17,9},{25,17},{2,26},{10... | collective-permute-start | bytes 1253384 | tf_op jit(solution)/shard_map/ppermute | solution.py:252
  36.7 3.2 %rows.1 = (f32[64,128,128]{2,1,0:T(8,128)S(1)}, f32[64,128,128]{2,1,0:T(8,128)S(1)}, f32[32,1024]{1,0:T(8,128)S(1)}) custom-call(bf16[272,128]{1,0:T(8,128)(2,1)S(1)} %pack.1.own_ref, bf16[8,272,128]{2,1,0:T(8,128)(2,1)S(1)} %slice_dynamic-update-slice_fusion.4.near_ref), custom_call_target="tpu_custom_call" | custom-call | tf_op jit(solution)/shard_map/rows/pallas_call | solution.py:278
  41.9 3.3 %collective-permute-start.13 = (bf16[4,272,128]{2,1,0:T(8,128)(2,1)S(1)}, bf16[4,272,128]{2,1,0:T(8,128)(2,1)S(1)}, u32[]{:S(2)}, u32[]{:S(2)}) collective-permute-start(bf16[4,272,128]{2,1,0:T(8,128)(2,1)S(1)} %pad_maximum_fusion.1), channel_id=1, source_target_pairs={{0,24},{8,0},{16,8},{24,16},{1,25},{9,1},{17,9},{25,17},{2,26},{10... | collective-permute-start | bytes 835592 | tf_op jit(solution)/shard_map/ppermute | solution.py:252
  45.3 3.0 %bins.1 = (s32[1600]{0:T(1024)S(1)}, s32[2]{0:T(128)S(1)}) custom-call(s32[1]{0:T(128)S(6)} %copy.30.live_ref, s32[2,1536]{1,0:T(2,128)S(1)} %copy-done.4, bf16[16,128]{1,0:T(8,128)(2,1)S(1)} %slice_bitcast_fusion.3.after_ref), custom_call_target="tpu_custom_call" | custom-call | tf_op jit(solution)/shard_map/bins/pallas_call | solution.py:269
  49.8 8.7 %pairs_first.1 = (f32[64,32,128]{2,1,0:T(8,128)S(1)}, bf16[8,192,128]{2,1,0:T(8,128)(2,1)S(1)}, bf16[8,192,128]{2,1,0:T(8,128)(2,1)S(1)}, bf16[8,192,128]{2,1,0:T(8,128)(2,1)S(1)}, bf16[8,192,128]{2,1,0:T(8,128)(2,1)S(1)}) custom-call(s32[4]{0:T(128)S(1)} %pad_add_fusion.place_ref, s32[2]{0:T(128)S(1)} %get-tuple-element.23.count_ref, ...), custom_call_target="tpu_custom_call" | custom-call | tf_op jit(solution)/shard_map/pairs_first/pallas_call | solution.py:295
  58.6 3.0 %collective-permute-start.18 = (bf16[8,192,128]{2,1,0:T(8,128)(2,1)S(1)}, bf16[8,192,128]{2,1,0:T(8,128)(2,1)S(1)}, u32[]{:S(2)}, u32[]{:S(2)}) collective-permute-start(bf16[8,192,128]{2,1,0:T(8,128)(2,1)S(1)} %get-tuple-element.30), channel_id=1, source_target_pairs={{0,24},{8,0},{16,8},{24,16},{1,25},{9,1},{17,9},{25,17},{2,26},{10... | collective-permute-start | bytes 1179656 | tf_op jit(solution)/shard_map/ppermute | solution.py:293
  61.6 39.3 %collective-permute-start.19 = (bf16[8,192,128]{2,1,0:T(8,128)(2,1)S(1)}, bf16[8,192,128]{2,1,0:T(8,128)(2,1)S(1)}, u32[]{:S(2)}, u32[]{:S(2)}) collective-permute-start(bf16[8,192,128]{2,1,0:T(8,128)(2,1)S(1)} %get-tuple-element.31), channel_id=1, source_target_pairs={{0,16},{8,24},{16,0},{24,8},{1,17},{9,25},{17,1},{25,9},{2,18},{10... | collective-permute-start | bytes 1179656 | tf_op jit(solution)/shard_map/ppermute | solution.py:293
  102.1 4.1 %pairs_second.1 = (bf16[8,256,128]{2,1,0:T(8,128)(2,1)S(1)}, bf16[8,64,128]{2,1,0:T(8,128)(2,1)S(1)}, bf16[8,64,128]{2,1,0:T(8,128)(2,1)S(1)}, bf16[8,64,128]{2,1,0:T(8,128)(2,1)S(1)}, bf16[8,64,128]{2,1,0:T(8,128)(2,1)S(1)}) custom-call(s32[4]{0:T(128)S(1)} %pad_add_fusion.place_ref, s32[2]{0:T(128)S(1)} %get-tuple-element.23.count_ref, ...), custom_call_target="tpu_custom_call" | custom-call | tf_op jit(solution)/shard_map/pairs_second/pallas_call | solution.py:304
  108.4 12.0 %collective-permute-start.22 = (bf16[8,64,128]{2,1,0:T(8,128)(2,1)S(1)}, bf16[8,64,128]{2,1,0:T(8,128)(2,1)S(1)}, u32[]{:S(2)}, u32[]{:S(2)}) collective-permute-start(bf16[8,64,128]{2,1,0:T(8,128)(2,1)S(1)} %get-tuple-element.35), channel_id=1, source_target_pairs={{0,16},{8,24},{16,0},{24,8},{1,17},{9,25},{17,1},{25,9},{2,18},{10... | collective-permute-start | bytes 393224 | tf_op jit(solution)/shard_map/ppermute | solution.py:293
  124.5 2.9 %collective-permute-done.23.c1 = bf16[8,64,128]{2,1,0:T(8,128)(2,1)S(1)} collective-permute-done((bf16[8,64,128]{2,1,0:T(8,128)(2,1)S(1)}, bf16[8,64,128]{2,1,0:T(8,128)(2,1)S(1)}, u32[]{:S(2)}, u32[]{:S(2)}) %collective-permute-start.23) | collective-permute-done | bytes 131104 | tf_op jit(solution)/shard_map/ppermute | solution.py:293
  128.5 8.5 %all-to-all-start = ((bf16[8,256,128]{2,1,0:T(8,128)(2,1)}), bf16[8,256,128]{2,1,0:T(8,128)(2,1)S(1)}, u32[]{:S(2)}, u32[]{:S(2)}) async-start(bf16[8,256,128]{2,1,0:T(8,128)(2,1)} %add.65), calls=%async_computation | async-start | bytes 1048576 | tf_op jit(solution)/shard_map/all_to_all | solution.py:321
  138.5 3.5 %collective-permute-start.16 = (bf16[256,128]{1,0:T(8,128)(2,1)S(1)}, bf16[256,128]{1,0:T(8,128)(2,1)S(1)}, u32[]{:S(2)}, u32[]{:S(2)}) collective-permute-start(bf16[256,128]{1,0:T(8,128)(2,1)S(1)} %get-tuple-element.41), channel_id=1, source_target_pairs={{0,4},{2,6},{4,0},{6,2},{1,5},{3,7},{5,1},{7,3},{8,12},{10,14},{12... | collective-permute-start | bytes 196616 | tf_op jit(solution)/shard_map/ppermute | solution.py:324
  146.2 6.1 %all-to-all-done.col_ref = bf16[8,256,128]{2,1,0:T(8,128)(2,1)S(1)} async-done(((bf16[8,256,128]{2,1,0:T(8,128)(2,1)}), bf16[8,256,128]{2,1,0:T(8,128)(2,1)S(1)}, u32[]{:S(2)}, u32[]{:S(2)}) %all-to-all-start) | async-done | bytes 524320 | tf_op jit(solution)/shard_map/all_to_all | solution.py:321
  158.6 3.1 %collective-permute-done.26 = f32[40,128]{1,0:T(8,128)S(1)} collective-permute-done((f32[40,128]{1,0:T(8,128)S(1)}, f32[40,128]{1,0:T(8,128)S(1)}, u32[]{:S(2)}, u32[]{:S(2)}) %collective-permute-start.26) | collective-permute-done | bytes 20512 | tf_op jit(solution)/shard_map/ppermute | solution.py:238
  161.7 2.3 %collective-permute-start.30 = (f32[40,128]{1,0:T(8,128)S(1)}, f32[40,128]{1,0:T(8,128)S(1)}, u32[]{:S(2)}, u32[]{:S(2)}) collective-permute-start(f32[40,128]{1,0:T(8,128)S(1)} %add_add_fusion.2), channel_id=1, source_target_pairs={{0,24},{8,0},{16,8},{24,16},{1,25},{9,1},{17,9},{25,17},{2,26},{10... | collective-permute-start | bytes 61448 | tf_op jit(solution)/shard_map/ppermute | solution.py:238
  165.9 3.4 %collective-permute-done.29 = f32[40,128]{1,0:T(8,128)S(1)} collective-permute-done((f32[40,128]{1,0:T(8,128)S(1)}, f32[40,128]{1,0:T(8,128)S(1)}, u32[]{:S(2)}, u32[]{:S(2)}) %collective-permute-start.29) | collective-permute-done | bytes 20512 | tf_op jit(solution)/shard_map/ppermute | solution.py:238
  170.5 7.3 %collective-permute-done.31 = f32[40,128]{1,0:T(8,128)S(1)} collective-permute-done((f32[40,128]{1,0:T(8,128)S(1)}, f32[40,128]{1,0:T(8,128)S(1)}, u32[]{:S(2)}, u32[]{:S(2)}) %collective-permute-start.31) | collective-permute-done | bytes 20512 | tf_op jit(solution)/shard_map/ppermute | solution.py:338
  181.1 3.5 %collective-permute-done.34 = f32[40,128]{1,0:T(8,128)S(1)} collective-permute-done((f32[40,128]{1,0:T(8,128)S(1)}, f32[40,128]{1,0:T(8,128)S(1)}, u32[]{:S(2)}, u32[]{:S(2)}) %collective-permute-start.34) | collective-permute-done | bytes 20512 | tf_op jit(solution)/shard_map/ppermute | solution.py:238
  184.9 4.7 %solve.1 = (f32[32,1024]{1,0:T(8,128)}, f32[32,1024]{1,0:T(8,128)}, f32[32,1024]{1,0:T(8,128)}) custom-call(f32[40,128]{1,0:T(8,128)S(1)} %add_add_fusion.gram_ref, f32[32,1024]{1,0:T(8,128)S(1)} %copy-done.3, f32[32,1024]{1,0:T(8,128)S(1)} %copy-done.2, f32[32,1024]{1,0:T(8,128)S(1)} %copy-done.1, f32[32,1024]{1,0:T(8,128)S(1)} %get-tuple-element.38.image_ref), custom_call_target="tpu_custom_call" | custom-call | tf_op jit(solution)/shard_map/solve/pallas_call | solution.py:340
  (107 shorter events, 39.3 us)
Async XLA Ops:
  2.2 9.9 %collective-permute-start.1 = (bf16[272,128]{1,0:T(8,128)(2,1)S(1)}, bf16[272,128]{1,0:T(8,128)(2,1)S(1)}, u32[]{:S(2)}, u32[]{:S(2)}) collective-permute-start(bf16[272,128]{1,0:T(8,128)(2,1)S(1)} %pack.1.own_ref), channel_id=1, source_target_pairs={{0,128},{32,160},{64,192},{96,224},{128,0},{160,32},{192,64},{224,... | collective-permute-start | bytes 208904 | tf_op jit(solution)/shard_map/ppermute | solution.py:252
  12.2 19.9 %collective-permute-start.12 = (bf16[2,272,128]{2,1,0:T(8,128)(2,1)S(1)}, bf16[2,272,128]{2,1,0:T(8,128)(2,1)S(1)}, u32[]{:S(2)}, u32[]{:S(2)}) collective-permute-start(bf16[2,272,128]{2,1,0:T(8,128)(2,1)S(1)} %get-tuple-element.49), channel_id=1, source_target_pairs={{0,24},{8,0},{16,8},{24,16},{1,25},{9,1},{17,9},{25,17},{2,26},{10... | collective-permute-start | bytes 417800 | tf_op jit(solution)/shard_map/ppermute | solution.py:252
  15.0 16.9 %collective-permute-start.8 = (bf16[2,272,128]{2,1,0:T(8,128)(2,1)S(1)}, bf16[2,272,128]{2,1,0:T(8,128)(2,1)S(1)}, u32[]{:S(2)}, u32[]{:S(2)}) collective-permute-start(bf16[2,272,128]{2,1,0:T(8,128)(2,1)S(1)} %get-tuple-element.49), channel_id=1, source_target_pairs={{0,224},{32,0},{64,32},{96,64},{128,96},{160,128},{192,160},{224,1... | collective-permute-start | bytes 417800 | tf_op jit(solution)/shard_map/ppermute | solution.py:252
  19.4 10.3 %collective-permute-start.7 = (bf16[2,272,128]{2,1,0:T(8,128)(2,1)S(1)}, bf16[2,272,128]{2,1,0:T(8,128)(2,1)S(1)}, u32[]{:S(2)}, u32[]{:S(2)}) collective-permute-start(bf16[2,272,128]{2,1,0:T(8,128)(2,1)S(1)} %get-tuple-element.49), channel_id=1, source_target_pairs={{0,64},{32,96},{64,128},{96,160},{128,192},{160,224},{192,0},{224,... | collective-permute-start | bytes 417800 | tf_op jit(solution)/shard_map/ppermute | solution.py:252
  19.4 9.8 %collective-permute-start.6 = (bf16[2,272,128]{2,1,0:T(8,128)(2,1)S(1)}, bf16[2,272,128]{2,1,0:T(8,128)(2,1)S(1)}, u32[]{:S(2)}, u32[]{:S(2)}) collective-permute-start(bf16[2,272,128]{2,1,0:T(8,128)(2,1)S(1)} %get-tuple-element.49), channel_id=1, source_target_pairs={{0,32},{32,64},{64,96},{96,128},{128,160},{160,192},{192,224},{224... | collective-permute-start | bytes 417800 | tf_op jit(solution)/shard_map/ppermute | solution.py:252
  19.9 6.3 %collective-permute-start.2 = (bf16[2,272,128]{2,1,0:T(8,128)(2,1)S(1)}, bf16[2,272,128]{2,1,0:T(8,128)(2,1)S(1)}, u32[]{:S(2)}, u32[]{:S(2)}) collective-permute-start(bf16[2,272,128]{2,1,0:T(8,128)(2,1)S(1)} %get-tuple-element.49), channel_id=1, source_target_pairs={{0,8},{8,16},{16,24},{24,0},{1,9},{9,17},{17,25},{25,1},{2,10},{10... | collective-permute-start | bytes 417800 | tf_op jit(solution)/shard_map/ppermute | solution.py:252
  26.2 10.4 %collective-permute-start.5 = (bf16[2,272,128]{2,1,0:T(8,128)(2,1)S(1)}, bf16[2,272,128]{2,1,0:T(8,128)(2,1)S(1)}, u32[]{:S(2)}, u32[]{:S(2)}) collective-permute-start(bf16[2,272,128]{2,1,0:T(8,128)(2,1)S(1)} %get-tuple-element.21), channel_id=1, source_target_pairs={{0,6},{2,0},{4,2},{6,4},{1,7},{3,1},{5,3},{7,5},{8,14},{10,8},{12,... | collective-permute-start | bytes 417800 | tf_op jit(solution)/shard_map/ppermute | solution.py:238
  29.2 7.4 %collective-permute-start.4 = (bf16[2,272,128]{2,1,0:T(8,128)(2,1)S(1)}, bf16[2,272,128]{2,1,0:T(8,128)(2,1)S(1)}, u32[]{:S(2)}, u32[]{:S(2)}) collective-permute-start(bf16[2,272,128]{2,1,0:T(8,128)(2,1)S(1)} %get-tuple-element.21), channel_id=1, source_target_pairs={{0,4},{2,6},{4,0},{6,2},{1,5},{3,7},{5,1},{7,3},{8,12},{10,14},{12... | collective-permute-start | bytes 417800 | tf_op jit(solution)/shard_map/ppermute | solution.py:238
  29.7 6.9 %collective-permute-start.3 = (bf16[2,272,128]{2,1,0:T(8,128)(2,1)S(1)}, bf16[2,272,128]{2,1,0:T(8,128)(2,1)S(1)}, u32[]{:S(2)}, u32[]{:S(2)}) collective-permute-start(bf16[2,272,128]{2,1,0:T(8,128)(2,1)S(1)} %get-tuple-element.21), channel_id=1, source_target_pairs={{0,2},{2,4},{4,6},{6,0},{1,3},{3,5},{5,7},{7,1},{8,10},{10,12},{12... | collective-permute-start | bytes 417800 | tf_op jit(solution)/shard_map/ppermute | solution.py:238
  31.9 9.8 %collective-permute-start.10 = (bf16[6,272,128]{2,1,0:T(8,128)(2,1)S(1)}, bf16[6,272,128]{2,1,0:T(8,128)(2,1)S(1)}, u32[]{:S(2)}, u32[]{:S(2)}) collective-permute-start(bf16[6,272,128]{2,1,0:T(8,128)(2,1)S(1)} %get-tuple-element.44), channel_id=1, source_target_pairs={{0,8},{8,16},{16,24},{24,0},{1,9},{9,17},{17,25},{25,1},{2,10},{10... | collective-permute-start | bytes 1253384 | tf_op jit(solution)/shard_map/ppermute | solution.py:252
  32.1 9.8 %collective-permute-start.9 = (bf16[6,272,128]{2,1,0:T(8,128)(2,1)S(1)}, bf16[6,272,128]{2,1,0:T(8,128)(2,1)S(1)}, u32[]{:S(2)}, u32[]{:S(2)}) collective-permute-start(bf16[6,272,128]{2,1,0:T(8,128)(2,1)S(1)} %get-tuple-element.44), channel_id=1, source_target_pairs={{0,24},{8,0},{16,8},{24,16},{1,25},{9,1},{17,9},{25,17},{2,26},{10... | collective-permute-start | bytes 1253384 | tf_op jit(solution)/shard_map/ppermute | solution.py:252
  41.7 7.8 %collective-permute-start.11 = (bf16[4,272,128]{2,1,0:T(8,128)(2,1)S(1)}, bf16[4,272,128]{2,1,0:T(8,128)(2,1)S(1)}, u32[]{:S(2)}, u32[]{:S(2)}) collective-permute-start(bf16[4,272,128]{2,1,0:T(8,128)(2,1)S(1)} %pad_maximum_fusion), channel_id=1, source_target_pairs={{0,8},{8,16},{16,24},{24,0},{1,9},{9,17},{17,25},{25,1},{2,10},{10... | collective-permute-start | bytes 835592 | tf_op jit(solution)/shard_map/ppermute | solution.py:252
  41.9 7.7 %collective-permute-start.13 = (bf16[4,272,128]{2,1,0:T(8,128)(2,1)S(1)}, bf16[4,272,128]{2,1,0:T(8,128)(2,1)S(1)}, u32[]{:S(2)}, u32[]{:S(2)}) collective-permute-start(bf16[4,272,128]{2,1,0:T(8,128)(2,1)S(1)} %pad_maximum_fusion.1), channel_id=1, source_target_pairs={{0,24},{8,0},{16,8},{24,16},{1,25},{9,1},{17,9},{25,17},{2,26},{10... | collective-permute-start | bytes 835592 | tf_op jit(solution)/shard_map/ppermute | solution.py:252
  58.6 68.9 %collective-permute-start.18 = (bf16[8,192,128]{2,1,0:T(8,128)(2,1)S(1)}, bf16[8,192,128]{2,1,0:T(8,128)(2,1)S(1)}, u32[]{:S(2)}, u32[]{:S(2)}) collective-permute-start(bf16[8,192,128]{2,1,0:T(8,128)(2,1)S(1)} %get-tuple-element.30), channel_id=1, source_target_pairs={{0,24},{8,0},{16,8},{24,16},{1,25},{9,1},{17,9},{25,17},{2,26},{10... | collective-permute-start | bytes 1179656 | tf_op jit(solution)/shard_map/ppermute | solution.py:293
  61.6 65.8 %collective-permute-start.19 = (bf16[8,192,128]{2,1,0:T(8,128)(2,1)S(1)}, bf16[8,192,128]{2,1,0:T(8,128)(2,1)S(1)}, u32[]{:S(2)}, u32[]{:S(2)}) collective-permute-start(bf16[8,192,128]{2,1,0:T(8,128)(2,1)S(1)} %get-tuple-element.31), channel_id=1, source_target_pairs={{0,16},{8,24},{16,0},{24,8},{1,17},{9,25},{17,1},{25,9},{2,18},{10... | collective-permute-start | bytes 1179656 | tf_op jit(solution)/shard_map/ppermute | solution.py:293
  100.9 26.6 %collective-permute-start.20 = (bf16[8,192,128]{2,1,0:T(8,128)(2,1)S(1)}, bf16[8,192,128]{2,1,0:T(8,128)(2,1)S(1)}, u32[]{:S(2)}, u32[]{:S(2)}) collective-permute-start(bf16[8,192,128]{2,1,0:T(8,128)(2,1)S(1)} %get-tuple-element.32), channel_id=1, source_target_pairs={{0,8},{8,16},{16,24},{24,0},{1,9},{9,17},{17,25},{25,1},{2,10},{10... | collective-permute-start | bytes 1179656 | tf_op jit(solution)/shard_map/ppermute | solution.py:293
  106.3 15.0 %collective-permute-start.21 = (bf16[8,64,128]{2,1,0:T(8,128)(2,1)S(1)}, bf16[8,64,128]{2,1,0:T(8,128)(2,1)S(1)}, u32[]{:S(2)}, u32[]{:S(2)}) collective-permute-start(bf16[8,64,128]{2,1,0:T(8,128)(2,1)S(1)} %get-tuple-element.34), channel_id=1, source_target_pairs={{0,24},{8,0},{16,8},{24,16},{1,25},{9,1},{17,9},{25,17},{2,26},{10... | collective-permute-start | bytes 393224 | tf_op jit(solution)/shard_map/ppermute | solution.py:293
  108.4 16.2 %collective-permute-start.22 = (bf16[8,64,128]{2,1,0:T(8,128)(2,1)S(1)}, bf16[8,64,128]{2,1,0:T(8,128)(2,1)S(1)}, u32[]{:S(2)}, u32[]{:S(2)}) collective-permute-start(bf16[8,64,128]{2,1,0:T(8,128)(2,1)S(1)} %get-tuple-element.35), channel_id=1, source_target_pairs={{0,16},{8,24},{16,0},{24,8},{1,17},{9,25},{17,1},{25,9},{2,18},{10... | collective-permute-start | bytes 393224 | tf_op jit(solution)/shard_map/ppermute | solution.py:293
  124.5 12.5 %collective-permute-start.14 = (bf16[4,256,128]{2,1,0:T(8,128)(2,1)S(1)}, bf16[4,256,128]{2,1,0:T(8,128)(2,1)S(1)}, u32[]{:S(2)}, u32[]{:S(2)}) collective-permute-start(bf16[4,256,128]{2,1,0:T(8,128)(2,1)S(1)} %slice.87), channel_id=1, source_target_pairs={{0,1},{1,0},{2,3},{3,2},{4,5},{5,4},{6,7},{7,6},{8,9},{9,8},{10,11... | collective-permute-start | bytes 786440 | tf_op jit(solution)/shard_map/ppermute | solution.py:242
  128.5 23.8 %all-to-all-start = ((bf16[8,256,128]{2,1,0:T(8,128)(2,1)}), bf16[8,256,128]{2,1,0:T(8,128)(2,1)S(1)}, u32[]{:S(2)}, u32[]{:S(2)}) async-start(bf16[8,256,128]{2,1,0:T(8,128)(2,1)} %add.65), calls=%async_computation | async-start | bytes 1048576 | tf_op jit(solution)/shard_map/all_to_all | solution.py:321
  138.5 6.4 %collective-permute-start.16 = (bf16[256,128]{1,0:T(8,128)(2,1)S(1)}, bf16[256,128]{1,0:T(8,128)(2,1)S(1)}, u32[]{:S(2)}, u32[]{:S(2)}) collective-permute-start(bf16[256,128]{1,0:T(8,128)(2,1)S(1)} %get-tuple-element.41), channel_id=1, source_target_pairs={{0,4},{2,6},{4,0},{6,2},{1,5},{3,7},{5,1},{7,3},{8,12},{10,14},{12... | collective-permute-start | bytes 196616 | tf_op jit(solution)/shard_map/ppermute | solution.py:324
  169.9 7.9 %collective-permute-start.31 = (f32[40,128]{1,0:T(8,128)S(1)}, f32[40,128]{1,0:T(8,128)S(1)}, u32[]{:S(2)}, u32[]{:S(2)}) collective-permute-start(f32[40,128]{1,0:T(8,128)S(1)} %add_add_fusion.1), channel_id=1, source_target_pairs={{0,128},{32,160},{64,192},{96,224},{128,0},{160,32},{192,64},{224,... | collective-permute-start | bytes 61448 | tf_op jit(solution)/shard_map/ppermute | solution.py:338
  177.8 6.8 %collective-permute-start.34 = (f32[40,128]{1,0:T(8,128)S(1)}, f32[40,128]{1,0:T(8,128)S(1)}, u32[]{:S(2)}, u32[]{:S(2)}) collective-permute-start(f32[40,128]{1,0:T(8,128)S(1)} %add.45), channel_id=1, source_target_pairs={{0,96},{32,128},{64,160},{96,192},{128,224},{160,0},{192,32},{224,... | collective-permute-start | bytes 61448 | tf_op jit(solution)/shard_map/ppermute | solution.py:238
  177.8 6.8 %collective-permute-start.33 = (f32[40,128]{1,0:T(8,128)S(1)}, f32[40,128]{1,0:T(8,128)S(1)}, u32[]{:S(2)}, u32[]{:S(2)}) collective-permute-start(f32[40,128]{1,0:T(8,128)S(1)} %add.45), channel_id=1, source_target_pairs={{0,64},{32,96},{64,128},{96,160},{128,192},{160,224},{192,0},{224,... | collective-permute-start | bytes 61448 | tf_op jit(solution)/shard_map/ppermute | solution.py:238
  (18 other events, 171.6 us)

commit v7 on v6

--- a/solution.py
+++ b/solution.py
@@ -72,7 +72,7 @@
     return jnp.broadcast_to(strip[:, t : t + 1], (TILE, TILE))
 
 
-def row_kernel(own_ref, near_ref, px, py, own_out):
+def row_kernel(own_ref, near_ref, after_ref, px, py, own_out):
     def row_prepare(r, carry):
         strip = near_ref[r, 256:272, :].astype(f32).T
         for t in range(8):
@@ -118,18 +118,20 @@
 
     lax.fori_loop(0, 32, col_prepare, 0)
 
-    def several(start, size):
+    def several(start, size, masked):
         results = []
         for u in range(size):
             e = start + u
             both = bins_ref[e if part == 0 else BIN - 1 - e]
             a, b = both & 255, both >> 8
-            keep = jnp.where(e < live, 1.0, 0.0).astype(bf16)
             near_slot = ((y_own - (a >> 4)) & 3) + ((((a >> 3) & 1) ^ core_own) << 2)
             z_far = (z_own - (b >> 5)) & 7
             far_slot = (((x_own - (b >> 3)) & 3) << 3) + z_slot(z_far)
-            near = near_ref[near_slot, pl.ds(pl.multiple_of((a & 7) * 32, 32), 32), :] * keep
-            far = col_ref[far_slot, pl.ds(pl.multiple_of((b & 7) * 32, 32), 32), :] * keep
+            near = near_ref[near_slot, pl.ds(pl.multiple_of((a & 7) * 32, 32), 32), :]
+            far = col_ref[far_slot, pl.ds(pl.multiple_of((b & 7) * 32, 32), 32), :]
+            if masked:
+                keep = jnp.where(e < live, 1.0, 0.0).astype(bf16)
+                near, far = near * keep, far * keep
             a = (near_slot << 3) + (a & 7)
             b = (far_slot << 3) + (b & 7)
             dx = px[a].reshape(16, 8, TILE) - qx[b][None]
@@ -145,11 +147,11 @@
     whole = live // UNROLL
 
     def body(i, carry):
-        several(i * UNROLL, UNROLL)
+        several(i * UNROLL, UNROLL, False)
         return carry
 
     def tail(i, carry):
-        several(whole * UNROLL + i * TAIL, TAIL)
+        several(whole * UNROLL + i * TAIL, TAIL, True)
         return carry
 
     lax.fori_loop(0, whole, body, 0)
@@ -251,20 +253,19 @@
     def moved(value, axis, size, shift):
         return lax.ppermute(value, axis, [(i, (i + shift) % size) for i in range(size)])
 
-    other = swap(packed)
+    row_half = jnp.stack([packed] + shifts(packed, "y", 4))
     pair = jnp.stack([packed, moved(packed, "z", 8, 4)])
     one, two, back = [moved(pair, "z", 8, shift) for shift in (1, 2, -1)]
     pair_below, pair_above = moved(pair, "x", 4, 1), moved(pair, "x", 4, -1)
     rest = jnp.concatenate([one, two, back], 0)
+    row_half, rest = lax.optimization_barrier((row_half, rest))
     rest_below, rest_above = moved(rest, "x", 4, 1), moved(rest, "x", 4, -1)
     far_below = moved(jnp.concatenate([pair_below[:1], rest_below[:3]], 0), "x", 4, 1)
     far_above = moved(jnp.concatenate([pair_above[1:], rest_above[3:]], 0), "x", 4, -1)
     col_all = jnp.concatenate(
         [pair, rest, pair_below, rest_below, far_below[:1], far_above[:1], far_below[1:], far_above[1:], pair_above, rest_above], 0
     )
-    chip, pair_below = lax.optimization_barrier((jnp.stack([packed, other]), pair_below))
-    around = shifts(chip, "y", 4)
-    row_all = jnp.concatenate([v[:1] for v in [chip] + around] + [v[1:] for v in [chip] + around], 0)
+    row_all = jnp.concatenate([row_half, swap(row_half)], 0)
     place = jnp.stack([lax.axis_index(name) for name in ("x", "y", "z", "core")]).astype(jnp.int32)
     bins, counts = pl.pallas_call(
         bin_kernel,
@@ -273,16 +274,16 @@
         out_specs=(SMEM, SMEM),
         compiler_params=SMALL,
         name="bins",
-    )(pair_count, tile_pairs, rest_above[0, :16])
+    )(pair_count, tile_pairs, pair_above[0, :16])
     spread_shape = shape((64, TILE, TILE), f32)
     px, py, own_product = pl.pallas_call(
         row_kernel,
         out_shape=(spread_shape, spread_shape, shape((PROBES, own_points), f32)),
-        in_specs=[VMEM] * 2,
+        in_specs=[VMEM] * 3,
         out_specs=(VMEM,) * 3,
         compiler_params=PARAMS,
         name="rows",
-    )(packed, row_all)
+    )(packed, row_all, rest_above[0, :16])
     acc = shape((64, PROBES, TILE), f32)
     scratch = [pltpu.VMEM((256, 8, TILE), f32), pltpu.VMEM((256, 8, TILE), f32), pltpu.VMEM((256, PROBES, TILE), f32)]
 

time: 190 us -> 184 us (0.968)
  Pallas kernels: 25.7 us -> 77.5 us
  starting transfers between devices: 110 us -> 59.8 us
  waiting for transfers between devices: 49.5 us -> 42.1 us
    ppermute x6, starting transfers between devices: 59.7 us -> 12.4 us  [sent(): lax.ppermute(col_out[k], 'x', [(i, (i - k) % 4) for i in range(4)])]
    pallas_call x1, Pallas kernels: 8.75 us -> 42.8 us  [on_device(): pl.pallas_call(functools.partial(part_kernel, 0), out_shape=(acc,) + bloc...]
    pallas_call x1, Pallas kernels: 4.15 us -> 14 us  [on_device(): pl.pallas_call(functools.partial(part_kernel, 1), out_shape=(shape((8, 25...]
    pallas_call x1, Pallas kernels: 3.01 us -> 10.9 us  [on_device(): pl.pallas_call(bin_kernel, out_shape=(shape((BIN,), jnp.int32), shape((2,...]
    ppermute x10, waiting for transfers between devices: 13.7 us -> 9.92 us  [moved(): lax.ppermute(value, axis, [(i, (i + shift) % size) for i in range(size)])]
    all_to_all x1, starting transfers between devices: 8.47 us -> 5.4 us  [on_device(): col_parts = lax.all_to_all(sums, 'z', 0, 0)]
    ppermute x6, waiting for transfers between devices: 5.02 us -> 2.61 us  [sent(): lax.ppermute(col_out[k], 'x', [(i, (i - k) % 4) for i in range(4)])]
  transfers between devices with their start and end apart: 36 -> 36, of which waited for: 20 -> 16; matrix products, arithmetic and copies ran while one was open for 0% -> 0% of each run, Pallas kernels for 6% -> 16%
where the time goes in v7:
time: 184 us; the launch traced here: 183 us
  Pallas kernels  77.5 us (42%)
  starting transfers between devices  59.8 us (32%)
  waiting for transfers between devices  42.1 us (23%)
  local copies, waits for them, and re-layouts  2.07 us (1%)
    pallas_call x1, Pallas kernels, on_device(): pl.pallas_call(functools.partial(part_kernel, 0), out_shape=(acc,) + bloc...  42.8 us
    ppermute x10, starting transfers between devices, moved(): lax.ppermute(value, axis, [(i, (i + shift) % size) for i in range(size)])  20.9 us
    ppermute x12, starting transfers between devices, shifts(): lax.ppermute(value, axis, [(i, (i + k) % size) for i in range(size)])  15.3 us
    pallas_call x1, Pallas kernels, on_device(): pl.pallas_call(functools.partial(part_kernel, 1), out_shape=(shape((8, 25...  14 us
    ppermute x6, starting transfers between devices, sent(): lax.ppermute(col_out[k], 'x', [(i, (i - k) % 4) for i in range(4)])  12.4 us
    ppermute x12, waiting for transfers between devices, shifts(): lax.ppermute(value, axis, [(i, (i + k) % size) for i in range(size)])  11.4 us
    pallas_call x1, Pallas kernels, on_device(): pl.pallas_call(bin_kernel, out_shape=(shape((BIN,), jnp.int32), shape((2,...  10.9 us
    ppermute x10, waiting for transfers between devices, moved(): lax.ppermute(value, axis, [(i, (i + shift) % size) for i in range(size)])  9.92 us
  transfers between devices with their start and end apart: 36, of which 16 were waited for; matrix products, arithmetic and copies ran while one was open for 0% of the time, Pallas kernels for 16%

profile of v7, /device:TPU:16, one launch (start us, length us, event | category | flops | bytes accessed | tf_op | source)
XLA Modules:
  0.0 183.4 jit_solution(1727708673760453222)
XLA Ops:
  2.2 7.3 %collective-permute-start.3 = (bf16[272,128]{1,0:T(8,128)(2,1)S(1)}, bf16[272,128]{1,0:T(8,128)(2,1)S(1)}, u32[]{:S(2)}, u32[]{:S(2)}) collective-permute-start(bf16[272,128]{1,0:T(8,128)(2,1)S(1)} %pack.1.own_ref), channel_id=1, source_target_pairs={{0,128},{32,160},{64,192},{96,224},{128,0},{160,32},{192,64},{224,... | collective-permute-start | bytes 208904 | tf_op jit(solution)/shard_map/ppermute | solution.py:254
  10.0 2.9 %collective-permute-start.1 = (bf16[272,128]{1,0:T(8,128)(2,1)S(1)}, bf16[272,128]{1,0:T(8,128)(2,1)S(1)}, u32[]{:S(2)}, u32[]{:S(2)}) collective-permute-start(bf16[272,128]{1,0:T(8,128)(2,1)S(1)} %pack.1.own_ref), channel_id=1, source_target_pairs={{0,4},{2,6},{4,0},{6,2},{1,5},{3,7},{5,1},{7,3},{8,12},{10,14},{12... | collective-permute-start | bytes 208904 | tf_op jit(solution)/shard_map/ppermute | solution.py:240
  13.6 3.0 %collective-permute-start.6 = (bf16[2,272,128]{2,1,0:T(8,128)(2,1)S(1)}, bf16[2,272,128]{2,1,0:T(8,128)(2,1)S(1)}, u32[]{:S(2)}, u32[]{:S(2)}) collective-permute-start(bf16[2,272,128]{2,1,0:T(8,128)(2,1)S(1)} %pad_maximum_fusion.5), channel_id=1, source_target_pairs={{0,224},{32,0},{64,32},{96,64},{128,96},{160,128},{192,160},{224,1... | collective-permute-start | bytes 417800 | tf_op jit(solution)/shard_map/ppermute | solution.py:254
  20.6 6.2 %collective-permute-done.5 = bf16[2,272,128]{2,1,0:T(8,128)(2,1)S(1)} collective-permute-done((bf16[2,272,128]{2,1,0:T(8,128)(2,1)S(1)}, bf16[2,272,128]{2,1,0:T(8,128)(2,1)S(1)}, u32[]{:S(2)}, u32[]{:S(2)}) %collective-permute-start.5) | collective-permute-done | bytes 139296 | tf_op jit(solution)/shard_map/ppermute | solution.py:254
  30.3 10.9 %bins.1 = (s32[1600]{0:T(1024)S(1)}, s32[2]{0:T(128)S(1)}) custom-call(s32[1]{0:T(128)S(6)} %copy.20.live_ref, s32[2,1536]{1,0:T(2,128)S(1)} %copy-done.4, bf16[16,128]{1,0:T(8,128)(2,1)S(1)} %slice_bitcast_fusion.3.after_ref), custom_call_target="tpu_custom_call" | custom-call | tf_op jit(solution)/shard_map/bins/pallas_call | solution.py:270
  41.6 3.3 %collective-permute-start.13 = (bf16[4,272,128]{2,1,0:T(8,128)(2,1)S(1)}, bf16[4,272,128]{2,1,0:T(8,128)(2,1)S(1)}, u32[]{:S(2)}, u32[]{:S(2)}) collective-permute-start(bf16[4,272,128]{2,1,0:T(8,128)(2,1)S(1)} %pad_maximum_fusion.3), channel_id=1, source_target_pairs={{0,24},{8,0},{16,8},{24,16},{1,25},{9,1},{17,9},{25,17},{2,26},{10... | collective-permute-start | bytes 835592 | tf_op jit(solution)/shard_map/ppermute | solution.py:254
  44.9 3.2 %rows.1 = (f32[64,128,128]{2,1,0:T(8,128)S(1)}, f32[64,128,128]{2,1,0:T(8,128)S(1)}, f32[32,1024]{1,0:T(8,128)S(1)}) custom-call(bf16[272,128]{1,0:T(8,128)(2,1)S(1)} %pack.1.own_ref, bf16[8,272,128]{2,1,0:T(8,128)(2,1)S(1)} %constant_dynamic-update-slice_fusion.near_ref, bf16[16,128]{1,0:T(8,128)(2,1)S(1)} %slice_bitcast_fusion.4.after_ref), custom_call_target="tpu_custom_call" | custom-call | tf_op jit(solution)/shard_map/rows/pallas_call | solution.py:279
  48.2 3.6 %collective-permute-done.12 = bf16[4,272,128]{2,1,0:T(8,128)(2,1)S(1)} collective-permute-done((bf16[4,272,128]{2,1,0:T(8,128)(2,1)S(1)}, bf16[4,272,128]{2,1,0:T(8,128)(2,1)S(1)}, u32[]{:S(2)}, u32[]{:S(2)}) %collective-permute-start.12) | collective-permute-done | bytes 278560 | tf_op jit(solution)/shard_map/ppermute | solution.py:254
  52.0 42.8 %pairs_first.1 = (f32[64,32,128]{2,1,0:T(8,128)S(1)}, bf16[8,192,128]{2,1,0:T(8,128)(2,1)S(1)}, bf16[8,192,128]{2,1,0:T(8,128)(2,1)S(1)}, bf16[8,192,128]{2,1,0:T(8,128)(2,1)S(1)}, bf16[8,192,128]{2,1,0:T(8,128)(2,1)S(1)}) custom-call(s32[4]{0:T(128)S(1)} %pad_add_fusion.place_ref, s32[2]{0:T(128)S(1)} %get-tuple-element.25.count_ref, ...), custom_call_target="tpu_custom_call" | custom-call | tf_op jit(solution)/shard_map/pairs_first/pallas_call | solution.py:296
  95.0 1.9 %collective-permute-start.20 = (bf16[8,192,128]{2,1,0:T(8,128)(2,1)S(1)}, bf16[8,192,128]{2,1,0:T(8,128)(2,1)S(1)}, u32[]{:S(2)}, u32[]{:S(2)}) collective-permute-start(bf16[8,192,128]{2,1,0:T(8,128)(2,1)S(1)} %get-tuple-element.34), channel_id=1, source_target_pairs={{0,8},{8,16},{16,24},{24,0},{1,9},{9,17},{17,25},{25,1},{2,10},{10... | collective-permute-start | bytes 1179656 | tf_op jit(solution)/shard_map/ppermute | solution.py:294
  96.9 14.0 %pairs_second.1 = (bf16[8,256,128]{2,1,0:T(8,128)(2,1)S(1)}, bf16[8,64,128]{2,1,0:T(8,128)(2,1)S(1)}, bf16[8,64,128]{2,1,0:T(8,128)(2,1)S(1)}, bf16[8,64,128]{2,1,0:T(8,128)(2,1)S(1)}, bf16[8,64,128]{2,1,0:T(8,128)(2,1)S(1)}) custom-call(s32[4]{0:T(128)S(1)} %pad_add_fusion.place_ref, s32[2]{0:T(128)S(1)} %get-tuple-element.25.count_ref, ...), custom_call_target="tpu_custom_call" | custom-call | tf_op jit(solution)/shard_map/pairs_second/pallas_call | solution.py:305
  111.1 6.5 %collective-permute-start.22 = (bf16[8,64,128]{2,1,0:T(8,128)(2,1)S(1)}, bf16[8,64,128]{2,1,0:T(8,128)(2,1)S(1)}, u32[]{:S(2)}, u32[]{:S(2)}) collective-permute-start(bf16[8,64,128]{2,1,0:T(8,128)(2,1)S(1)} %get-tuple-element.37), channel_id=1, source_target_pairs={{0,16},{8,24},{16,0},{24,8},{1,17},{9,25},{17,1},{25,9},{2,18},{10... | collective-permute-start | bytes 393224 | tf_op jit(solution)/shard_map/ppermute | solution.py:294
  117.6 3.7 %collective-permute-start.23 = (bf16[8,64,128]{2,1,0:T(8,128)(2,1)S(1)}, bf16[8,64,128]{2,1,0:T(8,128)(2,1)S(1)}, u32[]{:S(2)}, u32[]{:S(2)}) collective-permute-start(bf16[8,64,128]{2,1,0:T(8,128)(2,1)S(1)} %get-tuple-element.38), channel_id=1, source_target_pairs={{0,8},{8,16},{16,24},{24,0},{1,9},{9,17},{17,25},{25,1},{2,10},{10... | collective-permute-start | bytes 393224 | tf_op jit(solution)/shard_map/ppermute | solution.py:294
  121.4 2.6 %collective-permute-done.23.c1 = bf16[8,64,128]{2,1,0:T(8,128)(2,1)S(1)} collective-permute-done((bf16[8,64,128]{2,1,0:T(8,128)(2,1)S(1)}, bf16[8,64,128]{2,1,0:T(8,128)(2,1)S(1)}, u32[]{:S(2)}, u32[]{:S(2)}) %collective-permute-start.23) | collective-permute-done | bytes 131104 | tf_op jit(solution)/shard_map/ppermute | solution.py:294
  125.1 5.4 %all-to-all-start = ((bf16[8,256,128]{2,1,0:T(8,128)(2,1)}), bf16[8,256,128]{2,1,0:T(8,128)(2,1)S(1)}, u32[]{:S(2)}, u32[]{:S(2)}) async-start(bf16[8,256,128]{2,1,0:T(8,128)(2,1)} %add.65), calls=%async_computation | async-start | bytes 1048576 | tf_op jit(solution)/shard_map/all_to_all | solution.py:322
  130.6 3.4 %collective-permute-start.17 = (bf16[256,128]{1,0:T(8,128)(2,1)S(1)}, bf16[256,128]{1,0:T(8,128)(2,1)S(1)}, u32[]{:S(2)}, u32[]{:S(2)}) collective-permute-start(bf16[256,128]{1,0:T(8,128)(2,1)S(1)} %get-tuple-element.42), channel_id=1, source_target_pairs={{0,2},{2,4},{4,6},{6,0},{1,3},{3,5},{5,7},{7,1},{8,10},{10,12},{12... | collective-permute-start | bytes 196616 | tf_op jit(solution)/shard_map/ppermute | solution.py:325
  136.0 3.9 %collective-permute-done.16 = bf16[256,128]{1,0:T(8,128)(2,1)S(1)} collective-permute-done((bf16[256,128]{1,0:T(8,128)(2,1)S(1)}, bf16[256,128]{1,0:T(8,128)(2,1)S(1)}, u32[]{:S(2)}, u32[]{:S(2)}) %collective-permute-start.16) | collective-permute-done | bytes 65568 | tf_op jit(solution)/shard_map/ppermute | solution.py:325
  139.9 5.7 %all-to-all-done.col_ref = bf16[8,256,128]{2,1,0:T(8,128)(2,1)S(1)} async-done(((bf16[8,256,128]{2,1,0:T(8,128)(2,1)}), bf16[8,256,128]{2,1,0:T(8,128)(2,1)S(1)}, u32[]{:S(2)}, u32[]{:S(2)}) %all-to-all-start) | async-done | bytes 524320 | tf_op jit(solution)/shard_map/all_to_all | solution.py:322
  147.6 5.5 %collective-permute-start.26 = (f32[40,128]{1,0:T(8,128)S(1)}, f32[40,128]{1,0:T(8,128)S(1)}, u32[]{:S(2)}, u32[]{:S(2)}) collective-permute-start(f32[40,128]{1,0:T(8,128)S(1)} %add.38), channel_id=1, source_target_pairs={{0,4},{2,6},{4,0},{6,2},{1,5},{3,7},{5,1},{7,3},{8,12},{10,14},{12... | collective-permute-start | bytes 61448 | tf_op jit(solution)/shard_map/ppermute | solution.py:240
  155.0 1.9 %collective-permute-done.25 = f32[40,128]{1,0:T(8,128)S(1)} collective-permute-done((f32[40,128]{1,0:T(8,128)S(1)}, f32[40,128]{1,0:T(8,128)S(1)}, u32[]{:S(2)}, u32[]{:S(2)}) %collective-permute-start.25) | collective-permute-done | bytes 20512 | tf_op jit(solution)/shard_map/ppermute | solution.py:240
  160.8 2.9 %collective-permute-done.29 = f32[40,128]{1,0:T(8,128)S(1)} collective-permute-done((f32[40,128]{1,0:T(8,128)S(1)}, f32[40,128]{1,0:T(8,128)S(1)}, u32[]{:S(2)}, u32[]{:S(2)}) %collective-permute-start.29) | collective-permute-done | bytes 20512 | tf_op jit(solution)/shard_map/ppermute | solution.py:240
  164.6 7.1 %collective-permute-done.31 = f32[40,128]{1,0:T(8,128)S(1)} collective-permute-done((f32[40,128]{1,0:T(8,128)S(1)}, f32[40,128]{1,0:T(8,128)S(1)}, u32[]{:S(2)}, u32[]{:S(2)}) %collective-permute-start.31) | collective-permute-done | bytes 20512 | tf_op jit(solution)/shard_map/ppermute | solution.py:339
  175.0 3.5 %collective-permute-done.34 = f32[40,128]{1,0:T(8,128)S(1)} collective-permute-done((f32[40,128]{1,0:T(8,128)S(1)}, f32[40,128]{1,0:T(8,128)S(1)}, u32[]{:S(2)}, u32[]{:S(2)}) %collective-permute-start.34) | collective-permute-done | bytes 20512 | tf_op jit(solution)/shard_map/ppermute | solution.py:240
  178.7 4.7 %solve.1 = (f32[32,1024]{1,0:T(8,128)}, f32[32,1024]{1,0:T(8,128)}, f32[32,1024]{1,0:T(8,128)}) custom-call(f32[40,128]{1,0:T(8,128)S(1)} %add_add_fusion.gram_ref, f32[32,1024]{1,0:T(8,128)S(1)} %copy-done.3, f32[32,1024]{1,0:T(8,128)S(1)} %copy-done.2, f32[32,1024]{1,0:T(8,128)S(1)} %copy-done.1, f32[32,1024]{1,0:T(8,128)S(1)} %get-tuple-element.40.image_ref), custom_call_target="tpu_custom_call" | custom-call | tf_op jit(solution)/shard_map/solve/pallas_call | solution.py:341
  (102 shorter events, 25.8 us)
Async XLA Ops:
  2.2 11.4 %collective-permute-start.3 = (bf16[272,128]{1,0:T(8,128)(2,1)S(1)}, bf16[272,128]{1,0:T(8,128)(2,1)S(1)}, u32[]{:S(2)}, u32[]{:S(2)}) collective-permute-start(bf16[272,128]{1,0:T(8,128)(2,1)S(1)} %pack.1.own_ref), channel_id=1, source_target_pairs={{0,128},{32,160},{64,192},{96,224},{128,0},{160,32},{192,64},{224,... | collective-permute-start | bytes 208904 | tf_op jit(solution)/shard_map/ppermute | solution.py:254
  9.5 7.1 %collective-permute-start.2 = (bf16[272,128]{1,0:T(8,128)(2,1)S(1)}, bf16[272,128]{1,0:T(8,128)(2,1)S(1)}, u32[]{:S(2)}, u32[]{:S(2)}) collective-permute-start(bf16[272,128]{1,0:T(8,128)(2,1)S(1)} %pack.1.own_ref), channel_id=1, source_target_pairs={{0,6},{2,0},{4,2},{6,4},{1,7},{3,1},{5,3},{7,5},{8,14},{10,8},{12,... | collective-permute-start | bytes 208904 | tf_op jit(solution)/shard_map/ppermute | solution.py:240
  10.0 7.3 %collective-permute-start.1 = (bf16[272,128]{1,0:T(8,128)(2,1)S(1)}, bf16[272,128]{1,0:T(8,128)(2,1)S(1)}, u32[]{:S(2)}, u32[]{:S(2)}) collective-permute-start(bf16[272,128]{1,0:T(8,128)(2,1)S(1)} %pack.1.own_ref), channel_id=1, source_target_pairs={{0,4},{2,6},{4,0},{6,2},{1,5},{3,7},{5,1},{7,3},{8,12},{10,14},{12... | collective-permute-start | bytes 208904 | tf_op jit(solution)/shard_map/ppermute | solution.py:240
  13.6 7.0 %collective-permute-start.6 = (bf16[2,272,128]{2,1,0:T(8,128)(2,1)S(1)}, bf16[2,272,128]{2,1,0:T(8,128)(2,1)S(1)}, u32[]{:S(2)}, u32[]{:S(2)}) collective-permute-start(bf16[2,272,128]{2,1,0:T(8,128)(2,1)S(1)} %pad_maximum_fusion.5), channel_id=1, source_target_pairs={{0,224},{32,0},{64,32},{96,64},{128,96},{160,128},{192,160},{224,1... | collective-permute-start | bytes 417800 | tf_op jit(solution)/shard_map/ppermute | solution.py:254
  16.6 10.2 %collective-permute-start.5 = (bf16[2,272,128]{2,1,0:T(8,128)(2,1)S(1)}, bf16[2,272,128]{2,1,0:T(8,128)(2,1)S(1)}, u32[]{:S(2)}, u32[]{:S(2)}) collective-permute-start(bf16[2,272,128]{2,1,0:T(8,128)(2,1)S(1)} %pad_maximum_fusion.5), channel_id=1, source_target_pairs={{0,64},{32,96},{64,128},{96,160},{128,192},{160,224},{192,0},{224,... | collective-permute-start | bytes 417800 | tf_op jit(solution)/shard_map/ppermute | solution.py:254
  16.6 10.3 %collective-permute-start.4 = (bf16[2,272,128]{2,1,0:T(8,128)(2,1)S(1)}, bf16[2,272,128]{2,1,0:T(8,128)(2,1)S(1)}, u32[]{:S(2)}, u32[]{:S(2)}) collective-permute-start(bf16[2,272,128]{2,1,0:T(8,128)(2,1)S(1)} %pad_maximum_fusion.5), channel_id=1, source_target_pairs={{0,32},{32,64},{64,96},{96,128},{128,160},{160,192},{192,224},{224... | collective-permute-start | bytes 417800 | tf_op jit(solution)/shard_map/ppermute | solution.py:254
  17.2 24.0 %collective-permute-start.10 = (bf16[2,272,128]{2,1,0:T(8,128)(2,1)S(1)}, bf16[2,272,128]{2,1,0:T(8,128)(2,1)S(1)}, u32[]{:S(2)}, u32[]{:S(2)}) collective-permute-start(bf16[2,272,128]{2,1,0:T(8,128)(2,1)S(1)} %pad_maximum_fusion.5), channel_id=1, source_target_pairs={{0,8},{8,16},{16,24},{24,0},{1,9},{9,17},{17,25},{25,1},{2,10},{10... | collective-permute-start | bytes 417800 | tf_op jit(solution)/shard_map/ppermute | solution.py:254
  18.8 11.4 %collective-permute-start.9 = (bf16[2,272,128]{2,1,0:T(8,128)(2,1)S(1)}, bf16[2,272,128]{2,1,0:T(8,128)(2,1)S(1)}, u32[]{:S(2)}, u32[]{:S(2)}) collective-permute-start(bf16[2,272,128]{2,1,0:T(8,128)(2,1)S(1)} %pad_maximum_fusion.5), channel_id=1, source_target_pairs={{0,24},{8,0},{16,8},{24,16},{1,25},{9,1},{17,9},{25,17},{2,26},{10... | collective-permute-start | bytes 417800 | tf_op jit(solution)/shard_map/ppermute | solution.py:254
  26.9 14.4 %collective-permute-start.11 = (bf16[6,272,128]{2,1,0:T(8,128)(2,1)S(1)}, bf16[6,272,128]{2,1,0:T(8,128)(2,1)S(1)}, u32[]{:S(2)}, u32[]{:S(2)}) collective-permute-start(bf16[6,272,128]{2,1,0:T(8,128)(2,1)S(1)} %pad_maximum_fusion), channel_id=1, source_target_pairs={{0,8},{8,16},{16,24},{24,0},{1,9},{9,17},{17,25},{25,1},{2,10},{10... | collective-permute-start | bytes 1253384 | tf_op jit(solution)/shard_map/ppermute | solution.py:254
  28.5 13.0 %collective-permute-start.8 = (bf16[6,272,128]{2,1,0:T(8,128)(2,1)S(1)}, bf16[6,272,128]{2,1,0:T(8,128)(2,1)S(1)}, u32[]{:S(2)}, u32[]{:S(2)}) collective-permute-start(bf16[6,272,128]{2,1,0:T(8,128)(2,1)S(1)} %pad_maximum_fusion), channel_id=1, source_target_pairs={{0,24},{8,0},{16,8},{24,16},{1,25},{9,1},{17,9},{25,17},{2,26},{10... | collective-permute-start | bytes 1253384 | tf_op jit(solution)/shard_map/ppermute | solution.py:254
  30.3 11.1 %collective-permute-start.7 = (bf16[4,272,128]{2,1,0:T(8,128)(2,1)S(1)}, bf16[4,272,128]{2,1,0:T(8,128)(2,1)S(1)}, u32[]{:S(2)}, u32[]{:S(2)}) collective-permute-start(bf16[4,272,128]{2,1,0:T(8,128)(2,1)S(1)} %pad_maximum_fusion.1), channel_id=1, source_target_pairs={{0,1},{1,0},{2,3},{3,2},{4,5},{5,4},{6,7},{7,6},{8,9},{9,8},{10,11... | collective-permute-start | bytes 835592 | tf_op jit(solution)/shard_map/ppermute | solution.py:244
  41.4 10.3 %collective-permute-start.12 = (bf16[4,272,128]{2,1,0:T(8,128)(2,1)S(1)}, bf16[4,272,128]{2,1,0:T(8,128)(2,1)S(1)}, u32[]{:S(2)}, u32[]{:S(2)}) collective-permute-start(bf16[4,272,128]{2,1,0:T(8,128)(2,1)S(1)} %pad_maximum_fusion.2), channel_id=1, source_target_pairs={{0,8},{8,16},{16,24},{24,0},{1,9},{9,17},{17,25},{25,1},{2,10},{10... | collective-permute-start | bytes 835592 | tf_op jit(solution)/shard_map/ppermute | solution.py:254
  41.6 10.2 %collective-permute-start.13 = (bf16[4,272,128]{2,1,0:T(8,128)(2,1)S(1)}, bf16[4,272,128]{2,1,0:T(8,128)(2,1)S(1)}, u32[]{:S(2)}, u32[]{:S(2)}) collective-permute-start(bf16[4,272,128]{2,1,0:T(8,128)(2,1)S(1)} %pad_maximum_fusion.3), channel_id=1, source_target_pairs={{0,24},{8,0},{16,8},{24,16},{1,25},{9,1},{17,9},{25,17},{2,26},{10... | collective-permute-start | bytes 835592 | tf_op jit(solution)/shard_map/ppermute | solution.py:254
  94.8 29.2 %collective-permute-start.18 = (bf16[8,192,128]{2,1,0:T(8,128)(2,1)S(1)}, bf16[8,192,128]{2,1,0:T(8,128)(2,1)S(1)}, u32[]{:S(2)}, u32[]{:S(2)}) collective-permute-start(bf16[8,192,128]{2,1,0:T(8,128)(2,1)S(1)} %get-tuple-element.32), channel_id=1, source_target_pairs={{0,24},{8,0},{16,8},{24,16},{1,25},{9,1},{17,9},{25,17},{2,26},{10... | collective-permute-start | bytes 1179656 | tf_op jit(solution)/shard_map/ppermute | solution.py:294
  94.9 29.1 %collective-permute-start.19 = (bf16[8,192,128]{2,1,0:T(8,128)(2,1)S(1)}, bf16[8,192,128]{2,1,0:T(8,128)(2,1)S(1)}, u32[]{:S(2)}, u32[]{:S(2)}) collective-permute-start(bf16[8,192,128]{2,1,0:T(8,128)(2,1)S(1)} %get-tuple-element.33), channel_id=1, source_target_pairs={{0,16},{8,24},{16,0},{24,8},{1,17},{9,25},{17,1},{25,9},{2,18},{10... | collective-permute-start | bytes 1179656 | tf_op jit(solution)/shard_map/ppermute | solution.py:294
  95.0 29.0 %collective-permute-start.20 = (bf16[8,192,128]{2,1,0:T(8,128)(2,1)S(1)}, bf16[8,192,128]{2,1,0:T(8,128)(2,1)S(1)}, u32[]{:S(2)}, u32[]{:S(2)}) collective-permute-start(bf16[8,192,128]{2,1,0:T(8,128)(2,1)S(1)} %get-tuple-element.34), channel_id=1, source_target_pairs={{0,8},{8,16},{16,24},{24,0},{1,9},{9,17},{17,25},{25,1},{2,10},{10... | collective-permute-start | bytes 1179656 | tf_op jit(solution)/shard_map/ppermute | solution.py:294
  111.0 6.6 %collective-permute-start.21 = (bf16[8,64,128]{2,1,0:T(8,128)(2,1)S(1)}, bf16[8,64,128]{2,1,0:T(8,128)(2,1)S(1)}, u32[]{:S(2)}, u32[]{:S(2)}) collective-permute-start(bf16[8,64,128]{2,1,0:T(8,128)(2,1)S(1)} %get-tuple-element.36), channel_id=1, source_target_pairs={{0,24},{8,0},{16,8},{24,16},{1,25},{9,1},{17,9},{25,17},{2,26},{10... | collective-permute-start | bytes 393224 | tf_op jit(solution)/shard_map/ppermute | solution.py:294
  111.1 10.2 %collective-permute-start.22 = (bf16[8,64,128]{2,1,0:T(8,128)(2,1)S(1)}, bf16[8,64,128]{2,1,0:T(8,128)(2,1)S(1)}, u32[]{:S(2)}, u32[]{:S(2)}) collective-permute-start(bf16[8,64,128]{2,1,0:T(8,128)(2,1)S(1)} %get-tuple-element.37), channel_id=1, source_target_pairs={{0,16},{8,24},{16,0},{24,8},{1,17},{9,25},{17,1},{25,9},{2,18},{10... | collective-permute-start | bytes 393224 | tf_op jit(solution)/shard_map/ppermute | solution.py:294
  121.3 9.2 %collective-permute-start.14 = (bf16[4,256,128]{2,1,0:T(8,128)(2,1)S(1)}, bf16[4,256,128]{2,1,0:T(8,128)(2,1)S(1)}, u32[]{:S(2)}, u32[]{:S(2)}) collective-permute-start(bf16[4,256,128]{2,1,0:T(8,128)(2,1)S(1)} %slice.59), channel_id=1, source_target_pairs={{0,1},{1,0},{2,3},{3,2},{4,5},{5,4},{6,7},{7,6},{8,9},{9,8},{10,11... | collective-permute-start | bytes 786440 | tf_op jit(solution)/shard_map/ppermute | solution.py:244
  125.1 20.4 %all-to-all-start = ((bf16[8,256,128]{2,1,0:T(8,128)(2,1)}), bf16[8,256,128]{2,1,0:T(8,128)(2,1)S(1)}, u32[]{:S(2)}, u32[]{:S(2)}) async-start(bf16[8,256,128]{2,1,0:T(8,128)(2,1)} %add.65), calls=%async_computation | async-start | bytes 1048576 | tf_op jit(solution)/shard_map/all_to_all | solution.py:322
  147.6 7.3 %collective-permute-start.26 = (f32[40,128]{1,0:T(8,128)S(1)}, f32[40,128]{1,0:T(8,128)S(1)}, u32[]{:S(2)}, u32[]{:S(2)}) collective-permute-start(f32[40,128]{1,0:T(8,128)S(1)} %add.38), channel_id=1, source_target_pairs={{0,4},{2,6},{4,0},{6,2},{1,5},{3,7},{5,1},{7,3},{8,12},{10,14},{12... | collective-permute-start | bytes 61448 | tf_op jit(solution)/shard_map/ppermute | solution.py:240
  163.9 7.8 %collective-permute-start.31 = (f32[40,128]{1,0:T(8,128)S(1)}, f32[40,128]{1,0:T(8,128)S(1)}, u32[]{:S(2)}, u32[]{:S(2)}) collective-permute-start(f32[40,128]{1,0:T(8,128)S(1)} %add_add_fusion.1), channel_id=1, source_target_pairs={{0,128},{32,160},{64,192},{96,224},{128,0},{160,32},{192,64},{224,... | collective-permute-start | bytes 61448 | tf_op jit(solution)/shard_map/ppermute | solution.py:339
  171.7 6.8 %collective-permute-start.34 = (f32[40,128]{1,0:T(8,128)S(1)}, f32[40,128]{1,0:T(8,128)S(1)}, u32[]{:S(2)}, u32[]{:S(2)}) collective-permute-start(f32[40,128]{1,0:T(8,128)S(1)} %add.45), channel_id=1, source_target_pairs={{0,96},{32,128},{64,160},{96,192},{128,224},{160,0},{192,32},{224,... | collective-permute-start | bytes 61448 | tf_op jit(solution)/shard_map/ppermute | solution.py:240
  171.8 6.7 %collective-permute-start.33 = (f32[40,128]{1,0:T(8,128)S(1)}, f32[40,128]{1,0:T(8,128)S(1)}, u32[]{:S(2)}, u32[]{:S(2)}) collective-permute-start(f32[40,128]{1,0:T(8,128)S(1)} %add.45), channel_id=1, source_target_pairs={{0,64},{32,96},{64,128},{96,160},{128,192},{160,224},{192,0},{224,... | collective-permute-start | bytes 61448 | tf_op jit(solution)/shard_map/ppermute | solution.py:240
  (18 other events, 185.6 us)

commit v8 on v7

--- a/solution.py
+++ b/solution.py
@@ -13,8 +13,8 @@
 PROBES = 32
 UNROLL = 32
 TAIL = 8
-SPLIT = 6
-BIN = 1536 + 2 * UNROLL
+PARTS = (2, 1, 1)
+LIST = 1536 + UNROLL
 NUGGET = 2.0
 KERNEL_SCALE = 0.1
 HIGHEST = lax.Precision.HIGHEST
@@ -43,36 +43,36 @@
     return ((remain2 * remain2) * (1.25 - remain)).astype(bf16)
 
 
-def bin_kernel(live_ref, pairs_ref, after_ref, bins_ref, count_ref):
+def bin_kernel(live_ref, entries_ref, after_ref, bins_ref, count_ref):
     live = live_ref[0]
 
-    def put(e, front):
-        a, b = pairs_ref[0, e], pairs_ref[1, e]
-        first = (b & 7) < SPLIT
-        bins_ref[jnp.where(first, front, BIN - 1 - e + front)] = a + (b << 8)
-        return front + first.astype(jnp.int32)
-
-    def step(i, front):
+    def put(e, ends):
+        first, second = ends
+        entry = entries_ref[e]
+        bins_ref[first] = entry
+        bins_ref[LIST + second] = entry
+        bins_ref[2 * LIST + e - first - second] = entry
+        return first + ((entry >> 16) & 1), second + ((entry >> 17) & 1)
+
+    def step(i, ends):
         for u in range(8):
-            front = put(i * 8 + u, front)
-        return front
+            ends = put(i * 8 + u, ends)
+        return ends
 
     groups = live >> 3
-    front = lax.fori_loop(0, groups, step, jnp.int32(0))
-    front = lax.fori_loop(groups * 8, live, put, front)
-    back = live - front
-    count_ref[0] = front
-    count_ref[1] = back
-    for j in range(TAIL):
-        bins_ref[front + j] = 0
-        bins_ref[BIN - 1 - back - j] = SPLIT << 8
+    ends = lax.fori_loop(0, groups, step, (jnp.int32(0), jnp.int32(0)))
+    first, second = lax.fori_loop(groups * 8, live, put, ends)
+    for part, end in enumerate((first, second, live - first - second)):
+        count_ref[part] = end
+        for j in range(TAIL):
+            bins_ref[part * LIST + end + j] = 0
 
 
 def spread(strip, t):
     return jnp.broadcast_to(strip[:, t : t + 1], (TILE, TILE))
 
 
-def row_kernel(own_ref, near_ref, after_ref, px, py, own_out):
+def row_kernel(own_ref, near_ref, px, py, own_out):
     def row_prepare(r, carry):
         strip = near_ref[r, 256:272, :].astype(f32).T
         for t in range(8):
@@ -101,39 +101,36 @@
     if part == 0:
         row_acc, *col_out, qx, qy, col_acc = refs
         row_acc[...] = jnp.zeros_like(row_acc)
+    elif part == 1:
+        before, row_acc, *col_out, qx, qy, col_acc = refs
+        row_acc[...] = before[...]
     else:
-        row_acc, row_out, *col_out, qx, qy, col_acc = refs
-    x_own, y_own, z_own, core_own = place_ref[0], place_ref[1], place_ref[2], place_ref[3]
-    tiles = range(SPLIT) if part == 0 else range(SPLIT, 8)
-    first, number = tiles[0], len(tiles)
+        before, row_acc, row_out, *col_out, qx, qy, col_acc = refs
+        row_acc[...] = before[...]
+    z_own = place_ref[0]
     live = count_ref[part]
     col_acc[...] = jnp.zeros_like(col_acc)
 
     def col_prepare(r, carry):
         where = col_ref[r, 256:272, :].astype(f32)
-        for t in tiles:
+        for t in range(8):
             qx[r * 8 + t] = jnp.broadcast_to(where[t : t + 1], (8, TILE))
             qy[r * 8 + t] = jnp.broadcast_to(where[8 + t : 9 + t], (8, TILE))
         return carry
 
-    lax.fori_loop(0, 32, col_prepare, 0)
+    lax.fori_loop(0, 8 * PARTS[part], col_prepare, 0)
 
     def several(start, size, masked):
         results = []
         for u in range(size):
             e = start + u
-            both = bins_ref[e if part == 0 else BIN - 1 - e]
-            a, b = both & 255, both >> 8
-            near_slot = ((y_own - (a >> 4)) & 3) + ((((a >> 3) & 1) ^ core_own) << 2)
-            z_far = (z_own - (b >> 5)) & 7
-            far_slot = (((x_own - (b >> 3)) & 3) << 3) + z_slot(z_far)
-            near = near_ref[near_slot, pl.ds(pl.multiple_of((a & 7) * 32, 32), 32), :]
-            far = col_ref[far_slot, pl.ds(pl.multiple_of((b & 7) * 32, 32), 32), :]
+            entry = bins_ref[part * LIST + e]
+            a, b = entry & 255, (entry >> 8) & 255
+            near = near_ref[a >> 3, pl.ds(pl.multiple_of((a & 7) * 32, 32), 32), :]
+            far = col_ref[b >> 3, pl.ds(pl.multiple_of((b & 7) * 32, 32), 32), :]
             if masked:
                 keep = jnp.where(e < live, 1.0, 0.0).astype(bf16)
                 near, far = near * keep, far * keep
-            a = (near_slot << 3) + (a & 7)
-            b = (far_slot << 3) + (b & 7)
             dx = px[a].reshape(16, 8, TILE) - qx[b][None]
             dy = py[a].reshape(16, 8, TILE) - qy[b][None]
             block = radial((dx * dx + dy * dy).reshape(TILE, TILE))
@@ -158,14 +155,14 @@
     lax.fori_loop(0, (live - whole * UNROLL + TAIL - 1) // TAIL, tail, 0)
 
     def finish(z, carry):
-        for k in range(4):
-            for t in range(number):
-                total = KERNEL_SCALE * col_acc[k * 64 + z_slot(z) * 8 + first + t]
+        for k in range(PARTS[part]):
+            for t in range(8):
+                total = KERNEL_SCALE * col_acc[k * 64 + z_slot(z) * 8 + t]
                 col_out[k][(z_own - z) & 7, t * 32 : (t + 1) * 32, :] = total.astype(bf16)
         return carry
 
     lax.fori_loop(0, 8, finish, 0)
-    if part == 1:
+    if part == 2:
 
         def finish_row(r, carry):
             for t in range(8):
@@ -175,13 +172,10 @@
         lax.fori_loop(0, 8, finish_row, 0)
 
 
-def add_kernel(own0, a0, b0, c0, own1, a1, b1, c1, out):
+def add_kernel(own, below, far, above, out):
     for z in range(8):
-        for rows, parts in ((slice(0, SPLIT * 32), (own0, a0, b0, c0)), (slice(SPLIT * 32, 256), (own1, a1, b1, c1))):
-            total = parts[0][z].astype(f32)
-            for part in parts[1:]:
-                total = total + part[z].astype(f32)
-            out[z, rows, :] = total.astype(bf16)
+        total = (own[z].astype(f32) + below[z].astype(f32)) + (far[z].astype(f32) + above[z].astype(f32))
+        out[z] = total.astype(bf16)
 
 
 def dot32(former, latter, dims):
@@ -260,65 +254,71 @@
     rest = jnp.concatenate([one, two, back], 0)
     row_half, rest = lax.optimization_barrier((row_half, rest))
     rest_below, rest_above = moved(rest, "x", 4, 1), moved(rest, "x", 4, -1)
-    far_below = moved(jnp.concatenate([pair_below[:1], rest_below[:3]], 0), "x", 4, 1)
-    far_above = moved(jnp.concatenate([pair_above[1:], rest_above[3:]], 0), "x", 4, -1)
-    col_all = jnp.concatenate(
-        [pair, rest, pair_below, rest_below, far_below[:1], far_above[:1], far_below[1:], far_above[1:], pair_above, rest_above], 0
-    )
     row_all = jnp.concatenate([row_half, swap(row_half)], 0)
-    place = jnp.stack([lax.axis_index(name) for name in ("x", "y", "z", "core")]).astype(jnp.int32)
+    x_own, y_own, z_own, core_own = [lax.axis_index(name).astype(jnp.int32) for name in ("x", "y", "z", "core")]
+    place = z_own.reshape(1)
+    a, b = tile_pairs[0], tile_pairs[1]
+    near_slot = ((y_own - (a >> 4)) & 3) + ((((a >> 3) & 1) ^ core_own) << 2)
+    x_far = (x_own - (b >> 3)) & 3
+    far_slot = z_slot((z_own - (b >> 5)) & 7) + jnp.where(x_far == 3, 8, 0)
+    entries = (near_slot << 3) + (a & 7) + (far_slot << 11) + ((b & 7) << 8)
+    entries = entries + ((x_far & 1) << 16) + jnp.where(x_far == 2, 1 << 17, 0)
     bins, counts = pl.pallas_call(
         bin_kernel,
-        out_shape=(shape((BIN,), jnp.int32), shape((2,), jnp.int32)),
+        out_shape=(shape((3 * LIST,), jnp.int32), shape((3,), jnp.int32)),
         in_specs=[SMEM, SMEM, VMEM],
         out_specs=(SMEM, SMEM),
         compiler_params=SMALL,
         name="bins",
-    )(pair_count, tile_pairs, pair_above[0, :16])
+    )(pair_count, entries, pair_above[0, :16])
     spread_shape = shape((64, TILE, TILE), f32)
     px, py, own_product = pl.pallas_call(
         row_kernel,
         out_shape=(spread_shape, spread_shape, shape((PROBES, own_points), f32)),
-        in_specs=[VMEM] * 3,
+        in_specs=[VMEM] * 2,
         out_specs=(VMEM,) * 3,
         compiler_params=PARAMS,
         name="rows",
-    )(packed, row_all, rest_above[0, :16])
+    )(packed, row_all)
+    rest_below, rest_above, bins, px = lax.optimization_barrier((rest_below, rest_above, bins, px))
+    far_below = moved(jnp.concatenate([pair_below[:1], rest_below[:3]], 0), "x", 4, 1)
+    far_above = moved(jnp.concatenate([pair_above[1:], rest_above[3:]], 0), "x", 4, -1)
+    columns = (
+        jnp.concatenate([pair_below, rest_below, pair_above, rest_above], 0),
+        jnp.concatenate([far_below[:1], far_above[:1], far_below[1:], far_above[1:]], 0),
+        jnp.concatenate([pair, rest], 0),
+    )
     acc = shape((64, PROBES, TILE), f32)
-    scratch = [pltpu.VMEM((256, 8, TILE), f32), pltpu.VMEM((256, 8, TILE), f32), pltpu.VMEM((256, PROBES, TILE), f32)]
-
-    def blocks(number):
-        return (shape((8, number * 32, TILE), bf16),) * 4
-
-    def sent(col_out):
-        return [lax.ppermute(col_out[k], "x", [(i, (i - k) % 4) for i in range(4)]) for k in range(1, 4)]
-
-    row_acc, *col_first = pl.pallas_call(
-        functools.partial(part_kernel, 0),
-        out_shape=(acc,) + blocks(SPLIT),
-        in_specs=[SMEM] * 3 + [VMEM] * 4,
-        out_specs=(VMEM,) * 5,
-        scratch_shapes=scratch,
-        compiler_params=PARAMS,
-        name="pairs_first",
-    )(place, counts, bins, row_all, px, py, col_all)
-    row_sum, *col_second = pl.pallas_call(
-        functools.partial(part_kernel, 1),
-        out_shape=(shape((8, 256, TILE), bf16),) + blocks(8 - SPLIT),
-        in_specs=[SMEM] * 3 + [VMEM] * 5,
-        out_specs=(VMEM,) * 5,
-        scratch_shapes=scratch,
-        compiler_params=PARAMS,
-        name="pairs_second",
-    )(place, counts, bins, row_all, px, py, col_all, row_acc)
+    block = shape((8, 256, TILE), bf16)
+
+    def pairs(part, totals=None):
+        tiles = PARTS[part] * 64
+        outs = (acc,) + (block,) * (PARTS[part] + (part == 2))
+        operands = (place, counts, bins, row_all, px, py, columns[part]) + (() if part == 0 else (totals,))
+        return pl.pallas_call(
+            functools.partial(part_kernel, part),
+            out_shape=outs,
+            in_specs=[SMEM] * 3 + [VMEM] * (len(operands) - 3),
+            out_specs=(VMEM,) * len(outs),
+            scratch_shapes=[pltpu.VMEM((tiles, 8, TILE), f32)] * 2 + [pltpu.VMEM((tiles, PROBES, TILE), f32)],
+            input_output_aliases={} if part == 0 else {7: 0},
+            compiler_params=PARAMS,
+            name="pairs",
+        )(*operands)
+
+    totals, for_below, for_above = pairs(0)
+    below, above = moved(for_below, "x", 4, -1), moved(for_above, "x", 4, 1)
+    totals, for_far = pairs(1, totals)
+    far = moved(for_far, "x", 4, 2)
+    totals, row_sum, own = pairs(2, totals)
     sums = pl.pallas_call(
         add_kernel,
-        out_shape=shape((8, 256, TILE), bf16),
-        in_specs=[VMEM] * 8,
+        out_shape=block,
+        in_specs=[VMEM] * 4,
         out_specs=VMEM,
         compiler_params=PARAMS,
         name="add",
-    )(col_first[0], *sent(col_first), col_second[0], *sent(col_second))
+    )(own, below, far, above)
     col_parts = lax.all_to_all(sums, "z", 0, 0)
     half = (row_sum[:4].astype(f32) + swap(row_sum[4:]).astype(f32)).astype(bf16)
     row_parts = [half[0]] + [

time: 184 us -> 172 us (0.935)
  waiting for transfers between devices: 42.1 us -> 33.1 us
  starting transfers between devices: 59.8 us -> 56.6 us
    ppermute x6 -> x0, starting transfers between devices: 12.4 us -> none  [sent(): lax.ppermute(col_out[k], 'x', [(i, (i - k) % 4) for i in range(4)])]
    ppermute x10 -> x13, waiting for transfers between devices: 9.92 us -> 5.44 us  [moved(): lax.ppermute(value, axis, [(i, (i + shift) % size) for i in range(size)])]
    ppermute x12, starting transfers between devices: 15.3 us -> 19.7 us  [shifts(): lax.ppermute(value, axis, [(i, (i + k) % size) for i in range(size)])]
    ppermute x3, starting transfers between devices: 4.99 us -> 8.24 us  [on_device(): lax.ppermute(half[k], 'y', [(i, (i - k) % 4) for i in range(4)])]
    ppermute x6 -> x0, waiting for transfers between devices: 2.61 us -> none  [sent(): lax.ppermute(col_out[k], 'x', [(i, (i - k) % 4) for i in range(4)])]
    ppermute x3, waiting for transfers between devices: 4.21 us -> 1.9 us  [on_device(): lax.ppermute(half[k], 'y', [(i, (i - k) % 4) for i in range(4)])]
    ppermute x10 -> x13, starting transfers between devices: 20.9 us -> 21.4 us  [moved(): lax.ppermute(value, axis, [(i, (i + shift) % size) for i in range(size)])]
    pallas_call x4 -> x5, Pallas kernels: 68.8 us -> 69 us  [the longest x3 58.2 us: pairs(): pl.pallas_call(functools.partial(part_kernel, part), out_shape=outs, in_s...]
  transfers between devices with their start and end apart: 36 -> 33, of which waited for: 16 -> 13; matrix products, arithmetic and copies ran while one was open for 0% -> 1% of each run, Pallas kernels for 16% -> 42%
where the time goes in v8:
time: 172 us
  Pallas kernels  77.7 us (45%)
  starting transfers between devices  56.6 us (33%)
  waiting for transfers between devices  33.1 us (19%)
  local copies, waits for them, and re-layouts  1.79 us (1%)
    pallas_call x3, Pallas kernels, pairs(): pl.pallas_call(functools.partial(part_kernel, part), out_shape=outs, in_s...  58.2 us
    ppermute x13, starting transfers between devices, moved(): lax.ppermute(value, axis, [(i, (i + shift) % size) for i in range(size)])  21.4 us
    ppermute x12, starting transfers between devices, shifts(): lax.ppermute(value, axis, [(i, (i + k) % size) for i in range(size)])  19.7 us
    ppermute x12, waiting for transfers between devices, shifts(): lax.ppermute(value, axis, [(i, (i + k) % size) for i in range(size)])  11.9 us
    pallas_call x1, Pallas kernels, on_device(): pl.pallas_call(bin_kernel, out_shape=(shape((3 * LIST,), jnp.int32), shap...  9.75 us
    ppermute x3, starting transfers between devices, on_device(): lax.ppermute(half[k], 'y', [(i, (i - k) % 4) for i in range(4)])  8.24 us
    ppermute x1, waiting for transfers between devices, on_device(): gram = gram + lax.ppermute(gram, 'z', [(i, (i + 4) % 8) for i in range(8)])  7.19 us
    all_to_all x1, starting transfers between devices, on_device(): col_parts = lax.all_to_all(sums, 'z', 0, 0)  6.47 us
  transfers between devices with their start and end apart: 33, of which 13 were waited for; matrix products, arithmetic and copies ran while one was open for 1% of the time, Pallas kernels for 42%

profile of v8, /device:TPU:16, one launch (start us, length us, event | category | flops | bytes accessed | tf_op | source)
XLA Modules:
  0.0 172.4 jit_solution(3345828875184937123)
XLA Ops:
  2.2 7.3 %collective-permute-start.3 = (bf16[272,128]{1,0:T(8,128)(2,1)S(1)}, bf16[272,128]{1,0:T(8,128)(2,1)S(1)}, u32[]{:S(2)}, u32[]{:S(2)}) collective-permute-start(bf16[272,128]{1,0:T(8,128)(2,1)S(1)} %pack.1.own_ref), channel_id=1, source_target_pairs={{0,128},{32,160},{64,192},{96,224},{128,0},{160,32},{192,64},{224,... | collective-permute-start | bytes 208904 | tf_op jit(solution)/shard_map/ppermute | solution.py:248
  10.0 2.9 %collective-permute-start.1 = (bf16[272,128]{1,0:T(8,128)(2,1)S(1)}, bf16[272,128]{1,0:T(8,128)(2,1)S(1)}, u32[]{:S(2)}, u32[]{:S(2)}) collective-permute-start(bf16[272,128]{1,0:T(8,128)(2,1)S(1)} %pack.1.own_ref), channel_id=1, source_target_pairs={{0,4},{2,6},{4,0},{6,2},{1,5},{3,7},{5,1},{7,3},{8,12},{10,14},{12... | collective-permute-start | bytes 208904 | tf_op jit(solution)/shard_map/ppermute | solution.py:234
  13.9 2.8 %collective-permute-start.6 = (bf16[2,272,128]{2,1,0:T(8,128)(2,1)S(1)}, bf16[2,272,128]{2,1,0:T(8,128)(2,1)S(1)}, u32[]{:S(2)}, u32[]{:S(2)}) collective-permute-start(bf16[2,272,128]{2,1,0:T(8,128)(2,1)S(1)} %pad_maximum_fusion.8), channel_id=1, source_target_pairs={{0,224},{32,0},{64,32},{96,64},{128,96},{160,128},{192,160},{224,1... | collective-permute-start | bytes 417800 | tf_op jit(solution)/shard_map/ppermute | solution.py:248
  21.5 5.3 %collective-permute-done.5 = bf16[2,272,128]{2,1,0:T(8,128)(2,1)S(1)} collective-permute-done((bf16[2,272,128]{2,1,0:T(8,128)(2,1)S(1)}, bf16[2,272,128]{2,1,0:T(8,128)(2,1)S(1)}, u32[]{:S(2)}, u32[]{:S(2)}) %collective-permute-start.5) | collective-permute-done | bytes 139296 | tf_op jit(solution)/shard_map/ppermute | solution.py:248
  26.9 2.8 %collective-permute-start.10 = (bf16[6,272,128]{2,1,0:T(8,128)(2,1)S(1)}, bf16[6,272,128]{2,1,0:T(8,128)(2,1)S(1)}, u32[]{:S(2)}, u32[]{:S(2)}) collective-permute-start(bf16[6,272,128]{2,1,0:T(8,128)(2,1)S(1)} %pad_maximum_fusion.3), channel_id=1, source_target_pairs={{0,24},{8,0},{16,8},{24,16},{1,25},{9,1},{17,9},{25,17},{2,26},{10... | collective-permute-start | bytes 1253384 | tf_op jit(solution)/shard_map/ppermute | solution.py:248
  29.8 9.7 %bins.1 = (s32[4704]{0:T(1024)S(1)}, s32[3]{0:T(128)S(1)}) custom-call(s32[1]{0:T(128)S(6)} %copy.14.live_ref, s32[1536]{0:T(1024)S(1)} %fusion.7.entries_ref, bf16[16,128]{1,0:T(8,128)(2,1)S(1)} %slice_bitcast_fusion.3.after_ref), custom_call_target="tpu_custom_call" | custom-call | tf_op jit(solution)/shard_map/bins/pallas_call | solution.py:266
  39.7 3.2 %rows.1 = (f32[64,128,128]{2,1,0:T(8,128)S(1)}, f32[64,128,128]{2,1,0:T(8,128)S(1)}, f32[32,1024]{1,0:T(8,128)S(1)}) custom-call(bf16[272,128]{1,0:T(8,128)(2,1)S(1)} %pack.1.own_ref, bf16[8,272,128]{2,1,0:T(8,128)(2,1)S(1)} %constant_dynamic-update-slice_fusion.near_ref), custom_call_target="tpu_custom_call" | custom-call | tf_op jit(solution)/shard_map/rows/pallas_call | solution.py:275
  43.1 2.1 %collective-permute-start.12 = (bf16[4,272,128]{2,1,0:T(8,128)(2,1)S(1)}, bf16[4,272,128]{2,1,0:T(8,128)(2,1)S(1)}, u32[]{:S(2)}, u32[]{:S(2)}) collective-permute-start(bf16[4,272,128]{2,1,0:T(8,128)(2,1)S(1)} %pad_maximum_fusion.5), channel_id=1, source_target_pairs={{0,8},{8,16},{16,24},{24,0},{1,9},{9,17},{17,25},{25,1},{2,10},{10... | collective-permute-start | bytes 835592 | tf_op jit(solution)/shard_map/ppermute | solution.py:248
  45.4 28.9 %pairs.3 = (f32[64,32,128]{2,1,0:T(8,128)S(1)}, bf16[8,256,128]{2,1,0:T(8,128)(2,1)S(1)}, bf16[8,256,128]{2,1,0:T(8,128)(2,1)S(1)}) custom-call(s32[1]{0:T(128)} %bitcast.5.place_ref, s32[3]{0:T(128)S(1)} %get-tuple-element.25.count_ref, s32[4704]{0:T(1024)S(1)} %get-tuple-element.29.bins_ref, ...), custom_call_target="tpu_custom_call" | custom-call | tf_op jit(solution)/shard_map/pairs/pallas_call | solution.py:298
  76.5 14.9 %pairs.4 = (f32[64,32,128]{2,1,0:T(8,128)S(1)}, bf16[8,256,128]{2,1,0:T(8,128)(2,1)S(1)}) custom-call(s32[1]{0:T(128)} %bitcast.5.place_ref, s32[3]{0:T(128)S(1)} %get-tuple-element.25.count_ref, s32[4704]{0:T(1024)S(1)} %get-tuple-element.29.bins_ref, ...), custom_call_target="tpu_custom_call", output_to_operand_aliasing={{0}: (7, {})} | custom-call | tf_op jit(solution)/shard_map/pairs/pallas_call | solution.py:298
  91.6 14.3 %pairs.5 = (f32[64,32,128]{2,1,0:T(8,128)S(1)}, bf16[8,256,128]{2,1,0:T(8,128)(2,1)S(1)}, bf16[8,256,128]{2,1,0:T(8,128)(2,1)S(1)}) custom-call(s32[1]{0:T(128)} %bitcast.5.place_ref, s32[3]{0:T(128)S(1)} %get-tuple-element.25.count_ref, s32[4704]{0:T(1024)S(1)} %get-tuple-element.29.bins_ref, ...), custom_call_target="tpu_custom_call", output_to_operand_aliasing={{0}: (7, {})} | custom-call | tf_op jit(solution)/shard_map/pairs/pallas_call | solution.py:298
  107.2 6.5 %all-to-all-start = ((bf16[8,256,128]{2,1,0:T(8,128)(2,1)}), bf16[8,256,128]{2,1,0:T(8,128)(2,1)S(1)}, u32[]{:S(2)}, u32[]{:S(2)}) async-start(bf16[8,256,128]{2,1,0:T(8,128)(2,1)} %add.142), calls=%async_computation | async-start | bytes 1048576 | tf_op jit(solution)/shard_map/all_to_all | solution.py:322
  113.8 2.2 %collective-permute-start.17 = (bf16[256,128]{1,0:T(8,128)(2,1)S(1)}, bf16[256,128]{1,0:T(8,128)(2,1)S(1)}, u32[]{:S(2)}, u32[]{:S(2)}) collective-permute-start(bf16[256,128]{1,0:T(8,128)(2,1)S(1)} %get-tuple-element.51), channel_id=1, source_target_pairs={{0,2},{2,4},{4,6},{6,0},{1,3},{3,5},{5,7},{7,1},{8,10},{10,12},{12... | collective-permute-start | bytes 196616 | tf_op jit(solution)/shard_map/ppermute | solution.py:325
  116.0 3.5 %collective-permute-start.16 = (bf16[256,128]{1,0:T(8,128)(2,1)S(1)}, bf16[256,128]{1,0:T(8,128)(2,1)S(1)}, u32[]{:S(2)}, u32[]{:S(2)}) collective-permute-start(bf16[256,128]{1,0:T(8,128)(2,1)S(1)} %get-tuple-element.52), channel_id=1, source_target_pairs={{0,4},{2,6},{4,0},{6,2},{1,5},{3,7},{5,1},{7,3},{8,12},{10,14},{12... | collective-permute-start | bytes 196616 | tf_op jit(solution)/shard_map/ppermute | solution.py:325
  119.5 2.5 %collective-permute-start.15 = (bf16[256,128]{1,0:T(8,128)(2,1)S(1)}, bf16[256,128]{1,0:T(8,128)(2,1)S(1)}, u32[]{:S(2)}, u32[]{:S(2)}) collective-permute-start(bf16[256,128]{1,0:T(8,128)(2,1)S(1)} %get-tuple-element.53), channel_id=1, source_target_pairs={{0,6},{2,0},{4,2},{6,4},{1,7},{3,1},{5,3},{7,5},{8,14},{10,8},{12,... | collective-permute-start | bytes 196616 | tf_op jit(solution)/shard_map/ppermute | solution.py:325
  124.0 5.5 %all-to-all-done.col_ref = bf16[8,256,128]{2,1,0:T(8,128)(2,1)S(1)} async-done(((bf16[8,256,128]{2,1,0:T(8,128)(2,1)}), bf16[8,256,128]{2,1,0:T(8,128)(2,1)S(1)}, u32[]{:S(2)}, u32[]{:S(2)}) %all-to-all-start) | async-done | bytes 524320 | tf_op jit(solution)/shard_map/all_to_all | solution.py:322
  131.6 3.8 %collective-permute-start.24 = (f32[40,128]{1,0:T(8,128)S(1)}, f32[40,128]{1,0:T(8,128)S(1)}, u32[]{:S(2)}, u32[]{:S(2)}) collective-permute-start(f32[40,128]{1,0:T(8,128)S(1)} %add.70), channel_id=1, source_target_pairs={{0,6},{2,0},{4,2},{6,4},{1,7},{3,1},{5,3},{7,5},{8,14},{10,8},{12,... | collective-permute-start | bytes 61448 | tf_op jit(solution)/shard_map/ppermute | solution.py:234
  135.3 3.0 %collective-permute-start.23 = (f32[40,128]{1,0:T(8,128)S(1)}, f32[40,128]{1,0:T(8,128)S(1)}, u32[]{:S(2)}, u32[]{:S(2)}) collective-permute-start(f32[40,128]{1,0:T(8,128)S(1)} %add.70), channel_id=1, source_target_pairs={{0,4},{2,6},{4,0},{6,2},{1,5},{3,7},{5,1},{7,3},{8,12},{10,14},{12... | collective-permute-start | bytes 61448 | tf_op jit(solution)/shard_map/ppermute | solution.py:234
  138.3 2.3 %collective-permute-done.23 = f32[40,128]{1,0:T(8,128)S(1)} collective-permute-done((f32[40,128]{1,0:T(8,128)S(1)}, f32[40,128]{1,0:T(8,128)S(1)}, u32[]{:S(2)}, u32[]{:S(2)}) %collective-permute-start.23) | collective-permute-done | bytes 20512 | tf_op jit(solution)/shard_map/ppermute | solution.py:234
  142.1 5.4 %collective-permute-start.27 = (f32[40,128]{1,0:T(8,128)S(1)}, f32[40,128]{1,0:T(8,128)S(1)}, u32[]{:S(2)}, u32[]{:S(2)}) collective-permute-start(f32[40,128]{1,0:T(8,128)S(1)} %add_add_fusion.2), channel_id=1, source_target_pairs={{0,24},{8,0},{16,8},{24,16},{1,25},{9,1},{17,9},{25,17},{2,26},{10... | collective-permute-start | bytes 61448 | tf_op jit(solution)/shard_map/ppermute | solution.py:234
  149.0 3.8 %collective-permute-done.26 = f32[40,128]{1,0:T(8,128)S(1)} collective-permute-done((f32[40,128]{1,0:T(8,128)S(1)}, f32[40,128]{1,0:T(8,128)S(1)}, u32[]{:S(2)}, u32[]{:S(2)}) %collective-permute-start.26) | collective-permute-done | bytes 20512 | tf_op jit(solution)/shard_map/ppermute | solution.py:234
  153.4 7.2 %collective-permute-done.28 = f32[40,128]{1,0:T(8,128)S(1)} collective-permute-done((f32[40,128]{1,0:T(8,128)S(1)}, f32[40,128]{1,0:T(8,128)S(1)}, u32[]{:S(2)}, u32[]{:S(2)}) %collective-permute-start.28) | collective-permute-done | bytes 20512 | tf_op jit(solution)/shard_map/ppermute | solution.py:339
  163.9 3.5 %collective-permute-done.31 = f32[40,128]{1,0:T(8,128)S(1)} collective-permute-done((f32[40,128]{1,0:T(8,128)S(1)}, f32[40,128]{1,0:T(8,128)S(1)}, u32[]{:S(2)}, u32[]{:S(2)}) %collective-permute-start.31) | collective-permute-done | bytes 20512 | tf_op jit(solution)/shard_map/ppermute | solution.py:234
  167.7 4.7 %solve.1 = (f32[32,1024]{1,0:T(8,128)}, f32[32,1024]{1,0:T(8,128)}, f32[32,1024]{1,0:T(8,128)}) custom-call(f32[40,128]{1,0:T(8,128)S(1)} %add_add_fusion.gram_ref, f32[32,1024]{1,0:T(8,128)S(1)} %copy-done.3, f32[32,1024]{1,0:T(8,128)S(1)} %copy-done.2, f32[32,1024]{1,0:T(8,128)S(1)} %copy-done.1, f32[32,1024]{1,0:T(8,128)S(1)} %get-tuple-element.42.image_ref), custom_call_target="tpu_custom_call" | custom-call | tf_op jit(solution)/shard_map/solve/pallas_call | solution.py:341
  (92 shorter events, 22.4 us)
Async XLA Ops:
  2.2 11.6 %collective-permute-start.3 = (bf16[272,128]{1,0:T(8,128)(2,1)S(1)}, bf16[272,128]{1,0:T(8,128)(2,1)S(1)}, u32[]{:S(2)}, u32[]{:S(2)}) collective-permute-start(bf16[272,128]{1,0:T(8,128)(2,1)S(1)} %pack.1.own_ref), channel_id=1, source_target_pairs={{0,128},{32,160},{64,192},{96,224},{128,0},{160,32},{192,64},{224,... | collective-permute-start | bytes 208904 | tf_op jit(solution)/shard_map/ppermute | solution.py:248
  9.5 7.1 %collective-permute-start.2 = (bf16[272,128]{1,0:T(8,128)(2,1)S(1)}, bf16[272,128]{1,0:T(8,128)(2,1)S(1)}, u32[]{:S(2)}, u32[]{:S(2)}) collective-permute-start(bf16[272,128]{1,0:T(8,128)(2,1)S(1)} %pack.1.own_ref), channel_id=1, source_target_pairs={{0,6},{2,0},{4,2},{6,4},{1,7},{3,1},{5,3},{7,5},{8,14},{10,8},{12,... | collective-permute-start | bytes 208904 | tf_op jit(solution)/shard_map/ppermute | solution.py:234
  10.0 8.1 %collective-permute-start.1 = (bf16[272,128]{1,0:T(8,128)(2,1)S(1)}, bf16[272,128]{1,0:T(8,128)(2,1)S(1)}, u32[]{:S(2)}, u32[]{:S(2)}) collective-permute-start(bf16[272,128]{1,0:T(8,128)(2,1)S(1)} %pack.1.own_ref), channel_id=1, source_target_pairs={{0,4},{2,6},{4,0},{6,2},{1,5},{3,7},{5,1},{7,3},{8,12},{10,14},{12... | collective-permute-start | bytes 208904 | tf_op jit(solution)/shard_map/ppermute | solution.py:234
  12.9 6.8 %collective-permute-start = (bf16[272,128]{1,0:T(8,128)(2,1)S(1)}, bf16[272,128]{1,0:T(8,128)(2,1)S(1)}, u32[]{:S(2)}, u32[]{:S(2)}) collective-permute-start(bf16[272,128]{1,0:T(8,128)(2,1)S(1)} %pack.1.own_ref), channel_id=1, source_target_pairs={{0,2},{2,4},{4,6},{6,0},{1,3},{3,5},{5,7},{7,1},{8,10},{10,12},{12... | collective-permute-start | bytes 208904 | tf_op jit(solution)/shard_map/ppermute | solution.py:234
  13.9 7.6 %collective-permute-start.6 = (bf16[2,272,128]{2,1,0:T(8,128)(2,1)S(1)}, bf16[2,272,128]{2,1,0:T(8,128)(2,1)S(1)}, u32[]{:S(2)}, u32[]{:S(2)}) collective-permute-start(bf16[2,272,128]{2,1,0:T(8,128)(2,1)S(1)} %pad_maximum_fusion.8), channel_id=1, source_target_pairs={{0,224},{32,0},{64,32},{96,64},{128,96},{160,128},{192,160},{224,1... | collective-permute-start | bytes 417800 | tf_op jit(solution)/shard_map/ppermute | solution.py:248
  16.6 10.2 %collective-permute-start.5 = (bf16[2,272,128]{2,1,0:T(8,128)(2,1)S(1)}, bf16[2,272,128]{2,1,0:T(8,128)(2,1)S(1)}, u32[]{:S(2)}, u32[]{:S(2)}) collective-permute-start(bf16[2,272,128]{2,1,0:T(8,128)(2,1)S(1)} %pad_maximum_fusion.8), channel_id=1, source_target_pairs={{0,64},{32,96},{64,128},{96,160},{128,192},{160,224},{192,0},{224,... | collective-permute-start | bytes 417800 | tf_op jit(solution)/shard_map/ppermute | solution.py:248
  16.6 10.3 %collective-permute-start.4 = (bf16[2,272,128]{2,1,0:T(8,128)(2,1)S(1)}, bf16[2,272,128]{2,1,0:T(8,128)(2,1)S(1)}, u32[]{:S(2)}, u32[]{:S(2)}) collective-permute-start(bf16[2,272,128]{2,1,0:T(8,128)(2,1)S(1)} %pad_maximum_fusion.8), channel_id=1, source_target_pairs={{0,32},{32,64},{64,96},{96,128},{128,160},{160,192},{192,224},{224... | collective-permute-start | bytes 417800 | tf_op jit(solution)/shard_map/ppermute | solution.py:248
  18.1 21.5 %collective-permute-start.11 = (bf16[2,272,128]{2,1,0:T(8,128)(2,1)S(1)}, bf16[2,272,128]{2,1,0:T(8,128)(2,1)S(1)}, u32[]{:S(2)}, u32[]{:S(2)}) collective-permute-start(bf16[2,272,128]{2,1,0:T(8,128)(2,1)S(1)} %pad_maximum_fusion.8), channel_id=1, source_target_pairs={{0,8},{8,16},{16,24},{24,0},{1,9},{9,17},{17,25},{25,1},{2,10},{10... | collective-permute-start | bytes 417800 | tf_op jit(solution)/shard_map/ppermute | solution.py:248
  19.7 10.1 %collective-permute-start.8 = (bf16[2,272,128]{2,1,0:T(8,128)(2,1)S(1)}, bf16[2,272,128]{2,1,0:T(8,128)(2,1)S(1)}, u32[]{:S(2)}, u32[]{:S(2)}) collective-permute-start(bf16[2,272,128]{2,1,0:T(8,128)(2,1)S(1)} %pad_maximum_fusion.8), channel_id=1, source_target_pairs={{0,24},{8,0},{16,8},{24,16},{1,25},{9,1},{17,9},{25,17},{2,26},{10... | collective-permute-start | bytes 417800 | tf_op jit(solution)/shard_map/ppermute | solution.py:248
  26.9 16.0 %collective-permute-start.10 = (bf16[6,272,128]{2,1,0:T(8,128)(2,1)S(1)}, bf16[6,272,128]{2,1,0:T(8,128)(2,1)S(1)}, u32[]{:S(2)}, u32[]{:S(2)}) collective-permute-start(bf16[6,272,128]{2,1,0:T(8,128)(2,1)S(1)} %pad_maximum_fusion.3), channel_id=1, source_target_pairs={{0,24},{8,0},{16,8},{24,16},{1,25},{9,1},{17,9},{25,17},{2,26},{10... | collective-permute-start | bytes 1253384 | tf_op jit(solution)/shard_map/ppermute | solution.py:248
  29.8 13.1 %collective-permute-start.9 = (bf16[6,272,128]{2,1,0:T(8,128)(2,1)S(1)}, bf16[6,272,128]{2,1,0:T(8,128)(2,1)S(1)}, u32[]{:S(2)}, u32[]{:S(2)}) collective-permute-start(bf16[6,272,128]{2,1,0:T(8,128)(2,1)S(1)} %pad_maximum_fusion.3), channel_id=1, source_target_pairs={{0,8},{8,16},{16,24},{24,0},{1,9},{9,17},{17,25},{25,1},{2,10},{10... | collective-permute-start | bytes 1253384 | tf_op jit(solution)/shard_map/ppermute | solution.py:248
  29.8 9.8 %collective-permute-start.7 = (bf16[4,272,128]{2,1,0:T(8,128)(2,1)S(1)}, bf16[4,272,128]{2,1,0:T(8,128)(2,1)S(1)}, u32[]{:S(2)}, u32[]{:S(2)}) collective-permute-start(bf16[4,272,128]{2,1,0:T(8,128)(2,1)S(1)} %pad_maximum_fusion.4), channel_id=1, source_target_pairs={{0,1},{1,0},{2,3},{3,2},{4,5},{5,4},{6,7},{7,6},{8,9},{9,8},{10,11... | collective-permute-start | bytes 835592 | tf_op jit(solution)/shard_map/ppermute | solution.py:238
  43.0 33.4 %collective-permute-start.13 = (bf16[4,272,128]{2,1,0:T(8,128)(2,1)S(1)}, bf16[4,272,128]{2,1,0:T(8,128)(2,1)S(1)}, u32[]{:S(2)}, u32[]{:S(2)}) collective-permute-start(bf16[4,272,128]{2,1,0:T(8,128)(2,1)S(1)} %pad_maximum_fusion.6), channel_id=1, source_target_pairs={{0,24},{8,0},{16,8},{24,16},{1,25},{9,1},{17,9},{25,17},{2,26},{10... | collective-permute-start | bytes 835592 | tf_op jit(solution)/shard_map/ppermute | solution.py:248
  43.1 33.3 %collective-permute-start.12 = (bf16[4,272,128]{2,1,0:T(8,128)(2,1)S(1)}, bf16[4,272,128]{2,1,0:T(8,128)(2,1)S(1)}, u32[]{:S(2)}, u32[]{:S(2)}) collective-permute-start(bf16[4,272,128]{2,1,0:T(8,128)(2,1)S(1)} %pad_maximum_fusion.5), channel_id=1, source_target_pairs={{0,8},{8,16},{16,24},{24,0},{1,9},{9,17},{17,25},{25,1},{2,10},{10... | collective-permute-start | bytes 835592 | tf_op jit(solution)/shard_map/ppermute | solution.py:248
  74.3 31.8 %collective-permute-start.18 = (bf16[8,256,128]{2,1,0:T(8,128)(2,1)S(1)}, bf16[8,256,128]{2,1,0:T(8,128)(2,1)S(1)}, u32[]{:S(2)}, u32[]{:S(2)}) collective-permute-start(bf16[8,256,128]{2,1,0:T(8,128)(2,1)S(1)} %get-tuple-element.38), channel_id=1, source_target_pairs={{0,24},{8,0},{16,8},{24,16},{1,25},{9,1},{17,9},{25,17},{2,26},{10... | collective-permute-start | bytes 1572872 | tf_op jit(solution)/shard_map/ppermute | solution.py:248
  74.4 31.8 %collective-permute-start.20 = (bf16[8,256,128]{2,1,0:T(8,128)(2,1)S(1)}, bf16[8,256,128]{2,1,0:T(8,128)(2,1)S(1)}, u32[]{:S(2)}, u32[]{:S(2)}) collective-permute-start(bf16[8,256,128]{2,1,0:T(8,128)(2,1)S(1)} %get-tuple-element.40), channel_id=1, source_target_pairs={{0,8},{8,16},{16,24},{24,0},{1,9},{9,17},{17,25},{25,1},{2,10},{10... | collective-permute-start | bytes 1572872 | tf_op jit(solution)/shard_map/ppermute | solution.py:248
  91.5 14.7 %collective-permute-start.19 = (bf16[8,256,128]{2,1,0:T(8,128)(2,1)S(1)}, bf16[8,256,128]{2,1,0:T(8,128)(2,1)S(1)}, u32[]{:S(2)}, u32[]{:S(2)}) collective-permute-start(bf16[8,256,128]{2,1,0:T(8,128)(2,1)S(1)} %get-tuple-element.39), channel_id=1, source_target_pairs={{0,16},{8,24},{16,0},{24,8},{1,17},{9,25},{17,1},{25,9},{2,18},{10... | collective-permute-start | bytes 1572872 | tf_op jit(solution)/shard_map/ppermute | solution.py:248
  106.0 7.7 %collective-permute-start.14 = (bf16[4,256,128]{2,1,0:T(8,128)(2,1)S(1)}, bf16[4,256,128]{2,1,0:T(8,128)(2,1)S(1)}, u32[]{:S(2)}, u32[]{:S(2)}) collective-permute-start(bf16[4,256,128]{2,1,0:T(8,128)(2,1)S(1)} %slice.63), channel_id=1, source_target_pairs={{0,1},{1,0},{2,3},{3,2},{4,5},{5,4},{6,7},{7,6},{8,9},{9,8},{10,11... | collective-permute-start | bytes 786440 | tf_op jit(solution)/shard_map/ppermute | solution.py:238
  107.2 22.3 %all-to-all-start = ((bf16[8,256,128]{2,1,0:T(8,128)(2,1)}), bf16[8,256,128]{2,1,0:T(8,128)(2,1)S(1)}, u32[]{:S(2)}, u32[]{:S(2)}) async-start(bf16[8,256,128]{2,1,0:T(8,128)(2,1)} %add.142), calls=%async_computation | async-start | bytes 1048576 | tf_op jit(solution)/shard_map/all_to_all | solution.py:322
  113.8 8.2 %collective-permute-start.17 = (bf16[256,128]{1,0:T(8,128)(2,1)S(1)}, bf16[256,128]{1,0:T(8,128)(2,1)S(1)}, u32[]{:S(2)}, u32[]{:S(2)}) collective-permute-start(bf16[256,128]{1,0:T(8,128)(2,1)S(1)} %get-tuple-element.51), channel_id=1, source_target_pairs={{0,2},{2,4},{4,6},{6,0},{1,3},{3,5},{5,7},{7,1},{8,10},{10,12},{12... | collective-permute-start | bytes 196616 | tf_op jit(solution)/shard_map/ppermute | solution.py:325
  142.1 6.9 %collective-permute-start.27 = (f32[40,128]{1,0:T(8,128)S(1)}, f32[40,128]{1,0:T(8,128)S(1)}, u32[]{:S(2)}, u32[]{:S(2)}) collective-permute-start(f32[40,128]{1,0:T(8,128)S(1)} %add_add_fusion.2), channel_id=1, source_target_pairs={{0,24},{8,0},{16,8},{24,16},{1,25},{9,1},{17,9},{25,17},{2,26},{10... | collective-permute-start | bytes 61448 | tf_op jit(solution)/shard_map/ppermute | solution.py:234
  152.8 7.8 %collective-permute-start.28 = (f32[40,128]{1,0:T(8,128)S(1)}, f32[40,128]{1,0:T(8,128)S(1)}, u32[]{:S(2)}, u32[]{:S(2)}) collective-permute-start(f32[40,128]{1,0:T(8,128)S(1)} %add_add_fusion.1), channel_id=1, source_target_pairs={{0,128},{32,160},{64,192},{96,224},{128,0},{160,32},{192,64},{224,... | collective-permute-start | bytes 61448 | tf_op jit(solution)/shard_map/ppermute | solution.py:339
  160.6 6.8 %collective-permute-start.31 = (f32[40,128]{1,0:T(8,128)S(1)}, f32[40,128]{1,0:T(8,128)S(1)}, u32[]{:S(2)}, u32[]{:S(2)}) collective-permute-start(f32[40,128]{1,0:T(8,128)S(1)} %add.77), channel_id=1, source_target_pairs={{0,96},{32,128},{64,160},{96,192},{128,224},{160,0},{192,32},{224,... | collective-permute-start | bytes 61448 | tf_op jit(solution)/shard_map/ppermute | solution.py:234
  160.6 6.8 %collective-permute-start.30 = (f32[40,128]{1,0:T(8,128)S(1)}, f32[40,128]{1,0:T(8,128)S(1)}, u32[]{:S(2)}, u32[]{:S(2)}) collective-permute-start(f32[40,128]{1,0:T(8,128)S(1)} %add.77), channel_id=1, source_target_pairs={{0,64},{32,96},{64,128},{96,160},{128,192},{160,224},{192,0},{224,... | collective-permute-start | bytes 61448 | tf_op jit(solution)/shard_map/ppermute | solution.py:234
  (14 other events, 130.6 us)

commit v9 on v8

--- a/solution.py
+++ b/solution.py
@@ -46,22 +46,22 @@
 def bin_kernel(live_ref, entries_ref, after_ref, bins_ref, count_ref):
     live = live_ref[0]
 
-    def put(e, ends):
+    def put(e, entry, ends):
         first, second = ends
-        entry = entries_ref[e]
         bins_ref[first] = entry
         bins_ref[LIST + second] = entry
         bins_ref[2 * LIST + e - first - second] = entry
         return first + ((entry >> 16) & 1), second + ((entry >> 17) & 1)
 
     def step(i, ends):
-        for u in range(8):
-            ends = put(i * 8 + u, ends)
+        entries = [entries_ref[i * 16 + u] for u in range(16)]
+        for u in range(16):
+            ends = put(i * 16 + u, entries[u], ends)
         return ends
 
-    groups = live >> 3
+    groups = live >> 4
     ends = lax.fori_loop(0, groups, step, (jnp.int32(0), jnp.int32(0)))
-    first, second = lax.fori_loop(groups * 8, live, put, ends)
+    first, second = lax.fori_loop(groups * 16, live, lambda e, ends: put(e, entries_ref[e], ends), ends)
     for part, end in enumerate((first, second, live - first - second)):
         count_ref[part] = end
         for j in range(TAIL):
@@ -336,8 +336,8 @@
     gram = gram + swap(gram)
     gram = sum(shifts(gram, "y", 4), gram)
     gram = sum(shifts(gram, "x", 4), gram)
-    gram = gram + lax.ppermute(gram, "z", [(i, (i + 4) % 8) for i in range(8)])
-    gram = sum(shifts(gram, "z", 8)[:3], gram)
+    gram = gram + moved(gram, "z", 8, 1)
+    gram = sum([moved(gram, "z", 8, shift) for shift in (4, 2, -2)], gram)
     return pl.pallas_call(
         solve_kernel,
         out_shape=(shape((PROBES, own_points), f32),) * 3,

time: 172 us -> 173 us (level)
  waiting for transfers between devices: 33.1 us -> 41.2 us
  starting transfers between devices: 56.6 us -> 49.1 us
    ppermute x13 -> x17, waiting for transfers between devices: 5.44 us -> 17.4 us  [moved(): lax.ppermute(value, axis, [(i, (i + shift) % size) for i in range(size)])]
    ppermute x1 -> x0, waiting for transfers between devices: 7.19 us -> none  [on_device(): gram = gram + lax.ppermute(gram, 'z', [(i, (i + 4) % 8) for i in range(8)])]
    ppermute x13 -> x17, starting transfers between devices: 21.4 us -> 27.5 us  [moved(): lax.ppermute(value, axis, [(i, (i + shift) % size) for i in range(size)])]
    ppermute x12 -> x9, starting transfers between devices: 19.7 us -> 13.9 us  [shifts(): lax.ppermute(value, axis, [(i, (i + k) % size) for i in range(size)])]
    ppermute x3, starting transfers between devices: 8.24 us -> 3.34 us  [on_device(): lax.ppermute(half[k], 'y', [(i, (i - k) % 4) for i in range(4)])]
    all_to_all x1, waiting for transfers between devices: 5.5 us -> 9.69 us  [on_device(): col_parts = lax.all_to_all(sums, 'z', 0, 0)]
    ppermute x12 -> x9, waiting for transfers between devices: 11.9 us -> 8.78 us  [shifts(): lax.ppermute(value, axis, [(i, (i + k) % size) for i in range(size)])]
    all_to_all x1, starting transfers between devices: 6.47 us -> 4.11 us  [on_device(): col_parts = lax.all_to_all(sums, 'z', 0, 0)]
  transfers between devices with their start and end apart: 33 -> 33, of which waited for: 13 -> 16; matrix products, arithmetic and copies ran while one was open for 1% -> 1% of each run, Pallas kernels for 42% -> 42%
where the time goes in v9:
time: 173 us
  Pallas kernels  77.7 us (45%)
  starting transfers between devices  49.1 us (28%)
  waiting for transfers between devices  41.2 us (24%)
  local copies, waits for them, and re-layouts  1.79 us (1%)
    pallas_call x3, Pallas kernels, pairs(): pl.pallas_call(functools.partial(part_kernel, part), out_shape=outs, in_s...  58.2 us
    ppermute x17, starting transfers between devices, moved(): lax.ppermute(value, axis, [(i, (i + shift) % size) for i in range(size)])  27.5 us
    ppermute x17, waiting for transfers between devices, moved(): lax.ppermute(value, axis, [(i, (i + shift) % size) for i in range(size)])  17.4 us
    ppermute x9, starting transfers between devices, shifts(): lax.ppermute(value, axis, [(i, (i + k) % size) for i in range(size)])  13.9 us
    pallas_call x1, Pallas kernels, on_device(): pl.pallas_call(bin_kernel, out_shape=(shape((3 * LIST,), jnp.int32), shap...  9.76 us
    all_to_all x1, waiting for transfers between devices, on_device(): col_parts = lax.all_to_all(sums, 'z', 0, 0)  9.69 us
    ppermute x9, waiting for transfers between devices, shifts(): lax.ppermute(value, axis, [(i, (i + k) % size) for i in range(size)])  8.78 us
    pallas_call x1, Pallas kernels, on_device(): pl.pallas_call(solve_kernel, out_shape=(shape((PROBES, own_points), f32),...  4.68 us
  transfers between devices with their start and end apart: 33, of which 16 were waited for; matrix products, arithmetic and copies ran while one was open for 1% of the time, Pallas kernels for 42%

profile of v9, /device:TPU:16, one launch (start us, length us, event | category | flops | bytes accessed | tf_op | source)
XLA Modules:
  0.0 173.0 jit_solution(10795998970216700909)
XLA Ops:
  2.2 7.3 %collective-permute-start.3 = (bf16[272,128]{1,0:T(8,128)(2,1)S(1)}, bf16[272,128]{1,0:T(8,128)(2,1)S(1)}, u32[]{:S(2)}, u32[]{:S(2)}) collective-permute-start(bf16[272,128]{1,0:T(8,128)(2,1)S(1)} %pack.1.own_ref), channel_id=1, source_target_pairs={{0,128},{32,160},{64,192},{96,224},{128,0},{160,32},{192,64},{224,... | collective-permute-start | bytes 208904 | tf_op jit(solution)/shard_map/ppermute | solution.py:248
  10.0 2.9 %collective-permute-start.1 = (bf16[272,128]{1,0:T(8,128)(2,1)S(1)}, bf16[272,128]{1,0:T(8,128)(2,1)S(1)}, u32[]{:S(2)}, u32[]{:S(2)}) collective-permute-start(bf16[272,128]{1,0:T(8,128)(2,1)S(1)} %pack.1.own_ref), channel_id=1, source_target_pairs={{0,4},{2,6},{4,0},{6,2},{1,5},{3,7},{5,1},{7,3},{8,12},{10,14},{12... | collective-permute-start | bytes 208904 | tf_op jit(solution)/shard_map/ppermute | solution.py:234
  13.9 2.8 %collective-permute-start.6 = (bf16[2,272,128]{2,1,0:T(8,128)(2,1)S(1)}, bf16[2,272,128]{2,1,0:T(8,128)(2,1)S(1)}, u32[]{:S(2)}, u32[]{:S(2)}) collective-permute-start(bf16[2,272,128]{2,1,0:T(8,128)(2,1)S(1)} %pad_maximum_fusion.8), channel_id=1, source_target_pairs={{0,224},{32,0},{64,32},{96,64},{128,96},{160,128},{192,160},{224,1... | collective-permute-start | bytes 417800 | tf_op jit(solution)/shard_map/ppermute | solution.py:248
  21.5 5.3 %collective-permute-done.5 = bf16[2,272,128]{2,1,0:T(8,128)(2,1)S(1)} collective-permute-done((bf16[2,272,128]{2,1,0:T(8,128)(2,1)S(1)}, bf16[2,272,128]{2,1,0:T(8,128)(2,1)S(1)}, u32[]{:S(2)}, u32[]{:S(2)}) %collective-permute-start.5) | collective-permute-done | bytes 139296 | tf_op jit(solution)/shard_map/ppermute | solution.py:248
  26.9 2.8 %collective-permute-start.10 = (bf16[6,272,128]{2,1,0:T(8,128)(2,1)S(1)}, bf16[6,272,128]{2,1,0:T(8,128)(2,1)S(1)}, u32[]{:S(2)}, u32[]{:S(2)}) collective-permute-start(bf16[6,272,128]{2,1,0:T(8,128)(2,1)S(1)} %pad_maximum_fusion.3), channel_id=1, source_target_pairs={{0,24},{8,0},{16,8},{24,16},{1,25},{9,1},{17,9},{25,17},{2,26},{10... | collective-permute-start | bytes 1253384 | tf_op jit(solution)/shard_map/ppermute | solution.py:248
  29.8 9.8 %bins.1 = (s32[4704]{0:T(1024)S(1)}, s32[3]{0:T(128)S(1)}) custom-call(s32[1]{0:T(128)S(6)} %copy.14.live_ref, s32[1536]{0:T(1024)S(1)} %fusion.7.entries_ref, bf16[16,128]{1,0:T(8,128)(2,1)S(1)} %slice_bitcast_fusion.3.after_ref), custom_call_target="tpu_custom_call" | custom-call | tf_op jit(solution)/shard_map/bins/pallas_call | solution.py:266
  39.7 3.2 %rows.1 = (f32[64,128,128]{2,1,0:T(8,128)S(1)}, f32[64,128,128]{2,1,0:T(8,128)S(1)}, f32[32,1024]{1,0:T(8,128)S(1)}) custom-call(bf16[272,128]{1,0:T(8,128)(2,1)S(1)} %pack.1.own_ref, bf16[8,272,128]{2,1,0:T(8,128)(2,1)S(1)} %constant_dynamic-update-slice_fusion.near_ref), custom_call_target="tpu_custom_call" | custom-call | tf_op jit(solution)/shard_map/rows/pallas_call | solution.py:275
  43.0 3.3 %collective-permute-start.13 = (bf16[4,272,128]{2,1,0:T(8,128)(2,1)S(1)}, bf16[4,272,128]{2,1,0:T(8,128)(2,1)S(1)}, u32[]{:S(2)}, u32[]{:S(2)}) collective-permute-start(bf16[4,272,128]{2,1,0:T(8,128)(2,1)S(1)} %pad_maximum_fusion.6), channel_id=1, source_target_pairs={{0,24},{8,0},{16,8},{24,16},{1,25},{9,1},{17,9},{25,17},{2,26},{10... | collective-permute-start | bytes 835592 | tf_op jit(solution)/shard_map/ppermute | solution.py:248
  46.6 28.9 %pairs.3 = (f32[64,32,128]{2,1,0:T(8,128)S(1)}, bf16[8,256,128]{2,1,0:T(8,128)(2,1)S(1)}, bf16[8,256,128]{2,1,0:T(8,128)(2,1)S(1)}) custom-call(s32[1]{0:T(128)} %bitcast.5.place_ref, s32[3]{0:T(128)S(1)} %get-tuple-element.25.count_ref, s32[4704]{0:T(1024)S(1)} %get-tuple-element.29.bins_ref, ...), custom_call_target="tpu_custom_call" | custom-call | tf_op jit(solution)/shard_map/pairs/pallas_call | solution.py:298
  75.5 1.8 %collective-permute-start.18 = (bf16[8,256,128]{2,1,0:T(8,128)(2,1)S(1)}, bf16[8,256,128]{2,1,0:T(8,128)(2,1)S(1)}, u32[]{:S(2)}, u32[]{:S(2)}) collective-permute-start(bf16[8,256,128]{2,1,0:T(8,128)(2,1)S(1)} %get-tuple-element.38), channel_id=1, source_target_pairs={{0,24},{8,0},{16,8},{24,16},{1,25},{9,1},{17,9},{25,17},{2,26},{10... | collective-permute-start | bytes 1572872 | tf_op jit(solution)/shard_map/ppermute | solution.py:248
  77.8 14.9 %pairs.4 = (f32[64,32,128]{2,1,0:T(8,128)S(1)}, bf16[8,256,128]{2,1,0:T(8,128)(2,1)S(1)}) custom-call(s32[1]{0:T(128)} %bitcast.5.place_ref, s32[3]{0:T(128)S(1)} %get-tuple-element.25.count_ref, s32[4704]{0:T(1024)S(1)} %get-tuple-element.29.bins_ref, ...), custom_call_target="tpu_custom_call", output_to_operand_aliasing={{0}: (7, {})} | custom-call | tf_op jit(solution)/shard_map/pairs/pallas_call | solution.py:298
  93.8 14.3 %pairs.5 = (f32[64,32,128]{2,1,0:T(8,128)S(1)}, bf16[8,256,128]{2,1,0:T(8,128)(2,1)S(1)}, bf16[8,256,128]{2,1,0:T(8,128)(2,1)S(1)}) custom-call(s32[1]{0:T(128)} %bitcast.5.place_ref, s32[3]{0:T(128)S(1)} %get-tuple-element.25.count_ref, s32[4704]{0:T(1024)S(1)} %get-tuple-element.29.bins_ref, ...), custom_call_target="tpu_custom_call", output_to_operand_aliasing={{0}: (7, {})} | custom-call | tf_op jit(solution)/shard_map/pairs/pallas_call | solution.py:298
  109.6 4.1 %all-to-all-start = ((bf16[8,256,128]{2,1,0:T(8,128)(2,1)}), bf16[8,256,128]{2,1,0:T(8,128)(2,1)S(1)}, u32[]{:S(2)}, u32[]{:S(2)}) async-start(bf16[8,256,128]{2,1,0:T(8,128)(2,1)} %add.142), calls=%async_computation | async-start | bytes 1048576 | tf_op jit(solution)/shard_map/all_to_all | solution.py:322
  113.9 1.8 %collective-permute-start.17 = (bf16[256,128]{1,0:T(8,128)(2,1)S(1)}, bf16[256,128]{1,0:T(8,128)(2,1)S(1)}, u32[]{:S(2)}, u32[]{:S(2)}) collective-permute-start(bf16[256,128]{1,0:T(8,128)(2,1)S(1)} %get-tuple-element.51), channel_id=1, source_target_pairs={{0,2},{2,4},{4,6},{6,0},{1,3},{3,5},{5,7},{7,1},{8,10},{10,12},{12... | collective-permute-start | bytes 196616 | tf_op jit(solution)/shard_map/ppermute | solution.py:325
  118.2 3.2 %collective-permute-done.16 = bf16[256,128]{1,0:T(8,128)(2,1)S(1)} collective-permute-done((bf16[256,128]{1,0:T(8,128)(2,1)S(1)}, bf16[256,128]{1,0:T(8,128)(2,1)S(1)}, u32[]{:S(2)}, u32[]{:S(2)}) %collective-permute-start.16) | collective-permute-done | bytes 65568 | tf_op jit(solution)/shard_map/ppermute | solution.py:325
  121.5 9.7 %all-to-all-done.col_ref = bf16[8,256,128]{2,1,0:T(8,128)(2,1)S(1)} async-done(((bf16[8,256,128]{2,1,0:T(8,128)(2,1)}), bf16[8,256,128]{2,1,0:T(8,128)(2,1)S(1)}, u32[]{:S(2)}, u32[]{:S(2)}) %all-to-all-start) | async-done | bytes 524320 | tf_op jit(solution)/shard_map/all_to_all | solution.py:322
  134.6 3.4 %collective-permute-start.23 = (f32[40,128]{1,0:T(8,128)S(1)}, f32[40,128]{1,0:T(8,128)S(1)}, u32[]{:S(2)}, u32[]{:S(2)}) collective-permute-start(f32[40,128]{1,0:T(8,128)S(1)} %add.70), channel_id=1, source_target_pairs={{0,4},{2,6},{4,0},{6,2},{1,5},{3,7},{5,1},{7,3},{8,12},{10,14},{12... | collective-permute-start | bytes 61448 | tf_op jit(solution)/shard_map/ppermute | solution.py:234
  137.9 2.0 %collective-permute-done.23 = f32[40,128]{1,0:T(8,128)S(1)} collective-permute-done((f32[40,128]{1,0:T(8,128)S(1)}, f32[40,128]{1,0:T(8,128)S(1)}, u32[]{:S(2)}, u32[]{:S(2)}) %collective-permute-start.23) | collective-permute-done | bytes 20512 | tf_op jit(solution)/shard_map/ppermute | solution.py:234
  141.7 4.8 %collective-permute-start.27 = (f32[40,128]{1,0:T(8,128)S(1)}, f32[40,128]{1,0:T(8,128)S(1)}, u32[]{:S(2)}, u32[]{:S(2)}) collective-permute-start(f32[40,128]{1,0:T(8,128)S(1)} %add_add_fusion.2), channel_id=1, source_target_pairs={{0,24},{8,0},{16,8},{24,16},{1,25},{9,1},{17,9},{25,17},{2,26},{10... | collective-permute-start | bytes 61448 | tf_op jit(solution)/shard_map/ppermute | solution.py:234
  148.1 3.8 %collective-permute-done.26 = f32[40,128]{1,0:T(8,128)S(1)} collective-permute-done((f32[40,128]{1,0:T(8,128)S(1)}, f32[40,128]{1,0:T(8,128)S(1)}, u32[]{:S(2)}, u32[]{:S(2)}) %collective-permute-start.26) | collective-permute-done | bytes 20512 | tf_op jit(solution)/shard_map/ppermute | solution.py:234
  153.2 4.5 %collective-permute-done.28 = f32[40,128]{1,0:T(8,128)S(1)} collective-permute-done((f32[40,128]{1,0:T(8,128)S(1)}, f32[40,128]{1,0:T(8,128)S(1)}, u32[]{:S(2)}, u32[]{:S(2)}) %collective-permute-start.28) | collective-permute-done | bytes 20512 | tf_op jit(solution)/shard_map/ppermute | solution.py:248
  157.7 2.9 %collective-permute-start.30 = (f32[40,128]{1,0:T(8,128)S(1)}, f32[40,128]{1,0:T(8,128)S(1)}, u32[]{:S(2)}, u32[]{:S(2)}) collective-permute-start(f32[40,128]{1,0:T(8,128)S(1)} %add.77), channel_id=1, source_target_pairs={{0,64},{32,96},{64,128},{96,160},{128,192},{160,224},{192,0},{224,... | collective-permute-start | bytes 61448 | tf_op jit(solution)/shard_map/ppermute | solution.py:248
  163.6 4.6 %collective-permute-done.29 = f32[40,128]{1,0:T(8,128)S(1)} collective-permute-done((f32[40,128]{1,0:T(8,128)S(1)}, f32[40,128]{1,0:T(8,128)S(1)}, u32[]{:S(2)}, u32[]{:S(2)}) %collective-permute-start.29) | collective-permute-done | bytes 20512 | tf_op jit(solution)/shard_map/ppermute | solution.py:248
  168.3 4.7 %solve.1 = (f32[32,1024]{1,0:T(8,128)}, f32[32,1024]{1,0:T(8,128)}, f32[32,1024]{1,0:T(8,128)}) custom-call(f32[40,128]{1,0:T(8,128)S(1)} %add_add_fusion.gram_ref, f32[32,1024]{1,0:T(8,128)S(1)} %copy-done.3, f32[32,1024]{1,0:T(8,128)S(1)} %copy-done.2, f32[32,1024]{1,0:T(8,128)S(1)} %copy-done.1, f32[32,1024]{1,0:T(8,128)S(1)} %get-tuple-element.42.image_ref), custom_call_target="tpu_custom_call" | custom-call | tf_op jit(solution)/shard_map/solve/pallas_call | solution.py:341
  (92 shorter events, 24.4 us)
Async XLA Ops:
  2.2 11.6 %collective-permute-start.3 = (bf16[272,128]{1,0:T(8,128)(2,1)S(1)}, bf16[272,128]{1,0:T(8,128)(2,1)S(1)}, u32[]{:S(2)}, u32[]{:S(2)}) collective-permute-start(bf16[272,128]{1,0:T(8,128)(2,1)S(1)} %pack.1.own_ref), channel_id=1, source_target_pairs={{0,128},{32,160},{64,192},{96,224},{128,0},{160,32},{192,64},{224,... | collective-permute-start | bytes 208904 | tf_op jit(solution)/shard_map/ppermute | solution.py:248
  9.5 7.1 %collective-permute-start.2 = (bf16[272,128]{1,0:T(8,128)(2,1)S(1)}, bf16[272,128]{1,0:T(8,128)(2,1)S(1)}, u32[]{:S(2)}, u32[]{:S(2)}) collective-permute-start(bf16[272,128]{1,0:T(8,128)(2,1)S(1)} %pack.1.own_ref), channel_id=1, source_target_pairs={{0,6},{2,0},{4,2},{6,4},{1,7},{3,1},{5,3},{7,5},{8,14},{10,8},{12,... | collective-permute-start | bytes 208904 | tf_op jit(solution)/shard_map/ppermute | solution.py:234
  10.0 8.1 %collective-permute-start.1 = (bf16[272,128]{1,0:T(8,128)(2,1)S(1)}, bf16[272,128]{1,0:T(8,128)(2,1)S(1)}, u32[]{:S(2)}, u32[]{:S(2)}) collective-permute-start(bf16[272,128]{1,0:T(8,128)(2,1)S(1)} %pack.1.own_ref), channel_id=1, source_target_pairs={{0,4},{2,6},{4,0},{6,2},{1,5},{3,7},{5,1},{7,3},{8,12},{10,14},{12... | collective-permute-start | bytes 208904 | tf_op jit(solution)/shard_map/ppermute | solution.py:234
  12.9 6.8 %collective-permute-start = (bf16[272,128]{1,0:T(8,128)(2,1)S(1)}, bf16[272,128]{1,0:T(8,128)(2,1)S(1)}, u32[]{:S(2)}, u32[]{:S(2)}) collective-permute-start(bf16[272,128]{1,0:T(8,128)(2,1)S(1)} %pack.1.own_ref), channel_id=1, source_target_pairs={{0,2},{2,4},{4,6},{6,0},{1,3},{3,5},{5,7},{7,1},{8,10},{10,12},{12... | collective-permute-start | bytes 208904 | tf_op jit(solution)/shard_map/ppermute | solution.py:234
  13.9 7.6 %collective-permute-start.6 = (bf16[2,272,128]{2,1,0:T(8,128)(2,1)S(1)}, bf16[2,272,128]{2,1,0:T(8,128)(2,1)S(1)}, u32[]{:S(2)}, u32[]{:S(2)}) collective-permute-start(bf16[2,272,128]{2,1,0:T(8,128)(2,1)S(1)} %pad_maximum_fusion.8), channel_id=1, source_target_pairs={{0,224},{32,0},{64,32},{96,64},{128,96},{160,128},{192,160},{224,1... | collective-permute-start | bytes 417800 | tf_op jit(solution)/shard_map/ppermute | solution.py:248
  16.6 10.2 %collective-permute-start.5 = (bf16[2,272,128]{2,1,0:T(8,128)(2,1)S(1)}, bf16[2,272,128]{2,1,0:T(8,128)(2,1)S(1)}, u32[]{:S(2)}, u32[]{:S(2)}) collective-permute-start(bf16[2,272,128]{2,1,0:T(8,128)(2,1)S(1)} %pad_maximum_fusion.8), channel_id=1, source_target_pairs={{0,64},{32,96},{64,128},{96,160},{128,192},{160,224},{192,0},{224,... | collective-permute-start | bytes 417800 | tf_op jit(solution)/shard_map/ppermute | solution.py:248
  16.6 10.3 %collective-permute-start.4 = (bf16[2,272,128]{2,1,0:T(8,128)(2,1)S(1)}, bf16[2,272,128]{2,1,0:T(8,128)(2,1)S(1)}, u32[]{:S(2)}, u32[]{:S(2)}) collective-permute-start(bf16[2,272,128]{2,1,0:T(8,128)(2,1)S(1)} %pad_maximum_fusion.8), channel_id=1, source_target_pairs={{0,32},{32,64},{64,96},{96,128},{128,160},{160,192},{192,224},{224... | collective-permute-start | bytes 417800 | tf_op jit(solution)/shard_map/ppermute | solution.py:248
  18.1 21.5 %collective-permute-start.11 = (bf16[2,272,128]{2,1,0:T(8,128)(2,1)S(1)}, bf16[2,272,128]{2,1,0:T(8,128)(2,1)S(1)}, u32[]{:S(2)}, u32[]{:S(2)}) collective-permute-start(bf16[2,272,128]{2,1,0:T(8,128)(2,1)S(1)} %pad_maximum_fusion.8), channel_id=1, source_target_pairs={{0,8},{8,16},{16,24},{24,0},{1,9},{9,17},{17,25},{25,1},{2,10},{10... | collective-permute-start | bytes 417800 | tf_op jit(solution)/shard_map/ppermute | solution.py:248
  19.7 10.1 %collective-permute-start.8 = (bf16[2,272,128]{2,1,0:T(8,128)(2,1)S(1)}, bf16[2,272,128]{2,1,0:T(8,128)(2,1)S(1)}, u32[]{:S(2)}, u32[]{:S(2)}) collective-permute-start(bf16[2,272,128]{2,1,0:T(8,128)(2,1)S(1)} %pad_maximum_fusion.8), channel_id=1, source_target_pairs={{0,24},{8,0},{16,8},{24,16},{1,25},{9,1},{17,9},{25,17},{2,26},{10... | collective-permute-start | bytes 417800 | tf_op jit(solution)/shard_map/ppermute | solution.py:248
  26.9 16.0 %collective-permute-start.10 = (bf16[6,272,128]{2,1,0:T(8,128)(2,1)S(1)}, bf16[6,272,128]{2,1,0:T(8,128)(2,1)S(1)}, u32[]{:S(2)}, u32[]{:S(2)}) collective-permute-start(bf16[6,272,128]{2,1,0:T(8,128)(2,1)S(1)} %pad_maximum_fusion.3), channel_id=1, source_target_pairs={{0,24},{8,0},{16,8},{24,16},{1,25},{9,1},{17,9},{25,17},{2,26},{10... | collective-permute-start | bytes 1253384 | tf_op jit(solution)/shard_map/ppermute | solution.py:248
  29.8 13.1 %collective-permute-start.9 = (bf16[6,272,128]{2,1,0:T(8,128)(2,1)S(1)}, bf16[6,272,128]{2,1,0:T(8,128)(2,1)S(1)}, u32[]{:S(2)}, u32[]{:S(2)}) collective-permute-start(bf16[6,272,128]{2,1,0:T(8,128)(2,1)S(1)} %pad_maximum_fusion.3), channel_id=1, source_target_pairs={{0,8},{8,16},{16,24},{24,0},{1,9},{9,17},{17,25},{25,1},{2,10},{10... | collective-permute-start | bytes 1253384 | tf_op jit(solution)/shard_map/ppermute | solution.py:248
  29.8 9.9 %collective-permute-start.7 = (bf16[4,272,128]{2,1,0:T(8,128)(2,1)S(1)}, bf16[4,272,128]{2,1,0:T(8,128)(2,1)S(1)}, u32[]{:S(2)}, u32[]{:S(2)}) collective-permute-start(bf16[4,272,128]{2,1,0:T(8,128)(2,1)S(1)} %pad_maximum_fusion.4), channel_id=1, source_target_pairs={{0,1},{1,0},{2,3},{3,2},{4,5},{5,4},{6,7},{7,6},{8,9},{9,8},{10,11... | collective-permute-start | bytes 835592 | tf_op jit(solution)/shard_map/ppermute | solution.py:238
  43.0 34.6 %collective-permute-start.13 = (bf16[4,272,128]{2,1,0:T(8,128)(2,1)S(1)}, bf16[4,272,128]{2,1,0:T(8,128)(2,1)S(1)}, u32[]{:S(2)}, u32[]{:S(2)}) collective-permute-start(bf16[4,272,128]{2,1,0:T(8,128)(2,1)S(1)} %pad_maximum_fusion.6), channel_id=1, source_target_pairs={{0,24},{8,0},{16,8},{24,16},{1,25},{9,1},{17,9},{25,17},{2,26},{10... | collective-permute-start | bytes 835592 | tf_op jit(solution)/shard_map/ppermute | solution.py:248
  46.3 31.3 %collective-permute-start.12 = (bf16[4,272,128]{2,1,0:T(8,128)(2,1)S(1)}, bf16[4,272,128]{2,1,0:T(8,128)(2,1)S(1)}, u32[]{:S(2)}, u32[]{:S(2)}) collective-permute-start(bf16[4,272,128]{2,1,0:T(8,128)(2,1)S(1)} %pad_maximum_fusion.5), channel_id=1, source_target_pairs={{0,8},{8,16},{16,24},{24,0},{1,9},{9,17},{17,25},{25,1},{2,10},{10... | collective-permute-start | bytes 835592 | tf_op jit(solution)/shard_map/ppermute | solution.py:248
  75.5 32.7 %collective-permute-start.18 = (bf16[8,256,128]{2,1,0:T(8,128)(2,1)S(1)}, bf16[8,256,128]{2,1,0:T(8,128)(2,1)S(1)}, u32[]{:S(2)}, u32[]{:S(2)}) collective-permute-start(bf16[8,256,128]{2,1,0:T(8,128)(2,1)S(1)} %get-tuple-element.38), channel_id=1, source_target_pairs={{0,24},{8,0},{16,8},{24,16},{1,25},{9,1},{17,9},{25,17},{2,26},{10... | collective-permute-start | bytes 1572872 | tf_op jit(solution)/shard_map/ppermute | solution.py:248
  77.3 30.9 %collective-permute-start.20 = (bf16[8,256,128]{2,1,0:T(8,128)(2,1)S(1)}, bf16[8,256,128]{2,1,0:T(8,128)(2,1)S(1)}, u32[]{:S(2)}, u32[]{:S(2)}) collective-permute-start(bf16[8,256,128]{2,1,0:T(8,128)(2,1)S(1)} %get-tuple-element.40), channel_id=1, source_target_pairs={{0,8},{8,16},{16,24},{24,0},{1,9},{9,17},{17,25},{25,1},{2,10},{10... | collective-permute-start | bytes 1572872 | tf_op jit(solution)/shard_map/ppermute | solution.py:248
  92.7 15.8 %collective-permute-start.19 = (bf16[8,256,128]{2,1,0:T(8,128)(2,1)S(1)}, bf16[8,256,128]{2,1,0:T(8,128)(2,1)S(1)}, u32[]{:S(2)}, u32[]{:S(2)}) collective-permute-start(bf16[8,256,128]{2,1,0:T(8,128)(2,1)S(1)} %get-tuple-element.39), channel_id=1, source_target_pairs={{0,16},{8,24},{16,0},{24,8},{1,17},{9,25},{17,1},{25,9},{2,18},{10... | collective-permute-start | bytes 1572872 | tf_op jit(solution)/shard_map/ppermute | solution.py:248
  108.1 5.6 %collective-permute-start.14 = (bf16[4,256,128]{2,1,0:T(8,128)(2,1)S(1)}, bf16[4,256,128]{2,1,0:T(8,128)(2,1)S(1)}, u32[]{:S(2)}, u32[]{:S(2)}) collective-permute-start(bf16[4,256,128]{2,1,0:T(8,128)(2,1)S(1)} %slice.63), channel_id=1, source_target_pairs={{0,1},{1,0},{2,3},{3,2},{4,5},{5,4},{6,7},{7,6},{8,9},{9,8},{10,11... | collective-permute-start | bytes 786440 | tf_op jit(solution)/shard_map/ppermute | solution.py:238
  109.6 21.5 %all-to-all-start = ((bf16[8,256,128]{2,1,0:T(8,128)(2,1)}), bf16[8,256,128]{2,1,0:T(8,128)(2,1)S(1)}, u32[]{:S(2)}, u32[]{:S(2)}) async-start(bf16[8,256,128]{2,1,0:T(8,128)(2,1)} %add.142), calls=%async_computation | async-start | bytes 1048576 | tf_op jit(solution)/shard_map/all_to_all | solution.py:322
  115.7 5.8 %collective-permute-start.16 = (bf16[256,128]{1,0:T(8,128)(2,1)S(1)}, bf16[256,128]{1,0:T(8,128)(2,1)S(1)}, u32[]{:S(2)}, u32[]{:S(2)}) collective-permute-start(bf16[256,128]{1,0:T(8,128)(2,1)S(1)} %get-tuple-element.52), channel_id=1, source_target_pairs={{0,4},{2,6},{4,0},{6,2},{1,5},{3,7},{5,1},{7,3},{8,12},{10,14},{12... | collective-permute-start | bytes 196616 | tf_op jit(solution)/shard_map/ppermute | solution.py:325
  134.6 5.4 %collective-permute-start.23 = (f32[40,128]{1,0:T(8,128)S(1)}, f32[40,128]{1,0:T(8,128)S(1)}, u32[]{:S(2)}, u32[]{:S(2)}) collective-permute-start(f32[40,128]{1,0:T(8,128)S(1)} %add.70), channel_id=1, source_target_pairs={{0,4},{2,6},{4,0},{6,2},{1,5},{3,7},{5,1},{7,3},{8,12},{10,14},{12... | collective-permute-start | bytes 61448 | tf_op jit(solution)/shard_map/ppermute | solution.py:234
  141.7 6.3 %collective-permute-start.27 = (f32[40,128]{1,0:T(8,128)S(1)}, f32[40,128]{1,0:T(8,128)S(1)}, u32[]{:S(2)}, u32[]{:S(2)}) collective-permute-start(f32[40,128]{1,0:T(8,128)S(1)} %add_add_fusion.2), channel_id=1, source_target_pairs={{0,24},{8,0},{16,8},{24,16},{1,25},{9,1},{17,9},{25,17},{2,26},{10... | collective-permute-start | bytes 61448 | tf_op jit(solution)/shard_map/ppermute | solution.py:234
  157.7 6.0 %collective-permute-start.30 = (f32[40,128]{1,0:T(8,128)S(1)}, f32[40,128]{1,0:T(8,128)S(1)}, u32[]{:S(2)}, u32[]{:S(2)}) collective-permute-start(f32[40,128]{1,0:T(8,128)S(1)} %add.77), channel_id=1, source_target_pairs={{0,64},{32,96},{64,128},{96,160},{128,192},{160,224},{192,0},{224,... | collective-permute-start | bytes 61448 | tf_op jit(solution)/shard_map/ppermute | solution.py:248
  160.6 7.7 %collective-permute-start.29 = (f32[40,128]{1,0:T(8,128)S(1)}, f32[40,128]{1,0:T(8,128)S(1)}, u32[]{:S(2)}, u32[]{:S(2)}) collective-permute-start(f32[40,128]{1,0:T(8,128)S(1)} %add.77), channel_id=1, source_target_pairs={{0,128},{32,160},{64,192},{96,224},{128,0},{160,32},{192,64},{224,... | collective-permute-start | bytes 61448 | tf_op jit(solution)/shard_map/ppermute | solution.py:248
  (14 other events, 129.6 us)

commit v10 on v8

--- a/solution.py
+++ b/solution.py
@@ -43,29 +43,26 @@
     return ((remain2 * remain2) * (1.25 - remain)).astype(bf16)
 
 
-def bin_kernel(live_ref, entries_ref, after_ref, bins_ref, count_ref):
+def bin_kernel(live_ref, entries_ref, count_ref, after_ref, bins_ref):
     live = live_ref[0]
 
-    def put(e, ends):
-        first, second = ends
+    def step(i, carry):
+        entries = [entries_ref[i * 16 + u] for u in range(16)]
+        for entry in entries:
+            bins_ref[entry >> 16] = entry
+        return carry
+
+    def last(e, carry):
         entry = entries_ref[e]
-        bins_ref[first] = entry
-        bins_ref[LIST + second] = entry
-        bins_ref[2 * LIST + e - first - second] = entry
-        return first + ((entry >> 16) & 1), second + ((entry >> 17) & 1)
-
-    def step(i, ends):
-        for u in range(8):
-            ends = put(i * 8 + u, ends)
-        return ends
-
-    groups = live >> 3
-    ends = lax.fori_loop(0, groups, step, (jnp.int32(0), jnp.int32(0)))
-    first, second = lax.fori_loop(groups * 8, live, put, ends)
-    for part, end in enumerate((first, second, live - first - second)):
-        count_ref[part] = end
+        bins_ref[entry >> 16] = entry
+        return carry
+
+    groups = live >> 4
+    lax.fori_loop(0, groups, step, 0)
+    lax.fori_loop(groups * 16, live, last, 0)
+    for part in range(3):
         for j in range(TAIL):
-            bins_ref[part * LIST + end + j] = 0
+            bins_ref[part * LIST + count_ref[part] + j] = 0
 
 
 def spread(strip, t):
@@ -257,20 +254,32 @@
     row_all = jnp.concatenate([row_half, swap(row_half)], 0)
     x_own, y_own, z_own, core_own = [lax.axis_index(name).astype(jnp.int32) for name in ("x", "y", "z", "core")]
     place = z_own.reshape(1)
+    tile_pairs, counted, pair_above, row_half = lax.optimization_barrier((tile_pairs, pair_count, pair_above, row_half))
     a, b = tile_pairs[0], tile_pairs[1]
     near_slot = ((y_own - (a >> 4)) & 3) + ((((a >> 3) & 1) ^ core_own) << 2)
     x_far = (x_own - (b >> 3)) & 3
     far_slot = z_slot((z_own - (b >> 5)) & 7) + jnp.where(x_far == 3, 8, 0)
     entries = (near_slot << 3) + (a & 7) + (far_slot << 11) + ((b & 7) << 8)
-    entries = entries + ((x_far & 1) << 16) + jnp.where(x_far == 2, 1 << 17, 0)
-    bins, counts = pl.pallas_call(
+    part = jnp.where(x_far == 2, 1, jnp.where(x_far == 0, 2, 0))
+    part = jnp.where(jnp.arange(part.shape[0], dtype=jnp.int32) < counted[0], part, 3).reshape(-1, TILE)
+    hot = (part[None] == jnp.arange(3, dtype=jnp.int32)[:, None, None]).astype(bf16)
+    ahead = jnp.triu(jnp.ones((TILE, TILE), bf16), 1)
+    rows = hot.shape[1]
+    ahead_row = jnp.einsum("prl,lm->prm", hot, ahead, preferred_element_type=f32)
+    row_count = jnp.sum(hot.astype(f32), 2)
+    ahead_rows = jnp.sum(row_count[:, :, None] * jnp.triu(jnp.ones((rows, rows), f32), 1)[None], 1)
+    spot = ahead_row + ahead_rows[:, :, None] + (jnp.arange(3, dtype=jnp.int32) * LIST).astype(f32)[:, None, None]
+    spot = jnp.sum(hot.astype(f32) * spot, 0).astype(jnp.int32).reshape(-1)
+    entries = entries + (spot << 16)
+    counts = jnp.sum(row_count, 1).astype(jnp.int32)
+    bins = pl.pallas_call(
         bin_kernel,
-        out_shape=(shape((3 * LIST,), jnp.int32), shape((3,), jnp.int32)),
-        in_specs=[SMEM, SMEM, VMEM],
-        out_specs=(SMEM, SMEM),
+        out_shape=shape((3 * LIST,), jnp.int32),
+        in_specs=[SMEM, SMEM, SMEM, VMEM],
+        out_specs=SMEM,
         compiler_params=SMALL,
         name="bins",
-    )(pair_count, entries, pair_above[0, :16])
+    )(pair_count, entries, counts, pair_above[0, :16])
     spread_shape = shape((64, TILE, TILE), f32)
     px, py, own_product = pl.pallas_call(
         row_kernel,

time: 172 us -> 171 us (level)
  waiting for transfers between devices: 33.1 us -> 43 us
  starting transfers between devices: 56.6 us -> 50.3 us
  Pallas kernels: 77.7 us -> 72.4 us
    pallas_call x1, Pallas kernels: 9.75 us -> 4.03 us  [on_device(): pl.pallas_call(bin_kernel, out_shape=shape((3 * LIST,), jnp.int32), in_sp...]
    all_to_all x1, waiting for transfers between devices: 5.5 us -> 10.5 us  [on_device(): col_parts = lax.all_to_all(sums, 'z', 0, 0)]
    ppermute x3, starting transfers between devices: 8.24 us -> 3.35 us  [on_device(): lax.ppermute(half[k], 'y', [(i, (i - k) % 4) for i in range(4)])]
    ppermute x13, waiting for transfers between devices: 5.44 us -> 8.19 us  [moved(): lax.ppermute(value, axis, [(i, (i + shift) % size) for i in range(size)])]
    ppermute x3, waiting for transfers between devices: 1.9 us -> 4.11 us  [on_device(): lax.ppermute(half[k], 'y', [(i, (i - k) % 4) for i in range(4)])]
    all_to_all x1, starting transfers between devices: 6.47 us -> 4.62 us  [on_device(): col_parts = lax.all_to_all(sums, 'z', 0, 0)]
  transfers between devices with their start and end apart: 33 -> 33, of which waited for: 13 -> 16; matrix products, arithmetic and copies ran while one was open for 1% -> 1% of each run, Pallas kernels for 42% -> 39%
where the time goes in v10:
time: 171 us; the launch traced here: 170 us
  Pallas kernels  72.4 us (42%)
  starting transfers between devices  50.3 us (29%)
  waiting for transfers between devices  43 us (25%)
  local copies, waits for them, and re-layouts  1.79 us (1%)
    pallas_call x3, Pallas kernels, pairs(): pl.pallas_call(functools.partial(part_kernel, part), out_shape=outs, in_s...  58.6 us
    ppermute x13, starting transfers between devices, moved(): lax.ppermute(value, axis, [(i, (i + shift) % size) for i in range(size)])  22 us
    ppermute x12, starting transfers between devices, shifts(): lax.ppermute(value, axis, [(i, (i + k) % size) for i in range(size)])  19.1 us
    ppermute x12, waiting for transfers between devices, shifts(): lax.ppermute(value, axis, [(i, (i + k) % size) for i in range(size)])  11.9 us
    all_to_all x1, waiting for transfers between devices, on_device(): col_parts = lax.all_to_all(sums, 'z', 0, 0)  10.5 us
    ppermute x13, waiting for transfers between devices, moved(): lax.ppermute(value, axis, [(i, (i + shift) % size) for i in range(size)])  8.19 us
    ppermute x1, waiting for transfers between devices, on_device(): gram = gram + lax.ppermute(gram, 'z', [(i, (i + 4) % 8) for i in range(8)])  7.19 us
    pallas_call x1, Pallas kernels, on_device(): pl.pallas_call(solve_kernel, out_shape=(shape((PROBES, own_points), f32),...  4.68 us
  transfers between devices with their start and end apart: 33, of which 16 were waited for; matrix products, arithmetic and copies ran while one was open for 1% of the time, Pallas kernels for 39%

profile of v10, /device:TPU:16, one launch (start us, length us, event | category | flops | bytes accessed | tf_op | source)
XLA Modules:
  0.0 170.2 jit_solution(873602641749009257)
XLA Ops:
  2.2 7.3 %collective-permute-start.3 = (bf16[272,128]{1,0:T(8,128)(2,1)S(1)}, bf16[272,128]{1,0:T(8,128)(2,1)S(1)}, u32[]{:S(2)}, u32[]{:S(2)}) collective-permute-start(bf16[272,128]{1,0:T(8,128)(2,1)S(1)} %pack.1.own_ref), channel_id=1, source_target_pairs={{0,128},{32,160},{64,192},{96,224},{128,0},{160,32},{192,64},{224,... | collective-permute-start | bytes 208904 | tf_op jit(solution)/shard_map/ppermute | solution.py:245
  10.0 2.9 %collective-permute-start.1 = (bf16[272,128]{1,0:T(8,128)(2,1)S(1)}, bf16[272,128]{1,0:T(8,128)(2,1)S(1)}, u32[]{:S(2)}, u32[]{:S(2)}) collective-permute-start(bf16[272,128]{1,0:T(8,128)(2,1)S(1)} %pack.1.own_ref), channel_id=1, source_target_pairs={{0,4},{2,6},{4,0},{6,2},{1,5},{3,7},{5,1},{7,3},{8,12},{10,14},{12... | collective-permute-start | bytes 208904 | tf_op jit(solution)/shard_map/ppermute | solution.py:231
  12.9 3.7 %collective-permute-start.6 = (bf16[2,272,128]{2,1,0:T(8,128)(2,1)S(1)}, bf16[2,272,128]{2,1,0:T(8,128)(2,1)S(1)}, u32[]{:S(2)}, u32[]{:S(2)}) collective-permute-start(bf16[2,272,128]{2,1,0:T(8,128)(2,1)S(1)} %pad_maximum_fusion.8), channel_id=1, source_target_pairs={{0,224},{32,0},{64,32},{96,64},{128,96},{160,128},{192,160},{224,1... | collective-permute-start | bytes 417800 | tf_op jit(solution)/shard_map/ppermute | solution.py:245
  19.4 1.7 %collective-permute-start.8 = (bf16[2,272,128]{2,1,0:T(8,128)(2,1)S(1)}, bf16[2,272,128]{2,1,0:T(8,128)(2,1)S(1)}, u32[]{:S(2)}, u32[]{:S(2)}) collective-permute-start(bf16[2,272,128]{2,1,0:T(8,128)(2,1)S(1)} %pad_maximum_fusion.8), channel_id=1, source_target_pairs={{0,24},{8,0},{16,8},{24,16},{1,25},{9,1},{17,9},{25,17},{2,26},{10... | collective-permute-start | bytes 417800 | tf_op jit(solution)/shard_map/ppermute | solution.py:245
  21.2 5.6 %collective-permute-done.5 = bf16[2,272,128]{2,1,0:T(8,128)(2,1)S(1)} collective-permute-done((bf16[2,272,128]{2,1,0:T(8,128)(2,1)S(1)}, bf16[2,272,128]{2,1,0:T(8,128)(2,1)S(1)}, u32[]{:S(2)}, u32[]{:S(2)}) %collective-permute-start.5) | collective-permute-done | bytes 139296 | tf_op jit(solution)/shard_map/ppermute | solution.py:245
  26.9 2.8 %collective-permute-start.10 = (bf16[6,272,128]{2,1,0:T(8,128)(2,1)S(1)}, bf16[6,272,128]{2,1,0:T(8,128)(2,1)S(1)}, u32[]{:S(2)}, u32[]{:S(2)}) collective-permute-start(bf16[6,272,128]{2,1,0:T(8,128)(2,1)S(1)} %pad_maximum_fusion.3), channel_id=1, source_target_pairs={{0,24},{8,0},{16,8},{24,16},{1,25},{9,1},{17,9},{25,17},{2,26},{10... | collective-permute-start | bytes 1253384 | tf_op jit(solution)/shard_map/ppermute | solution.py:245
  30.3 4.0 %bins.1.bins_ref = s32[4704]{0:T(1024)S(1)} custom-call(s32[1]{0:T(128)} %copy.14.live_ref, s32[1536]{0:T(1024)S(1)} %fusion.16.entries_ref, s32[3]{0:T(128)S(1)} %convert_element_type.33.count_ref, bf16[16,128]{1,0:T(8,128)(2,1)S(1)} %slice_bitcast_fusion.3.after_ref), custom_call_target="tpu_custom_call" | custom-call | tf_op jit(solution)/shard_map/bins/pallas_call | solution.py:275
  34.5 3.2 %rows.1 = (f32[64,128,128]{2,1,0:T(8,128)S(1)}, f32[64,128,128]{2,1,0:T(8,128)S(1)}, f32[32,1024]{1,0:T(8,128)S(1)}) custom-call(bf16[272,128]{1,0:T(8,128)(2,1)S(1)} %pack.1.own_ref, bf16[8,272,128]{2,1,0:T(8,128)(2,1)S(1)} %constant_dynamic-update-slice_fusion.near_ref), custom_call_target="tpu_custom_call" | custom-call | tf_op jit(solution)/shard_map/rows/pallas_call | solution.py:284
  37.7 2.4 %collective-permute-done.9 = bf16[6,272,128]{2,1,0:T(8,128)(2,1)S(1)} collective-permute-done((bf16[6,272,128]{2,1,0:T(8,128)(2,1)S(1)}, bf16[6,272,128]{2,1,0:T(8,128)(2,1)S(1)}, u32[]{:S(2)}, u32[]{:S(2)}) %collective-permute-start.9) | collective-permute-done | bytes 417824 | tf_op jit(solution)/shard_map/ppermute | solution.py:245
  42.6 28.5 %pairs.3 = (f32[64,32,128]{2,1,0:T(8,128)S(1)}, bf16[8,256,128]{2,1,0:T(8,128)(2,1)S(1)}, bf16[8,256,128]{2,1,0:T(8,128)(2,1)S(1)}) custom-call(s32[1]{0:T(128)} %bitcast.5.place_ref, s32[3]{0:T(128)S(1)} %convert_element_type.33.count_ref, s32[4704]{0:T(1024)S(1)} %bins.1.bins_ref, bf16[8,272,128]{2,1,0:T(8,128)(2,1)S(1)} %constant_dynamic-update-slice_fusion.near_ref, ...), custom_call_target="tpu_custom_call" | custom-call | tf_op jit(solution)/shard_map/pairs/pallas_call | solution.py:307
  73.4 15.3 %pairs.4 = (f32[64,32,128]{2,1,0:T(8,128)S(1)}, bf16[8,256,128]{2,1,0:T(8,128)(2,1)S(1)}) custom-call(s32[1]{0:T(128)} %bitcast.5.place_ref, s32[3]{0:T(128)S(1)} %convert_element_type.33.count_ref, s32[4704]{0:T(1024)S(1)} %bins.1.bins_ref, bf16[8,272,128]{2,1,0:T(8,128)(2,1)S(1)} %constant_dynamic-update-slice_fusion.near_ref, ...), custom_call_target="tpu_custom_call", output_to_operand_aliasing={{0}: (7, {})} | custom-call | tf_op jit(solution)/shard_map/pairs/pallas_call | solution.py:307
  88.9 14.7 %pairs.5 = (f32[64,32,128]{2,1,0:T(8,128)S(1)}, bf16[8,256,128]{2,1,0:T(8,128)(2,1)S(1)}, bf16[8,256,128]{2,1,0:T(8,128)(2,1)S(1)}) custom-call(s32[1]{0:T(128)} %bitcast.5.place_ref, s32[3]{0:T(128)S(1)} %convert_element_type.33.count_ref, s32[4704]{0:T(1024)S(1)} %bins.1.bins_ref, ...), custom_call_target="tpu_custom_call", output_to_operand_aliasing={{0}: (7, {})} | custom-call | tf_op jit(solution)/shard_map/pairs/pallas_call | solution.py:307
  105.2 4.6 %all-to-all-start = ((bf16[8,256,128]{2,1,0:T(8,128)(2,1)}), bf16[8,256,128]{2,1,0:T(8,128)(2,1)S(1)}, u32[]{:S(2)}, u32[]{:S(2)}) async-start(bf16[8,256,128]{2,1,0:T(8,128)(2,1)} %add.164), calls=%async_computation | async-start | bytes 1048576 | tf_op jit(solution)/shard_map/all_to_all | solution.py:331
  111.4 2.0 %collective-permute-start.15 = (bf16[256,128]{1,0:T(8,128)(2,1)S(1)}, bf16[256,128]{1,0:T(8,128)(2,1)S(1)}, u32[]{:S(2)}, u32[]{:S(2)}) collective-permute-start(bf16[256,128]{1,0:T(8,128)(2,1)S(1)} %get-tuple-element.56), channel_id=1, source_target_pairs={{0,6},{2,0},{4,2},{6,4},{1,7},{3,1},{5,3},{7,5},{8,14},{10,8},{12,... | collective-permute-start | bytes 196616 | tf_op jit(solution)/shard_map/ppermute | solution.py:334
  114.4 2.8 %collective-permute-done.16 = bf16[256,128]{1,0:T(8,128)(2,1)S(1)} collective-permute-done((bf16[256,128]{1,0:T(8,128)(2,1)S(1)}, bf16[256,128]{1,0:T(8,128)(2,1)S(1)}, u32[]{:S(2)}, u32[]{:S(2)}) %collective-permute-start.16) | collective-permute-done | bytes 65568 | tf_op jit(solution)/shard_map/ppermute | solution.py:334
  117.5 10.5 %all-to-all-done.col_ref = bf16[8,256,128]{2,1,0:T(8,128)(2,1)S(1)} async-done(((bf16[8,256,128]{2,1,0:T(8,128)(2,1)}), bf16[8,256,128]{2,1,0:T(8,128)(2,1)S(1)}, u32[]{:S(2)}, u32[]{:S(2)}) %all-to-all-start) | async-done | bytes 524320 | tf_op jit(solution)/shard_map/all_to_all | solution.py:331
  130.1 3.4 %collective-permute-start.23 = (f32[40,128]{1,0:T(8,128)S(1)}, f32[40,128]{1,0:T(8,128)S(1)}, u32[]{:S(2)}, u32[]{:S(2)}) collective-permute-start(f32[40,128]{1,0:T(8,128)S(1)} %add.90), channel_id=1, source_target_pairs={{0,4},{2,6},{4,0},{6,2},{1,5},{3,7},{5,1},{7,3},{8,12},{10,14},{12... | collective-permute-start | bytes 61448 | tf_op jit(solution)/shard_map/ppermute | solution.py:231
  133.9 1.8 %collective-permute-done.23 = f32[40,128]{1,0:T(8,128)S(1)} collective-permute-done((f32[40,128]{1,0:T(8,128)S(1)}, f32[40,128]{1,0:T(8,128)S(1)}, u32[]{:S(2)}, u32[]{:S(2)}) %collective-permute-start.23) | collective-permute-done | bytes 20512 | tf_op jit(solution)/shard_map/ppermute | solution.py:231
  137.3 8.2 %collective-permute-start.27 = (f32[40,128]{1,0:T(8,128)S(1)}, f32[40,128]{1,0:T(8,128)S(1)}, u32[]{:S(2)}, u32[]{:S(2)}) collective-permute-start(f32[40,128]{1,0:T(8,128)S(1)} %add_add_fusion.2), channel_id=1, source_target_pairs={{0,24},{8,0},{16,8},{24,16},{1,25},{9,1},{17,9},{25,17},{2,26},{10... | collective-permute-start | bytes 61448 | tf_op jit(solution)/shard_map/ppermute | solution.py:231
  146.9 3.8 %collective-permute-done.26 = f32[40,128]{1,0:T(8,128)S(1)} collective-permute-done((f32[40,128]{1,0:T(8,128)S(1)}, f32[40,128]{1,0:T(8,128)S(1)}, u32[]{:S(2)}, u32[]{:S(2)}) %collective-permute-start.26) | collective-permute-done | bytes 20512 | tf_op jit(solution)/shard_map/ppermute | solution.py:231
  151.3 7.2 %collective-permute-done.28 = f32[40,128]{1,0:T(8,128)S(1)} collective-permute-done((f32[40,128]{1,0:T(8,128)S(1)}, f32[40,128]{1,0:T(8,128)S(1)}, u32[]{:S(2)}, u32[]{:S(2)}) %collective-permute-start.28) | collective-permute-done | bytes 20512 | tf_op jit(solution)/shard_map/ppermute | solution.py:348
  158.5 2.0 %collective-permute-start.30 = (f32[40,128]{1,0:T(8,128)S(1)}, f32[40,128]{1,0:T(8,128)S(1)}, u32[]{:S(2)}, u32[]{:S(2)}) collective-permute-start(f32[40,128]{1,0:T(8,128)S(1)} %add.97), channel_id=1, source_target_pairs={{0,64},{32,96},{64,128},{96,160},{128,192},{160,224},{192,0},{224,... | collective-permute-start | bytes 61448 | tf_op jit(solution)/shard_map/ppermute | solution.py:231
  161.8 3.5 %collective-permute-done.31 = f32[40,128]{1,0:T(8,128)S(1)} collective-permute-done((f32[40,128]{1,0:T(8,128)S(1)}, f32[40,128]{1,0:T(8,128)S(1)}, u32[]{:S(2)}, u32[]{:S(2)}) %collective-permute-start.31) | collective-permute-done | bytes 20512 | tf_op jit(solution)/shard_map/ppermute | solution.py:231
  165.6 4.7 %solve.1 = (f32[32,1024]{1,0:T(8,128)}, f32[32,1024]{1,0:T(8,128)}, f32[32,1024]{1,0:T(8,128)}) custom-call(f32[40,128]{1,0:T(8,128)S(1)} %add_add_fusion.gram_ref, f32[32,1024]{1,0:T(8,128)S(1)} %copy-done.3, f32[32,1024]{1,0:T(8,128)S(1)} %copy-done.2, f32[32,1024]{1,0:T(8,128)S(1)} %copy-done.1, f32[32,1024]{1,0:T(8,128)S(1)} %get-tuple-element.44.image_ref), custom_call_target="tpu_custom_call" | custom-call | tf_op jit(solution)/shard_map/solve/pallas_call | solution.py:350
  (100 shorter events, 21.8 us)
Async XLA Ops:
  2.2 10.6 %collective-permute-start.3 = (bf16[272,128]{1,0:T(8,128)(2,1)S(1)}, bf16[272,128]{1,0:T(8,128)(2,1)S(1)}, u32[]{:S(2)}, u32[]{:S(2)}) collective-permute-start(bf16[272,128]{1,0:T(8,128)(2,1)S(1)} %pack.1.own_ref), channel_id=1, source_target_pairs={{0,128},{32,160},{64,192},{96,224},{128,0},{160,32},{192,64},{224,... | collective-permute-start | bytes 208904 | tf_op jit(solution)/shard_map/ppermute | solution.py:245
  9.5 7.1 %collective-permute-start.2 = (bf16[272,128]{1,0:T(8,128)(2,1)S(1)}, bf16[272,128]{1,0:T(8,128)(2,1)S(1)}, u32[]{:S(2)}, u32[]{:S(2)}) collective-permute-start(bf16[272,128]{1,0:T(8,128)(2,1)S(1)} %pack.1.own_ref), channel_id=1, source_target_pairs={{0,6},{2,0},{4,2},{6,4},{1,7},{3,1},{5,3},{7,5},{8,14},{10,8},{12,... | collective-permute-start | bytes 208904 | tf_op jit(solution)/shard_map/ppermute | solution.py:231
  10.0 7.8 %collective-permute-start.1 = (bf16[272,128]{1,0:T(8,128)(2,1)S(1)}, bf16[272,128]{1,0:T(8,128)(2,1)S(1)}, u32[]{:S(2)}, u32[]{:S(2)}) collective-permute-start(bf16[272,128]{1,0:T(8,128)(2,1)S(1)} %pack.1.own_ref), channel_id=1, source_target_pairs={{0,4},{2,6},{4,0},{6,2},{1,5},{3,7},{5,1},{7,3},{8,12},{10,14},{12... | collective-permute-start | bytes 208904 | tf_op jit(solution)/shard_map/ppermute | solution.py:231
  12.9 6.5 %collective-permute-start = (bf16[272,128]{1,0:T(8,128)(2,1)S(1)}, bf16[272,128]{1,0:T(8,128)(2,1)S(1)}, u32[]{:S(2)}, u32[]{:S(2)}) collective-permute-start(bf16[272,128]{1,0:T(8,128)(2,1)S(1)} %pack.1.own_ref), channel_id=1, source_target_pairs={{0,2},{2,4},{4,6},{6,0},{1,3},{3,5},{5,7},{7,1},{8,10},{10,12},{12... | collective-permute-start | bytes 208904 | tf_op jit(solution)/shard_map/ppermute | solution.py:231
  12.9 8.3 %collective-permute-start.6 = (bf16[2,272,128]{2,1,0:T(8,128)(2,1)S(1)}, bf16[2,272,128]{2,1,0:T(8,128)(2,1)S(1)}, u32[]{:S(2)}, u32[]{:S(2)}) collective-permute-start(bf16[2,272,128]{2,1,0:T(8,128)(2,1)S(1)} %pad_maximum_fusion.8), channel_id=1, source_target_pairs={{0,224},{32,0},{64,32},{96,64},{128,96},{160,128},{192,160},{224,1... | collective-permute-start | bytes 417800 | tf_op jit(solution)/shard_map/ppermute | solution.py:245
  16.6 10.2 %collective-permute-start.5 = (bf16[2,272,128]{2,1,0:T(8,128)(2,1)S(1)}, bf16[2,272,128]{2,1,0:T(8,128)(2,1)S(1)}, u32[]{:S(2)}, u32[]{:S(2)}) collective-permute-start(bf16[2,272,128]{2,1,0:T(8,128)(2,1)S(1)} %pad_maximum_fusion.8), channel_id=1, source_target_pairs={{0,64},{32,96},{64,128},{96,160},{128,192},{160,224},{192,0},{224,... | collective-permute-start | bytes 417800 | tf_op jit(solution)/shard_map/ppermute | solution.py:245
  16.6 10.3 %collective-permute-start.4 = (bf16[2,272,128]{2,1,0:T(8,128)(2,1)S(1)}, bf16[2,272,128]{2,1,0:T(8,128)(2,1)S(1)}, u32[]{:S(2)}, u32[]{:S(2)}) collective-permute-start(bf16[2,272,128]{2,1,0:T(8,128)(2,1)S(1)} %pad_maximum_fusion.8), channel_id=1, source_target_pairs={{0,32},{32,64},{64,96},{96,128},{128,160},{160,192},{192,224},{224... | collective-permute-start | bytes 417800 | tf_op jit(solution)/shard_map/ppermute | solution.py:245
  17.8 16.6 %collective-permute-start.11 = (bf16[2,272,128]{2,1,0:T(8,128)(2,1)S(1)}, bf16[2,272,128]{2,1,0:T(8,128)(2,1)S(1)}, u32[]{:S(2)}, u32[]{:S(2)}) collective-permute-start(bf16[2,272,128]{2,1,0:T(8,128)(2,1)S(1)} %pad_maximum_fusion.8), channel_id=1, source_target_pairs={{0,8},{8,16},{16,24},{24,0},{1,9},{9,17},{17,25},{25,1},{2,10},{10... | collective-permute-start | bytes 417800 | tf_op jit(solution)/shard_map/ppermute | solution.py:245
  19.4 10.4 %collective-permute-start.8 = (bf16[2,272,128]{2,1,0:T(8,128)(2,1)S(1)}, bf16[2,272,128]{2,1,0:T(8,128)(2,1)S(1)}, u32[]{:S(2)}, u32[]{:S(2)}) collective-permute-start(bf16[2,272,128]{2,1,0:T(8,128)(2,1)S(1)} %pad_maximum_fusion.8), channel_id=1, source_target_pairs={{0,24},{8,0},{16,8},{24,16},{1,25},{9,1},{17,9},{25,17},{2,26},{10... | collective-permute-start | bytes 417800 | tf_op jit(solution)/shard_map/ppermute | solution.py:245
  26.9 10.8 %collective-permute-start.10 = (bf16[6,272,128]{2,1,0:T(8,128)(2,1)S(1)}, bf16[6,272,128]{2,1,0:T(8,128)(2,1)S(1)}, u32[]{:S(2)}, u32[]{:S(2)}) collective-permute-start(bf16[6,272,128]{2,1,0:T(8,128)(2,1)S(1)} %pad_maximum_fusion.3), channel_id=1, source_target_pairs={{0,24},{8,0},{16,8},{24,16},{1,25},{9,1},{17,9},{25,17},{2,26},{10... | collective-permute-start | bytes 1253384 | tf_op jit(solution)/shard_map/ppermute | solution.py:245
  29.8 10.4 %collective-permute-start.9 = (bf16[6,272,128]{2,1,0:T(8,128)(2,1)S(1)}, bf16[6,272,128]{2,1,0:T(8,128)(2,1)S(1)}, u32[]{:S(2)}, u32[]{:S(2)}) collective-permute-start(bf16[6,272,128]{2,1,0:T(8,128)(2,1)S(1)} %pad_maximum_fusion.3), channel_id=1, source_target_pairs={{0,8},{8,16},{16,24},{24,0},{1,9},{9,17},{17,25},{25,1},{2,10},{10... | collective-permute-start | bytes 1253384 | tf_op jit(solution)/shard_map/ppermute | solution.py:245
  40.2 33.0 %collective-permute-start.13 = (bf16[4,272,128]{2,1,0:T(8,128)(2,1)S(1)}, bf16[4,272,128]{2,1,0:T(8,128)(2,1)S(1)}, u32[]{:S(2)}, u32[]{:S(2)}) collective-permute-start(bf16[4,272,128]{2,1,0:T(8,128)(2,1)S(1)} %pad_maximum_fusion.6), channel_id=1, source_target_pairs={{0,24},{8,0},{16,8},{24,16},{1,25},{9,1},{17,9},{25,17},{2,26},{10... | collective-permute-start | bytes 835592 | tf_op jit(solution)/shard_map/ppermute | solution.py:245
  41.2 32.1 %collective-permute-start.12 = (bf16[4,272,128]{2,1,0:T(8,128)(2,1)S(1)}, bf16[4,272,128]{2,1,0:T(8,128)(2,1)S(1)}, u32[]{:S(2)}, u32[]{:S(2)}) collective-permute-start(bf16[4,272,128]{2,1,0:T(8,128)(2,1)S(1)} %pad_maximum_fusion.5), channel_id=1, source_target_pairs={{0,8},{8,16},{16,24},{24,0},{1,9},{9,17},{17,25},{25,1},{2,10},{10... | collective-permute-start | bytes 835592 | tf_op jit(solution)/shard_map/ppermute | solution.py:245
  71.1 33.0 %collective-permute-start.18 = (bf16[8,256,128]{2,1,0:T(8,128)(2,1)S(1)}, bf16[8,256,128]{2,1,0:T(8,128)(2,1)S(1)}, u32[]{:S(2)}, u32[]{:S(2)}) collective-permute-start(bf16[8,256,128]{2,1,0:T(8,128)(2,1)S(1)} %get-tuple-element.40), channel_id=1, source_target_pairs={{0,24},{8,0},{16,8},{24,16},{1,25},{9,1},{17,9},{25,17},{2,26},{10... | collective-permute-start | bytes 1572872 | tf_op jit(solution)/shard_map/ppermute | solution.py:245
  72.2 32.0 %collective-permute-start.20 = (bf16[8,256,128]{2,1,0:T(8,128)(2,1)S(1)}, bf16[8,256,128]{2,1,0:T(8,128)(2,1)S(1)}, u32[]{:S(2)}, u32[]{:S(2)}) collective-permute-start(bf16[8,256,128]{2,1,0:T(8,128)(2,1)S(1)} %get-tuple-element.42), channel_id=1, source_target_pairs={{0,8},{8,16},{16,24},{24,0},{1,9},{9,17},{17,25},{25,1},{2,10},{10... | collective-permute-start | bytes 1572872 | tf_op jit(solution)/shard_map/ppermute | solution.py:245
  88.7 15.5 %collective-permute-start.19 = (bf16[8,256,128]{2,1,0:T(8,128)(2,1)S(1)}, bf16[8,256,128]{2,1,0:T(8,128)(2,1)S(1)}, u32[]{:S(2)}, u32[]{:S(2)}) collective-permute-start(bf16[8,256,128]{2,1,0:T(8,128)(2,1)S(1)} %get-tuple-element.41), channel_id=1, source_target_pairs={{0,16},{8,24},{16,0},{24,8},{1,17},{9,25},{17,1},{25,9},{2,18},{10... | collective-permute-start | bytes 1572872 | tf_op jit(solution)/shard_map/ppermute | solution.py:245
  103.6 6.3 %collective-permute-start.14 = (bf16[4,256,128]{2,1,0:T(8,128)(2,1)S(1)}, bf16[4,256,128]{2,1,0:T(8,128)(2,1)S(1)}, u32[]{:S(2)}, u32[]{:S(2)}) collective-permute-start(bf16[4,256,128]{2,1,0:T(8,128)(2,1)S(1)} %slice.63), channel_id=1, source_target_pairs={{0,1},{1,0},{2,3},{3,2},{4,5},{5,4},{6,7},{7,6},{8,9},{9,8},{10,11... | collective-permute-start | bytes 786440 | tf_op jit(solution)/shard_map/ppermute | solution.py:235
  105.2 22.8 %all-to-all-start = ((bf16[8,256,128]{2,1,0:T(8,128)(2,1)}), bf16[8,256,128]{2,1,0:T(8,128)(2,1)S(1)}, u32[]{:S(2)}, u32[]{:S(2)}) async-start(bf16[8,256,128]{2,1,0:T(8,128)(2,1)} %add.164), calls=%async_computation | async-start | bytes 1048576 | tf_op jit(solution)/shard_map/all_to_all | solution.py:331
  111.4 5.8 %collective-permute-start.16 = (bf16[256,128]{1,0:T(8,128)(2,1)S(1)}, bf16[256,128]{1,0:T(8,128)(2,1)S(1)}, u32[]{:S(2)}, u32[]{:S(2)}) collective-permute-start(bf16[256,128]{1,0:T(8,128)(2,1)S(1)} %get-tuple-element.55), channel_id=1, source_target_pairs={{0,4},{2,6},{4,0},{6,2},{1,5},{3,7},{5,1},{7,3},{8,12},{10,14},{12... | collective-permute-start | bytes 196616 | tf_op jit(solution)/shard_map/ppermute | solution.py:334
  111.4 6.1 %collective-permute-start.15 = (bf16[256,128]{1,0:T(8,128)(2,1)S(1)}, bf16[256,128]{1,0:T(8,128)(2,1)S(1)}, u32[]{:S(2)}, u32[]{:S(2)}) collective-permute-start(bf16[256,128]{1,0:T(8,128)(2,1)S(1)} %get-tuple-element.56), channel_id=1, source_target_pairs={{0,6},{2,0},{4,2},{6,4},{1,7},{3,1},{5,3},{7,5},{8,14},{10,8},{12,... | collective-permute-start | bytes 196616 | tf_op jit(solution)/shard_map/ppermute | solution.py:334
  137.3 9.6 %collective-permute-start.27 = (f32[40,128]{1,0:T(8,128)S(1)}, f32[40,128]{1,0:T(8,128)S(1)}, u32[]{:S(2)}, u32[]{:S(2)}) collective-permute-start(f32[40,128]{1,0:T(8,128)S(1)} %add_add_fusion.2), channel_id=1, source_target_pairs={{0,24},{8,0},{16,8},{24,16},{1,25},{9,1},{17,9},{25,17},{2,26},{10... | collective-permute-start | bytes 61448 | tf_op jit(solution)/shard_map/ppermute | solution.py:231
  150.7 7.8 %collective-permute-start.28 = (f32[40,128]{1,0:T(8,128)S(1)}, f32[40,128]{1,0:T(8,128)S(1)}, u32[]{:S(2)}, u32[]{:S(2)}) collective-permute-start(f32[40,128]{1,0:T(8,128)S(1)} %add_add_fusion.1), channel_id=1, source_target_pairs={{0,128},{32,160},{64,192},{96,224},{128,0},{160,32},{192,64},{224,... | collective-permute-start | bytes 61448 | tf_op jit(solution)/shard_map/ppermute | solution.py:348
  158.5 6.8 %collective-permute-start.31 = (f32[40,128]{1,0:T(8,128)S(1)}, f32[40,128]{1,0:T(8,128)S(1)}, u32[]{:S(2)}, u32[]{:S(2)}) collective-permute-start(f32[40,128]{1,0:T(8,128)S(1)} %add.97), channel_id=1, source_target_pairs={{0,96},{32,128},{64,160},{96,192},{128,224},{160,0},{192,32},{224,... | collective-permute-start | bytes 61448 | tf_op jit(solution)/shard_map/ppermute | solution.py:231
  158.5 6.8 %collective-permute-start.30 = (f32[40,128]{1,0:T(8,128)S(1)}, f32[40,128]{1,0:T(8,128)S(1)}, u32[]{:S(2)}, u32[]{:S(2)}) collective-permute-start(f32[40,128]{1,0:T(8,128)S(1)} %add.97), channel_id=1, source_target_pairs={{0,64},{32,96},{64,128},{96,160},{128,192},{160,224},{192,0},{224,... | collective-permute-start | bytes 61448 | tf_op jit(solution)/shard_map/ppermute | solution.py:231
  (15 other events, 160.1 us)

commit v11 on v10

--- a/solution.py
+++ b/solution.py
@@ -211,10 +211,14 @@
     second = jnp.concatenate([0.5 * (norm_old + norm_old.T), unit], 1)
 
     def eliminate(table, k):
-        pivot_row = table[k : k + 1, :] / table[k : k + 1, k : k + 1]
-        return jnp.where(row == k, pivot_row, table - table[:, k : k + 1] * pivot_row)
-
-    for k in range(32):
+        upper = table[k : k + 1, :] / table[k : k + 1, k : k + 1]
+        lower = table[k + 1 : k + 2, :] - table[k + 1 : k + 2, k : k + 1] * upper
+        lower = lower / lower[:, k + 1 : k + 2]
+        upper = upper - upper[:, k + 1 : k + 2] * lower
+        others = table - table[:, k : k + 1] * upper - table[:, k + 1 : k + 2] * lower
+        return jnp.where(row == k, upper, jnp.where(row == k + 1, lower, others))
+
+    for k in range(0, 32, 2):
         first, second = eliminate(first, k), eliminate(second, k)
     alpha, inverse = first[:, 32:64], second[:, 32:64]
     cross = dot32(mixed, alpha, NN)

time: 171 us -> 170 us (level)
  transfers between devices with their start and end apart: 33 -> 33, of which waited for: 16 -> 14; matrix products, arithmetic and copies ran while one was open for 1% -> 1% of each run, Pallas kernels for 39% -> 39%
where the time goes in v11:
time: 170 us
  Pallas kernels  72.6 us (43%)
  starting transfers between devices  51.7 us (30%)
  waiting for transfers between devices  41.7 us (25%)
  local copies, waits for them, and re-layouts  1.8 us (1%)
  between operations  1.7 us (1%)
    pallas_call x3, Pallas kernels, pairs(): pl.pallas_call(functools.partial(part_kernel, part), out_shape=outs, in_s...  58.6 us
    ppermute x13, starting transfers between devices, moved(): lax.ppermute(value, axis, [(i, (i + shift) % size) for i in range(size)])  22 us
    ppermute x12, starting transfers between devices, shifts(): lax.ppermute(value, axis, [(i, (i + k) % size) for i in range(size)])  20.5 us
    ppermute x12, waiting for transfers between devices, shifts(): lax.ppermute(value, axis, [(i, (i + k) % size) for i in range(size)])  11.9 us
    all_to_all x1, waiting for transfers between devices, on_device(): col_parts = lax.all_to_all(sums, 'z', 0, 0)  9.17 us
    ppermute x13, waiting for transfers between devices, moved(): lax.ppermute(value, axis, [(i, (i + shift) % size) for i in range(size)])  8.17 us
    ppermute x1, waiting for transfers between devices, on_device(): gram = gram + lax.ppermute(gram, 'z', [(i, (i + 4) % 8) for i in range(8)])  7.13 us
    pallas_call x1, Pallas kernels, on_device(): pl.pallas_call(solve_kernel, out_shape=(shape((PROBES, own_points), f32),...  4.8 us
  transfers between devices with their start and end apart: 33, of which 14 were waited for; matrix products, arithmetic and copies ran while one was open for 1% of the time, Pallas kernels for 39%

profile of v11, /device:TPU:16, one launch (start us, length us, event | category | flops | bytes accessed | tf_op | source)
XLA Modules:
  0.0 170.5 jit_solution(5430417055760206312)
XLA Ops:
  2.2 7.3 %collective-permute-start.3 = (bf16[272,128]{1,0:T(8,128)(2,1)S(1)}, bf16[272,128]{1,0:T(8,128)(2,1)S(1)}, u32[]{:S(2)}, u32[]{:S(2)}) collective-permute-start(bf16[272,128]{1,0:T(8,128)(2,1)S(1)} %pack.1.own_ref), channel_id=1, source_target_pairs={{0,128},{32,160},{64,192},{96,224},{128,0},{160,32},{192,64},{224,... | collective-permute-start | bytes 208904 | tf_op jit(solution)/shard_map/ppermute | solution.py:249
  10.0 2.9 %collective-permute-start.1 = (bf16[272,128]{1,0:T(8,128)(2,1)S(1)}, bf16[272,128]{1,0:T(8,128)(2,1)S(1)}, u32[]{:S(2)}, u32[]{:S(2)}) collective-permute-start(bf16[272,128]{1,0:T(8,128)(2,1)S(1)} %pack.1.own_ref), channel_id=1, source_target_pairs={{0,4},{2,6},{4,0},{6,2},{1,5},{3,7},{5,1},{7,3},{8,12},{10,14},{12... | collective-permute-start | bytes 208904 | tf_op jit(solution)/shard_map/ppermute | solution.py:235
  12.9 3.7 %collective-permute-start.6 = (bf16[2,272,128]{2,1,0:T(8,128)(2,1)S(1)}, bf16[2,272,128]{2,1,0:T(8,128)(2,1)S(1)}, u32[]{:S(2)}, u32[]{:S(2)}) collective-permute-start(bf16[2,272,128]{2,1,0:T(8,128)(2,1)S(1)} %pad_maximum_fusion.8), channel_id=1, source_target_pairs={{0,224},{32,0},{64,32},{96,64},{128,96},{160,128},{192,160},{224,1... | collective-permute-start | bytes 417800 | tf_op jit(solution)/shard_map/ppermute | solution.py:249
  21.2 5.6 %collective-permute-done.5 = bf16[2,272,128]{2,1,0:T(8,128)(2,1)S(1)} collective-permute-done((bf16[2,272,128]{2,1,0:T(8,128)(2,1)S(1)}, bf16[2,272,128]{2,1,0:T(8,128)(2,1)S(1)}, u32[]{:S(2)}, u32[]{:S(2)}) %collective-permute-start.5) | collective-permute-done | bytes 139296 | tf_op jit(solution)/shard_map/ppermute | solution.py:249
  26.9 2.8 %collective-permute-start.10 = (bf16[6,272,128]{2,1,0:T(8,128)(2,1)S(1)}, bf16[6,272,128]{2,1,0:T(8,128)(2,1)S(1)}, u32[]{:S(2)}, u32[]{:S(2)}) collective-permute-start(bf16[6,272,128]{2,1,0:T(8,128)(2,1)S(1)} %pad_maximum_fusion.3), channel_id=1, source_target_pairs={{0,24},{8,0},{16,8},{24,16},{1,25},{9,1},{17,9},{25,17},{2,26},{10... | collective-permute-start | bytes 1253384 | tf_op jit(solution)/shard_map/ppermute | solution.py:249
  30.3 4.0 %bins.1.bins_ref = s32[4704]{0:T(1024)S(1)} custom-call(s32[1]{0:T(128)} %copy.14.live_ref, s32[1536]{0:T(1024)S(1)} %fusion.16.entries_ref, s32[3]{0:T(128)S(1)} %convert_element_type.33.count_ref, bf16[16,128]{1,0:T(8,128)(2,1)S(1)} %slice_bitcast_fusion.3.after_ref), custom_call_target="tpu_custom_call" | custom-call | tf_op jit(solution)/shard_map/bins/pallas_call | solution.py:279
  34.5 3.2 %rows.1 = (f32[64,128,128]{2,1,0:T(8,128)S(1)}, f32[64,128,128]{2,1,0:T(8,128)S(1)}, f32[32,1024]{1,0:T(8,128)S(1)}) custom-call(bf16[272,128]{1,0:T(8,128)(2,1)S(1)} %pack.1.own_ref, bf16[8,272,128]{2,1,0:T(8,128)(2,1)S(1)} %constant_dynamic-update-slice_fusion.near_ref), custom_call_target="tpu_custom_call" | custom-call | tf_op jit(solution)/shard_map/rows/pallas_call | solution.py:288
  37.7 2.4 %collective-permute-done.9 = bf16[6,272,128]{2,1,0:T(8,128)(2,1)S(1)} collective-permute-done((bf16[6,272,128]{2,1,0:T(8,128)(2,1)S(1)}, bf16[6,272,128]{2,1,0:T(8,128)(2,1)S(1)}, u32[]{:S(2)}, u32[]{:S(2)}) %collective-permute-start.9) | collective-permute-done | bytes 417824 | tf_op jit(solution)/shard_map/ppermute | solution.py:249
  42.6 29.7 %pairs.3 = (f32[64,32,128]{2,1,0:T(8,128)S(1)}, bf16[8,256,128]{2,1,0:T(8,128)(2,1)S(1)}, bf16[8,256,128]{2,1,0:T(8,128)(2,1)S(1)}) custom-call(s32[1]{0:T(128)} %bitcast.5.place_ref, s32[3]{0:T(128)S(1)} %convert_element_type.33.count_ref, s32[4704]{0:T(1024)S(1)} %bins.1.bins_ref, bf16[8,272,128]{2,1,0:T(8,128)(2,1)S(1)} %constant_dynamic-update-slice_fusion.near_ref, ...), custom_call_target="tpu_custom_call" | custom-call | tf_op jit(solution)/shard_map/pairs/pallas_call | solution.py:311
  72.4 2.0 %collective-permute-start.20 = (bf16[8,256,128]{2,1,0:T(8,128)(2,1)S(1)}, bf16[8,256,128]{2,1,0:T(8,128)(2,1)S(1)}, u32[]{:S(2)}, u32[]{:S(2)}) collective-permute-start(bf16[8,256,128]{2,1,0:T(8,128)(2,1)S(1)} %get-tuple-element.42), channel_id=1, source_target_pairs={{0,8},{8,16},{16,24},{24,0},{1,9},{9,17},{17,25},{25,1},{2,10},{10... | collective-permute-start | bytes 1572872 | tf_op jit(solution)/shard_map/ppermute | solution.py:249
  74.6 14.2 %pairs.4 = (f32[64,32,128]{2,1,0:T(8,128)S(1)}, bf16[8,256,128]{2,1,0:T(8,128)(2,1)S(1)}) custom-call(s32[1]{0:T(128)} %bitcast.5.place_ref, s32[3]{0:T(128)S(1)} %convert_element_type.33.count_ref, s32[4704]{0:T(1024)S(1)} %bins.1.bins_ref, bf16[8,272,128]{2,1,0:T(8,128)(2,1)S(1)} %constant_dynamic-update-slice_fusion.near_ref, ...), custom_call_target="tpu_custom_call", output_to_operand_aliasing={{0}: (7, {})} | custom-call | tf_op jit(solution)/shard_map/pairs/pallas_call | solution.py:311
  88.9 14.7 %pairs.5 = (f32[64,32,128]{2,1,0:T(8,128)S(1)}, bf16[8,256,128]{2,1,0:T(8,128)(2,1)S(1)}, bf16[8,256,128]{2,1,0:T(8,128)(2,1)S(1)}) custom-call(s32[1]{0:T(128)} %bitcast.5.place_ref, s32[3]{0:T(128)S(1)} %convert_element_type.33.count_ref, s32[4704]{0:T(1024)S(1)} %bins.1.bins_ref, ...), custom_call_target="tpu_custom_call", output_to_operand_aliasing={{0}: (7, {})} | custom-call | tf_op jit(solution)/shard_map/pairs/pallas_call | solution.py:311
  104.9 3.5 %all-to-all-start = ((bf16[8,256,128]{2,1,0:T(8,128)(2,1)}), bf16[8,256,128]{2,1,0:T(8,128)(2,1)S(1)}, u32[]{:S(2)}, u32[]{:S(2)}) async-start(bf16[8,256,128]{2,1,0:T(8,128)(2,1)} %add.164), calls=%async_computation | async-start | bytes 1048576 | tf_op jit(solution)/shard_map/all_to_all | solution.py:335
  108.5 3.2 %collective-permute-start.17 = (bf16[256,128]{1,0:T(8,128)(2,1)S(1)}, bf16[256,128]{1,0:T(8,128)(2,1)S(1)}, u32[]{:S(2)}, u32[]{:S(2)}) collective-permute-start(bf16[256,128]{1,0:T(8,128)(2,1)S(1)} %get-tuple-element.54), channel_id=1, source_target_pairs={{0,2},{2,4},{4,6},{6,0},{1,3},{3,5},{5,7},{7,1},{8,10},{10,12},{12... | collective-permute-start | bytes 196616 | tf_op jit(solution)/shard_map/ppermute | solution.py:338
  114.2 3.3 %collective-permute-done.16 = bf16[256,128]{1,0:T(8,128)(2,1)S(1)} collective-permute-done((bf16[256,128]{1,0:T(8,128)(2,1)S(1)}, bf16[256,128]{1,0:T(8,128)(2,1)S(1)}, u32[]{:S(2)}, u32[]{:S(2)}) %collective-permute-start.16) | collective-permute-done | bytes 65568 | tf_op jit(solution)/shard_map/ppermute | solution.py:338
  117.6 9.2 %all-to-all-done.col_ref = bf16[8,256,128]{2,1,0:T(8,128)(2,1)S(1)} async-done(((bf16[8,256,128]{2,1,0:T(8,128)(2,1)}), bf16[8,256,128]{2,1,0:T(8,128)(2,1)S(1)}, u32[]{:S(2)}, u32[]{:S(2)}) %all-to-all-start) | async-done | bytes 524320 | tf_op jit(solution)/shard_map/all_to_all | solution.py:335
  129.5 4.4 %collective-permute-start.23 = (f32[40,128]{1,0:T(8,128)S(1)}, f32[40,128]{1,0:T(8,128)S(1)}, u32[]{:S(2)}, u32[]{:S(2)}) collective-permute-start(f32[40,128]{1,0:T(8,128)S(1)} %add.90), channel_id=1, source_target_pairs={{0,4},{2,6},{4,0},{6,2},{1,5},{3,7},{5,1},{7,3},{8,12},{10,14},{12... | collective-permute-start | bytes 61448 | tf_op jit(solution)/shard_map/ppermute | solution.py:235
  133.9 1.9 %collective-permute-done.23 = f32[40,128]{1,0:T(8,128)S(1)} collective-permute-done((f32[40,128]{1,0:T(8,128)S(1)}, f32[40,128]{1,0:T(8,128)S(1)}, u32[]{:S(2)}, u32[]{:S(2)}) %collective-permute-start.23) | collective-permute-done | bytes 20512 | tf_op jit(solution)/shard_map/ppermute | solution.py:235
  137.6 7.9 %collective-permute-start.27 = (f32[40,128]{1,0:T(8,128)S(1)}, f32[40,128]{1,0:T(8,128)S(1)}, u32[]{:S(2)}, u32[]{:S(2)}) collective-permute-start(f32[40,128]{1,0:T(8,128)S(1)} %add_add_fusion.2), channel_id=1, source_target_pairs={{0,24},{8,0},{16,8},{24,16},{1,25},{9,1},{17,9},{25,17},{2,26},{10... | collective-permute-start | bytes 61448 | tf_op jit(solution)/shard_map/ppermute | solution.py:235
  147.1 3.8 %collective-permute-done.26 = f32[40,128]{1,0:T(8,128)S(1)} collective-permute-done((f32[40,128]{1,0:T(8,128)S(1)}, f32[40,128]{1,0:T(8,128)S(1)}, u32[]{:S(2)}, u32[]{:S(2)}) %collective-permute-start.26) | collective-permute-done | bytes 20512 | tf_op jit(solution)/shard_map/ppermute | solution.py:235
  151.5 7.1 %collective-permute-done.28 = f32[40,128]{1,0:T(8,128)S(1)} collective-permute-done((f32[40,128]{1,0:T(8,128)S(1)}, f32[40,128]{1,0:T(8,128)S(1)}, u32[]{:S(2)}, u32[]{:S(2)}) %collective-permute-start.28) | collective-permute-done | bytes 20512 | tf_op jit(solution)/shard_map/ppermute | solution.py:352
  158.7 2.0 %collective-permute-start.30 = (f32[40,128]{1,0:T(8,128)S(1)}, f32[40,128]{1,0:T(8,128)S(1)}, u32[]{:S(2)}, u32[]{:S(2)}) collective-permute-start(f32[40,128]{1,0:T(8,128)S(1)} %add.97), channel_id=1, source_target_pairs={{0,64},{32,96},{64,128},{96,160},{128,192},{160,224},{192,0},{224,... | collective-permute-start | bytes 61448 | tf_op jit(solution)/shard_map/ppermute | solution.py:235
  161.9 3.5 %collective-permute-done.31 = f32[40,128]{1,0:T(8,128)S(1)} collective-permute-done((f32[40,128]{1,0:T(8,128)S(1)}, f32[40,128]{1,0:T(8,128)S(1)}, u32[]{:S(2)}, u32[]{:S(2)}) %collective-permute-start.31) | collective-permute-done | bytes 20512 | tf_op jit(solution)/shard_map/ppermute | solution.py:235
  165.7 4.8 %solve.1 = (f32[32,1024]{1,0:T(8,128)}, f32[32,1024]{1,0:T(8,128)}, f32[32,1024]{1,0:T(8,128)}) custom-call(f32[40,128]{1,0:T(8,128)S(1)} %add_add_fusion.gram_ref, f32[32,1024]{1,0:T(8,128)S(1)} %copy-done.3, f32[32,1024]{1,0:T(8,128)S(1)} %copy-done.2, f32[32,1024]{1,0:T(8,128)S(1)} %copy-done.1, f32[32,1024]{1,0:T(8,128)S(1)} %get-tuple-element.44.image_ref), custom_call_target="tpu_custom_call" | custom-call | tf_op jit(solution)/shard_map/solve/pallas_call | solution.py:354
  (100 shorter events, 21.4 us)
Async XLA Ops:
  2.2 10.6 %collective-permute-start.3 = (bf16[272,128]{1,0:T(8,128)(2,1)S(1)}, bf16[272,128]{1,0:T(8,128)(2,1)S(1)}, u32[]{:S(2)}, u32[]{:S(2)}) collective-permute-start(bf16[272,128]{1,0:T(8,128)(2,1)S(1)} %pack.1.own_ref), channel_id=1, source_target_pairs={{0,128},{32,160},{64,192},{96,224},{128,0},{160,32},{192,64},{224,... | collective-permute-start | bytes 208904 | tf_op jit(solution)/shard_map/ppermute | solution.py:249
  9.5 7.1 %collective-permute-start.2 = (bf16[272,128]{1,0:T(8,128)(2,1)S(1)}, bf16[272,128]{1,0:T(8,128)(2,1)S(1)}, u32[]{:S(2)}, u32[]{:S(2)}) collective-permute-start(bf16[272,128]{1,0:T(8,128)(2,1)S(1)} %pack.1.own_ref), channel_id=1, source_target_pairs={{0,6},{2,0},{4,2},{6,4},{1,7},{3,1},{5,3},{7,5},{8,14},{10,8},{12,... | collective-permute-start | bytes 208904 | tf_op jit(solution)/shard_map/ppermute | solution.py:235
  10.0 7.8 %collective-permute-start.1 = (bf16[272,128]{1,0:T(8,128)(2,1)S(1)}, bf16[272,128]{1,0:T(8,128)(2,1)S(1)}, u32[]{:S(2)}, u32[]{:S(2)}) collective-permute-start(bf16[272,128]{1,0:T(8,128)(2,1)S(1)} %pack.1.own_ref), channel_id=1, source_target_pairs={{0,4},{2,6},{4,0},{6,2},{1,5},{3,7},{5,1},{7,3},{8,12},{10,14},{12... | collective-permute-start | bytes 208904 | tf_op jit(solution)/shard_map/ppermute | solution.py:235
  12.9 6.5 %collective-permute-start = (bf16[272,128]{1,0:T(8,128)(2,1)S(1)}, bf16[272,128]{1,0:T(8,128)(2,1)S(1)}, u32[]{:S(2)}, u32[]{:S(2)}) collective-permute-start(bf16[272,128]{1,0:T(8,128)(2,1)S(1)} %pack.1.own_ref), channel_id=1, source_target_pairs={{0,2},{2,4},{4,6},{6,0},{1,3},{3,5},{5,7},{7,1},{8,10},{10,12},{12... | collective-permute-start | bytes 208904 | tf_op jit(solution)/shard_map/ppermute | solution.py:235
  12.9 8.3 %collective-permute-start.6 = (bf16[2,272,128]{2,1,0:T(8,128)(2,1)S(1)}, bf16[2,272,128]{2,1,0:T(8,128)(2,1)S(1)}, u32[]{:S(2)}, u32[]{:S(2)}) collective-permute-start(bf16[2,272,128]{2,1,0:T(8,128)(2,1)S(1)} %pad_maximum_fusion.8), channel_id=1, source_target_pairs={{0,224},{32,0},{64,32},{96,64},{128,96},{160,128},{192,160},{224,1... | collective-permute-start | bytes 417800 | tf_op jit(solution)/shard_map/ppermute | solution.py:249
  16.6 10.2 %collective-permute-start.5 = (bf16[2,272,128]{2,1,0:T(8,128)(2,1)S(1)}, bf16[2,272,128]{2,1,0:T(8,128)(2,1)S(1)}, u32[]{:S(2)}, u32[]{:S(2)}) collective-permute-start(bf16[2,272,128]{2,1,0:T(8,128)(2,1)S(1)} %pad_maximum_fusion.8), channel_id=1, source_target_pairs={{0,64},{32,96},{64,128},{96,160},{128,192},{160,224},{192,0},{224,... | collective-permute-start | bytes 417800 | tf_op jit(solution)/shard_map/ppermute | solution.py:249
  16.6 10.3 %collective-permute-start.4 = (bf16[2,272,128]{2,1,0:T(8,128)(2,1)S(1)}, bf16[2,272,128]{2,1,0:T(8,128)(2,1)S(1)}, u32[]{:S(2)}, u32[]{:S(2)}) collective-permute-start(bf16[2,272,128]{2,1,0:T(8,128)(2,1)S(1)} %pad_maximum_fusion.8), channel_id=1, source_target_pairs={{0,32},{32,64},{64,96},{96,128},{128,160},{160,192},{192,224},{224... | collective-permute-start | bytes 417800 | tf_op jit(solution)/shard_map/ppermute | solution.py:249
  17.8 16.6 %collective-permute-start.11 = (bf16[2,272,128]{2,1,0:T(8,128)(2,1)S(1)}, bf16[2,272,128]{2,1,0:T(8,128)(2,1)S(1)}, u32[]{:S(2)}, u32[]{:S(2)}) collective-permute-start(bf16[2,272,128]{2,1,0:T(8,128)(2,1)S(1)} %pad_maximum_fusion.8), channel_id=1, source_target_pairs={{0,8},{8,16},{16,24},{24,0},{1,9},{9,17},{17,25},{25,1},{2,10},{10... | collective-permute-start | bytes 417800 | tf_op jit(solution)/shard_map/ppermute | solution.py:249
  19.4 10.4 %collective-permute-start.8 = (bf16[2,272,128]{2,1,0:T(8,128)(2,1)S(1)}, bf16[2,272,128]{2,1,0:T(8,128)(2,1)S(1)}, u32[]{:S(2)}, u32[]{:S(2)}) collective-permute-start(bf16[2,272,128]{2,1,0:T(8,128)(2,1)S(1)} %pad_maximum_fusion.8), channel_id=1, source_target_pairs={{0,24},{8,0},{16,8},{24,16},{1,25},{9,1},{17,9},{25,17},{2,26},{10... | collective-permute-start | bytes 417800 | tf_op jit(solution)/shard_map/ppermute | solution.py:249
  26.9 10.8 %collective-permute-start.10 = (bf16[6,272,128]{2,1,0:T(8,128)(2,1)S(1)}, bf16[6,272,128]{2,1,0:T(8,128)(2,1)S(1)}, u32[]{:S(2)}, u32[]{:S(2)}) collective-permute-start(bf16[6,272,128]{2,1,0:T(8,128)(2,1)S(1)} %pad_maximum_fusion.3), channel_id=1, source_target_pairs={{0,24},{8,0},{16,8},{24,16},{1,25},{9,1},{17,9},{25,17},{2,26},{10... | collective-permute-start | bytes 1253384 | tf_op jit(solution)/shard_map/ppermute | solution.py:249
  29.8 10.4 %collective-permute-start.9 = (bf16[6,272,128]{2,1,0:T(8,128)(2,1)S(1)}, bf16[6,272,128]{2,1,0:T(8,128)(2,1)S(1)}, u32[]{:S(2)}, u32[]{:S(2)}) collective-permute-start(bf16[6,272,128]{2,1,0:T(8,128)(2,1)S(1)} %pad_maximum_fusion.3), channel_id=1, source_target_pairs={{0,8},{8,16},{16,24},{24,0},{1,9},{9,17},{17,25},{25,1},{2,10},{10... | collective-permute-start | bytes 1253384 | tf_op jit(solution)/shard_map/ppermute | solution.py:249
  40.2 34.2 %collective-permute-start.13 = (bf16[4,272,128]{2,1,0:T(8,128)(2,1)S(1)}, bf16[4,272,128]{2,1,0:T(8,128)(2,1)S(1)}, u32[]{:S(2)}, u32[]{:S(2)}) collective-permute-start(bf16[4,272,128]{2,1,0:T(8,128)(2,1)S(1)} %pad_maximum_fusion.6), channel_id=1, source_target_pairs={{0,24},{8,0},{16,8},{24,16},{1,25},{9,1},{17,9},{25,17},{2,26},{10... | collective-permute-start | bytes 835592 | tf_op jit(solution)/shard_map/ppermute | solution.py:249
  40.6 33.8 %collective-permute-start.12 = (bf16[4,272,128]{2,1,0:T(8,128)(2,1)S(1)}, bf16[4,272,128]{2,1,0:T(8,128)(2,1)S(1)}, u32[]{:S(2)}, u32[]{:S(2)}) collective-permute-start(bf16[4,272,128]{2,1,0:T(8,128)(2,1)S(1)} %pad_maximum_fusion.5), channel_id=1, source_target_pairs={{0,8},{8,16},{16,24},{24,0},{1,9},{9,17},{17,25},{25,1},{2,10},{10... | collective-permute-start | bytes 835592 | tf_op jit(solution)/shard_map/ppermute | solution.py:249
  72.3 31.5 %collective-permute-start.18 = (bf16[8,256,128]{2,1,0:T(8,128)(2,1)S(1)}, bf16[8,256,128]{2,1,0:T(8,128)(2,1)S(1)}, u32[]{:S(2)}, u32[]{:S(2)}) collective-permute-start(bf16[8,256,128]{2,1,0:T(8,128)(2,1)S(1)} %get-tuple-element.40), channel_id=1, source_target_pairs={{0,24},{8,0},{16,8},{24,16},{1,25},{9,1},{17,9},{25,17},{2,26},{10... | collective-permute-start | bytes 1572872 | tf_op jit(solution)/shard_map/ppermute | solution.py:249
  72.4 31.4 %collective-permute-start.20 = (bf16[8,256,128]{2,1,0:T(8,128)(2,1)S(1)}, bf16[8,256,128]{2,1,0:T(8,128)(2,1)S(1)}, u32[]{:S(2)}, u32[]{:S(2)}) collective-permute-start(bf16[8,256,128]{2,1,0:T(8,128)(2,1)S(1)} %get-tuple-element.42), channel_id=1, source_target_pairs={{0,8},{8,16},{16,24},{24,0},{1,9},{9,17},{17,25},{25,1},{2,10},{10... | collective-permute-start | bytes 1572872 | tf_op jit(solution)/shard_map/ppermute | solution.py:249
  88.8 15.0 %collective-permute-start.19 = (bf16[8,256,128]{2,1,0:T(8,128)(2,1)S(1)}, bf16[8,256,128]{2,1,0:T(8,128)(2,1)S(1)}, u32[]{:S(2)}, u32[]{:S(2)}) collective-permute-start(bf16[8,256,128]{2,1,0:T(8,128)(2,1)S(1)} %get-tuple-element.41), channel_id=1, source_target_pairs={{0,16},{8,24},{16,0},{24,8},{1,17},{9,25},{17,1},{25,9},{2,18},{10... | collective-permute-start | bytes 1572872 | tf_op jit(solution)/shard_map/ppermute | solution.py:249
  104.9 21.9 %all-to-all-start = ((bf16[8,256,128]{2,1,0:T(8,128)(2,1)}), bf16[8,256,128]{2,1,0:T(8,128)(2,1)S(1)}, u32[]{:S(2)}, u32[]{:S(2)}) async-start(bf16[8,256,128]{2,1,0:T(8,128)(2,1)} %add.164), calls=%async_computation | async-start | bytes 1048576 | tf_op jit(solution)/shard_map/all_to_all | solution.py:335
  111.8 5.8 %collective-permute-start.16 = (bf16[256,128]{1,0:T(8,128)(2,1)S(1)}, bf16[256,128]{1,0:T(8,128)(2,1)S(1)}, u32[]{:S(2)}, u32[]{:S(2)}) collective-permute-start(bf16[256,128]{1,0:T(8,128)(2,1)S(1)} %get-tuple-element.55), channel_id=1, source_target_pairs={{0,4},{2,6},{4,0},{6,2},{1,5},{3,7},{5,1},{7,3},{8,12},{10,14},{12... | collective-permute-start | bytes 196616 | tf_op jit(solution)/shard_map/ppermute | solution.py:338
  111.8 5.8 %collective-permute-start.15 = (bf16[256,128]{1,0:T(8,128)(2,1)S(1)}, bf16[256,128]{1,0:T(8,128)(2,1)S(1)}, u32[]{:S(2)}, u32[]{:S(2)}) collective-permute-start(bf16[256,128]{1,0:T(8,128)(2,1)S(1)} %get-tuple-element.56), channel_id=1, source_target_pairs={{0,6},{2,0},{4,2},{6,4},{1,7},{3,1},{5,3},{7,5},{8,14},{10,8},{12,... | collective-permute-start | bytes 196616 | tf_op jit(solution)/shard_map/ppermute | solution.py:338
  129.5 6.3 %collective-permute-start.23 = (f32[40,128]{1,0:T(8,128)S(1)}, f32[40,128]{1,0:T(8,128)S(1)}, u32[]{:S(2)}, u32[]{:S(2)}) collective-permute-start(f32[40,128]{1,0:T(8,128)S(1)} %add.90), channel_id=1, source_target_pairs={{0,4},{2,6},{4,0},{6,2},{1,5},{3,7},{5,1},{7,3},{8,12},{10,14},{12... | collective-permute-start | bytes 61448 | tf_op jit(solution)/shard_map/ppermute | solution.py:235
  137.6 9.4 %collective-permute-start.27 = (f32[40,128]{1,0:T(8,128)S(1)}, f32[40,128]{1,0:T(8,128)S(1)}, u32[]{:S(2)}, u32[]{:S(2)}) collective-permute-start(f32[40,128]{1,0:T(8,128)S(1)} %add_add_fusion.2), channel_id=1, source_target_pairs={{0,24},{8,0},{16,8},{24,16},{1,25},{9,1},{17,9},{25,17},{2,26},{10... | collective-permute-start | bytes 61448 | tf_op jit(solution)/shard_map/ppermute | solution.py:235
  150.9 7.8 %collective-permute-start.28 = (f32[40,128]{1,0:T(8,128)S(1)}, f32[40,128]{1,0:T(8,128)S(1)}, u32[]{:S(2)}, u32[]{:S(2)}) collective-permute-start(f32[40,128]{1,0:T(8,128)S(1)} %add_add_fusion.1), channel_id=1, source_target_pairs={{0,128},{32,160},{64,192},{96,224},{128,0},{160,32},{192,64},{224,... | collective-permute-start | bytes 61448 | tf_op jit(solution)/shard_map/ppermute | solution.py:352
  158.7 6.8 %collective-permute-start.31 = (f32[40,128]{1,0:T(8,128)S(1)}, f32[40,128]{1,0:T(8,128)S(1)}, u32[]{:S(2)}, u32[]{:S(2)}) collective-permute-start(f32[40,128]{1,0:T(8,128)S(1)} %add.97), channel_id=1, source_target_pairs={{0,96},{32,128},{64,160},{96,192},{128,224},{160,0},{192,32},{224,... | collective-permute-start | bytes 61448 | tf_op jit(solution)/shard_map/ppermute | solution.py:235
  158.7 6.8 %collective-permute-start.30 = (f32[40,128]{1,0:T(8,128)S(1)}, f32[40,128]{1,0:T(8,128)S(1)}, u32[]{:S(2)}, u32[]{:S(2)}) collective-permute-start(f32[40,128]{1,0:T(8,128)S(1)} %add.97), channel_id=1, source_target_pairs={{0,64},{32,96},{64,128},{96,160},{128,192},{160,224},{192,0},{224,... | collective-permute-start | bytes 61448 | tf_op jit(solution)/shard_map/ppermute | solution.py:235
  (15 other events, 163.8 us)

commit v12 on v10

--- a/solution.py
+++ b/solution.py
@@ -28,7 +28,15 @@
 SMALL = pltpu.CompilerParams(vmem_limit_bytes=4 * 2**20)
 
 
-def pack_kernel(direction_ref, positions_ref, packed_ref):
+def pack_kernel(direction_in, positions_in, packed_ref, direction_ref, positions_ref, sems):
+    copies = [
+        pltpu.make_async_copy(direction_in, direction_ref, sems.at[0]),
+        pltpu.make_async_copy(positions_in, positions_ref, sems.at[1]),
+    ]
+    for copy in copies:
+        copy.start()
+    for copy in copies:
+        copy.wait()
     for t in range(8):
         packed_ref[t * 32 : (t + 1) * 32, :] = direction_ref[:, t * TILE : (t + 1) * TILE].astype(bf16)
     where = positions_ref[...].astype(f32)
@@ -239,7 +247,17 @@
     shape = jax.ShapeDtypeStruct
     own_points = direction.shape[1]
     packed = pl.pallas_call(
-        pack_kernel, out_shape=shape((272, TILE), bf16), in_specs=[VMEM] * 2, out_specs=VMEM, compiler_params=SMALL, name="pack"
+        pack_kernel,
+        out_shape=shape((272, TILE), bf16),
+        in_specs=[pl.BlockSpec(memory_space=pl.ANY)] * 2,
+        out_specs=VMEM,
+        scratch_shapes=[
+            pltpu.VMEM((PROBES, own_points), f32),
+            pltpu.VMEM((2, own_points), bf16),
+            pltpu.SemaphoreType.DMA((2,)),
+        ],
+        compiler_params=SMALL,
+        name="pack",
     )(direction, positions)
     def moved(value, axis, size, shift):
         return lax.ppermute(value, axis, [(i, (i + shift) % size) for i in range(size)])

time: 171 us -> 171 us (level)
  waiting for transfers between devices: 43 us -> 32.3 us
  starting transfers between devices: 50.3 us -> 60.8 us
    ppermute x3, starting transfers between devices: 3.35 us -> 12 us  [on_device(): lax.ppermute(half[k], 'y', [(i, (i - k) % 4) for i in range(4)])]
    all_to_all x1, waiting for transfers between devices: 10.5 us -> 4.31 us  [on_device(): col_parts = lax.all_to_all(sums, 'z', 0, 0)]
    ppermute x12, starting transfers between devices: 19.1 us -> 22.5 us  [shifts(): lax.ppermute(value, axis, [(i, (i + k) % size) for i in range(size)])]
    ppermute x12, waiting for transfers between devices: 11.9 us -> 9.57 us  [shifts(): lax.ppermute(value, axis, [(i, (i + k) % size) for i in range(size)])]
    ppermute x3, waiting for transfers between devices: 4.11 us -> 1.9 us  [on_device(): lax.ppermute(half[k], 'y', [(i, (i - k) % 4) for i in range(4)])]
  transfers between devices with their start and end apart: 33 -> 33, of which waited for: 16 -> 14; matrix products, arithmetic and copies ran while one was open for 1% -> 1% of each run, Pallas kernels for 39% -> 39%
where the time goes in v12:
time: 171 us; the launch traced here: 170 us
  Pallas kernels  72.6 us (42%)
  starting transfers between devices  60.8 us (36%)
  waiting for transfers between devices  32.3 us (19%)
  local copies, waits for them, and re-layouts  1.8 us (1%)
    pallas_call x3, Pallas kernels, pairs(): pl.pallas_call(functools.partial(part_kernel, part), out_shape=outs, in_s...  58.6 us
    ppermute x12, starting transfers between devices, shifts(): lax.ppermute(value, axis, [(i, (i + k) % size) for i in range(size)])  22.5 us
    ppermute x13, starting transfers between devices, moved(): lax.ppermute(value, axis, [(i, (i + shift) % size) for i in range(size)])  22 us
    ppermute x3, starting transfers between devices, on_device(): lax.ppermute(half[k], 'y', [(i, (i - k) % 4) for i in range(4)])  12 us
    ppermute x12, waiting for transfers between devices, shifts(): lax.ppermute(value, axis, [(i, (i + k) % size) for i in range(size)])  9.57 us
    ppermute x13, waiting for transfers between devices, moved(): lax.ppermute(value, axis, [(i, (i + shift) % size) for i in range(size)])  8.17 us
    ppermute x1, waiting for transfers between devices, on_device(): gram = gram + lax.ppermute(gram, 'z', [(i, (i + 4) % 8) for i in range(8)])  7.19 us
    pallas_call x1, Pallas kernels, on_device(): pl.pallas_call(solve_kernel, out_shape=(shape((PROBES, own_points), f32),...  4.68 us
  transfers between devices with their start and end apart: 33, of which 14 were waited for; matrix products, arithmetic and copies ran while one was open for 1% of the time, Pallas kernels for 39%

profile of v12, /device:TPU:16, one launch (start us, length us, event | category | flops | bytes accessed | tf_op | source)
XLA Modules:
  0.0 170.2 jit_solution(10476298901444626563)
XLA Ops:
  2.4 7.3 %collective-permute-start.3 = (bf16[272,128]{1,0:T(8,128)(2,1)S(1)}, bf16[272,128]{1,0:T(8,128)(2,1)S(1)}, u32[]{:S(2)}, u32[]{:S(2)}) collective-permute-start(bf16[272,128]{1,0:T(8,128)(2,1)S(1)} %pack.1.own_ref), channel_id=1, source_target_pairs={{0,128},{32,160},{64,192},{96,224},{128,0},{160,32},{192,64},{224,... | collective-permute-start | bytes 208904 | tf_op jit(solution)/shard_map/ppermute | solution.py:263
  10.1 2.9 %collective-permute-start.1 = (bf16[272,128]{1,0:T(8,128)(2,1)S(1)}, bf16[272,128]{1,0:T(8,128)(2,1)S(1)}, u32[]{:S(2)}, u32[]{:S(2)}) collective-permute-start(bf16[272,128]{1,0:T(8,128)(2,1)S(1)} %pack.1.own_ref), channel_id=1, source_target_pairs={{0,4},{2,6},{4,0},{6,2},{1,5},{3,7},{5,1},{7,3},{8,12},{10,14},{12... | collective-permute-start | bytes 208904 | tf_op jit(solution)/shard_map/ppermute | solution.py:239
  13.1 3.7 %collective-permute-start.6 = (bf16[2,272,128]{2,1,0:T(8,128)(2,1)S(1)}, bf16[2,272,128]{2,1,0:T(8,128)(2,1)S(1)}, u32[]{:S(2)}, u32[]{:S(2)}) collective-permute-start(bf16[2,272,128]{2,1,0:T(8,128)(2,1)S(1)} %pad_maximum_fusion.8), channel_id=1, source_target_pairs={{0,224},{32,0},{64,32},{96,64},{128,96},{160,128},{192,160},{224,1... | collective-permute-start | bytes 417800 | tf_op jit(solution)/shard_map/ppermute | solution.py:263
  21.4 5.6 %collective-permute-done.5 = bf16[2,272,128]{2,1,0:T(8,128)(2,1)S(1)} collective-permute-done((bf16[2,272,128]{2,1,0:T(8,128)(2,1)S(1)}, bf16[2,272,128]{2,1,0:T(8,128)(2,1)S(1)}, u32[]{:S(2)}, u32[]{:S(2)}) %collective-permute-start.5) | collective-permute-done | bytes 139296 | tf_op jit(solution)/shard_map/ppermute | solution.py:263
  27.1 2.8 %collective-permute-start.10 = (bf16[6,272,128]{2,1,0:T(8,128)(2,1)S(1)}, bf16[6,272,128]{2,1,0:T(8,128)(2,1)S(1)}, u32[]{:S(2)}, u32[]{:S(2)}) collective-permute-start(bf16[6,272,128]{2,1,0:T(8,128)(2,1)S(1)} %pad_maximum_fusion.3), channel_id=1, source_target_pairs={{0,24},{8,0},{16,8},{24,16},{1,25},{9,1},{17,9},{25,17},{2,26},{10... | collective-permute-start | bytes 1253384 | tf_op jit(solution)/shard_map/ppermute | solution.py:263
  30.5 4.0 %bins.1.bins_ref = s32[4704]{0:T(1024)S(1)} custom-call(s32[1]{0:T(128)} %copy.14.live_ref, s32[1536]{0:T(1024)S(1)} %fusion.16.entries_ref, s32[3]{0:T(128)S(1)} %convert_element_type.33.count_ref, bf16[16,128]{1,0:T(8,128)(2,1)S(1)} %slice_bitcast_fusion.3.after_ref), custom_call_target="tpu_custom_call" | custom-call | tf_op jit(solution)/shard_map/bins/pallas_call | solution.py:293
  34.7 3.2 %rows.1 = (f32[64,128,128]{2,1,0:T(8,128)S(1)}, f32[64,128,128]{2,1,0:T(8,128)S(1)}, f32[32,1024]{1,0:T(8,128)S(1)}) custom-call(bf16[272,128]{1,0:T(8,128)(2,1)S(1)} %pack.1.own_ref, bf16[8,272,128]{2,1,0:T(8,128)(2,1)S(1)} %constant_dynamic-update-slice_fusion.near_ref), custom_call_target="tpu_custom_call" | custom-call | tf_op jit(solution)/shard_map/rows/pallas_call | solution.py:302
  37.9 2.4 %collective-permute-done.9 = bf16[6,272,128]{2,1,0:T(8,128)(2,1)S(1)} collective-permute-done((bf16[6,272,128]{2,1,0:T(8,128)(2,1)S(1)}, bf16[6,272,128]{2,1,0:T(8,128)(2,1)S(1)}, u32[]{:S(2)}, u32[]{:S(2)}) %collective-permute-start.9) | collective-permute-done | bytes 417824 | tf_op jit(solution)/shard_map/ppermute | solution.py:263
  42.8 29.7 %pairs.3 = (f32[64,32,128]{2,1,0:T(8,128)S(1)}, bf16[8,256,128]{2,1,0:T(8,128)(2,1)S(1)}, bf16[8,256,128]{2,1,0:T(8,128)(2,1)S(1)}) custom-call(s32[1]{0:T(128)} %bitcast.5.place_ref, s32[3]{0:T(128)S(1)} %convert_element_type.33.count_ref, s32[4704]{0:T(1024)S(1)} %bins.1.bins_ref, bf16[8,272,128]{2,1,0:T(8,128)(2,1)S(1)} %constant_dynamic-update-slice_fusion.near_ref, ...), custom_call_target="tpu_custom_call" | custom-call | tf_op jit(solution)/shard_map/pairs/pallas_call | solution.py:325
  74.7 14.6 %pairs.4 = (f32[64,32,128]{2,1,0:T(8,128)S(1)}, bf16[8,256,128]{2,1,0:T(8,128)(2,1)S(1)}) custom-call(s32[1]{0:T(128)} %bitcast.5.place_ref, s32[3]{0:T(128)S(1)} %convert_element_type.33.count_ref, s32[4704]{0:T(1024)S(1)} %bins.1.bins_ref, bf16[8,272,128]{2,1,0:T(8,128)(2,1)S(1)} %constant_dynamic-update-slice_fusion.near_ref, ...), custom_call_target="tpu_custom_call", output_to_operand_aliasing={{0}: (7, {})} | custom-call | tf_op jit(solution)/shard_map/pairs/pallas_call | solution.py:325
  89.5 14.3 %pairs.5 = (f32[64,32,128]{2,1,0:T(8,128)S(1)}, bf16[8,256,128]{2,1,0:T(8,128)(2,1)S(1)}, bf16[8,256,128]{2,1,0:T(8,128)(2,1)S(1)}) custom-call(s32[1]{0:T(128)} %bitcast.5.place_ref, s32[3]{0:T(128)S(1)} %convert_element_type.33.count_ref, s32[4704]{0:T(1024)S(1)} %bins.1.bins_ref, ...), custom_call_target="tpu_custom_call", output_to_operand_aliasing={{0}: (7, {})} | custom-call | tf_op jit(solution)/shard_map/pairs/pallas_call | solution.py:325
  105.1 3.5 %all-to-all-start = ((bf16[8,256,128]{2,1,0:T(8,128)(2,1)}), bf16[8,256,128]{2,1,0:T(8,128)(2,1)S(1)}, u32[]{:S(2)}, u32[]{:S(2)}) async-start(bf16[8,256,128]{2,1,0:T(8,128)(2,1)} %add.164), calls=%async_computation | async-start | bytes 1048576 | tf_op jit(solution)/shard_map/all_to_all | solution.py:349
  108.7 2.4 %collective-permute-start.17 = (bf16[256,128]{1,0:T(8,128)(2,1)S(1)}, bf16[256,128]{1,0:T(8,128)(2,1)S(1)}, u32[]{:S(2)}, u32[]{:S(2)}) collective-permute-start(bf16[256,128]{1,0:T(8,128)(2,1)S(1)} %get-tuple-element.54), channel_id=1, source_target_pairs={{0,2},{2,4},{4,6},{6,0},{1,3},{3,5},{5,7},{7,1},{8,10},{10,12},{12... | collective-permute-start | bytes 196616 | tf_op jit(solution)/shard_map/ppermute | solution.py:352
  111.1 7.1 %collective-permute-start.16 = (bf16[256,128]{1,0:T(8,128)(2,1)S(1)}, bf16[256,128]{1,0:T(8,128)(2,1)S(1)}, u32[]{:S(2)}, u32[]{:S(2)}) collective-permute-start(bf16[256,128]{1,0:T(8,128)(2,1)S(1)} %get-tuple-element.55), channel_id=1, source_target_pairs={{0,4},{2,6},{4,0},{6,2},{1,5},{3,7},{5,1},{7,3},{8,12},{10,14},{12... | collective-permute-start | bytes 196616 | tf_op jit(solution)/shard_map/ppermute | solution.py:352
  118.1 2.5 %collective-permute-start.15 = (bf16[256,128]{1,0:T(8,128)(2,1)S(1)}, bf16[256,128]{1,0:T(8,128)(2,1)S(1)}, u32[]{:S(2)}, u32[]{:S(2)}) collective-permute-start(bf16[256,128]{1,0:T(8,128)(2,1)S(1)} %get-tuple-element.56), channel_id=1, source_target_pairs={{0,6},{2,0},{4,2},{6,4},{1,7},{3,1},{5,3},{7,5},{8,14},{10,8},{12,... | collective-permute-start | bytes 196616 | tf_op jit(solution)/shard_map/ppermute | solution.py:352
  122.6 4.3 %all-to-all-done.col_ref = bf16[8,256,128]{2,1,0:T(8,128)(2,1)S(1)} async-done(((bf16[8,256,128]{2,1,0:T(8,128)(2,1)}), bf16[8,256,128]{2,1,0:T(8,128)(2,1)S(1)}, u32[]{:S(2)}, u32[]{:S(2)}) %all-to-all-start) | async-done | bytes 524320 | tf_op jit(solution)/shard_map/all_to_all | solution.py:349
  129.0 2.0 %collective-permute-start.24 = (f32[40,128]{1,0:T(8,128)S(1)}, f32[40,128]{1,0:T(8,128)S(1)}, u32[]{:S(2)}, u32[]{:S(2)}) collective-permute-start(f32[40,128]{1,0:T(8,128)S(1)} %add.90), channel_id=1, source_target_pairs={{0,6},{2,0},{4,2},{6,4},{1,7},{3,1},{5,3},{7,5},{8,14},{10,8},{12,... | collective-permute-start | bytes 61448 | tf_op jit(solution)/shard_map/ppermute | solution.py:239
  131.0 2.5 %collective-permute-start.23 = (f32[40,128]{1,0:T(8,128)S(1)}, f32[40,128]{1,0:T(8,128)S(1)}, u32[]{:S(2)}, u32[]{:S(2)}) collective-permute-start(f32[40,128]{1,0:T(8,128)S(1)} %add.90), channel_id=1, source_target_pairs={{0,4},{2,6},{4,0},{6,2},{1,5},{3,7},{5,1},{7,3},{8,12},{10,14},{12... | collective-permute-start | bytes 61448 | tf_op jit(solution)/shard_map/ppermute | solution.py:239
  133.5 2.3 %collective-permute-start.22 = (f32[40,128]{1,0:T(8,128)S(1)}, f32[40,128]{1,0:T(8,128)S(1)}, u32[]{:S(2)}, u32[]{:S(2)}) collective-permute-start(f32[40,128]{1,0:T(8,128)S(1)} %add.90), channel_id=1, source_target_pairs={{0,2},{2,4},{4,6},{6,0},{1,3},{3,5},{5,7},{7,1},{8,10},{10,12},{12... | collective-permute-start | bytes 61448 | tf_op jit(solution)/shard_map/ppermute | solution.py:239
  137.3 8.1 %collective-permute-start.27 = (f32[40,128]{1,0:T(8,128)S(1)}, f32[40,128]{1,0:T(8,128)S(1)}, u32[]{:S(2)}, u32[]{:S(2)}) collective-permute-start(f32[40,128]{1,0:T(8,128)S(1)} %add_add_fusion.2), channel_id=1, source_target_pairs={{0,24},{8,0},{16,8},{24,16},{1,25},{9,1},{17,9},{25,17},{2,26},{10... | collective-permute-start | bytes 61448 | tf_op jit(solution)/shard_map/ppermute | solution.py:239
  146.8 3.8 %collective-permute-done.26 = f32[40,128]{1,0:T(8,128)S(1)} collective-permute-done((f32[40,128]{1,0:T(8,128)S(1)}, f32[40,128]{1,0:T(8,128)S(1)}, u32[]{:S(2)}, u32[]{:S(2)}) %collective-permute-start.26) | collective-permute-done | bytes 20512 | tf_op jit(solution)/shard_map/ppermute | solution.py:239
  151.3 7.2 %collective-permute-done.28 = f32[40,128]{1,0:T(8,128)S(1)} collective-permute-done((f32[40,128]{1,0:T(8,128)S(1)}, f32[40,128]{1,0:T(8,128)S(1)}, u32[]{:S(2)}, u32[]{:S(2)}) %collective-permute-start.28) | collective-permute-done | bytes 20512 | tf_op jit(solution)/shard_map/ppermute | solution.py:366
  161.7 3.5 %collective-permute-done.31 = f32[40,128]{1,0:T(8,128)S(1)} collective-permute-done((f32[40,128]{1,0:T(8,128)S(1)}, f32[40,128]{1,0:T(8,128)S(1)}, u32[]{:S(2)}, u32[]{:S(2)}) %collective-permute-start.31) | collective-permute-done | bytes 20512 | tf_op jit(solution)/shard_map/ppermute | solution.py:239
  165.5 4.7 %solve.1 = (f32[32,1024]{1,0:T(8,128)}, f32[32,1024]{1,0:T(8,128)}, f32[32,1024]{1,0:T(8,128)}) custom-call(f32[40,128]{1,0:T(8,128)S(1)} %add_add_fusion.gram_ref, f32[32,1024]{1,0:T(8,128)S(1)} %copy-done.3, f32[32,1024]{1,0:T(8,128)S(1)} %copy-done.2, f32[32,1024]{1,0:T(8,128)S(1)} %copy-done.1, f32[32,1024]{1,0:T(8,128)S(1)} %get-tuple-element.44.image_ref), custom_call_target="tpu_custom_call" | custom-call | tf_op jit(solution)/shard_map/solve/pallas_call | solution.py:368
  (100 shorter events, 24.0 us)
Async XLA Ops:
  2.4 10.6 %collective-permute-start.3 = (bf16[272,128]{1,0:T(8,128)(2,1)S(1)}, bf16[272,128]{1,0:T(8,128)(2,1)S(1)}, u32[]{:S(2)}, u32[]{:S(2)}) collective-permute-start(bf16[272,128]{1,0:T(8,128)(2,1)S(1)} %pack.1.own_ref), channel_id=1, source_target_pairs={{0,128},{32,160},{64,192},{96,224},{128,0},{160,32},{192,64},{224,... | collective-permute-start | bytes 208904 | tf_op jit(solution)/shard_map/ppermute | solution.py:263
  9.7 7.1 %collective-permute-start.2 = (bf16[272,128]{1,0:T(8,128)(2,1)S(1)}, bf16[272,128]{1,0:T(8,128)(2,1)S(1)}, u32[]{:S(2)}, u32[]{:S(2)}) collective-permute-start(bf16[272,128]{1,0:T(8,128)(2,1)S(1)} %pack.1.own_ref), channel_id=1, source_target_pairs={{0,6},{2,0},{4,2},{6,4},{1,7},{3,1},{5,3},{7,5},{8,14},{10,8},{12,... | collective-permute-start | bytes 208904 | tf_op jit(solution)/shard_map/ppermute | solution.py:239
  10.1 7.8 %collective-permute-start.1 = (bf16[272,128]{1,0:T(8,128)(2,1)S(1)}, bf16[272,128]{1,0:T(8,128)(2,1)S(1)}, u32[]{:S(2)}, u32[]{:S(2)}) collective-permute-start(bf16[272,128]{1,0:T(8,128)(2,1)S(1)} %pack.1.own_ref), channel_id=1, source_target_pairs={{0,4},{2,6},{4,0},{6,2},{1,5},{3,7},{5,1},{7,3},{8,12},{10,14},{12... | collective-permute-start | bytes 208904 | tf_op jit(solution)/shard_map/ppermute | solution.py:239
  13.0 6.5 %collective-permute-start = (bf16[272,128]{1,0:T(8,128)(2,1)S(1)}, bf16[272,128]{1,0:T(8,128)(2,1)S(1)}, u32[]{:S(2)}, u32[]{:S(2)}) collective-permute-start(bf16[272,128]{1,0:T(8,128)(2,1)S(1)} %pack.1.own_ref), channel_id=1, source_target_pairs={{0,2},{2,4},{4,6},{6,0},{1,3},{3,5},{5,7},{7,1},{8,10},{10,12},{12... | collective-permute-start | bytes 208904 | tf_op jit(solution)/shard_map/ppermute | solution.py:239
  13.1 8.3 %collective-permute-start.6 = (bf16[2,272,128]{2,1,0:T(8,128)(2,1)S(1)}, bf16[2,272,128]{2,1,0:T(8,128)(2,1)S(1)}, u32[]{:S(2)}, u32[]{:S(2)}) collective-permute-start(bf16[2,272,128]{2,1,0:T(8,128)(2,1)S(1)} %pad_maximum_fusion.8), channel_id=1, source_target_pairs={{0,224},{32,0},{64,32},{96,64},{128,96},{160,128},{192,160},{224,1... | collective-permute-start | bytes 417800 | tf_op jit(solution)/shard_map/ppermute | solution.py:263
  16.8 10.2 %collective-permute-start.5 = (bf16[2,272,128]{2,1,0:T(8,128)(2,1)S(1)}, bf16[2,272,128]{2,1,0:T(8,128)(2,1)S(1)}, u32[]{:S(2)}, u32[]{:S(2)}) collective-permute-start(bf16[2,272,128]{2,1,0:T(8,128)(2,1)S(1)} %pad_maximum_fusion.8), channel_id=1, source_target_pairs={{0,64},{32,96},{64,128},{96,160},{128,192},{160,224},{192,0},{224,... | collective-permute-start | bytes 417800 | tf_op jit(solution)/shard_map/ppermute | solution.py:263
  16.8 10.3 %collective-permute-start.4 = (bf16[2,272,128]{2,1,0:T(8,128)(2,1)S(1)}, bf16[2,272,128]{2,1,0:T(8,128)(2,1)S(1)}, u32[]{:S(2)}, u32[]{:S(2)}) collective-permute-start(bf16[2,272,128]{2,1,0:T(8,128)(2,1)S(1)} %pad_maximum_fusion.8), channel_id=1, source_target_pairs={{0,32},{32,64},{64,96},{96,128},{128,160},{160,192},{192,224},{224... | collective-permute-start | bytes 417800 | tf_op jit(solution)/shard_map/ppermute | solution.py:263
  18.0 16.6 %collective-permute-start.11 = (bf16[2,272,128]{2,1,0:T(8,128)(2,1)S(1)}, bf16[2,272,128]{2,1,0:T(8,128)(2,1)S(1)}, u32[]{:S(2)}, u32[]{:S(2)}) collective-permute-start(bf16[2,272,128]{2,1,0:T(8,128)(2,1)S(1)} %pad_maximum_fusion.8), channel_id=1, source_target_pairs={{0,8},{8,16},{16,24},{24,0},{1,9},{9,17},{17,25},{25,1},{2,10},{10... | collective-permute-start | bytes 417800 | tf_op jit(solution)/shard_map/ppermute | solution.py:263
  19.6 10.4 %collective-permute-start.8 = (bf16[2,272,128]{2,1,0:T(8,128)(2,1)S(1)}, bf16[2,272,128]{2,1,0:T(8,128)(2,1)S(1)}, u32[]{:S(2)}, u32[]{:S(2)}) collective-permute-start(bf16[2,272,128]{2,1,0:T(8,128)(2,1)S(1)} %pad_maximum_fusion.8), channel_id=1, source_target_pairs={{0,24},{8,0},{16,8},{24,16},{1,25},{9,1},{17,9},{25,17},{2,26},{10... | collective-permute-start | bytes 417800 | tf_op jit(solution)/shard_map/ppermute | solution.py:263
  27.1 10.8 %collective-permute-start.10 = (bf16[6,272,128]{2,1,0:T(8,128)(2,1)S(1)}, bf16[6,272,128]{2,1,0:T(8,128)(2,1)S(1)}, u32[]{:S(2)}, u32[]{:S(2)}) collective-permute-start(bf16[6,272,128]{2,1,0:T(8,128)(2,1)S(1)} %pad_maximum_fusion.3), channel_id=1, source_target_pairs={{0,24},{8,0},{16,8},{24,16},{1,25},{9,1},{17,9},{25,17},{2,26},{10... | collective-permute-start | bytes 1253384 | tf_op jit(solution)/shard_map/ppermute | solution.py:263
  30.0 10.4 %collective-permute-start.9 = (bf16[6,272,128]{2,1,0:T(8,128)(2,1)S(1)}, bf16[6,272,128]{2,1,0:T(8,128)(2,1)S(1)}, u32[]{:S(2)}, u32[]{:S(2)}) collective-permute-start(bf16[6,272,128]{2,1,0:T(8,128)(2,1)S(1)} %pad_maximum_fusion.3), channel_id=1, source_target_pairs={{0,8},{8,16},{16,24},{24,0},{1,9},{9,17},{17,25},{25,1},{2,10},{10... | collective-permute-start | bytes 1253384 | tf_op jit(solution)/shard_map/ppermute | solution.py:263
  40.4 34.2 %collective-permute-start.13 = (bf16[4,272,128]{2,1,0:T(8,128)(2,1)S(1)}, bf16[4,272,128]{2,1,0:T(8,128)(2,1)S(1)}, u32[]{:S(2)}, u32[]{:S(2)}) collective-permute-start(bf16[4,272,128]{2,1,0:T(8,128)(2,1)S(1)} %pad_maximum_fusion.6), channel_id=1, source_target_pairs={{0,24},{8,0},{16,8},{24,16},{1,25},{9,1},{17,9},{25,17},{2,26},{10... | collective-permute-start | bytes 835592 | tf_op jit(solution)/shard_map/ppermute | solution.py:263
  40.8 33.8 %collective-permute-start.12 = (bf16[4,272,128]{2,1,0:T(8,128)(2,1)S(1)}, bf16[4,272,128]{2,1,0:T(8,128)(2,1)S(1)}, u32[]{:S(2)}, u32[]{:S(2)}) collective-permute-start(bf16[4,272,128]{2,1,0:T(8,128)(2,1)S(1)} %pad_maximum_fusion.5), channel_id=1, source_target_pairs={{0,8},{8,16},{16,24},{24,0},{1,9},{9,17},{17,25},{25,1},{2,10},{10... | collective-permute-start | bytes 835592 | tf_op jit(solution)/shard_map/ppermute | solution.py:263
  72.5 31.5 %collective-permute-start.18 = (bf16[8,256,128]{2,1,0:T(8,128)(2,1)S(1)}, bf16[8,256,128]{2,1,0:T(8,128)(2,1)S(1)}, u32[]{:S(2)}, u32[]{:S(2)}) collective-permute-start(bf16[8,256,128]{2,1,0:T(8,128)(2,1)S(1)} %get-tuple-element.40), channel_id=1, source_target_pairs={{0,24},{8,0},{16,8},{24,16},{1,25},{9,1},{17,9},{25,17},{2,26},{10... | collective-permute-start | bytes 1572872 | tf_op jit(solution)/shard_map/ppermute | solution.py:263
  72.6 31.4 %collective-permute-start.20 = (bf16[8,256,128]{2,1,0:T(8,128)(2,1)S(1)}, bf16[8,256,128]{2,1,0:T(8,128)(2,1)S(1)}, u32[]{:S(2)}, u32[]{:S(2)}) collective-permute-start(bf16[8,256,128]{2,1,0:T(8,128)(2,1)S(1)} %get-tuple-element.42), channel_id=1, source_target_pairs={{0,8},{8,16},{16,24},{24,0},{1,9},{9,17},{17,25},{25,1},{2,10},{10... | collective-permute-start | bytes 1572872 | tf_op jit(solution)/shard_map/ppermute | solution.py:263
  89.3 14.7 %collective-permute-start.19 = (bf16[8,256,128]{2,1,0:T(8,128)(2,1)S(1)}, bf16[8,256,128]{2,1,0:T(8,128)(2,1)S(1)}, u32[]{:S(2)}, u32[]{:S(2)}) collective-permute-start(bf16[8,256,128]{2,1,0:T(8,128)(2,1)S(1)} %get-tuple-element.41), channel_id=1, source_target_pairs={{0,16},{8,24},{16,0},{24,8},{1,17},{9,25},{17,1},{25,9},{2,18},{10... | collective-permute-start | bytes 1572872 | tf_op jit(solution)/shard_map/ppermute | solution.py:263
  105.1 21.9 %all-to-all-start = ((bf16[8,256,128]{2,1,0:T(8,128)(2,1)}), bf16[8,256,128]{2,1,0:T(8,128)(2,1)S(1)}, u32[]{:S(2)}, u32[]{:S(2)}) async-start(bf16[8,256,128]{2,1,0:T(8,128)(2,1)} %add.164), calls=%async_computation | async-start | bytes 1048576 | tf_op jit(solution)/shard_map/all_to_all | solution.py:349
  108.7 12.0 %collective-permute-start.17 = (bf16[256,128]{1,0:T(8,128)(2,1)S(1)}, bf16[256,128]{1,0:T(8,128)(2,1)S(1)}, u32[]{:S(2)}, u32[]{:S(2)}) collective-permute-start(bf16[256,128]{1,0:T(8,128)(2,1)S(1)} %get-tuple-element.54), channel_id=1, source_target_pairs={{0,2},{2,4},{4,6},{6,0},{1,3},{3,5},{5,7},{7,1},{8,10},{10,12},{12... | collective-permute-start | bytes 196616 | tf_op jit(solution)/shard_map/ppermute | solution.py:352
  111.1 9.9 %collective-permute-start.16 = (bf16[256,128]{1,0:T(8,128)(2,1)S(1)}, bf16[256,128]{1,0:T(8,128)(2,1)S(1)}, u32[]{:S(2)}, u32[]{:S(2)}) collective-permute-start(bf16[256,128]{1,0:T(8,128)(2,1)S(1)} %get-tuple-element.55), channel_id=1, source_target_pairs={{0,4},{2,6},{4,0},{6,2},{1,5},{3,7},{5,1},{7,3},{8,12},{10,14},{12... | collective-permute-start | bytes 196616 | tf_op jit(solution)/shard_map/ppermute | solution.py:352
  129.0 6.8 %collective-permute-start.24 = (f32[40,128]{1,0:T(8,128)S(1)}, f32[40,128]{1,0:T(8,128)S(1)}, u32[]{:S(2)}, u32[]{:S(2)}) collective-permute-start(f32[40,128]{1,0:T(8,128)S(1)} %add.90), channel_id=1, source_target_pairs={{0,6},{2,0},{4,2},{6,4},{1,7},{3,1},{5,3},{7,5},{8,14},{10,8},{12,... | collective-permute-start | bytes 61448 | tf_op jit(solution)/shard_map/ppermute | solution.py:239
  137.3 9.5 %collective-permute-start.27 = (f32[40,128]{1,0:T(8,128)S(1)}, f32[40,128]{1,0:T(8,128)S(1)}, u32[]{:S(2)}, u32[]{:S(2)}) collective-permute-start(f32[40,128]{1,0:T(8,128)S(1)} %add_add_fusion.2), channel_id=1, source_target_pairs={{0,24},{8,0},{16,8},{24,16},{1,25},{9,1},{17,9},{25,17},{2,26},{10... | collective-permute-start | bytes 61448 | tf_op jit(solution)/shard_map/ppermute | solution.py:239
  150.7 7.8 %collective-permute-start.28 = (f32[40,128]{1,0:T(8,128)S(1)}, f32[40,128]{1,0:T(8,128)S(1)}, u32[]{:S(2)}, u32[]{:S(2)}) collective-permute-start(f32[40,128]{1,0:T(8,128)S(1)} %add_add_fusion.1), channel_id=1, source_target_pairs={{0,128},{32,160},{64,192},{96,224},{128,0},{160,32},{192,64},{224,... | collective-permute-start | bytes 61448 | tf_op jit(solution)/shard_map/ppermute | solution.py:366
  158.5 6.8 %collective-permute-start.31 = (f32[40,128]{1,0:T(8,128)S(1)}, f32[40,128]{1,0:T(8,128)S(1)}, u32[]{:S(2)}, u32[]{:S(2)}) collective-permute-start(f32[40,128]{1,0:T(8,128)S(1)} %add.97), channel_id=1, source_target_pairs={{0,96},{32,128},{64,160},{96,192},{128,224},{160,0},{192,32},{224,... | collective-permute-start | bytes 61448 | tf_op jit(solution)/shard_map/ppermute | solution.py:239
  158.5 6.8 %collective-permute-start.30 = (f32[40,128]{1,0:T(8,128)S(1)}, f32[40,128]{1,0:T(8,128)S(1)}, u32[]{:S(2)}, u32[]{:S(2)}) collective-permute-start(f32[40,128]{1,0:T(8,128)S(1)} %add.97), channel_id=1, source_target_pairs={{0,64},{32,96},{64,128},{96,160},{128,192},{160,224},{192,0},{224,... | collective-permute-start | bytes 61448 | tf_op jit(solution)/shard_map/ppermute | solution.py:239
  (15 other events, 162.7 us)
